TPU v7x, 32 devices: a whole 2x2x4 slice. The times are simulated.
32 devices in a mesh: rows: 8 (over z, y), cols: 2 (over x), dp: 2 (over core).
Axes of the slice: x: 2, y: 2, z: 4, core: 2. Of those that a mesh axis runs over, the one named last changes fastest.
Arguments:
- features: bfloat16 [2, 32, 256, 512], P('dp', None, 'rows', 'cols'), may hold values from -6 to 6
- shifts: int32 [2, 32, 2], P('dp'), may hold values from -16 to 16, as said below
- first_kernel: bfloat16 [9, 32, 32], replicated, may hold values from -0.375 to 0.375
- bottle_kernel: bfloat16 [9, 32, 32], replicated, may hold values from -0.375 to 0.375
- second_kernel: bfloat16 [9, 32, 32], replicated, may hold values from -0.375 to 0.375
- cotangent: bfloat16 [2, 32, 256, 512], P('dp', None, 'rows', 'cols'), may hold values from -6 to 6
Outputs:
- prediction: bfloat16 [2, 32, 256, 512], P('dp', None, 'rows', 'cols')
- first_grad: float32 [9, 32, 32], replicated
- second_grad: float32 [9, 32, 32], replicated
Inputs may be any that keep to these rules, and one draw needn't show every extreme that they name: `shifts`: every image has one channel displaced by exactly 16 and another by exactly -16 along one direction.
All inputs are finite; a program needn't handle non-finite values.
Results may differ from a plain program's by a relative error of at most 0.0059.
Values may be sent and summed in bfloat16 or wider, within the bound.
No kernel may reach another device: no remote copies, remote signals or barrier semaphores. Data moves between devices by JAX's collectives and lax.ppermute only.
A program may use at most 64 MiB of HBM per device.

v0:
```python
import math

import jax
import jax.numpy as jnp
from jax import lax
from jax.sharding import PartitionSpec as P

MAXSHIFT = 16
POOL = 4


def padded(block, sides, width):
    for axis, dim in sides:
        count = lax.axis_size(axis)
        forward = [(i, i + 1) for i in range(count - 1)]
        backward = [(target, source) for source, target in forward]
        low = lax.ppermute(
            lax.slice_in_dim(block, block.shape[dim] - width, None, axis=dim), axis, forward
        )
        high = lax.ppermute(lax.slice_in_dim(block, 0, width, axis=dim), axis, backward)
        block = jnp.concatenate([low, block, high], axis=dim)
    return block


def stored(values):
    return lax.optimization_barrier(values.astype(jnp.bfloat16))


def convolve_ext(extended, kernel, transpose):
    height = extended.shape[2] - 2
    span = extended.shape[3] - 2
    result = None
    for tap_index in range(9):
        row_off = tap_index // 3 - 1
        col_off = tap_index % 3 - 1
        if transpose:
            window = extended[
                :, :, 1 - row_off : 1 - row_off + height, 1 - col_off : 1 - col_off + span
            ]
            term = jnp.einsum(
                "oi,bohw->bihw", kernel[tap_index], window, preferred_element_type=jnp.float32
            )
        else:
            window = extended[
                :, :, 1 + row_off : 1 + row_off + height, 1 + col_off : 1 + col_off + span
            ]
            term = jnp.einsum(
                "oi,bihw->bohw", kernel[tap_index], window, preferred_element_type=jnp.float32
            )
        result = term if result is None else result + term
    return result


def correlate(grad_out, extended):
    height = grad_out.shape[2]
    span = grad_out.shape[3]
    pieces = []
    for tap_index in range(9):
        row_off = tap_index // 3 - 1
        col_off = tap_index % 3 - 1
        window = extended[
            :, :, 1 + row_off : 1 + row_off + height, 1 + col_off : 1 + col_off + span
        ]
        pieces.append(
            jnp.einsum("bohw,bihw->oi", grad_out, window, preferred_element_type=jnp.float32)
        )
    return jnp.stack(pieces)


def pool_sum(values):
    shape = values.shape
    return values.reshape(shape[0], shape[1], shape[2] // POOL, POOL, shape[3] // POOL, POOL).sum(
        axis=(3, 5)
    )


def upsample(values):
    return jnp.repeat(jnp.repeat(values, POOL, axis=2), POOL, axis=3)


def warp_planes(rimmed, shifts, margin_in, margin_out, height, span):

    def single_plane(channel_plane, row_shift, col_shift):
        return lax.dynamic_slice(
            channel_plane,
            (margin_in - margin_out + row_shift, margin_in - margin_out + col_shift),
            (height + 2 * margin_out, span + 2 * margin_out),
        )

    return jax.vmap(jax.vmap(single_plane))(rimmed, shifts[..., 0], shifts[..., 1])


def coarse_conv(coarse_in, kernel, transpose):
    extended = padded(coarse_in, (("rows", 2), ("cols", 3)), 1)
    return convolve_ext(extended, kernel, transpose)


def shards(features, shifts, first_kernel, bottle_kernel, second_kernel, cotangent):
    height = features.shape[2]
    span = features.shape[3]
    rimmed = padded(features, (("rows", 2), ("cols", 3)), MAXSHIFT)
    warped = warp_planes(rimmed, shifts, MAXSHIFT, 0, height, span)
    warped_ext = padded(warped, (("rows", 2), ("cols", 3)), 1)
    first_pre = convolve_ext(warped_ext, first_kernel, False)
    first_act = stored(jax.nn.silu(first_pre))
    pooled = stored(pool_sum(first_act.astype(jnp.float32)) / (POOL * POOL))
    bottle = coarse_conv(pooled, bottle_kernel, False)
    blended = stored(first_act.astype(jnp.float32) + upsample(bottle))
    channels = blended.shape[1]
    both_ext = padded(jnp.concatenate((blended, cotangent), axis=1), (("rows", 2), ("cols", 3)), 1)
    blended_ext = both_ext[:, :channels]
    cotangent_ext = both_ext[:, channels:]
    prediction = convolve_ext(blended_ext, second_kernel, False).astype(jnp.bfloat16)
    factor = 1.0 / math.sqrt(
        features.shape[0]
        * lax.axis_size("dp")
        * height
        * lax.axis_size("rows")
        * span
        * lax.axis_size("cols")
    )
    second_grad = correlate(cotangent, blended_ext) * factor
    blend_grad = stored(convolve_ext(cotangent_ext, second_kernel, True))
    coarse_grad = stored(pool_sum(blend_grad.astype(jnp.float32)))
    pooled_grad = coarse_conv(coarse_grad, bottle_kernel, True)
    act_grad = blend_grad.astype(jnp.float32) + upsample(pooled_grad) / (POOL * POOL)
    sigma = jax.nn.sigmoid(first_pre)
    pre_grad = (act_grad * sigma * (1.0 + first_pre * (1.0 - sigma))).astype(jnp.bfloat16)
    first_grad = correlate(pre_grad, warped_ext) * factor
    first_grad, second_grad = lax.psum((first_grad, second_grad), ("rows", "cols", "dp"))
    return (prediction, first_grad, second_grad)


def solution(mesh):
    placed = (
        P("dp", None, "rows", "cols"),
        P("dp", None, None),
        P(),
        P(),
        P(),
        P("dp", None, "rows", "cols"),
    )
    return jax.shard_map(
        shards,
        mesh=mesh,
        in_specs=placed,
        out_specs=(P("dp", None, "rows", "cols"), P(), P()),
        check_vma=False,
    )
```

profile of v0, /device:TPU:0, one launch (start us, length us, event | category | flops | bytes accessed | tf_op | source)
XLA Modules:
  0.0 413.2 jit_solution(12324718184134417861)
XLA Ops:
  8.3 4.9 %collective-permute-start = (bf16[1,32,16,256]{3,2,1,0:T(8,128)(2,1)S(1)}, bf16[1,32,16,256]{3,2,1,0:T(8,128)(2,1)S(1)}, u32[]{:S(2)}, u32[]{:S(2)}) collective-permute-start(bf16[1,32,16,256]{3,2,1,0:T(8,128)(2,1)S(1)} %get-tuple-element.51), channel_id=1, source_target_pairs={{0,4},{4,8},{8,12},{12,16},{16,20},{20,24},{24,28},{1,5},{5,9},{9,... | collective-permute-start | bytes 786440 | tf_op jit(solution)/shard_map/ppermute | solution.py:17
  15.3 9.1 %collective-permute-done = bf16[1,32,16,256]{3,2,1,0:T(8,128)(2,1)S(1)} collective-permute-done((bf16[1,32,16,256]{3,2,1,0:T(8,128)(2,1)S(1)}, bf16[1,32,16,256]{3,2,1,0:T(8,128)(2,1)S(1)}, u32[]{:S(2)}, u32[]{:S(2)}) %collective-permute-start) | collective-permute-done | bytes 262176 | tf_op jit(solution)/shard_map/ppermute | solution.py:17
  24.8 3.4 collective-permute-start.2
  29.6 7.0 %collective-permute-done.2 = bf16[1,32,64,16]{3,2,1,0:T(8,128)(2,1)S(1)} collective-permute-done((bf16[1,32,64,16]{3,2,1,0:T(8,128)(2,1)S(1)}, bf16[1,32,64,16]{3,2,1,0:T(8,128)(2,1)S(1)}, u32[]{:S(2)}, u32[]{:S(2)}) %collective-permute-start.2) | collective-permute-done | bytes 65568 | tf_op jit(solution)/shard_map/ppermute | solution.py:17
  36.6 4.1 %collective-permute-done.3 = bf16[1,32,64,16]{3,2,1,0:T(8,128)(2,1)S(1)} collective-permute-done((bf16[1,32,64,16]{3,2,1,0:T(8,128)(2,1)S(1)}, bf16[1,32,64,16]{3,2,1,0:T(8,128)(2,1)S(1)}, u32[]{:S(2)}, u32[]{:S(2)}) %collective-permute-start.3) | collective-permute-done | bytes 65568 | tf_op jit(solution)/shard_map/ppermute | solution.py:20
  41.8 85.4 %while.1 = (s32[]{:T(128)}, bf16[1,32,64,288]{3,2,1,0:T(8,128)(2,1)S(1)}, s32[32,4]{0,1:T(4,128)S(1)}, bf16[32,32,256]{2,1,0:T(8,128)(2,1)S(1)}, s32[]{:T(128)}) while((s32[]{:T(128)}, bf16[1,32,64,288]{3,2,1,0:T(8,128)(2,1)S(1)}, s32[32,4]{0,1:T(4,128)S(1)}, bf16[32,32,256]{2,1,0:T(8,128)(2,1)S(1)}, s32[]{:T(128)}) %tuple.45), condition=%wide.while_cond, body=%wide.while_body.sunk | while | flops 2 | bytes 32905 | solution.py:84
  127.5 6.3 %collective-permute-start.4 = (bf16[1,32,1,256]{3,1,2,0:T(8,128)(2,1)S(1)}, bf16[1,32,1,256]{3,1,2,0:T(8,128)(2,1)S(1)}, u32[]{:S(2)}, u32[]{:S(2)}) collective-permute-start(bf16[1,32,1,256]{3,1,2,0:T(8,128)(2,1)S(1)} %get-tuple-element.48), channel_id=1, source_target_pairs={{0,4},{4,8},{8,12},{12,16},{16,20},{20,24},{24,28},{1,5},{5,9},{9,... | collective-permute-start | bytes 49160 | tf_op jit(solution)/shard_map/ppermute | solution.py:17
  135.2 5.6 %collective-permute-done.5 = bf16[1,32,1,256]{3,1,2,0:T(8,128)(2,1)S(1)} collective-permute-done((bf16[1,32,1,256]{3,1,2,0:T(8,128)(2,1)S(1)}, bf16[1,32,1,256]{3,1,2,0:T(8,128)(2,1)S(1)}, u32[]{:S(2)}, u32[]{:S(2)}) %collective-permute-start.5) | collective-permute-done | bytes 16416 | tf_op jit(solution)/shard_map/ppermute | solution.py:20
  146.5 4.4 %collective-permute-done.7 = bf16[1,32,34,1]{3,1,2,0:T(8,128)(2,1)S(1)} collective-permute-done((bf16[1,32,34,1]{3,1,2,0:T(8,128)(2,1)S(1)}, bf16[1,32,34,1]{3,1,2,0:T(8,128)(2,1)S(1)}, u32[]{:S(2)}, u32[]{:S(2)}) %collective-permute-start.7) | collective-permute-done | bytes 2208 | tf_op jit(solution)/shard_map/ppermute | solution.py:20
  157.7 3.6 reduce_sum.18
  161.5 4.8 %collective-permute-start.8 = (bf16[1,32,1,64]{3,1,2,0:T(8,128)(2,1)S(1)}, bf16[1,32,1,64]{3,1,2,0:T(8,128)(2,1)S(1)}, u32[]{:S(2)}, u32[]{:S(2)}) collective-permute-start(bf16[1,32,1,64]{3,1,2,0:T(8,128)(2,1)S(1)} %get-tuple-element.62), channel_id=1, source_target_pairs={{0,4},{4,8},{8,12},{12,16},{16,20},{20,24},{24,28},{1,5},{5,9},{9,... | collective-permute-start | bytes 12296 | tf_op jit(solution)/shard_map/ppermute | solution.py:17
  175.5 4.3 %collective-permute-done.11 = bf16[1,32,10,1]{3,1,2,0:T(8,128)(2,1)S(1)} collective-permute-done((bf16[1,32,10,1]{3,1,2,0:T(8,128)(2,1)S(1)}, bf16[1,32,10,1]{3,1,2,0:T(8,128)(2,1)S(1)}, u32[]{:S(2)}, u32[]{:S(2)}) %collective-permute-start.11) | collective-permute-done | bytes 672 | tf_op jit(solution)/shard_map/ppermute | solution.py:20
  182.3 2.5 broadcast_in_dim.20
  184.9 4.1 copy.152
  190.4 4.5 %collective-permute-start.12 = (bf16[1,64,1,256]{3,1,2,0:T(8,128)(2,1)S(1)}, bf16[1,64,1,256]{3,1,2,0:T(8,128)(2,1)S(1)}, u32[]{:S(2)}, u32[]{:S(2)}) collective-permute-start(bf16[1,64,1,256]{3,1,2,0:T(8,128)(2,1)S(1)} %get-tuple-element.40), channel_id=1, source_target_pairs={{0,4},{4,8},{8,12},{12,16},{16,20},{20,24},{24,28},{1,5},{5,9},{9,... | collective-permute-start | bytes 98312 | tf_op jit(solution)/shard_map/ppermute | solution.py:17
  209.8 3.2 maximum_maximum_fusion
  224.4 3.3 copy.168
  227.7 3.6 reduce_sum.19
  232.9 5.0 %collective-permute-start.16 = (bf16[1,32,1,64]{3,1,2,0:T(8,128)(2,1)S(1)}, bf16[1,32,1,64]{3,1,2,0:T(8,128)(2,1)S(1)}, u32[]{:S(2)}, u32[]{:S(2)}) collective-permute-start(bf16[1,32,1,64]{3,1,2,0:T(8,128)(2,1)S(1)} %get-tuple-element.60), channel_id=1, source_target_pairs={{0,4},{4,8},{8,12},{12,16},{16,20},{20,24},{24,28},{1,5},{5,9},{9,... | collective-permute-start | bytes 12296 | tf_op jit(solution)/shard_map/ppermute | solution.py:17
  249.1 4.8 %collective-permute-start.19 = (bf16[1,32,10,1]{3,1,2,0:T(8,128)(2,1)S(1)}, bf16[1,32,10,1]{3,1,2,0:T(8,128)(2,1)S(1)}, u32[]{:S(2)}, u32[]{:S(2)}) collective-permute-start(bf16[1,32,10,1]{3,1,2,0:T(8,128)(2,1)S(1)} %get-tuple-element.55), channel_id=1, source_target_pairs={{0,2},{1,3},{4,6},{5,7},{8,10},{9,11},{12,14},{13,15},{16,18},{17,... | collective-permute-start | bytes 1928 | tf_op jit(solution)/shard_map/ppermute | solution.py:17
  260.4 2.5 broadcast_in_dim.23
  263.0 4.8 %copy.180 = f32[1,32,32,256]{3,1,2,0:T(8,128)} copy(f32[1,32,32,256]{2,1,3,0:T(8,128)} %bitcast.522) | data formatting | bytes 2097152 | tf_op jit(solution)/shard_map/div | solution.py:126
  274.2 3.7 fusion.11
  279.0 124.2 %all-reduce.3.cloned.1.call-done = (f32[9,32,32]{2,1,0:T(8,128)}, f32[9,32,32]{2,1,0:T(8,128)}) async-done(((f32[9,32,32]{2,1,0:T(8,128)}, f32[9,32,32]{2,1,0:T(8,128)}), (f32[9,32,32]{2,1,0:T(8,128)}, f32[9,32,32]{2,1,0:T(8,128)})) %all-reduce.3.cloned.1.call-update) | async-done | bytes 73744 | tf_op jit(solution)/shard_map/psum | solution.py:130
  (277 shorter events, 174.6 us)
Async XLA Ops:
  7.2 17.3 %copy-start.16 = (bf16[1,32,32,256]{3,2,1,0:T(8,128)(2,1)S(1)}, bf16[1,32,32,256]{3,2,1,0:T(8,128)(2,1)}, u32[]{:S(2)}) copy-start(bf16[1,32,32,256]{3,2,1,0:T(8,128)(2,1)} %param.6) | copy-start | bytes 1572868
  7.2 396.0 %all-reduce.3.cloned.1.call-start = ((), (), s32[]{:S(2)}) async-start(), calls=%async_computation | async-start | bytes 589824 | tf_op jit(solution)/shard_map/psum | solution.py:130
  8.3 16.0 %collective-permute-start = (bf16[1,32,16,256]{3,2,1,0:T(8,128)(2,1)S(1)}, bf16[1,32,16,256]{3,2,1,0:T(8,128)(2,1)S(1)}, u32[]{:S(2)}, u32[]{:S(2)}) collective-permute-start(bf16[1,32,16,256]{3,2,1,0:T(8,128)(2,1)S(1)} %get-tuple-element.51), channel_id=1, source_target_pairs={{0,4},{4,8},{8,12},{12,16},{16,20},{20,24},{24,28},{1,5},{5,9},{9,... | collective-permute-start | bytes 786440 | tf_op jit(solution)/shard_map/ppermute | solution.py:17
  13.2 11.2 %collective-permute-start.1 = (bf16[1,32,16,256]{3,2,1,0:T(8,128)(2,1)S(1)}, bf16[1,32,16,256]{3,2,1,0:T(8,128)(2,1)S(1)}, u32[]{:S(2)}, u32[]{:S(2)}) collective-permute-start(bf16[1,32,16,256]{3,2,1,0:T(8,128)(2,1)S(1)} %get-tuple-element.50), channel_id=1, source_target_pairs={{4,0},{8,4},{12,8},{16,12},{20,16},{24,20},{28,24},{5,1},{9,5},{13... | collective-permute-start | bytes 786440 | tf_op jit(solution)/shard_map/ppermute | solution.py:20
  24.8 11.8 %collective-permute-start.2 = (bf16[1,32,64,16]{3,2,1,0:T(8,128)(2,1)S(1)}, bf16[1,32,64,16]{3,2,1,0:T(8,128)(2,1)S(1)}, u32[]{:S(2)}, u32[]{:S(2)}) collective-permute-start(bf16[1,32,64,16]{3,2,1,0:T(8,128)(2,1)S(1)} %get-tuple-element.42), channel_id=1, source_target_pairs={{0,2},{1,3},{4,6},{5,7},{8,10},{9,11},{12,14},{13,15},{16,18},{17,... | collective-permute-start | bytes 196616 | tf_op jit(solution)/shard_map/ppermute | solution.py:17
  28.2 12.5 %collective-permute-start.3 = (bf16[1,32,64,16]{3,2,1,0:T(8,128)(2,1)S(1)}, bf16[1,32,64,16]{3,2,1,0:T(8,128)(2,1)S(1)}, u32[]{:S(2)}, u32[]{:S(2)}) collective-permute-start(bf16[1,32,64,16]{3,2,1,0:T(8,128)(2,1)S(1)} %get-tuple-element.43), channel_id=1, source_target_pairs={{2,0},{3,1},{6,4},{7,5},{10,8},{11,9},{14,12},{15,13},{18,16},{19,... | collective-permute-start | bytes 196616 | tf_op jit(solution)/shard_map/ppermute | solution.py:20
  127.2 25.6 %copy-start.14 = (bf16[32,32,256]{2,1,0:T(8,128)(2,1)}, bf16[32,32,256]{2,1,0:T(8,128)(2,1)S(1)}, u32[]{:S(2)}) copy-start(bf16[32,32,256]{2,1,0:T(8,128)(2,1)S(1)} %get-tuple-element.10) | copy-start | bytes 1572868
  127.2 16.6 %copy-start.21 = (bf16[9,32,32]{2,1,0:T(8,128)(2,1)S(1)}, bf16[9,32,32]{2,1,0:T(8,128)(2,1)}, u32[]{:S(2)}) copy-start(bf16[9,32,32]{2,1,0:T(8,128)(2,1)} %param.8) | copy-start | bytes 55300
  127.5 7.7 %collective-permute-start.4 = (bf16[1,32,1,256]{3,1,2,0:T(8,128)(2,1)S(1)}, bf16[1,32,1,256]{3,1,2,0:T(8,128)(2,1)S(1)}, u32[]{:S(2)}, u32[]{:S(2)}) collective-permute-start(bf16[1,32,1,256]{3,1,2,0:T(8,128)(2,1)S(1)} %get-tuple-element.48), channel_id=1, source_target_pairs={{0,4},{4,8},{8,12},{12,16},{16,20},{20,24},{24,28},{1,5},{5,9},{9,... | collective-permute-start | bytes 49160 | tf_op jit(solution)/shard_map/ppermute | solution.py:17
  133.8 7.0 %collective-permute-start.5 = (bf16[1,32,1,256]{3,1,2,0:T(8,128)(2,1)S(1)}, bf16[1,32,1,256]{3,1,2,0:T(8,128)(2,1)S(1)}, u32[]{:S(2)}, u32[]{:S(2)}) collective-permute-start(bf16[1,32,1,256]{3,1,2,0:T(8,128)(2,1)S(1)} %get-tuple-element.49), channel_id=1, source_target_pairs={{4,0},{8,4},{12,8},{16,12},{20,16},{24,20},{28,24},{5,1},{9,5},{13... | collective-permute-start | bytes 49160 | tf_op jit(solution)/shard_map/ppermute | solution.py:20
  141.0 5.5 %collective-permute-start.6 = (bf16[1,32,34,1]{3,1,2,0:T(8,128)(2,1)S(1)}, bf16[1,32,34,1]{3,1,2,0:T(8,128)(2,1)S(1)}, u32[]{:S(2)}, u32[]{:S(2)}) collective-permute-start(bf16[1,32,34,1]{3,1,2,0:T(8,128)(2,1)S(1)} %get-tuple-element.46), channel_id=1, source_target_pairs={{0,2},{1,3},{4,6},{5,7},{8,10},{9,11},{12,14},{13,15},{16,18},{17,... | collective-permute-start | bytes 6536 | tf_op jit(solution)/shard_map/ppermute | solution.py:17
  142.5 8.4 %collective-permute-start.7 = (bf16[1,32,34,1]{3,1,2,0:T(8,128)(2,1)S(1)}, bf16[1,32,34,1]{3,1,2,0:T(8,128)(2,1)S(1)}, u32[]{:S(2)}, u32[]{:S(2)}) collective-permute-start(bf16[1,32,34,1]{3,1,2,0:T(8,128)(2,1)S(1)} %get-tuple-element.47), channel_id=1, source_target_pairs={{2,0},{3,1},{6,4},{7,5},{10,8},{11,9},{14,12},{15,13},{18,16},{19,... | collective-permute-start | bytes 6536 | tf_op jit(solution)/shard_map/ppermute | solution.py:20
  161.5 7.9 %collective-permute-start.8 = (bf16[1,32,1,64]{3,1,2,0:T(8,128)(2,1)S(1)}, bf16[1,32,1,64]{3,1,2,0:T(8,128)(2,1)S(1)}, u32[]{:S(2)}, u32[]{:S(2)}) collective-permute-start(bf16[1,32,1,64]{3,1,2,0:T(8,128)(2,1)S(1)} %get-tuple-element.62), channel_id=1, source_target_pairs={{0,4},{4,8},{8,12},{12,16},{16,20},{20,24},{24,28},{1,5},{5,9},{9,... | collective-permute-start | bytes 12296 | tf_op jit(solution)/shard_map/ppermute | solution.py:17
  166.3 5.5 %collective-permute-start.9 = (bf16[1,32,1,64]{3,1,2,0:T(8,128)(2,1)S(1)}, bf16[1,32,1,64]{3,1,2,0:T(8,128)(2,1)S(1)}, u32[]{:S(2)}, u32[]{:S(2)}) collective-permute-start(bf16[1,32,1,64]{3,1,2,0:T(8,128)(2,1)S(1)} %get-tuple-element.63), channel_id=1, source_target_pairs={{4,0},{8,4},{12,8},{16,12},{20,16},{24,20},{28,24},{5,1},{9,5},{13... | collective-permute-start | bytes 12296 | tf_op jit(solution)/shard_map/ppermute | solution.py:20
  172.0 3.5 collective-permute-start.10
  173.5 6.3 %collective-permute-start.11 = (bf16[1,32,10,1]{3,1,2,0:T(8,128)(2,1)S(1)}, bf16[1,32,10,1]{3,1,2,0:T(8,128)(2,1)S(1)}, u32[]{:S(2)}, u32[]{:S(2)}) collective-permute-start(bf16[1,32,10,1]{3,1,2,0:T(8,128)(2,1)S(1)} %get-tuple-element.59), channel_id=1, source_target_pairs={{2,0},{3,1},{6,4},{7,5},{10,8},{11,9},{14,12},{15,13},{18,16},{19,... | collective-permute-start | bytes 1928 | tf_op jit(solution)/shard_map/ppermute | solution.py:20
  189.1 7.1 %collective-permute-start.13 = (bf16[1,64,1,256]{3,1,2,0:T(8,128)(2,1)S(1)}, bf16[1,64,1,256]{3,1,2,0:T(8,128)(2,1)S(1)}, u32[]{:S(2)}, u32[]{:S(2)}) collective-permute-start(bf16[1,64,1,256]{3,1,2,0:T(8,128)(2,1)S(1)} %get-tuple-element.41), channel_id=1, source_target_pairs={{4,0},{8,4},{12,8},{16,12},{20,16},{24,20},{28,24},{5,1},{9,5},{13... | collective-permute-start | bytes 98312 | tf_op jit(solution)/shard_map/ppermute | solution.py:20
  190.4 6.1 %collective-permute-start.12 = (bf16[1,64,1,256]{3,1,2,0:T(8,128)(2,1)S(1)}, bf16[1,64,1,256]{3,1,2,0:T(8,128)(2,1)S(1)}, u32[]{:S(2)}, u32[]{:S(2)}) collective-permute-start(bf16[1,64,1,256]{3,1,2,0:T(8,128)(2,1)S(1)} %get-tuple-element.40), channel_id=1, source_target_pairs={{0,4},{4,8},{8,12},{12,16},{16,20},{20,24},{24,28},{1,5},{5,9},{9,... | collective-permute-start | bytes 98312 | tf_op jit(solution)/shard_map/ppermute | solution.py:17
  199.1 8.4 %collective-permute-start.14 = (bf16[1,64,34,1]{1,2,3,0:T(8,128)(2,1)S(1)}, bf16[1,64,34,1]{1,2,3,0:T(8,128)(2,1)S(1)}, u32[]{:S(2)}, u32[]{:S(2)}) collective-permute-start(bf16[1,64,34,1]{1,2,3,0:T(8,128)(2,1)S(1)} %copy.154), channel_id=1, source_target_pairs={{0,2},{1,3},{4,6},{5,7},{8,10},{9,11},{12,14},{13,15},{16,18},{17,... | collective-permute-start | bytes 13064 | tf_op jit(solution)/shard_map/ppermute | solution.py:17
  201.0 7.7 %collective-permute-start.15 = (bf16[1,64,34,1]{1,2,3,0:T(8,128)(2,1)S(1)}, bf16[1,64,34,1]{1,2,3,0:T(8,128)(2,1)S(1)}, u32[]{:S(2)}, u32[]{:S(2)}) collective-permute-start(bf16[1,64,34,1]{1,2,3,0:T(8,128)(2,1)S(1)} %copy.156), channel_id=1, source_target_pairs={{2,0},{3,1},{6,4},{7,5},{10,8},{11,9},{14,12},{15,13},{18,16},{19,... | collective-permute-start | bytes 13064 | tf_op jit(solution)/shard_map/ppermute | solution.py:20
  231.4 16.3 %collective-permute-start.17 = (bf16[1,32,1,64]{3,1,2,0:T(8,128)(2,1)S(1)}, bf16[1,32,1,64]{3,1,2,0:T(8,128)(2,1)S(1)}, u32[]{:S(2)}, u32[]{:S(2)}) collective-permute-start(bf16[1,32,1,64]{3,1,2,0:T(8,128)(2,1)S(1)} %get-tuple-element.61), channel_id=1, source_target_pairs={{4,0},{8,4},{12,8},{16,12},{20,16},{24,20},{28,24},{5,1},{9,5},{13... | collective-permute-start | bytes 12296 | tf_op jit(solution)/shard_map/ppermute | solution.py:20
  232.9 14.8 %collective-permute-start.16 = (bf16[1,32,1,64]{3,1,2,0:T(8,128)(2,1)S(1)}, bf16[1,32,1,64]{3,1,2,0:T(8,128)(2,1)S(1)}, u32[]{:S(2)}, u32[]{:S(2)}) collective-permute-start(bf16[1,32,1,64]{3,1,2,0:T(8,128)(2,1)S(1)} %get-tuple-element.60), channel_id=1, source_target_pairs={{0,4},{4,8},{8,12},{12,16},{16,20},{20,24},{24,28},{1,5},{5,9},{9,... | collective-permute-start | bytes 12296 | tf_op jit(solution)/shard_map/ppermute | solution.py:17
  247.8 6.3 %collective-permute-start.18 = (bf16[1,32,10,1]{3,1,2,0:T(8,128)(2,1)S(1)}, bf16[1,32,10,1]{3,1,2,0:T(8,128)(2,1)S(1)}, u32[]{:S(2)}, u32[]{:S(2)}) collective-permute-start(bf16[1,32,10,1]{3,1,2,0:T(8,128)(2,1)S(1)} %get-tuple-element.54), channel_id=1, source_target_pairs={{2,0},{3,1},{6,4},{7,5},{10,8},{11,9},{14,12},{15,13},{18,16},{19,... | collective-permute-start | bytes 1928 | tf_op jit(solution)/shard_map/ppermute | solution.py:20
  249.1 6.6 %collective-permute-start.19 = (bf16[1,32,10,1]{3,1,2,0:T(8,128)(2,1)S(1)}, bf16[1,32,10,1]{3,1,2,0:T(8,128)(2,1)S(1)}, u32[]{:S(2)}, u32[]{:S(2)}) collective-permute-start(bf16[1,32,10,1]{3,1,2,0:T(8,128)(2,1)S(1)} %get-tuple-element.55), channel_id=1, source_target_pairs={{0,2},{1,3},{4,6},{5,7},{8,10},{9,11},{12,14},{13,15},{16,18},{17,... | collective-permute-start | bytes 1928 | tf_op jit(solution)/shard_map/ppermute | solution.py:17
  (19 other events, 93.0 us)
Sparse Core Ops, SparseCore 0:
  274.3 128.8 all-reduce.2
where the time goes:
time: 415 us; the launch traced here: 413 us
  waiting for transfers between devices  166 us (40%)
  local copies, waits for them, and re-layouts  122 us (29%)
  starting transfers between devices  51.4 us (12%)
  matrix products  43 us (10%)
  other arithmetic  16.2 us (4%)
  between operations  14.7 us (4%)
    psum x1, waiting for transfers between devices, shards(): lax.psum((first_grad, second_grad), ('rows', 'cols', 'dp'))  124 us
    gather x96, local copies, waits for them, and re-layouts  85.3 us
    ppermute x10, starting transfers between devices, padded(): lax.ppermute(lax.slice_in_dim(block, block.shape[dim] - width, None, axis...  38.2 us
    ppermute x10, waiting for transfers between devices, padded(): lax.ppermute(lax.slice_in_dim(block, block.shape[dim] - width, None, axis...  21 us
    ppermute x10, waiting for transfers between devices, padded(): lax.ppermute(lax.slice_in_dim(block, 0, width, axis=dim), axis, backward)  21 us
    dot_general x27, matrix products, convolve_ext(): jnp.einsum('oi,bihw->bohw', kernel[tap_index], window, preferred_element_...  19.6 us
    dot_general x18, matrix products, correlate(): jnp.einsum('bohw,bihw->oi', grad_out, window, preferred_element_type=jnp....  13.9 us
    ppermute x10, starting transfers between devices, padded(): lax.ppermute(lax.slice_in_dim(block, 0, width, axis=dim), axis, backward)  13.2 us
  transfers between devices with their start and end apart: 21, of which 13 were waited for; matrix products, arithmetic and copies ran while one was open for 6% of the time, Pallas kernels for 0%

commit v1 on v0

v1 whole, which is shorter than its diff:
```python
import functools
import math

import jax
import jax.numpy as jnp
from jax import lax
from jax.experimental import pallas as pl
from jax.experimental.pallas import tpu as pltpu
from jax.sharding import PartitionSpec as P


MAXSHIFT = 16
POOL = 4
TILE = 128
SLOT = 32
EXT = 9
FHALO = MAXSHIFT + EXT
CHALO = 5
F32 = jnp.float32
BF16 = jnp.bfloat16
VMEM = pl.BlockSpec(memory_space=pltpu.VMEM)
SMEM = pl.BlockSpec(memory_space=pltpu.SMEM)
LIMIT = 56 * 1024 * 1024


def lanes_of(shape):
    return lax.broadcasted_iota(jnp.int32, shape, len(shape) - 1)


def turn(values, shift):
    width = values.shape[-1]
    return pltpu.roll(values, shift % width, values.ndim - 1)


def sides():
    row, col = lax.axis_index("rows"), lax.axis_index("cols")
    return (
        row > 0,
        row < lax.axis_size("rows") - 1,
        col > 0,
        col < lax.axis_size("cols") - 1,
    )


def pack_kernel(edges, feat, cot, feat_rows, cot_rows, up_msg, down_msg, col_msg, *rest):
    corner_msgs, (fs, cs) = rest[:-2], rest[-2:]
    chans, height, span = feat.shape
    tiles = span // TILE
    for src, dst, out in ((feat, fs, feat_rows), (cot, cs, cot_rows)):
        for c in range(chans):
            for t in range(tiles):
                dst[t, pl.ds(c, height, stride=chans), :] = src[
                    c, :, t * TILE : (t + 1) * TILE
                ].astype(F32)
        for t in range(tiles):
            out[:, t * TILE : (t + 1) * TILE] = dst[t].astype(BF16)
    cut = FHALO * chans
    up_msg[0:cut] = feat_rows[0:cut]
    up_msg[cut:] = cot_rows[0 : CHALO * chans]
    down_msg[0:cut] = feat_rows[(height - FHALO) * chans :]
    down_msg[cut:] = cot_rows[(height - CHALO) * chans :]
    lane = lanes_of((chans, TILE))
    for r in range(height):
        at = slice(r * chans, (r + 1) * chans)
        cots = jnp.where(lane < 2 * SLOT, turn(cs[0, at], SLOT), turn(cs[tiles - 1, at], -SLOT))
        feats = jnp.where(lane < 2 * SLOT, fs[0, at], fs[tiles - 1, at])
        outer = (lane < SLOT) | (lane >= TILE - SLOT)
        col_msg[at] = jnp.where(outer, feats, cots).astype(BF16)
    is_left = lax.axis_index("cols") == 0
    for (vertical, edge), msg in zip(edges, corner_msgs):
        f0 = 0 if vertical == "up" else height - FHALO
        c0 = 0 if vertical == "up" else height - CHALO
        pieces = [(fs, f0 + j) for j in range(FHALO)] + [(cs, c0 + j) for j in range(CHALO)]
        for q in range(0, len(pieces), POOL):
            total = jnp.zeros((chans, TILE), F32)
            for k, (ref, r) in enumerate(pieces[q : q + POOL]):
                at = slice(r * chans, (r + 1) * chans)
                if edge == "left":
                    piece = ref[0, at]
                elif edge == "right":
                    piece = turn(ref[tiles - 1, at], SLOT)
                else:
                    piece = jnp.where(is_left, turn(ref[tiles - 1, at], SLOT), ref[0, at])
                inside = (lane >= k * SLOT) & (lane < (k + 1) * SLOT)
                total = jnp.where(inside, turn(piece, k * SLOT), total)
            msg[(q // POOL) * chans : (q // POOL + 1) * chans] = total.astype(BF16)


def conv_sum(parts, chans, step):
    width = parts.shape[1]
    return (
        pltpu.roll(parts[0:chans], step, 1)
        + parts[chans : 2 * chans]
        + pltpu.roll(parts[2 * chans : 3 * chans], width - step, 1)
    )


def block_sum(values):
    width = values.shape[1]
    lane = lanes_of(values.shape)
    even = (lane & 1) == 0
    pair = values + jnp.where(even, pltpu.roll(values, width - 1, 1), pltpu.roll(values, 1, 1))
    low = (lane & 2) == 0
    return pair + jnp.where(low, pltpu.roll(pair, width - 2, 1), pltpu.roll(pair, 2, 1))


def correlate(u, views, acc, height, chans, span):
    for b in range(3):
        acc[b] = jnp.zeros(acc.shape[1:], F32)

    def group(g, _):
        at = pl.multiple_of(g * POOL * chans, POOL * chans)
        left = u[pl.ds(at, POOL * chans), 0:span]
        for b in range(3):
            right = views[b][pl.ds(at, (POOL + 2) * chans), 0:span]
            acc[b, :, 0 : (POOL + 2) * chans] += lax.dot_general(
                left, right, (((1,), (1,)), ((), ())), preferred_element_type=F32
            )
        return 0

    lax.fori_loop(0, height // POOL, group, 0)


def folded(acc, b, chans):
    total = None
    for k in range(POOL):
        block = acc[b, k * chans : (k + 1) * chans, :]
        block = block if k == 0 else turn(block, -k * chans)
        total = block if total is None else total + block
    return total[:, 0:TILE]


def main_kernel(
    shifts, feat, cot, up, down, col_r, col_l, up_r, up_l, down_r, down_l,
    w_first, w_back, w_bottle, w_bottle_back,
    grads, blended,
    fs, ws, warped, warped_m, warped_p, cots, back, coarse, act_grad, act, pooled, pre_grad, bl_m, bl_p, acc,
):
    chans = shifts.shape[0]
    span = feat.shape[1]
    height = feat.shape[0] // chans
    tiles = span // TILE
    width = span + TILE
    has_up, has_down, has_left, has_right = sides()
    lane = lanes_of((chans, TILE))
    right_lanes = (lane < SLOT) & has_right
    left_lanes = (lane >= TILE - SLOT) & has_left
    wide = lanes_of((chans, width))
    in_cols = (wide < span) | ((wide < span + TILE // 2) & has_right) | (
        (wide >= span + TILE // 2) & has_left
    )

    def rows_at(r, count=1):
        return slice(r * chans, (r + count) * chans)

    def halo_tile(right, left):
        return jnp.where(right_lanes, right, jnp.where(left_lanes, left, 0.0))

    def corner(right_ref, left_ref, slot):
        at, k = rows_at(slot // POOL), slot % POOL
        return halo_tile(
            turn(right_ref[at].astype(F32), -k * SLOT),
            turn(left_ref[at].astype(F32), TILE - SLOT - k * SLOT),
        )

    cots[rows_at(0, CHALO), 0:span] = up[rows_at(FHALO, CHALO)]
    cots[rows_at(CHALO, height), 0:span] = cot[...]
    cots[rows_at(CHALO + height, CHALO), 0:span] = down[rows_at(FHALO, CHALO)]
    for j in range(CHALO):
        cots[rows_at(j), span:width] = corner(up_r, up_l, FHALO + j).astype(BF16)
        cots[rows_at(CHALO + height + j), span:width] = corner(
            down_r, down_l, FHALO + j
        ).astype(BF16)
    for r in range(height):
        cots[rows_at(CHALO + r), span:width] = halo_tile(
            turn(col_r[rows_at(r)].astype(F32), -SLOT), turn(col_l[rows_at(r)].astype(F32), SLOT)
        ).astype(BF16)

    def back_group(g, seen):
        at = pl.multiple_of(g * POOL * chans, POOL * chans)
        parts = jnp.dot(
            w_back[...], cots[pl.ds(at, (POOL + 2) * chans), :], preferred_element_type=F32
        )
        total = None
        for k in range(POOL):
            row = conv_sum(parts[3 * k * chans : 3 * (k + 1) * chans], chans, 1).astype(BF16)
            back[pl.ds(pl.multiple_of(at + k * chans, chans), chans), :] = row[:, 0:span]
            row = row.astype(F32)
            total = row if total is None else total + row
        block = jnp.where(in_cols & seen, block_sum(total), 0.0)
        coarse[pl.ds(pl.multiple_of(g * chans, chans), chans), :] = block.astype(BF16)
        return 0

    groups = height // POOL
    back_group(0, has_up)
    back_group(groups + 1, has_down)
    lax.fori_loop(1, groups + 1, lambda g, _: back_group(g, True), 0)

    def grad_group(g, _):
        parts = jnp.dot(
            w_bottle_back[...],
            coarse[pl.ds(pl.multiple_of(g * chans, chans), 3 * chans), :],
            preferred_element_type=F32,
        )
        mean = conv_sum(parts, chans, POOL)[:, 0:span] * (1.0 / POOL**2)
        for k in range(POOL):
            at = pl.multiple_of((g * POOL + k) * chans, chans)
            act_grad[pl.ds(at, chans), :] = (
                back[pl.ds(pl.multiple_of(at + POOL * chans, chans), chans), :].astype(F32) + mean
            )
        return 0

    lax.fori_loop(0, groups, grad_group, 0)

    for t in range(tiles):
        part = slice(t * TILE, (t + 1) * TILE)
        fs[t, rows_at(0, FHALO)] = up[rows_at(0, FHALO), part].astype(F32)
        fs[t, rows_at(FHALO, height)] = feat[:, part].astype(F32)
        fs[t, rows_at(FHALO + height, FHALO)] = down[rows_at(0, FHALO), part].astype(F32)
    for j in range(FHALO):
        fs[tiles, rows_at(j)] = corner(up_r, up_l, j)
        fs[tiles, rows_at(FHALO + height + j)] = corner(down_r, down_l, j)
    for r in range(height):
        fs[tiles, rows_at(FHALO + r)] = halo_tile(
            col_r[rows_at(r)].astype(F32), col_l[rows_at(r)].astype(F32)
        )

    tall = height + 2 * EXT

    def warp(c, _):
        start = (MAXSHIFT + shifts[c, 0]) * chans + c
        plane = jnp.concatenate(
            [fs[t, pl.ds(start, tall, stride=chans), :] for t in range(tiles + 1)], axis=1
        )
        moved = pltpu.roll(plane, lax.rem(width - shifts[c, 1], width), 1)
        for t in range(tiles + 1):
            ws[t, pl.ds(c, tall, stride=chans), :] = moved[:, t * TILE : (t + 1) * TILE]
        return 0

    lax.fori_loop(0, chans, warp, 0)
    for j in range(tall):
        row = jnp.concatenate([ws[t, rows_at(j)] for t in range(tiles + 1)], axis=1)
        if j < EXT:
            row = jnp.where(in_cols & has_up, row, 0.0)
        elif j >= EXT + height:
            row = jnp.where(in_cols & has_down, row, 0.0)
        else:
            row = jnp.where(in_cols, row, 0.0)
        warped[rows_at(j)] = row.astype(BF16)
        if EXT - 1 <= j <= EXT + height:
            at = rows_at(j - EXT + 1)
            warped_m[at] = turn(row, 1)[:, 0:span].astype(BF16)
            warped_p[at] = turn(row, -1)[:, 0:span].astype(BF16)

    def first_group(g, seen, own):
        at = pl.multiple_of(g * POOL * chans, POOL * chans)
        parts = jnp.dot(
            w_first[...], warped[pl.ds(at, (POOL + 2) * chans), :], preferred_element_type=F32
        )
        total = None
        for k in range(POOL):
            pre = conv_sum(parts[3 * k * chans : 3 * (k + 1) * chans], chans, 1)
            sigma = 0.5 * jnp.tanh(0.5 * pre) + 0.5
            row = (pre * sigma).astype(BF16)
            here = pl.multiple_of(at + k * chans, chans)
            act[pl.ds(here, chans), :] = row
            row = row.astype(F32)
            total = row if total is None else total + row
            if own:
                there = pl.ds(pl.multiple_of(here - 2 * POOL * chans, chans), chans)
                pre, sigma = pre[:, 0:span], sigma[:, 0:span]
                pre_grad[there, :] = (
                    act_grad[there, :] * (sigma * (1.0 + pre * (1.0 - sigma)))
                ).astype(BF16)
        block = jnp.where(in_cols & seen, block_sum(total) * (1.0 / POOL**2), 0.0)
        pooled[pl.ds(pl.multiple_of(g * chans, chans), chans), :] = block.astype(BF16)
        return 0

    for g in (0, 1):
        first_group(g, has_up, False)
    for g in (groups + 2, groups + 3):
        first_group(g, has_down, False)
    lax.fori_loop(2, groups + 2, lambda g, _: first_group(g, True, True), 0)

    def blend_group(g, rows, seen):
        parts = jnp.dot(
            w_bottle[...],
            pooled[pl.ds(pl.multiple_of(g * chans, chans), 3 * chans), :],
            preferred_element_type=F32,
        )
        bottle = conv_sum(parts, chans, POOL)
        for k in rows:
            here = pl.multiple_of(((g + 1) * POOL + k) * chans, chans)
            there = pl.ds(pl.multiple_of((g * POOL + k - POOL + 1) * chans, chans), chans)
            row = act[pl.ds(here, chans), :].astype(F32) + bottle
            row = jnp.where(in_cols & seen, row, 0.0).astype(BF16)
            blended[there, :] = row
            row = row.astype(F32)
            bl_m[there, :] = turn(row, 1)[:, 0:span].astype(BF16)
            bl_p[there, :] = turn(row, -1)[:, 0:span].astype(BF16)
        return 0

    blend_group(0, (POOL - 1,), has_up)
    blend_group(groups + 1, (0,), has_down)
    lax.fori_loop(1, groups + 1, lambda g, _: blend_group(g, range(POOL), True), 0)

    own_rows = warped.at[pl.ds((EXT - 1) * chans, (height + 2) * chans)]
    correlate(pre_grad, (warped_m, own_rows, warped_p), acc, height, chans, span)
    for b in range(3):
        grads[rows_at(b)] = folded(acc, b, chans)
    correlate(cot, (bl_m, blended, bl_p), acc, height, chans, span)
    for b in range(3):
        grads[rows_at(3 + b)] = folded(acc, b, chans)


def predict_kernel(blended, w_second, out, scratch):
    chans, height, span = out.shape
    tiles = span // TILE

    def group(g, _):
        at = pl.multiple_of(g * POOL * chans, POOL * chans)
        parts = jnp.dot(
            w_second[...], blended[pl.ds(at, (POOL + 2) * chans), :], preferred_element_type=F32
        )
        for k in range(POOL):
            row = conv_sum(parts[3 * k * chans : 3 * (k + 1) * chans], chans, 1)
            for t in range(tiles):
                scratch[t, pl.ds(g * POOL + k, chans, stride=height), :] = row[
                    :, t * TILE : (t + 1) * TILE
                ]
        return 0

    lax.fori_loop(0, height // POOL, group, 0)
    for c in range(chans):
        for t in range(tiles):
            out[c, :, t * TILE : (t + 1) * TILE] = scratch[
                t, c * height : (c + 1) * height
            ].astype(BF16)


def final_kernel(factor, mine, other, first, second):
    chans = first.shape[1]
    for index, out in enumerate((first, second)):
        for b in range(3):
            at = slice((3 * index + b) * chans, (3 * index + b + 1) * chans)
            total = (mine[at] + other[at]) * factor
            for a in range(3):
                block = total if a == 0 else turn(total, -a * chans)
                out[3 * a + b] = block[:, 0:chans]


def banded(kernel, count):
    chans = kernel.shape[1]
    taps = kernel.reshape(3, 3, chans, chans).transpose(1, 2, 0, 3).reshape(3 * chans, 3 * chans)
    bands = [
        jnp.pad(taps, ((0, 0), (k * chans, (count - 1 - k) * chans))) for k in range(count)
    ]
    return jnp.concatenate(bands, axis=0)


def turned(kernel):
    return kernel[::-1].transpose(0, 2, 1)


def call(kernel, outs, scratch, n_in, flops=0, smem_first=False):
    specs = [VMEM] * n_in
    if smem_first:
        specs[0] = SMEM
    return pl.pallas_call(
        kernel,
        out_shape=outs,
        in_specs=specs,
        out_specs=jax.tree.map(lambda _: VMEM, outs),
        scratch_shapes=scratch,
        compiler_params=pltpu.CompilerParams(vmem_limit_bytes=LIMIT),
        cost_estimate=pl.CostEstimate(flops=flops, bytes_accessed=4 << 20, transcendentals=0),
    )


def shards(features, shifts, first_kernel, bottle_kernel, second_kernel, cotangent):
    imgs, chans, height, span = features.shape
    rows, cols, dp = (lax.axis_size(a) for a in ("rows", "cols", "dp"))
    tiles = span // TILE
    width = span + TILE
    full = height * chans

    def bf(*shape):
        return jax.ShapeDtypeStruct(shape, BF16)

    if cols == 2:
        edges = (("up", "single"), ("down", "single"))
    else:
        edges = tuple((v, e) for v in ("up", "down") for e in ("left", "right"))
    halo = (FHALO + CHALO) * chans
    packed = pl.cdiv(FHALO + CHALO, POOL) * chans
    feat_rows, cot_rows, up_msg, down_msg, col_msg, *corner_msgs = call(
        functools.partial(pack_kernel, edges),
        (bf(full, span), bf(full, span), bf(halo, span), bf(halo, span), bf(full, TILE))
        + tuple(bf(packed, TILE) for _ in edges),
        [pltpu.VMEM((tiles, full, TILE), F32)] * 2,
        2,
    )(features[0], cotangent[0])

    ahead = [(i, i + 1) for i in range(rows - 1)]
    astern = [(i + 1, i) for i in range(rows - 1)]
    up = lax.ppermute(down_msg, "rows", ahead)
    down = lax.ppermute(up_msg, "rows", astern)

    def diagonal(message, step, turns):
        pairs = []
        for i in range(rows):
            for j in range(cols):
                for move in turns:
                    if 0 <= i + step < rows and 0 <= j + move < cols:
                        pairs.append((i * cols + j, (i + step) * cols + j + move))
        return lax.ppermute(message, ("rows", "cols"), pairs)

    if cols == 2:
        col_r = col_l = lax.ppermute(col_msg, "cols", [(0, 1), (1, 0)])
        up_r = up_l = diagonal(corner_msgs[1], 1, (-1, 1))
        down_r = down_l = diagonal(corner_msgs[0], -1, (-1, 1))
    else:
        col_r = lax.ppermute(col_msg, "cols", [(i + 1, i) for i in range(cols - 1)])
        col_l = lax.ppermute(col_msg, "cols", [(i, i + 1) for i in range(cols - 1)])
        up_r = diagonal(corner_msgs[2], 1, (-1,))
        up_l = diagonal(corner_msgs[3], 1, (1,))
        down_r = diagonal(corner_msgs[0], -1, (-1,))
        down_l = diagonal(corner_msgs[1], -1, (1,))

    tall = height + 2 * EXT
    groups = height // POOL
    grads, blended = call(
        main_kernel,
        (jax.ShapeDtypeStruct((6 * chans, TILE), F32), bf((height + 2) * chans, width)),
        [
            pltpu.VMEM((tiles + 1, (height + 2 * FHALO) * chans, TILE), F32),
            pltpu.VMEM((tiles + 1, tall * chans, TILE), F32),
            pltpu.VMEM((tall * chans, width), BF16),
            pltpu.VMEM(((height + 2) * chans, span), BF16),
            pltpu.VMEM(((height + 2) * chans, span), BF16),
            pltpu.VMEM(((height + 2 * CHALO) * chans, width), BF16),
            pltpu.VMEM(((height + 2 * POOL) * chans, span), BF16),
            pltpu.VMEM(((groups + 2) * chans, width), BF16),
            pltpu.VMEM((full, span), F32),
            pltpu.VMEM(((height + 4 * POOL) * chans, width), BF16),
            pltpu.VMEM(((groups + 4) * chans, width), BF16),
            pltpu.VMEM((full, span), BF16),
            pltpu.VMEM(((height + 2) * chans, span), BF16),
            pltpu.VMEM(((height + 2) * chans, span), BF16),
            pltpu.VMEM((3, POOL * chans, 2 * TILE), F32),
        ],
        15,
        flops=10**9,
        smem_first=True,
    )(
        shifts[0], feat_rows, cot_rows, up, down, col_r, col_l, up_r, up_l, down_r, down_l,
        banded(first_kernel, POOL), banded(turned(second_kernel), POOL),
        banded(bottle_kernel, 1), banded(turned(bottle_kernel), 1),
    )
    prediction = call(
        predict_kernel,
        bf(chans, height, span),
        [pltpu.VMEM((tiles, full, TILE), F32)],
        2,
        flops=2 * 10**8,
    )(blended, banded(second_kernel, POOL))

    steps = []
    for axis, size in (("dp", dp), ("cols", cols), ("rows", rows)):
        bit = 1
        while bit < size:
            steps.append((axis, [(i, i ^ bit) for i in range(size)]))
            bit *= 2
    for axis, pairs in steps[:-1]:
        grads = grads + lax.ppermute(grads, axis, pairs)
    other = lax.ppermute(grads, *steps[-1])
    factor = 1.0 / math.sqrt(imgs * dp * height * rows * span * cols)
    shape = jax.ShapeDtypeStruct((9, chans, chans), F32)
    first_grad, second_grad = call(
        functools.partial(final_kernel, factor), (shape, shape), [], 2
    )(grads, other)
    return (prediction[None], first_grad, second_grad)


def solution(mesh):
    placed = (
        P("dp", None, "rows", "cols"),
        P("dp", None, None),
        P(),
        P(),
        P(),
        P("dp", None, "rows", "cols"),
    )
    return jax.shard_map(
        shards,
        mesh=mesh,
        in_specs=placed,
        out_specs=(P("dp", None, "rows", "cols"), P(), P()),
        check_vma=False,
    )
```

time: 415 us -> 97 us (0.23)
  waiting for transfers between devices: 166 us -> 19.4 us
  local copies, waits for them, and re-layouts: 122 us -> 6.64 us
  Pallas kernels: 0 us -> 43.2 us
  matrix products: 43 us -> 0 us
  starting transfers between devices: 51.4 us -> 24 us
  between operations: 14.7 us -> 0.8 us
  other arithmetic: 16.2 us -> 2.65 us
    psum x1 -> x0, waiting for transfers between devices: 124 us -> none  [shards(): lax.psum((first_grad, second_grad), ('rows', 'cols', 'dp'))]
    gather x96 -> x0, local copies, waits for them, and re-layouts: 85.3 us -> none
    pallas_call x0 -> x4, Pallas kernels: none -> 43.2 us  [the longest x1 29.8 us: shards(): call(main_kernel, (jax.ShapeDtypeStruct((6 * chans, TILE), F32), bf((heig...]
    dot_general x63 -> x0, matrix products: 43 us -> none  [the longest x27 19.6 us: convolve_ext(): jnp.einsum('oi,bihw->bohw', kernel[tap_index], window, preferred_element_...]
    ppermute x20 -> x10, starting transfers between devices: 51.4 us -> 24 us  [the longest x4 6.88 us: shards(): grads = grads + lax.ppermute(grads, axis, pairs)]
    ppermute x20 -> x10, waiting for transfers between devices: 42 us -> 19.4 us  [the longest x4 9.88 us: shards(): grads = grads + lax.ppermute(grads, axis, pairs)]
    broadcast_in_dim x6 -> x0, local copies, waits for them, and re-layouts: 11 us -> none  [upsample(): return jnp.repeat(jnp.repeat(values, POOL, axis=2), POOL, axis=3)]
    reduce_sum x2 -> x0, other arithmetic: 7.22 us -> none  [pool_sum(): values.reshape(shape[0], shape[1], shape[2] // POOL, POOL, shape[3] // PO...]
  transfers between devices with their start and end apart: 21 -> 10, of which waited for: 13 -> 6; matrix products, arithmetic and copies ran while one was open for 6% -> 5% of each run, Pallas kernels for 0% -> 5%
where the time goes in v1:
time: 97 us; the launch traced here: 96.6 us
  Pallas kernels  43.2 us (45%)
  starting transfers between devices  24 us (25%)
  waiting for transfers between devices  19.4 us (20%)
  local copies, waits for them, and re-layouts  6.64 us (7%)
  other arithmetic  2.65 us (3%)
    pallas_call x1, Pallas kernels, shards(): call(main_kernel, (jax.ShapeDtypeStruct((6 * chans, TILE), F32), bf((heig...  29.8 us
    ppermute x4, waiting for transfers between devices, shards(): grads = grads + lax.ppermute(grads, axis, pairs)  9.88 us
    ppermute x1, waiting for transfers between devices, shards(): up = lax.ppermute(down_msg, 'rows', ahead)  8.92 us
    ppermute x4, starting transfers between devices, shards(): grads = grads + lax.ppermute(grads, axis, pairs)  6.88 us
    pallas_call x1, Pallas kernels, shards(): call(functools.partial(pack_kernel, edges), (bf(full, span), bf(full, spa...  6.35 us
    ppermute x2, starting transfers between devices, diagonal(): return lax.ppermute(message, ('rows', 'cols'), pairs)  5.8 us
    pallas_call x1, Pallas kernels, shards(): call(predict_kernel, bf(chans, height, span), [pltpu.VMEM((tiles, full, T...  5.21 us
    ppermute x1, starting transfers between devices, shards(): up = lax.ppermute(down_msg, 'rows', ahead)  4.89 us
  transfers between devices with their start and end apart: 10, of which 6 were waited for; matrix products, arithmetic and copies ran while one was open for 5% of the time, Pallas kernels for 5%

profile of v1, /device:TPU:0, one launch (start us, length us, event | category | flops | bytes accessed | tf_op | source)
XLA Modules:
  0.0 96.6 jit_solution(3523979088223532173)
XLA Ops:
  0.6 6.4 %shard_map.85 = (bf16[1024,256]{1,0:T(8,128)(2,1)}, bf16[1024,256]{1,0:T(8,128)(2,1)}, bf16[960,256]{1,0:T(8,128)(2,1)}, bf16[960,256]{1,0:T(8,128)(2,1)}, bf16[...) custom-call(bf16[32,32,256]{2,1,0:T(8,128)(2,1)} %bitcast.25, bf16[32,32,256]{2,1,0:T(8,128)(2,1)} %bitcast.26), custom_call_target="tpu_custom_call" | custom-call | bytes 4194304 | tf_op jit(solution)/shard_map/pallas_call | solution.py:396
  7.0 4.9 %collective-permute-start = (bf16[960,256]{1,0:T(8,128)(2,1)}, bf16[960,256]{1,0:T(8,128)(2,1)S(1)}, u32[]{:S(2)}, u32[]{:S(2)}) collective-permute-start(bf16[960,256]{1,0:T(8,128)(2,1)} %get-tuple-element.16), channel_id=1, source_target_pairs={{0,4},{4,8},{8,12},{12,16},{16,20},{20,24},{24,28},{1,5},{5,9},{9,... | collective-permute-start | bytes 1474568 | tf_op jit(solution)/shard_map/ppermute | solution.py:406
  11.9 1.3 %collective-permute-start.1 = (bf16[960,256]{1,0:T(8,128)(2,1)}, bf16[960,256]{1,0:T(8,128)(2,1)S(1)}, u32[]{:S(2)}, u32[]{:S(2)}) collective-permute-start(bf16[960,256]{1,0:T(8,128)(2,1)} %get-tuple-element.17), channel_id=1, source_target_pairs={{4,0},{8,4},{12,8},{16,12},{20,16},{24,20},{28,24},{5,1},{9,5},{13... | collective-permute-start | bytes 1474568 | tf_op jit(solution)/shard_map/ppermute | solution.py:407
  13.2 1.6 %collective-permute-start.2 = (bf16[1024,128]{1,0:T(8,128)(2,1)}, bf16[1024,128]{1,0:T(8,128)(2,1)S(1)}, u32[]{:S(2)}, u32[]{:S(2)}) collective-permute-start(bf16[1024,128]{1,0:T(8,128)(2,1)} %get-tuple-element.18), channel_id=1, source_target_pairs={{0,2},{2,0},{1,3},{3,1},{4,6},{6,4},{5,7},{7,5},{8,10},{10,8},{9,1... | collective-permute-start | bytes 786440 | tf_op jit(solution)/shard_map/ppermute | solution.py:419
  14.7 4.5 %collective-permute-start.3 = (bf16[256,128]{1,0:T(8,128)(2,1)}, bf16[256,128]{1,0:T(8,128)(2,1)S(1)}, u32[]{:S(2)}, u32[]{:S(2)}) collective-permute-start(bf16[256,128]{1,0:T(8,128)(2,1)} %get-tuple-element.19), channel_id=1, source_target_pairs={{0,6},{2,4},{4,10},{6,8},{8,14},{10,12},{12,18},{14,16},{16,22},{1... | collective-permute-start | bytes 196616 | tf_op jit(solution)/shard_map/ppermute | solution.py:416
  19.3 1.3 %collective-permute-start.4 = (bf16[256,128]{1,0:T(8,128)(2,1)}, bf16[256,128]{1,0:T(8,128)(2,1)S(1)}, u32[]{:S(2)}, u32[]{:S(2)}) collective-permute-start(bf16[256,128]{1,0:T(8,128)(2,1)} %get-tuple-element.20), channel_id=1, source_target_pairs={{4,2},{6,0},{8,6},{10,4},{12,10},{14,8},{16,14},{18,12},{20,18},{2... | collective-permute-start | bytes 196616 | tf_op jit(solution)/shard_map/ppermute | solution.py:416
  20.8 0.8 copy-done.4
  21.8 0.8 copy-done.1
  25.5 0.9 fusion.16
  27.1 8.9 %collective-permute-done.up = bf16[960,256]{1,0:T(8,128)(2,1)S(1)} collective-permute-done((bf16[960,256]{1,0:T(8,128)(2,1)}, bf16[960,256]{1,0:T(8,128)(2,1)S(1)}, u32[]{:S(2)}, u32[]{:S(2)}) %collective-permute-start) | collective-permute-done | bytes 491552 | tf_op jit(solution)/shard_map/ppermute | solution.py:406
  36.0 0.7 copy-done.6
  36.9 29.8 %shard_map.86 = (f32[192,128]{1,0:T(8,128)}, bf16[1088,384]{1,0:T(8,128)(2,1)}) custom-call(s32[32,2]{1,0:T(8,128)} %copy.19.shifts, bf16[1024,256]{1,0:T(8,128)(2,1)} %get-tuple-element.14.feat, bf16[1024,256]{1,0:T(8,128)(2,1)} %get-tuple-element.15.cot, bf16[960,256]{1,0:T(8,128)(2,1)} %copy-done.6, bf16[960,256]{1,0:T(8,128)(2,1)} %copy-done.7, ...), custom_call_target="tpu_custom_call" | custom-call | flops 1000000000 | bytes 4194304 | tf_op jit(solution)/shard_map/pallas_call | solution.py:432
  66.8 1.5 %collective-permute-done.5 = f32[192,128]{1,0:T(8,128)S(1)} collective-permute-done((f32[192,128]{1,0:T(8,128)}, f32[192,128]{1,0:T(8,128)S(1)}, u32[]{:S(2)}, u32[]{:S(2)}) %collective-permute-start.5) | collective-permute-done | bytes 98336 | tf_op jit(solution)/shard_map/ppermute | solution.py:475
  68.3 0.9 add.36
  69.2 1.6 %collective-permute-start.6 = (f32[192,128]{1,0:T(8,128)S(1)}, f32[192,128]{1,0:T(8,128)S(1)}, u32[]{:S(2)}, u32[]{:S(2)}) collective-permute-start(f32[192,128]{1,0:T(8,128)S(1)} %add.36), channel_id=1, source_target_pairs={{0,2},{2,0},{1,3},{3,1},{4,6},{6,4},{5,7},{7,5},{8,10},{10,8},{9,1... | collective-permute-start | bytes 294920 | tf_op jit(solution)/shard_map/ppermute | solution.py:475
  70.8 3.4 %collective-permute-done.6 = f32[192,128]{1,0:T(8,128)S(1)} collective-permute-done((f32[192,128]{1,0:T(8,128)S(1)}, f32[192,128]{1,0:T(8,128)S(1)}, u32[]{:S(2)}, u32[]{:S(2)}) %collective-permute-start.6) | collective-permute-done | bytes 98336 | tf_op jit(solution)/shard_map/ppermute | solution.py:475
  74.1 2.4 %collective-permute-start.7 = (f32[192,128]{1,0:T(8,128)S(1)}, f32[192,128]{1,0:T(8,128)S(1)}, u32[]{:S(2)}, u32[]{:S(2)}) collective-permute-start(f32[192,128]{1,0:T(8,128)S(1)} %add.37), channel_id=1, source_target_pairs={{0,4},{4,0},{8,12},{12,8},{16,20},{20,16},{24,28},{28,24},{1,5},{5... | collective-permute-start | bytes 294920 | tf_op jit(solution)/shard_map/ppermute | solution.py:475
  76.6 2.6 %collective-permute-done.7 = f32[192,128]{1,0:T(8,128)S(1)} collective-permute-done((f32[192,128]{1,0:T(8,128)S(1)}, f32[192,128]{1,0:T(8,128)S(1)}, u32[]{:S(2)}, u32[]{:S(2)}) %collective-permute-start.7) | collective-permute-done | bytes 98336 | tf_op jit(solution)/shard_map/ppermute | solution.py:475
  79.2 2.9 %collective-permute-start.8 = (f32[192,128]{1,0:T(8,128)S(1)}, f32[192,128]{1,0:T(8,128)S(1)}, u32[]{:S(2)}, u32[]{:S(2)}) collective-permute-start(f32[192,128]{1,0:T(8,128)S(1)} %add.38), channel_id=1, source_target_pairs={{0,8},{4,12},{8,0},{12,4},{16,24},{20,28},{24,16},{28,20},{1,9},{5... | collective-permute-start | bytes 294920 | tf_op jit(solution)/shard_map/ppermute | solution.py:475
  82.2 2.4 %collective-permute-done.8 = f32[192,128]{1,0:T(8,128)S(1)} collective-permute-done((f32[192,128]{1,0:T(8,128)S(1)}, f32[192,128]{1,0:T(8,128)S(1)}, u32[]{:S(2)}, u32[]{:S(2)}) %collective-permute-start.8) | collective-permute-done | bytes 98336 | tf_op jit(solution)/shard_map/ppermute | solution.py:475
  84.7 3.5 %collective-permute-start.9 = (f32[192,128]{1,0:T(8,128)S(1)}, f32[192,128]{1,0:T(8,128)S(1)}, u32[]{:S(2)}, u32[]{:S(2)}) collective-permute-start(f32[192,128]{1,0:T(8,128)S(1)} %add.39.mine), channel_id=1, source_target_pairs={{0,16},{4,20},{8,24},{12,28},{16,0},{20,4},{24,8},{28,12},{1,17},{... | collective-permute-start | bytes 294920 | tf_op jit(solution)/shard_map/ppermute | solution.py:476
  88.2 0.8 fusion.22.w_second
  89.0 5.2 %shard_map.87 = bf16[32,32,256]{2,1,0:T(8,128)(2,1)} custom-call(bf16[1088,384]{1,0:T(8,128)(2,1)} %get-tuple-element.21.blended, bf16[384,192]{1,0:T(8,128)(2,1)} %fusion.22.w_second), custom_call_target="tpu_custom_call" | custom-call | flops 200000000 | bytes 4194304 | tf_op jit(solution)/shard_map/pallas_call | solution.py:460
  94.9 1.7 %shard_map.88 = (f32[9,32,32]{2,1,0:T(8,128)}, f32[9,32,32]{2,1,0:T(8,128)}) custom-call(f32[192,128]{1,0:T(8,128)} %copy-done, f32[192,128]{1,0:T(8,128)} %copy-done.3), custom_call_target="tpu_custom_call" | custom-call | bytes 4194304 | tf_op jit(solution)/shard_map/pallas_call | solution.py:479
  (41 shorter events, 5.0 us)
Async XLA Ops:
  0.6 19.9 %copy-start.2 = (bf16[9,32,32]{2,1,0:T(8,128)(2,1)S(1)}, bf16[9,32,32]{2,1,0:T(8,128)(2,1)}, u32[]{:S(2)}) copy-start(bf16[9,32,32]{2,1,0:T(8,128)(2,1)} %param.10) | copy-start | bytes 55300
  7.0 29.0 %collective-permute-start = (bf16[960,256]{1,0:T(8,128)(2,1)}, bf16[960,256]{1,0:T(8,128)(2,1)S(1)}, u32[]{:S(2)}, u32[]{:S(2)}) collective-permute-start(bf16[960,256]{1,0:T(8,128)(2,1)} %get-tuple-element.16), channel_id=1, source_target_pairs={{0,4},{4,8},{8,12},{12,16},{16,20},{20,24},{24,28},{1,5},{5,9},{9,... | collective-permute-start | bytes 1474568 | tf_op jit(solution)/shard_map/ppermute | solution.py:406
  11.9 24.1 %collective-permute-start.1 = (bf16[960,256]{1,0:T(8,128)(2,1)}, bf16[960,256]{1,0:T(8,128)(2,1)S(1)}, u32[]{:S(2)}, u32[]{:S(2)}) collective-permute-start(bf16[960,256]{1,0:T(8,128)(2,1)} %get-tuple-element.17), channel_id=1, source_target_pairs={{4,0},{8,4},{12,8},{16,12},{20,16},{24,20},{28,24},{5,1},{9,5},{13... | collective-permute-start | bytes 1474568 | tf_op jit(solution)/shard_map/ppermute | solution.py:407
  13.2 13.9 %collective-permute-start.2 = (bf16[1024,128]{1,0:T(8,128)(2,1)}, bf16[1024,128]{1,0:T(8,128)(2,1)S(1)}, u32[]{:S(2)}, u32[]{:S(2)}) collective-permute-start(bf16[1024,128]{1,0:T(8,128)(2,1)} %get-tuple-element.18), channel_id=1, source_target_pairs={{0,2},{2,0},{1,3},{3,1},{4,6},{6,4},{5,7},{7,5},{8,10},{10,8},{9,1... | collective-permute-start | bytes 786440 | tf_op jit(solution)/shard_map/ppermute | solution.py:419
  14.7 11.7 %collective-permute-start.3 = (bf16[256,128]{1,0:T(8,128)(2,1)}, bf16[256,128]{1,0:T(8,128)(2,1)S(1)}, u32[]{:S(2)}, u32[]{:S(2)}) collective-permute-start(bf16[256,128]{1,0:T(8,128)(2,1)} %get-tuple-element.19), channel_id=1, source_target_pairs={{0,6},{2,4},{4,10},{6,8},{8,14},{10,12},{12,18},{14,16},{16,22},{1... | collective-permute-start | bytes 196616 | tf_op jit(solution)/shard_map/ppermute | solution.py:416
  19.3 7.8 %collective-permute-start.4 = (bf16[256,128]{1,0:T(8,128)(2,1)}, bf16[256,128]{1,0:T(8,128)(2,1)S(1)}, u32[]{:S(2)}, u32[]{:S(2)}) collective-permute-start(bf16[256,128]{1,0:T(8,128)(2,1)} %get-tuple-element.20), channel_id=1, source_target_pairs={{4,2},{6,0},{8,6},{10,4},{12,10},{14,8},{16,14},{18,12},{20,18},{2... | collective-permute-start | bytes 196616 | tf_op jit(solution)/shard_map/ppermute | solution.py:416
  20.7 0.9 copy-start.4
  21.7 0.9 copy-start.1
  24.2 0.7 copy-start.5
  26.5 9.5 %copy-start.9 = (bf16[256,128]{1,0:T(8,128)(2,1)}, bf16[256,128]{1,0:T(8,128)(2,1)S(1)}, u32[]{:S(2)}) copy-start(bf16[256,128]{1,0:T(8,128)(2,1)S(1)} %collective-permute-done.3.up_r.up_l) | copy-start | bytes 196612
  27.0 8.9 %copy-start.10 = (bf16[256,128]{1,0:T(8,128)(2,1)}, bf16[256,128]{1,0:T(8,128)(2,1)S(1)}, u32[]{:S(2)}) copy-start(bf16[256,128]{1,0:T(8,128)(2,1)S(1)} %collective-permute-done.4.down_r.down_l) | copy-start | bytes 196612
  27.1 9.0 %copy-start.8 = (bf16[1024,128]{1,0:T(8,128)(2,1)}, bf16[1024,128]{1,0:T(8,128)(2,1)S(1)}, u32[]{:S(2)}) copy-start(bf16[1024,128]{1,0:T(8,128)(2,1)S(1)} %collective-permute-done.2.col_r.col_l) | copy-start | bytes 786436
  36.0 0.8 copy-start.6
  36.0 0.9 copy-start.7
  66.8 1.5 %collective-permute-start.5 = (f32[192,128]{1,0:T(8,128)}, f32[192,128]{1,0:T(8,128)S(1)}, u32[]{:S(2)}, u32[]{:S(2)}) collective-permute-start(f32[192,128]{1,0:T(8,128)} %get-tuple-element.22), channel_id=1, source_target_pairs={{0,1},{1,0},{2,3},{3,2},{4,5},{5,4},{6,7},{7,6},{8,9},{9,8},{10,11... | collective-permute-start | bytes 294920 | tf_op jit(solution)/shard_map/ppermute | solution.py:475
  69.2 4.9 %collective-permute-start.6 = (f32[192,128]{1,0:T(8,128)S(1)}, f32[192,128]{1,0:T(8,128)S(1)}, u32[]{:S(2)}, u32[]{:S(2)}) collective-permute-start(f32[192,128]{1,0:T(8,128)S(1)} %add.36), channel_id=1, source_target_pairs={{0,2},{2,0},{1,3},{3,1},{4,6},{6,4},{5,7},{7,5},{8,10},{10,8},{9,1... | collective-permute-start | bytes 294920 | tf_op jit(solution)/shard_map/ppermute | solution.py:475
  74.1 5.0 %collective-permute-start.7 = (f32[192,128]{1,0:T(8,128)S(1)}, f32[192,128]{1,0:T(8,128)S(1)}, u32[]{:S(2)}, u32[]{:S(2)}) collective-permute-start(f32[192,128]{1,0:T(8,128)S(1)} %add.37), channel_id=1, source_target_pairs={{0,4},{4,0},{8,12},{12,8},{16,20},{20,16},{24,28},{28,24},{1,5},{5... | collective-permute-start | bytes 294920 | tf_op jit(solution)/shard_map/ppermute | solution.py:475
  79.2 5.5 %collective-permute-start.8 = (f32[192,128]{1,0:T(8,128)S(1)}, f32[192,128]{1,0:T(8,128)S(1)}, u32[]{:S(2)}, u32[]{:S(2)}) collective-permute-start(f32[192,128]{1,0:T(8,128)S(1)} %add.38), channel_id=1, source_target_pairs={{0,8},{4,12},{8,0},{12,4},{16,24},{20,28},{24,16},{28,20},{1,9},{5... | collective-permute-start | bytes 294920 | tf_op jit(solution)/shard_map/ppermute | solution.py:475
  84.7 4.3 %copy-start = (f32[192,128]{1,0:T(8,128)}, f32[192,128]{1,0:T(8,128)S(1)}, u32[]{:S(2)}) copy-start(f32[192,128]{1,0:T(8,128)S(1)} %add.39.mine) | copy-start | bytes 294916
  84.7 9.5 %collective-permute-start.9 = (f32[192,128]{1,0:T(8,128)S(1)}, f32[192,128]{1,0:T(8,128)S(1)}, u32[]{:S(2)}, u32[]{:S(2)}) collective-permute-start(f32[192,128]{1,0:T(8,128)S(1)} %add.39.mine), channel_id=1, source_target_pairs={{0,16},{4,20},{8,24},{12,28},{16,0},{20,4},{24,8},{28,12},{1,17},{... | collective-permute-start | bytes 294920 | tf_op jit(solution)/shard_map/ppermute | solution.py:476
  94.2 0.6 copy-start.3

commit v2 on v0

v2 whole, which is shorter than its diff:
```python
import functools
import math

import jax
import jax.numpy as jnp
from jax import lax
from jax.experimental import pallas as pl
from jax.experimental.pallas import tpu as pltpu
from jax.sharding import PartitionSpec as P


MAXSHIFT = 16
POOL = 4
TILE = 128
SLOT = 32
EXT = 9
FHALO = MAXSHIFT + EXT
CHALO = 5
F32 = jnp.float32
BF16 = jnp.bfloat16
VMEM = pl.BlockSpec(memory_space=pltpu.VMEM)
SMEM = pl.BlockSpec(memory_space=pltpu.SMEM)
MIB = 1024 * 1024


def lanes_of(shape):
    return lax.broadcasted_iota(jnp.int32, shape, len(shape) - 1)


def turn(values, shift):
    width = values.shape[-1]
    if isinstance(shift, int):
        shift = shift % width
        if shift == 0:
            return values
    return pltpu.roll(values, shift, values.ndim - 1)


def has_sides():
    row, col = lax.axis_index("rows"), lax.axis_index("cols")
    return (
        row > 0,
        row < lax.axis_size("rows") - 1,
        col > 0,
        col < lax.axis_size("cols") - 1,
    )


def rows_at(r, chans, count=1):
    if isinstance(r, int):
        return slice(r * chans, (r + count) * chans)
    return pl.ds(pl.multiple_of(r * chans, chans), count * chans)


def by_rows(source, out):
    chans, height, span = source.shape
    for t in range(0, span, TILE):
        part = jnp.transpose(source[:, :, t : t + TILE], (1, 0, 2))
        out[:, t : t + TILE] = part.reshape(height * chans, TILE)


def feature_kernel(feat, feat_rows, up_msg, down_msg):
    chans, height = feat.shape[0], feat.shape[1]
    by_rows(feat, feat_rows)
    up_msg[...] = feat_rows[0 : FHALO * chans]
    down_msg[...] = feat_rows[(height - FHALO) * chans :]


def pack_kernel(edges, feat_rows, cot, cot_rows, up_msg, down_msg, col_msg, *corner_msgs):
    chans, height, span = cot.shape
    last = slice(span - TILE, span)
    by_rows(cot, cot_rows)
    up_msg[...] = cot_rows[0 : CHALO * chans]
    down_msg[...] = cot_rows[(height - CHALO) * chans :]
    lane = lanes_of((chans, TILE))
    is_left = lax.axis_index("cols") == 0
    for (vertical, edge), msg in zip(edges, corner_msgs):
        f0 = 0 if vertical == "up" else height - FHALO
        c0 = 0 if vertical == "up" else height - CHALO
        pieces = [(feat_rows, f0 + j) for j in range(FHALO)]
        pieces += [(cot_rows, c0 + j) for j in range(CHALO)]
        for q in range(0, len(pieces), POOL):
            total = jnp.zeros((chans, TILE), F32)
            for k, (ref, r) in enumerate(pieces[q : q + POOL]):
                at = rows_at(r, chans)
                if edge == "left":
                    piece = turn(ref[at, 0:TILE].astype(F32), k * SLOT)
                elif edge == "right":
                    piece = turn(ref[at, last].astype(F32), (k + 1) * SLOT)
                else:
                    piece = jnp.where(is_left, ref[at, last].astype(F32), ref[at, 0:TILE].astype(F32))
                    piece = turn(piece, jnp.where(is_left, (k + 1) * SLOT % TILE, k * SLOT))
                inside = (lane >= k * SLOT) & (lane < (k + 1) * SLOT)
                total = jnp.where(inside, piece, total)
            msg[rows_at(q // POOL, chans)] = total.astype(BF16)
    for r in range(height):
        at = rows_at(r, chans)
        cots = jnp.where(
            lane < 2 * SLOT,
            turn(cot_rows[at, 0:TILE].astype(F32), SLOT),
            turn(cot_rows[at, last].astype(F32), -SLOT),
        )
        feats = jnp.where(
            lane < 2 * SLOT, feat_rows[at, 0:TILE].astype(F32), feat_rows[at, last].astype(F32)
        )
        outer = (lane < SLOT) | (lane >= TILE - SLOT)
        col_msg[at] = jnp.where(outer, feats, cots).astype(BF16)


class Halo:

    def __init__(self, chans, single):
        _, _, has_left, has_right = has_sides()
        lane = lanes_of((chans, TILE))
        self.chans, self.single, self.has_right = chans, single, has_right
        self.right_lanes = (lane < SLOT) & has_right
        self.left_lanes = (lane >= TILE - SLOT) & has_left

    def tile(self, right, left):
        return jnp.where(self.right_lanes, right, jnp.where(self.left_lanes, left, 0.0))

    def turned(self, right_ref, left_ref, at, right_shift, left_shift):
        if self.single:
            both = right_ref[at].astype(F32)
            shift = jnp.where(self.has_right, right_shift % TILE, left_shift % TILE)
            both = turn(both, shift)
            return self.tile(both, both)
        return self.tile(
            turn(right_ref[at].astype(F32), right_shift), turn(left_ref[at].astype(F32), left_shift)
        )

    def corner(self, right_ref, left_ref, slot):
        at, k = rows_at(slot // POOL, self.chans), slot % POOL
        return self.turned(right_ref, left_ref, at, -k * SLOT, TILE - SLOT - k * SLOT)


def columns_seen(shape, span):
    _, _, has_left, has_right = has_sides()
    lane = lanes_of(shape)
    middle = span + TILE // 2
    return (lane < span) | ((lane < middle) & has_right) | ((lane >= middle) & has_left)


def block_ones(width):
    row = lax.broadcasted_iota(jnp.int32, (width, width), 0) // POOL
    col = lax.broadcasted_iota(jnp.int32, (width, width), 1) // POOL
    return jnp.where(row == col, 1.0, 0.0).astype(BF16)


def store_split(high, low, at, total):
    top = total.astype(BF16)
    high[at, :] = top
    low[at, :] = (total - top.astype(F32)).astype(BF16)


def block_sums(high, low, ones):
    return jnp.dot(high[...], ones, preferred_element_type=F32) + jnp.dot(
        low[...], ones, preferred_element_type=F32
    )


def fill_bands(out, kernel, count):
    chans = kernel.shape[1]
    out[...] = jnp.zeros(out.shape, out.dtype)
    for k in range(count):
        for b in range(3):
            for a in range(3):
                at = (b * (count + 2) + k + a) * chans
                out[k * chans : (k + 1) * chans, at : at + chans] = kernel[3 * a + b].astype(
                    out.dtype
                )


def fill_turned_bands(out, kernel, count):
    chans = kernel.shape[1]
    out[...] = jnp.zeros(out.shape, out.dtype)
    for k in range(count):
        for b in range(3):
            for a in range(3):
                at = (b * (count + 2) + k + a) * chans
                out[at : at + chans, k * chans : (k + 1) * chans] = kernel[8 - 3 * a - b].astype(
                    out.dtype
                )


def stacked(views, at):
    return jnp.concatenate([view[at, :] for view in views], axis=0)


def conv_sum(parts, chans, step):
    return (
        turn(parts[0:chans], step)
        + parts[chans : 2 * chans]
        + turn(parts[2 * chans : 3 * chans], -step)
    )


def back_kernel(
    single, cot, up, down, col_r, col_l, up_r, up_l, down_r, down_l, second, bottle,
    act_grad, view_m, view_0, view_p,
    cot_m, cot_0, cot_p, back, high, low, coarse, bands_f, bands, small_f, small,
):
    chans = second.shape[1]
    full, span = cot.shape
    height = full // chans
    width = span + TILE
    groups = height // POOL
    has_up, has_down, _, _ = has_sides()
    halo = Halo(chans, single)
    seen_cols = columns_seen((chans, width), span)

    fill_turned_bands(bands_f, second, POOL)
    bands[...] = bands_f[...].T.astype(BF16)
    fill_turned_bands(small_f, bottle, 1)
    small_t = small_f[...].T
    for b in range(3):
        small[rows_at(b, chans)] = small_t[0:chans, 3 * b * chans : 3 * (b + 1) * chans].astype(BF16)

    cot_0[rows_at(0, chans, CHALO), 0:span] = up[...]
    cot_0[rows_at(CHALO, chans, height), 0:span] = cot[...]
    cot_0[rows_at(CHALO + height, chans, CHALO), 0:span] = down[...]
    for j in range(CHALO):
        cot_0[rows_at(j, chans), span:width] = halo.corner(up_r, up_l, FHALO + j).astype(BF16)
        cot_0[rows_at(CHALO + height + j, chans), span:width] = halo.corner(
            down_r, down_l, FHALO + j
        ).astype(BF16)
    for r in range(height):
        cot_0[rows_at(CHALO + r, chans), span:width] = halo.turned(
            col_r, col_l, rows_at(r, chans), -SLOT, SLOT
        ).astype(BF16)
    for j in range(height + 2 * CHALO):
        at = rows_at(j, chans)
        cot_m[at] = turn(cot_0[at], 1)
        cot_p[at] = turn(cot_0[at], -1)
    inner = rows_at(CHALO - 1, chans, height + 2)
    view_m[...] = cot_m[inner, 0:span]
    view_0[...] = cot_0[inner, 0:span]
    view_p[...] = cot_p[inner, 0:span]

    def group(g, _):
        at = rows_at(g * POOL, chans, POOL + 2)
        rows = jnp.dot(
            bands[...], stacked((cot_m, cot_0, cot_p), at), preferred_element_type=F32
        ).astype(BF16)
        back[rows_at(g * POOL, chans, POOL), :] = rows[:, 0:span]
        rows = rows.astype(F32)
        total = rows[0:chans]
        for k in range(1, POOL):
            total = total + rows[k * chans : (k + 1) * chans]
        store_split(high, low, rows_at(g, chans), total)
        return 0

    lax.fori_loop(0, groups + 2, group, 0, unroll=2)
    sums = block_sums(high, low, block_ones(width))
    for g in range(groups + 2):
        at = rows_at(g, chans)
        seen = seen_cols
        if g == 0:
            seen = seen & has_up
        elif g == groups + 1:
            seen = seen & has_down
        coarse[at] = jnp.where(seen, sums[at], 0.0).astype(BF16)
    for g in range(groups):
        parts = jnp.dot(small[...], coarse[rows_at(g, chans, 3), :], preferred_element_type=F32)
        mean = conv_sum(parts, chans, POOL)[:, 0:span] * (1.0 / POOL**2)
        for k in range(POOL):
            r = g * POOL + k
            act_grad[rows_at(r, chans), :] = back[rows_at(r + POOL, chans), :].astype(F32) + mean


def correlate(u, u0, views, v0, acc, height, chans, span):
    acc[...] = jnp.zeros(acc.shape, F32)

    def group(g, _):
        left = jnp.concatenate(
            [view[rows_at(v0 + g * POOL, chans, POOL + 2), 0:span] for view in views], axis=0
        )
        right = u[rows_at(u0 + g * POOL, chans, POOL), 0:span]
        acc[...] += lax.dot_general(
            left, right, (((1,), (1,)), ((), ())), preferred_element_type=F32
        )
        return 0

    lax.fori_loop(0, height // POOL, group, 0, unroll=2)


def folded(acc, chans):
    lane = lanes_of((3 * chans, TILE))
    result = jnp.zeros((3 * chans, TILE), F32)
    for b in range(3):
        total = None
        for k in range(POOL):
            block = turn(
                acc[rows_at(b * (POOL + 2) + k, chans, 3), 0:TILE], (b - k) * chans
            )
            total = block if total is None else total + block
        result = jnp.where((lane >= b * chans) & (lane < (b + 1) * chans), total, result)
    return result


def main_kernel(
    single, shifts, feat, up, down, col_r, col_l, up_r, up_l, down_r, down_l,
    act_grad, view_m, view_0, view_p, first, bottle,
    grads, blended,
    fs, ws, warp_m, warp_0, warp_p, act, high, low, pooled, pre_grad, acc, bands_f, bands, small_f, small,
):
    chans = first.shape[1]
    full, span = feat.shape
    height = full // chans
    tiles = span // TILE
    width = span + TILE
    groups = height // POOL
    has_up, has_down, _, _ = has_sides()
    halo = Halo(chans, single)
    seen_cols = columns_seen((chans, width), span)

    fill_bands(bands_f, first, POOL)
    bands[...] = bands_f[...].astype(BF16)
    fill_bands(small_f, bottle, 1)
    for b in range(3):
        small[rows_at(b, chans)] = small_f[:, 3 * b * chans : 3 * (b + 1) * chans].astype(BF16)

    for t in range(tiles):
        part = slice(t * TILE, (t + 1) * TILE)
        fs[t, rows_at(0, chans, FHALO)] = up[:, part].astype(F32)
        fs[t, rows_at(FHALO, chans, height)] = feat[:, part].astype(F32)
        fs[t, rows_at(FHALO + height, chans, FHALO)] = down[:, part].astype(F32)
    for j in range(FHALO):
        fs[tiles, rows_at(j, chans)] = halo.corner(up_r, up_l, j)
        fs[tiles, rows_at(FHALO + height + j, chans)] = halo.corner(down_r, down_l, j)
    for r in range(height):
        at = rows_at(r, chans)
        fs[tiles, rows_at(FHALO + r, chans)] = halo.tile(
            col_r[at].astype(F32), col_l[at].astype(F32)
        )

    tall = height + 2 * EXT
    lane = lanes_of((tall, TILE))

    def warp(c, _):
        start = (MAXSHIFT + shifts[c, 0]) * chans + c
        move = shifts[c, 1]
        planes = [
            turn(fs[t, pl.ds(start, tall, stride=chans), :], jnp.where(move > 0, TILE - move, -move))
            for t in range(tiles + 1)
        ]
        inside = jnp.where(move > 0, lane, TILE - 1 - lane) < TILE - jnp.abs(move)
        for t in range(tiles + 1):
            after, before = planes[(t + 1) % (tiles + 1)], planes[t - 1]
            ws[t, pl.ds(c, tall, stride=chans), :] = jnp.where(
                inside, planes[t], jnp.where(move > 0, after, before)
            )
        return 0

    lax.fori_loop(0, chans, warp, 0, unroll=4)
    for j in range(tall):
        row = jnp.concatenate([ws[t, rows_at(j, chans)] for t in range(tiles + 1)], axis=1)
        seen = seen_cols
        if j < EXT:
            seen = seen & has_up
        elif j >= EXT + height:
            seen = seen & has_down
        row = jnp.where(seen, row, 0.0).astype(BF16)
        at = rows_at(j, chans)
        warp_0[at] = row
        warp_m[at] = turn(row, 1)
        warp_p[at] = turn(row, -1)

    def first_group(g, own):
        at = rows_at(g * POOL, chans, POOL + 2)
        pre = jnp.dot(
            bands[...], stacked((warp_m, warp_0, warp_p), at), preferred_element_type=F32
        )
        sigma = 0.5 * jnp.tanh(0.5 * pre) + 0.5
        rows = (pre * sigma).astype(BF16)
        act[rows_at(g * POOL, chans, POOL), :] = rows
        rows = rows.astype(F32)
        total = rows[0:chans]
        for k in range(1, POOL):
            total = total + rows[k * chans : (k + 1) * chans]
        store_split(high, low, rows_at(g, chans), total)
        if own:
            there = rows_at(g * POOL - 2 * POOL, chans, POOL)
            pre, sigma = pre[:, 0:span], sigma[:, 0:span]
            pre_grad[there, :] = (
                act_grad[there, :] * (sigma * (1.0 + pre * (1.0 - sigma)))
            ).astype(BF16)
        return 0

    for g in (0, 1, groups + 2, groups + 3):
        first_group(g, False)
    lax.fori_loop(2, groups + 2, lambda g, _: first_group(g, True), 0, unroll=2)
    sums = block_sums(high, low, block_ones(width))
    for g in range(groups + 4):
        at = rows_at(g, chans)
        seen = seen_cols
        if g < 2:
            seen = seen & has_up
        elif g >= groups + 2:
            seen = seen & has_down
        pooled[at] = jnp.where(seen, sums[at] * (1.0 / POOL**2), 0.0).astype(BF16)

    for g in range(groups + 2):
        parts = jnp.dot(small[...], pooled[rows_at(g, chans, 3), :], preferred_element_type=F32)
        bottle_row = conv_sum(parts, chans, POOL)
        rows, seen = range(POOL), seen_cols
        if g == 0:
            rows, seen = (POOL - 1,), seen & has_up
        elif g == groups + 1:
            rows, seen = (0,), seen & has_down
        for k in rows:
            row = act[rows_at((g + 1) * POOL + k, chans), :].astype(F32) + bottle_row
            blended[rows_at(g * POOL + k - POOL + 1, chans), :] = jnp.where(seen, row, 0.0).astype(
                BF16
            )

    correlate(pre_grad, 0, (warp_m, warp_0, warp_p), EXT - 1, acc, height, chans, span)
    first_part = folded(acc, chans)
    correlate(blended, 1, (view_m, view_0, view_p), 0, acc, height, chans, span)
    second_part = folded(acc, chans)
    lane = lanes_of((3 * chans, TILE))
    grads[0 : 3 * chans] = jnp.where(lane < 3 * chans, first_part, turn(second_part, 3 * chans))
    half = 3 * chans // 2
    grads[3 * chans :] = jnp.where(
        lane[0:half] < TILE // 2,
        turn(second_part[0:half], -chans),
        turn(second_part[half:], TILE // 2 - chans),
    )


def predict_kernel(part, blended, second, *rest):
    out, scratch, bands_f, bands = rest[-4:]
    chans, height, span = out.shape
    tiles = span // TILE
    bands_f[...] = jnp.zeros(bands_f.shape, F32)
    for k in range(POOL):
        for b in range(3):
            for a in range(3):
                bands_f[rows_at(3 * k + b, chans), (k + a) * chans : (k + a + 1) * chans] = second[
                    3 * a + b
                ].astype(F32)
    bands[...] = bands_f[...].astype(BF16)

    def group(g, _):
        at = rows_at(part * height + g * POOL, chans, POOL + 2)
        parts = jnp.dot(bands[...], blended[at, :], preferred_element_type=F32)
        for k in range(POOL):
            row = conv_sum(parts[3 * k * chans : 3 * (k + 1) * chans], chans, 1)
            for t in range(tiles):
                scratch[t, pl.ds(g * POOL + k, chans, stride=height), :] = row[
                    :, t * TILE : (t + 1) * TILE
                ]
        return 0

    lax.fori_loop(0, height // POOL, group, 0)
    for c in range(chans):
        for t in range(tiles):
            out[c, :, t * TILE : (t + 1) * TILE] = scratch[
                t, c * height : (c + 1) * height
            ].astype(BF16)


def final_kernel(factor, mine, other, first, second):
    chans = first.shape[1]
    total = (mine[...] + other[...]) * factor
    turned = total[0 : 3 * chans].T
    for b in range(3):
        for a in range(3):
            first[3 * a + b] = turned[b * chans : (b + 1) * chans, a * chans : (a + 1) * chans]
    half = 3 * chans // 2
    low = total[3 * chans :]
    both = jnp.concatenate([low, turn(low, -(TILE // 2))], axis=0)
    for a in range(3):
        at = slice((2 - a) * chans, (3 - a) * chans)
        second[3 * a + 2] = turn(total[at], -3 * chans)[:, 0:chans]
        second[3 * a + 1] = both[at, 0:chans]
        second[3 * a + 0] = turn(both[at], -chans)[:, 0:chans]


def call(kernel, outs, scratch, n_in, limit, flops=0, smem_first=False, **more):
    specs = [VMEM] * n_in
    if smem_first:
        specs[0] = SMEM
    more.setdefault("in_specs", specs)
    more.setdefault("out_specs", jax.tree.map(lambda _: VMEM, outs))
    return pl.pallas_call(
        kernel,
        out_shape=outs,
        scratch_shapes=scratch,
        compiler_params=pltpu.CompilerParams(vmem_limit_bytes=limit * MIB),
        cost_estimate=pl.CostEstimate(flops=flops, bytes_accessed=4 * MIB, transcendentals=0),
        **more,
    )


def predict(blended, second, shape, parts, part, before):
    chans, height, span = shape
    rows = height // parts
    tiles = span // TILE
    block = pl.BlockSpec((chans, rows, span), lambda i: (0, part, 0))
    whole = lambda a: pl.BlockSpec(a.shape, lambda i: (0,) * a.ndim)
    args = (blended, second)
    specs = [whole(a) for a in args]
    more = {}
    if before is not None:
        args += (before,)
        specs.append(pl.BlockSpec(memory_space=pl.ANY))
        more["input_output_aliases"] = {2: 0}
    return call(
        functools.partial(predict_kernel, part),
        jax.ShapeDtypeStruct(shape, BF16),
        [
            pltpu.VMEM((tiles, chans * rows, TILE), F32),
            pltpu.VMEM((3 * POOL * chans, (POOL + 2) * chans), F32),
            pltpu.VMEM((3 * POOL * chans, (POOL + 2) * chans), BF16),
        ],
        len(args),
        12,
        flops=10**9,
        grid=(1,),
        in_specs=specs,
        out_specs=block,
        **more,
    )(*args)


def shards(features, shifts, first_kernel, bottle_kernel, second_kernel, cotangent):
    imgs, chans, height, span = features.shape
    rows, cols, dp = (lax.axis_size(a) for a in ("rows", "cols", "dp"))
    tiles = span // TILE
    width = span + TILE
    full = height * chans
    groups = height // POOL
    single = cols == 2

    def bf(*shape):
        return jax.ShapeDtypeStruct(shape, BF16)

    ahead = [(i, i + 1) for i in range(rows - 1)]
    astern = [(i + 1, i) for i in range(rows - 1)]

    def diagonal(message, step, turns):
        pairs = []
        for i in range(rows):
            for j in range(cols):
                for move in turns:
                    if 0 <= i + step < rows and 0 <= j + move < cols:
                        pairs.append((i * cols + j, (i + step) * cols + j + move))
        return lax.ppermute(message, ("rows", "cols"), pairs)

    feat_rows, up_feat, down_feat = call(
        feature_kernel,
        (bf(full, span), bf(FHALO * chans, span), bf(FHALO * chans, span)),
        [],
        1,
        8,
    )(features[0])
    up_f = lax.ppermute(down_feat, "rows", ahead)
    down_f = lax.ppermute(up_feat, "rows", astern)

    if single:
        edges = (("up", "single"), ("down", "single"))
    else:
        edges = tuple((v, e) for v in ("up", "down") for e in ("left", "right"))
    packed = pl.cdiv(FHALO + CHALO, POOL) * chans
    cot_rows, up_cot, down_cot, col_msg, *corner_msgs = call(
        functools.partial(pack_kernel, edges),
        (bf(full, span), bf(CHALO * chans, span), bf(CHALO * chans, span), bf(full, TILE))
        + tuple(bf(packed, TILE) for _ in edges),
        [],
        2,
        8,
    )(feat_rows, cotangent[0])
    up_c = lax.ppermute(down_cot, "rows", ahead)
    down_c = lax.ppermute(up_cot, "rows", astern)
    if single:
        up_r = up_l = diagonal(corner_msgs[1], 1, (-1, 1))
        down_r = down_l = diagonal(corner_msgs[0], -1, (-1, 1))
        col_r = col_l = lax.ppermute(col_msg, "cols", [(0, 1), (1, 0)])
    else:
        up_r = diagonal(corner_msgs[2], 1, (-1,))
        up_l = diagonal(corner_msgs[3], 1, (1,))
        down_r = diagonal(corner_msgs[0], -1, (-1,))
        down_l = diagonal(corner_msgs[1], -1, (1,))
        col_r = lax.ppermute(col_msg, "cols", [(i + 1, i) for i in range(cols - 1)])
        col_l = lax.ppermute(col_msg, "cols", [(i, i + 1) for i in range(cols - 1)])

    tall_c = (height + 2 * CHALO) * chans
    view = bf((height + 2) * chans, span)
    band = 3 * (POOL + 2) * chans
    act_grad, *views = call(
        functools.partial(back_kernel, single),
        (jax.ShapeDtypeStruct((full, span), F32), view, view, view),
        [pltpu.VMEM((tall_c, width), BF16)] * 3
        + [pltpu.VMEM(((height + 2 * POOL) * chans, span), BF16)]
        + [pltpu.VMEM(((groups + 2) * chans, width), BF16)] * 3
        + [
            pltpu.VMEM((band, POOL * chans), F32),
            pltpu.VMEM((POOL * chans, band), BF16),
            pltpu.VMEM((9 * chans, TILE), F32),
            pltpu.VMEM((3 * chans, 3 * chans), BF16),
        ],
        11,
        16,
        flops=8 * 10**9,
    )(
        cot_rows, up_c, down_c, col_r, col_l, up_r, up_l, down_r, down_l,
        second_kernel, bottle_kernel,
    )

    tall = (height + 2 * EXT) * chans
    grads, blended = call(
        functools.partial(main_kernel, single),
        (jax.ShapeDtypeStruct((9 * chans // 2, TILE), F32), bf((height + 2) * chans, width)),
        [
            pltpu.VMEM((tiles + 1, (height + 2 * FHALO) * chans, TILE), F32),
            pltpu.VMEM((tiles + 1, tall, TILE), F32),
        ]
        + [pltpu.VMEM((tall, width), BF16)] * 3
        + [pltpu.VMEM(((height + 4 * POOL) * chans, width), BF16)]
        + [pltpu.VMEM(((groups + 4) * chans, width), BF16)] * 3
        + [
            pltpu.VMEM((full, span), BF16),
            pltpu.VMEM((band, POOL * chans), F32),
            pltpu.VMEM((POOL * chans, band), F32),
            pltpu.VMEM((POOL * chans, band), BF16),
            pltpu.VMEM((chans, 9 * chans), F32),
            pltpu.VMEM((3 * chans, 3 * chans), BF16),
        ],
        16,
        32,
        flops=10**10,
        smem_first=True,
    )(
        shifts[0], feat_rows, up_f, down_f, col_r, col_l, up_r, up_l, down_r, down_l,
        act_grad, *views, first_kernel, bottle_kernel,
    )

    steps = []
    for axis, size in (("dp", dp), ("cols", cols), ("rows", rows)):
        bit = 1
        while bit < size:
            steps.append((axis, [(i, i ^ bit) for i in range(size)]))
            bit *= 2
    parts, prediction = 2, None
    for step, (axis, pairs) in enumerate(steps):
        other = lax.ppermute(grads, axis, pairs)
        if 1 <= step <= parts:
            prediction = predict(
                blended, second_kernel, (chans, height, span), parts, step - 1, prediction
            )
            other, prediction = lax.optimization_barrier((other, prediction))
        if step < len(steps) - 1:
            grads = grads + other
            if step < parts:
                grads, blended = lax.optimization_barrier((grads, blended))
    factor = 1.0 / math.sqrt(imgs * dp * height * rows * span * cols)
    shape = jax.ShapeDtypeStruct((9, chans, chans), F32)
    first_grad, second_grad = call(
        functools.partial(final_kernel, factor), (shape, shape), [], 2, 2
    )(grads, other)
    return (prediction[None], first_grad, second_grad)


def solution(mesh):
    placed = (
        P("dp", None, "rows", "cols"),
        P("dp", None, None),
        P(),
        P(),
        P(),
        P("dp", None, "rows", "cols"),
    )
    return jax.shard_map(
        shards,
        mesh=mesh,
        in_specs=placed,
        out_specs=(P("dp", None, "rows", "cols"), P(), P()),
        check_vma=False,
    )
```

time: 415 us -> 77 us (0.19)
  waiting for transfers between devices: 166 us -> 19.6 us
  local copies, waits for them, and re-layouts: 122 us -> 1.82 us
  matrix products: 43 us -> 0 us
  Pallas kernels: 0 us -> 22.4 us
  starting transfers between devices: 51.4 us -> 31.9 us
  other arithmetic: 16.2 us -> 0.04 us
  between operations: 14.7 us -> 0.81 us
    psum x1 -> x0, waiting for transfers between devices: 124 us -> none  [shards(): lax.psum((first_grad, second_grad), ('rows', 'cols', 'dp'))]
    gather x96 -> x0, local copies, waits for them, and re-layouts: 85.3 us -> none
    dot_general x63 -> x0, matrix products: 43 us -> none  [the longest x27 19.6 us: convolve_ext(): jnp.einsum('oi,bihw->bohw', kernel[tap_index], window, preferred_element_...]
    pallas_call x0 -> x7, Pallas kernels: none -> 22.4 us  [the longest x1 12.3 us: shards(): call(functools.partial(main_kernel, single), (jax.ShapeDtypeStruct((9 * c...]
    ppermute x20 -> x12, waiting for transfers between devices: 42 us -> 19.6 us  [the longest x1 11.5 us: shards(): up_f = lax.ppermute(down_feat, 'rows', ahead)]
    ppermute x20 -> x12, starting transfers between devices: 51.4 us -> 31.9 us  [the longest x5 11.9 us: shards(): other = lax.ppermute(grads, axis, pairs)]
    broadcast_in_dim x6 -> x0, local copies, waits for them, and re-layouts: 11 us -> none  [upsample(): return jnp.repeat(jnp.repeat(values, POOL, axis=2), POOL, axis=3)]
    reduce_sum x2 -> x0, other arithmetic: 7.22 us -> none  [pool_sum(): values.reshape(shape[0], shape[1], shape[2] // POOL, POOL, shape[3] // PO...]
  transfers between devices with their start and end apart: 21 -> 12, of which waited for: 13 -> 7; matrix products, arithmetic and copies ran while one was open for 6% -> 0% of each run, Pallas kernels for 0% -> 11%
where the time goes in v2:
time: 77 us; the launch traced here: 76.7 us
  starting transfers between devices  31.9 us (41%)
  Pallas kernels  22.4 us (29%)
  waiting for transfers between devices  19.6 us (25%)
  local copies, waits for them, and re-layouts  1.82 us (2%)
  between operations  0.81 us (1%)
    pallas_call x1, Pallas kernels, shards(): call(functools.partial(main_kernel, single), (jax.ShapeDtypeStruct((9 * c...  12.3 us
    ppermute x5, starting transfers between devices, shards(): other = lax.ppermute(grads, axis, pairs)  11.9 us
    ppermute x1, waiting for transfers between devices, shards(): up_f = lax.ppermute(down_feat, 'rows', ahead)  11.5 us
    ppermute x5, waiting for transfers between devices, shards(): other = lax.ppermute(grads, axis, pairs)  7.28 us
    ppermute x2, starting transfers between devices, diagonal(): return lax.ppermute(message, ('rows', 'cols'), pairs)  5.81 us
    ppermute x1, starting transfers between devices, shards(): up_f = lax.ppermute(down_feat, 'rows', ahead)  5.21 us
    pallas_call x2, Pallas kernels, predict(): call(functools.partial(predict_kernel, part), jax.ShapeDtypeStruct(shape,...  4.61 us
    pallas_call x1, Pallas kernels, shards(): call(functools.partial(back_kernel, single), (jax.ShapeDtypeStruct((full,...  3.59 us
  transfers between devices with their start and end apart: 12, of which 7 were waited for; matrix products, arithmetic and copies ran while one was open for 0% of the time, Pallas kernels for 11%

profile of v2, /device:TPU:0, one launch (start us, length us, event | category | flops | bytes accessed | tf_op | source)
XLA Modules:
  0.0 76.7 jit_solution(7607805170540344485)
XLA Ops:
  0.6 1.0 %copy-done = bf16[1,32,32,256]{3,2,1,0:T(8,128)(2,1)S(1)} copy-done((bf16[1,32,32,256]{3,2,1,0:T(8,128)(2,1)S(1)}, bf16[1,32,32,256]{3,2,1,0:T(8,128)(2,1)}, u32[]{:S(2)}) %copy-start) | copy-done | bytes 524312
  2.0 0.7 copy-done.1
  2.7 0.6 shard_map.86
  3.4 3.0 %collective-permute-start.2 = (bf16[1024,128]{1,0:T(8,128)(2,1)S(1)}, bf16[1024,128]{1,0:T(8,128)(2,1)S(1)}, u32[]{:S(2)}, u32[]{:S(2)}) collective-permute-start(bf16[1024,128]{1,0:T(8,128)(2,1)S(1)} %get-tuple-element.31), channel_id=1, source_target_pairs={{0,2},{2,0},{1,3},{3,1},{4,6},{6,4},{5,7},{7,5},{8,10},{10,8},{9,1... | collective-permute-start | bytes 786440 | tf_op jit(solution)/shard_map/ppermute | solution.py:579
  6.4 3.4 %collective-permute-start.5 = (bf16[160,256]{1,0:T(8,128)(2,1)S(1)}, bf16[160,256]{1,0:T(8,128)(2,1)S(1)}, u32[]{:S(2)}, u32[]{:S(2)}) collective-permute-start(bf16[160,256]{1,0:T(8,128)(2,1)S(1)} %get-tuple-element.35), channel_id=1, source_target_pairs={{0,4},{4,8},{8,12},{12,16},{16,20},{20,24},{24,28},{1,5},{5,9},{9,... | collective-permute-start | bytes 245768 | tf_op jit(solution)/shard_map/ppermute | solution.py:574
  9.8 1.3 %collective-permute-start.6 = (bf16[160,256]{1,0:T(8,128)(2,1)S(1)}, bf16[160,256]{1,0:T(8,128)(2,1)S(1)}, u32[]{:S(2)}, u32[]{:S(2)}) collective-permute-start(bf16[160,256]{1,0:T(8,128)(2,1)S(1)} %get-tuple-element.36), channel_id=1, source_target_pairs={{4,0},{8,4},{12,8},{16,12},{20,16},{24,20},{28,24},{5,1},{9,5},{13... | collective-permute-start | bytes 245768 | tf_op jit(solution)/shard_map/ppermute | solution.py:575
  11.1 4.5 %collective-permute-start.3 = (bf16[256,128]{1,0:T(8,128)(2,1)S(1)}, bf16[256,128]{1,0:T(8,128)(2,1)S(1)}, u32[]{:S(2)}, u32[]{:S(2)}) collective-permute-start(bf16[256,128]{1,0:T(8,128)(2,1)S(1)} %get-tuple-element.32), channel_id=1, source_target_pairs={{0,6},{2,4},{4,10},{6,8},{8,14},{10,12},{12,18},{14,16},{16,22},{1... | collective-permute-start | bytes 196616 | tf_op jit(solution)/shard_map/ppermute | solution.py:549
  15.6 1.3 %collective-permute-start.4 = (bf16[256,128]{1,0:T(8,128)(2,1)S(1)}, bf16[256,128]{1,0:T(8,128)(2,1)S(1)}, u32[]{:S(2)}, u32[]{:S(2)}) collective-permute-start(bf16[256,128]{1,0:T(8,128)(2,1)S(1)} %get-tuple-element.33), channel_id=1, source_target_pairs={{4,2},{6,0},{8,6},{10,4},{12,10},{14,8},{16,14},{18,12},{20,18},{2... | collective-permute-start | bytes 196616 | tf_op jit(solution)/shard_map/ppermute | solution.py:549
  17.5 5.2 %collective-permute-start = (bf16[800,256]{1,0:T(8,128)(2,1)S(1)}, bf16[800,256]{1,0:T(8,128)(2,1)S(1)}, u32[]{:S(2)}, u32[]{:S(2)}) collective-permute-start(bf16[800,256]{1,0:T(8,128)(2,1)S(1)} %get-tuple-element.29), channel_id=1, source_target_pairs={{0,4},{4,8},{8,12},{12,16},{16,20},{20,24},{24,28},{1,5},{5,9},{9,... | collective-permute-start | bytes 1228808 | tf_op jit(solution)/shard_map/ppermute | solution.py:558
  23.1 1.3 %collective-permute-start.1 = (bf16[800,256]{1,0:T(8,128)(2,1)S(1)}, bf16[800,256]{1,0:T(8,128)(2,1)S(1)}, u32[]{:S(2)}, u32[]{:S(2)}) collective-permute-start(bf16[800,256]{1,0:T(8,128)(2,1)S(1)} %get-tuple-element.30), channel_id=1, source_target_pairs={{4,0},{8,4},{12,8},{16,12},{20,16},{24,20},{28,24},{5,1},{9,5},{13... | collective-permute-start | bytes 1228808 | tf_op jit(solution)/shard_map/ppermute | solution.py:559
  24.5 3.6 %shard_map.87 = (f32[1024,256]{1,0:T(8,128)S(1)}, bf16[1088,256]{1,0:T(8,128)(2,1)S(1)}, bf16[1088,256]{1,0:T(8,128)(2,1)S(1)}, bf16[1088,256]{1,0:T(8,128)(2,1)S(1)}) custom-call(bf16[1024,256]{1,0:T(8,128)(2,1)S(1)} %get-tuple-element.34.cot, bf16[160,256]{1,0:T(8,128)(2,1)S(1)} %collective-permute-done.5.up, ...), custom_call_target="tpu_custom_call" | custom-call | flops 8000000000 | bytes 4194304 | tf_op jit(solution)/shard_map/pallas_call | solution.py:591
  28.1 11.5 %collective-permute-done.up = bf16[800,256]{1,0:T(8,128)(2,1)S(1)} collective-permute-done((bf16[800,256]{1,0:T(8,128)(2,1)S(1)}, bf16[800,256]{1,0:T(8,128)(2,1)S(1)}, u32[]{:S(2)}, u32[]{:S(2)}) %collective-permute-start) | collective-permute-done | bytes 409632 | tf_op jit(solution)/shard_map/ppermute | solution.py:558
  39.5 12.3 %shard_map.88 = (f32[144,128]{1,0:T(8,128)S(1)}, bf16[1088,384]{1,0:T(8,128)(2,1)S(1)}) custom-call(s32[32,2]{1,0:T(8,128)S(1)} %copy.10.shifts, bf16[1024,256]{1,0:T(8,128)(2,1)S(1)} %get-tuple-element.28.feat_rows.feat, bf16[800,256]{1,0:T(8,128)(2,1)S(1)} %collective-permute-done.up, bf16[800,256]{1,0:T(8,128)(2,1)S(1)} %collective-permute-done.1.down, ...), custom_call_target="tpu_custom_call" | custom-call | flops 10000000000 | bytes 4194304 | tf_op jit(solution)/shard_map/pallas_call | solution.py:612
  51.9 1.3 %collective-permute-done.7 = f32[144,128]{1,0:T(8,128)S(1)} collective-permute-done((f32[144,128]{1,0:T(8,128)S(1)}, f32[144,128]{1,0:T(8,128)S(1)}, u32[]{:S(2)}, u32[]{:S(2)}) %collective-permute-start.7) | collective-permute-done | bytes 73760 | tf_op jit(solution)/shard_map/ppermute | solution.py:647
  53.2 1.6 %collective-permute-start.8 = (f32[144,128]{1,0:T(8,128)S(1)}, f32[144,128]{1,0:T(8,128)S(1)}, u32[]{:S(2)}, u32[]{:S(2)}) collective-permute-start(f32[144,128]{1,0:T(8,128)S(1)} %add.12), channel_id=1, source_target_pairs={{0,2},{2,0},{1,3},{3,1},{4,6},{6,4},{5,7},{7,5},{8,10},{10,8},{9,1... | collective-permute-start | bytes 221192 | tf_op jit(solution)/shard_map/ppermute | solution.py:647
  54.8 2.3 %shard_map.89.rest_0_ = bf16[32,32,256]{2,1,0:T(8,128)(2,1)} custom-call(bf16[1088,384]{1,0:T(8,128)(2,1)S(1)} %get-tuple-element.47.blended, bf16[9,32,32]{2,1,0:T(8,128)(2,1)S(1)} %copy-done.4), custom_call_target="tpu_custom_call" | custom-call | flops 1000000000 | bytes 4194304 | tf_op jit(solution)/shard_map/pallas_call | solution.py:509
  57.1 0.5 collective-permute-done.8
  57.6 2.6 %collective-permute-start.9 = (f32[144,128]{1,0:T(8,128)S(1)}, f32[144,128]{1,0:T(8,128)S(1)}, u32[]{:S(2)}, u32[]{:S(2)}) collective-permute-start(f32[144,128]{1,0:T(8,128)S(1)} %add.13), channel_id=1, source_target_pairs={{0,4},{4,0},{8,12},{12,8},{16,20},{20,16},{24,28},{28,24},{1,5},{5... | collective-permute-start | bytes 221192 | tf_op jit(solution)/shard_map/ppermute | solution.py:647
  60.2 2.3 %shard_map.90 = bf16[32,32,256]{2,1,0:T(8,128)(2,1)} custom-call(bf16[1088,384]{1,0:T(8,128)(2,1)S(1)} %get-tuple-element.47.blended, bf16[9,32,32]{2,1,0:T(8,128)(2,1)S(1)} %copy-done.4, bf16[32,32,256]{2,1,0:T(8,128)(2,1)} %shard_map.89.rest_0_), custom_call_target="tpu_custom_call", output_to_operand_aliasing={{}: (2, {})} | custom-call | flops 1000000000 | bytes 4194304 | tf_op jit(solution)/shard_map/pallas_call | solution.py:509
  62.5 3.9 %collective-permute-start.10 = (f32[144,128]{1,0:T(8,128)S(1)}, f32[144,128]{1,0:T(8,128)S(1)}, u32[]{:S(2)}, u32[]{:S(2)}) collective-permute-start(f32[144,128]{1,0:T(8,128)S(1)} %add.14), channel_id=1, source_target_pairs={{0,8},{4,12},{8,0},{12,4},{16,24},{20,28},{24,16},{28,20},{1,9},{5... | collective-permute-start | bytes 221192 | tf_op jit(solution)/shard_map/ppermute | solution.py:647
  66.5 2.3 %collective-permute-done.10 = f32[144,128]{1,0:T(8,128)S(1)} collective-permute-done((f32[144,128]{1,0:T(8,128)S(1)}, f32[144,128]{1,0:T(8,128)S(1)}, u32[]{:S(2)}, u32[]{:S(2)}) %collective-permute-start.10) | collective-permute-done | bytes 73760 | tf_op jit(solution)/shard_map/ppermute | solution.py:647
  68.8 3.8 %collective-permute-start.11 = (f32[144,128]{1,0:T(8,128)S(1)}, f32[144,128]{1,0:T(8,128)S(1)}, u32[]{:S(2)}, u32[]{:S(2)}) collective-permute-start(f32[144,128]{1,0:T(8,128)S(1)} %add.15.mine), channel_id=1, source_target_pairs={{0,16},{4,20},{8,24},{12,28},{16,0},{20,4},{24,8},{28,12},{1,17},{... | collective-permute-start | bytes 221192 | tf_op jit(solution)/shard_map/ppermute | solution.py:647
  72.6 3.1 %collective-permute-done.11.other = f32[144,128]{1,0:T(8,128)S(1)} collective-permute-done((f32[144,128]{1,0:T(8,128)S(1)}, f32[144,128]{1,0:T(8,128)S(1)}, u32[]{:S(2)}, u32[]{:S(2)}) %collective-permute-start.11) | collective-permute-done | bytes 73760 | tf_op jit(solution)/shard_map/ppermute | solution.py:647
  75.7 0.9 %shard_map.91 = (f32[9,32,32]{2,1,0:T(8,128)}, f32[9,32,32]{2,1,0:T(8,128)}) custom-call(f32[144,128]{1,0:T(8,128)S(1)} %add.15.mine, f32[144,128]{1,0:T(8,128)S(1)} %collective-permute-done.11.other), custom_call_target="tpu_custom_call" | custom-call | bytes 4194304 | tf_op jit(solution)/shard_map/pallas_call | solution.py:659
  (24 shorter events, 1.5 us)
Async XLA Ops:
  0.6 1.0 %copy-start = (bf16[1,32,32,256]{3,2,1,0:T(8,128)(2,1)S(1)}, bf16[1,32,32,256]{3,2,1,0:T(8,128)(2,1)}, u32[]{:S(2)}) copy-start(bf16[1,32,32,256]{3,2,1,0:T(8,128)(2,1)} %param.6) | copy-start | bytes 1572868
  1.7 1.0 %copy-start.1 = (bf16[1,32,32,256]{3,2,1,0:T(8,128)(2,1)S(1)}, bf16[1,32,32,256]{3,2,1,0:T(8,128)(2,1)}, u32[]{:S(2)}) copy-start(bf16[1,32,32,256]{3,2,1,0:T(8,128)(2,1)} %param.11) | copy-start | bytes 1572868
  2.7 21.7 %copy-start.2 = (bf16[9,32,32]{2,1,0:T(8,128)(2,1)S(1)}, bf16[9,32,32]{2,1,0:T(8,128)(2,1)}, u32[]{:S(2)}) copy-start(bf16[9,32,32]{2,1,0:T(8,128)(2,1)} %bottle.3) | copy-start | bytes 55300
  2.7 21.7 %copy-start.4 = (bf16[9,32,32]{2,1,0:T(8,128)(2,1)S(1)}, bf16[9,32,32]{2,1,0:T(8,128)(2,1)}, u32[]{:S(2)}) copy-start(bf16[9,32,32]{2,1,0:T(8,128)(2,1)} %second.5) | copy-start | bytes 55300
  3.4 21.1 %collective-permute-start.2 = (bf16[1024,128]{1,0:T(8,128)(2,1)S(1)}, bf16[1024,128]{1,0:T(8,128)(2,1)S(1)}, u32[]{:S(2)}, u32[]{:S(2)}) collective-permute-start(bf16[1024,128]{1,0:T(8,128)(2,1)S(1)} %get-tuple-element.31), channel_id=1, source_target_pairs={{0,2},{2,0},{1,3},{3,1},{4,6},{6,4},{5,7},{7,5},{8,10},{10,8},{9,1... | collective-permute-start | bytes 786440 | tf_op jit(solution)/shard_map/ppermute | solution.py:579
  6.4 18.0 %collective-permute-start.5 = (bf16[160,256]{1,0:T(8,128)(2,1)S(1)}, bf16[160,256]{1,0:T(8,128)(2,1)S(1)}, u32[]{:S(2)}, u32[]{:S(2)}) collective-permute-start(bf16[160,256]{1,0:T(8,128)(2,1)S(1)} %get-tuple-element.35), channel_id=1, source_target_pairs={{0,4},{4,8},{8,12},{12,16},{16,20},{20,24},{24,28},{1,5},{5,9},{9,... | collective-permute-start | bytes 245768 | tf_op jit(solution)/shard_map/ppermute | solution.py:574
  9.8 14.6 %collective-permute-start.6 = (bf16[160,256]{1,0:T(8,128)(2,1)S(1)}, bf16[160,256]{1,0:T(8,128)(2,1)S(1)}, u32[]{:S(2)}, u32[]{:S(2)}) collective-permute-start(bf16[160,256]{1,0:T(8,128)(2,1)S(1)} %get-tuple-element.36), channel_id=1, source_target_pairs={{4,0},{8,4},{12,8},{16,12},{20,16},{24,20},{28,24},{5,1},{9,5},{13... | collective-permute-start | bytes 245768 | tf_op jit(solution)/shard_map/ppermute | solution.py:575
  11.1 6.4 %collective-permute-start.3 = (bf16[256,128]{1,0:T(8,128)(2,1)S(1)}, bf16[256,128]{1,0:T(8,128)(2,1)S(1)}, u32[]{:S(2)}, u32[]{:S(2)}) collective-permute-start(bf16[256,128]{1,0:T(8,128)(2,1)S(1)} %get-tuple-element.32), channel_id=1, source_target_pairs={{0,6},{2,4},{4,10},{6,8},{8,14},{10,12},{12,18},{14,16},{16,22},{1... | collective-permute-start | bytes 196616 | tf_op jit(solution)/shard_map/ppermute | solution.py:549
  15.6 1.3 %copy-start.5 = (s32[1,32,2]{1,2,0:T(2,128)S(1)}, s32[1,32,2]{1,2,0:T(2,128)}, u32[]{:S(2)}) copy-start(s32[1,32,2]{1,2,0:T(2,128)} %param.7) | copy-start | bytes 772
  15.6 7.5 %collective-permute-start.4 = (bf16[256,128]{1,0:T(8,128)(2,1)S(1)}, bf16[256,128]{1,0:T(8,128)(2,1)S(1)}, u32[]{:S(2)}, u32[]{:S(2)}) collective-permute-start(bf16[256,128]{1,0:T(8,128)(2,1)S(1)} %get-tuple-element.33), channel_id=1, source_target_pairs={{4,2},{6,0},{8,6},{10,4},{12,10},{14,8},{16,14},{18,12},{20,18},{2... | collective-permute-start | bytes 196616 | tf_op jit(solution)/shard_map/ppermute | solution.py:549
  17.5 22.0 %collective-permute-start = (bf16[800,256]{1,0:T(8,128)(2,1)S(1)}, bf16[800,256]{1,0:T(8,128)(2,1)S(1)}, u32[]{:S(2)}, u32[]{:S(2)}) collective-permute-start(bf16[800,256]{1,0:T(8,128)(2,1)S(1)} %get-tuple-element.29), channel_id=1, source_target_pairs={{0,4},{4,8},{8,12},{12,16},{16,20},{20,24},{24,28},{1,5},{5,9},{9,... | collective-permute-start | bytes 1228808 | tf_op jit(solution)/shard_map/ppermute | solution.py:558
  23.1 16.4 %collective-permute-start.1 = (bf16[800,256]{1,0:T(8,128)(2,1)S(1)}, bf16[800,256]{1,0:T(8,128)(2,1)S(1)}, u32[]{:S(2)}, u32[]{:S(2)}) collective-permute-start(bf16[800,256]{1,0:T(8,128)(2,1)S(1)} %get-tuple-element.30), channel_id=1, source_target_pairs={{4,0},{8,4},{12,8},{16,12},{20,16},{24,20},{28,24},{5,1},{9,5},{13... | collective-permute-start | bytes 1228808 | tf_op jit(solution)/shard_map/ppermute | solution.py:559
  24.5 15.1 %copy-start.3 = (bf16[9,32,32]{2,1,0:T(8,128)(2,1)S(1)}, bf16[9,32,32]{2,1,0:T(8,128)(2,1)}, u32[]{:S(2)}) copy-start(bf16[9,32,32]{2,1,0:T(8,128)(2,1)} %first.1) | copy-start | bytes 55300
  51.9 1.3 %collective-permute-start.7 = (f32[144,128]{1,0:T(8,128)S(1)}, f32[144,128]{1,0:T(8,128)S(1)}, u32[]{:S(2)}, u32[]{:S(2)}) collective-permute-start(f32[144,128]{1,0:T(8,128)S(1)} %get-tuple-element.41), channel_id=1, source_target_pairs={{0,1},{1,0},{2,3},{3,2},{4,5},{5,4},{6,7},{7,6},{8,9},{9,8},{10,11... | collective-permute-start | bytes 221192 | tf_op jit(solution)/shard_map/ppermute | solution.py:647
  53.2 4.4 %collective-permute-start.8 = (f32[144,128]{1,0:T(8,128)S(1)}, f32[144,128]{1,0:T(8,128)S(1)}, u32[]{:S(2)}, u32[]{:S(2)}) collective-permute-start(f32[144,128]{1,0:T(8,128)S(1)} %add.12), channel_id=1, source_target_pairs={{0,2},{2,0},{1,3},{3,1},{4,6},{6,4},{5,7},{7,5},{8,10},{10,8},{9,1... | collective-permute-start | bytes 221192 | tf_op jit(solution)/shard_map/ppermute | solution.py:647
  57.6 4.9 %collective-permute-start.9 = (f32[144,128]{1,0:T(8,128)S(1)}, f32[144,128]{1,0:T(8,128)S(1)}, u32[]{:S(2)}, u32[]{:S(2)}) collective-permute-start(f32[144,128]{1,0:T(8,128)S(1)} %add.13), channel_id=1, source_target_pairs={{0,4},{4,0},{8,12},{12,8},{16,20},{20,16},{24,28},{28,24},{1,5},{5... | collective-permute-start | bytes 221192 | tf_op jit(solution)/shard_map/ppermute | solution.py:647
  62.5 6.2 %collective-permute-start.10 = (f32[144,128]{1,0:T(8,128)S(1)}, f32[144,128]{1,0:T(8,128)S(1)}, u32[]{:S(2)}, u32[]{:S(2)}) collective-permute-start(f32[144,128]{1,0:T(8,128)S(1)} %add.14), channel_id=1, source_target_pairs={{0,8},{4,12},{8,0},{12,4},{16,24},{20,28},{24,16},{28,20},{1,9},{5... | collective-permute-start | bytes 221192 | tf_op jit(solution)/shard_map/ppermute | solution.py:647
  68.8 6.9 %collective-permute-start.11 = (f32[144,128]{1,0:T(8,128)S(1)}, f32[144,128]{1,0:T(8,128)S(1)}, u32[]{:S(2)}, u32[]{:S(2)}) collective-permute-start(f32[144,128]{1,0:T(8,128)S(1)} %add.15.mine), channel_id=1, source_target_pairs={{0,16},{4,20},{8,24},{12,28},{16,0},{20,4},{24,8},{28,12},{1,17},{... | collective-permute-start | bytes 221192 | tf_op jit(solution)/shard_map/ppermute | solution.py:647

commit v3 on v2

--- a/solution.py
+++ b/solution.py
@@ -570,6 +570,7 @@
         [],
         2,
         8,
+        flops=2 * 10**10,
     )(feat_rows, cotangent[0])
     up_c = lax.ppermute(down_cot, "rows", ahead)
     down_c = lax.ppermute(up_cot, "rows", astern)
@@ -602,7 +603,6 @@
         ],
         11,
         16,
-        flops=8 * 10**9,
     )(
         cot_rows, up_c, down_c, col_r, col_l, up_r, up_l, down_r, down_l,
         second_kernel, bottle_kernel,

time: 77 us -> 69.9 us (0.908)
  waiting for transfers between devices: 19.6 us -> 13.1 us
    ppermute x1, waiting for transfers between devices: 11.5 us -> 0.01 us  [shards(): up_f = lax.ppermute(down_feat, 'rows', ahead)]
    ppermute x1, waiting for transfers between devices: 0.01 us -> 4.94 us  [shards(): up_c = lax.ppermute(down_cot, 'rows', ahead)]
    ppermute x1, starting transfers between devices: 3.42 us -> 5.57 us  [shards(): up_c = lax.ppermute(down_cot, 'rows', ahead)]
    ppermute x1, starting transfers between devices: 3 us -> 1.49 us  [shards(): col_r = col_l = lax.ppermute(col_msg, 'cols', [(0, 1), (1, 0)])]
    ppermute x5, starting transfers between devices: 11.9 us -> 11.1 us  [shards(): other = lax.ppermute(grads, axis, pairs)]
    ppermute x5, waiting for transfers between devices: 7.28 us -> 6.48 us  [shards(): other = lax.ppermute(grads, axis, pairs)]
  transfers between devices with their start and end apart: 12 -> 12, of which waited for: 7 -> 7; matrix products, arithmetic and copies ran while one was open for 0% -> 0% of each run, Pallas kernels for 11% -> 14%
where the time goes in v3:
time: 69.9 us; the launch traced here: 69.6 us
  starting transfers between devices  31.4 us (45%)
  Pallas kernels  23.1 us (33%)
  waiting for transfers between devices  13.1 us (19%)
  local copies, waits for them, and re-layouts  1.15 us (2%)
  between operations  0.82 us (1%)
    pallas_call x1, Pallas kernels, shards(): call(functools.partial(main_kernel, single), (jax.ShapeDtypeStruct((9 * c...  12.3 us
    ppermute x5, starting transfers between devices, shards(): other = lax.ppermute(grads, axis, pairs)  11.1 us
    ppermute x5, waiting for transfers between devices, shards(): other = lax.ppermute(grads, axis, pairs)  6.48 us
    ppermute x2, starting transfers between devices, diagonal(): return lax.ppermute(message, ('rows', 'cols'), pairs)  5.8 us
    ppermute x1, starting transfers between devices, shards(): up_c = lax.ppermute(down_cot, 'rows', ahead)  5.57 us
    ppermute x1, waiting for transfers between devices, shards(): up_c = lax.ppermute(down_cot, 'rows', ahead)  4.94 us
    ppermute x1, starting transfers between devices, shards(): up_f = lax.ppermute(down_feat, 'rows', ahead)  4.9 us
    pallas_call x2, Pallas kernels, predict(): call(functools.partial(predict_kernel, part), jax.ShapeDtypeStruct(shape,...  4.61 us
  transfers between devices with their start and end apart: 12, of which 7 were waited for; matrix products, arithmetic and copies ran while one was open for 0% of the time, Pallas kernels for 14%

profile of v3, /device:TPU:0, one launch (start us, length us, event | category | flops | bytes accessed | tf_op | source)
XLA Modules:
  0.0 69.6 jit_solution(9673549367651161135)
XLA Ops:
  0.6 1.0 %copy-done = bf16[1,32,32,256]{3,2,1,0:T(8,128)(2,1)S(1)} copy-done((bf16[1,32,32,256]{3,2,1,0:T(8,128)(2,1)S(1)}, bf16[1,32,32,256]{3,2,1,0:T(8,128)(2,1)}, u32[]{:S(2)}) %copy-start) | copy-done | bytes 524312
  2.0 4.9 %collective-permute-start = (bf16[800,256]{1,0:T(8,128)(2,1)S(1)}, bf16[800,256]{1,0:T(8,128)(2,1)S(1)}, u32[]{:S(2)}, u32[]{:S(2)}) collective-permute-start(bf16[800,256]{1,0:T(8,128)(2,1)S(1)} %get-tuple-element.29), channel_id=1, source_target_pairs={{0,4},{4,8},{8,12},{12,16},{16,20},{20,24},{24,28},{1,5},{5,9},{9,... | collective-permute-start | bytes 1228808 | tf_op jit(solution)/shard_map/ppermute | solution.py:558
  7.0 1.3 %collective-permute-start.1 = (bf16[800,256]{1,0:T(8,128)(2,1)S(1)}, bf16[800,256]{1,0:T(8,128)(2,1)S(1)}, u32[]{:S(2)}, u32[]{:S(2)}) collective-permute-start(bf16[800,256]{1,0:T(8,128)(2,1)S(1)} %get-tuple-element.30), channel_id=1, source_target_pairs={{4,0},{8,4},{12,8},{16,12},{20,16},{24,20},{28,24},{5,1},{9,5},{13... | collective-permute-start | bytes 1228808 | tf_op jit(solution)/shard_map/ppermute | solution.py:559
  8.3 1.3 %shard_map.86 = (bf16[1024,256]{1,0:T(8,128)(2,1)S(1)}, bf16[160,256]{1,0:T(8,128)(2,1)S(1)}, bf16[160,256]{1,0:T(8,128)(2,1)}, bf16[1024,128]{1,0:T(8,128)(2,1)...) custom-call(bf16[1024,256]{1,0:T(8,128)(2,1)S(1)} %get-tuple-element.28.feat_rows.feat, ...), custom_call_target="tpu_custom_call" | custom-call | flops 20000000000 | bytes 4194304 | tf_op jit(solution)/shard_map/pallas_call | solution.py:566
  9.6 1.5 %collective-permute-start.2 = (bf16[1024,128]{1,0:T(8,128)(2,1)}, bf16[1024,128]{1,0:T(8,128)(2,1)S(1)}, u32[]{:S(2)}, u32[]{:S(2)}) collective-permute-start(bf16[1024,128]{1,0:T(8,128)(2,1)} %get-tuple-element.31), channel_id=1, source_target_pairs={{0,2},{2,0},{1,3},{3,1},{4,6},{6,4},{5,7},{7,5},{8,10},{10,8},{9,1... | collective-permute-start | bytes 786440 | tf_op jit(solution)/shard_map/ppermute | solution.py:580
  11.1 4.5 %collective-permute-start.3 = (bf16[256,128]{1,0:T(8,128)(2,1)S(1)}, bf16[256,128]{1,0:T(8,128)(2,1)S(1)}, u32[]{:S(2)}, u32[]{:S(2)}) collective-permute-start(bf16[256,128]{1,0:T(8,128)(2,1)S(1)} %get-tuple-element.32), channel_id=1, source_target_pairs={{0,6},{2,4},{4,10},{6,8},{8,14},{10,12},{12,18},{14,16},{16,22},{1... | collective-permute-start | bytes 196616 | tf_op jit(solution)/shard_map/ppermute | solution.py:549
  15.6 1.3 %collective-permute-start.4 = (bf16[256,128]{1,0:T(8,128)(2,1)S(1)}, bf16[256,128]{1,0:T(8,128)(2,1)S(1)}, u32[]{:S(2)}, u32[]{:S(2)}) collective-permute-start(bf16[256,128]{1,0:T(8,128)(2,1)S(1)} %get-tuple-element.33), channel_id=1, source_target_pairs={{4,2},{6,0},{8,6},{10,4},{12,10},{14,8},{16,14},{18,12},{20,18},{2... | collective-permute-start | bytes 196616 | tf_op jit(solution)/shard_map/ppermute | solution.py:549
  16.9 1.1 %collective-permute-done.3.up_r.up_l = bf16[256,128]{1,0:T(8,128)(2,1)S(1)} collective-permute-done((bf16[256,128]{1,0:T(8,128)(2,1)S(1)}, bf16[256,128]{1,0:T(8,128)(2,1)S(1)}, u32[]{:S(2)}, u32[]{:S(2)}) %collective-permute-start.3) | collective-permute-done | bytes 65568 | tf_op jit(solution)/shard_map/ppermute | solution.py:549
  18.0 5.6 %collective-permute-start.5 = (bf16[160,256]{1,0:T(8,128)(2,1)}, bf16[160,256]{1,0:T(8,128)(2,1)S(1)}, u32[]{:S(2)}, u32[]{:S(2)}) collective-permute-start(bf16[160,256]{1,0:T(8,128)(2,1)} %get-tuple-element.35), channel_id=1, source_target_pairs={{0,4},{4,8},{8,12},{12,16},{16,20},{20,24},{24,28},{1,5},{5,9},{9,... | collective-permute-start | bytes 245768 | tf_op jit(solution)/shard_map/ppermute | solution.py:575
  23.6 1.3 %collective-permute-start.6 = (bf16[160,256]{1,0:T(8,128)(2,1)S(1)}, bf16[160,256]{1,0:T(8,128)(2,1)S(1)}, u32[]{:S(2)}, u32[]{:S(2)}) collective-permute-start(bf16[160,256]{1,0:T(8,128)(2,1)S(1)} %get-tuple-element.36), channel_id=1, source_target_pairs={{4,0},{8,4},{12,8},{16,12},{20,16},{24,20},{28,24},{5,1},{9,5},{13... | collective-permute-start | bytes 245768 | tf_op jit(solution)/shard_map/ppermute | solution.py:576
  25.0 4.9 %collective-permute-done.5.up = bf16[160,256]{1,0:T(8,128)(2,1)S(1)} collective-permute-done((bf16[160,256]{1,0:T(8,128)(2,1)}, bf16[160,256]{1,0:T(8,128)(2,1)S(1)}, u32[]{:S(2)}, u32[]{:S(2)}) %collective-permute-start.5) | collective-permute-done | bytes 81952 | tf_op jit(solution)/shard_map/ppermute | solution.py:575
  30.0 0.6 collective-permute-done.6.down
  30.5 3.6 %shard_map.87 = (f32[1024,256]{1,0:T(8,128)S(1)}, bf16[1088,256]{1,0:T(8,128)(2,1)S(1)}, bf16[1088,256]{1,0:T(8,128)(2,1)S(1)}, bf16[1088,256]{1,0:T(8,128)(2,1)S(1)}) custom-call(bf16[1024,256]{1,0:T(8,128)(2,1)S(1)} %get-tuple-element.34.cot, bf16[160,256]{1,0:T(8,128)(2,1)S(1)} %collective-permute-done.5.up, ...), custom_call_target="tpu_custom_call" | custom-call | bytes 4194304 | tf_op jit(solution)/shard_map/pallas_call | solution.py:592
  34.2 12.3 %shard_map.88 = (f32[144,128]{1,0:T(8,128)S(1)}, bf16[1088,384]{1,0:T(8,128)(2,1)S(1)}) custom-call(s32[32,2]{1,0:T(8,128)S(1)} %copy.10.shifts, bf16[1024,256]{1,0:T(8,128)(2,1)S(1)} %get-tuple-element.28.feat_rows.feat, bf16[800,256]{1,0:T(8,128)(2,1)S(1)} %collective-permute-done.up, bf16[800,256]{1,0:T(8,128)(2,1)S(1)} %collective-permute-done.1.down, ...), custom_call_target="tpu_custom_call" | custom-call | flops 10000000000 | bytes 4194304 | tf_op jit(solution)/shard_map/pallas_call | solution.py:612
  46.6 1.3 %collective-permute-done.7 = f32[144,128]{1,0:T(8,128)S(1)} collective-permute-done((f32[144,128]{1,0:T(8,128)S(1)}, f32[144,128]{1,0:T(8,128)S(1)}, u32[]{:S(2)}, u32[]{:S(2)}) %collective-permute-start.7) | collective-permute-done | bytes 73760 | tf_op jit(solution)/shard_map/ppermute | solution.py:647
  47.9 1.6 %collective-permute-start.8 = (f32[144,128]{1,0:T(8,128)S(1)}, f32[144,128]{1,0:T(8,128)S(1)}, u32[]{:S(2)}, u32[]{:S(2)}) collective-permute-start(f32[144,128]{1,0:T(8,128)S(1)} %add.12), channel_id=1, source_target_pairs={{0,2},{2,0},{1,3},{3,1},{4,6},{6,4},{5,7},{7,5},{8,10},{10,8},{9,1... | collective-permute-start | bytes 221192 | tf_op jit(solution)/shard_map/ppermute | solution.py:647
  49.4 2.3 %shard_map.89.rest_0_ = bf16[32,32,256]{2,1,0:T(8,128)(2,1)} custom-call(bf16[1088,384]{1,0:T(8,128)(2,1)S(1)} %get-tuple-element.47.blended, bf16[9,32,32]{2,1,0:T(8,128)(2,1)S(1)} %copy-done.2), custom_call_target="tpu_custom_call" | custom-call | flops 1000000000 | bytes 4194304 | tf_op jit(solution)/shard_map/pallas_call | solution.py:509
  52.3 3.0 %collective-permute-start.9 = (f32[144,128]{1,0:T(8,128)S(1)}, f32[144,128]{1,0:T(8,128)S(1)}, u32[]{:S(2)}, u32[]{:S(2)}) collective-permute-start(f32[144,128]{1,0:T(8,128)S(1)} %add.13), channel_id=1, source_target_pairs={{0,4},{4,0},{8,12},{12,8},{16,20},{20,16},{24,28},{28,24},{1,5},{5... | collective-permute-start | bytes 221192 | tf_op jit(solution)/shard_map/ppermute | solution.py:647
  55.3 2.3 %shard_map.90 = bf16[32,32,256]{2,1,0:T(8,128)(2,1)} custom-call(bf16[1088,384]{1,0:T(8,128)(2,1)S(1)} %get-tuple-element.47.blended, bf16[9,32,32]{2,1,0:T(8,128)(2,1)S(1)} %copy-done.2, bf16[32,32,256]{2,1,0:T(8,128)(2,1)} %shard_map.89.rest_0_), custom_call_target="tpu_custom_call", output_to_operand_aliasing={{}: (2, {})} | custom-call | flops 1000000000 | bytes 4194304 | tf_op jit(solution)/shard_map/pallas_call | solution.py:509
  57.6 2.8 %collective-permute-start.10 = (f32[144,128]{1,0:T(8,128)S(1)}, f32[144,128]{1,0:T(8,128)S(1)}, u32[]{:S(2)}, u32[]{:S(2)}) collective-permute-start(f32[144,128]{1,0:T(8,128)S(1)} %add.14), channel_id=1, source_target_pairs={{0,8},{4,12},{8,0},{12,4},{16,24},{20,28},{24,16},{28,20},{1,9},{5... | collective-permute-start | bytes 221192 | tf_op jit(solution)/shard_map/ppermute | solution.py:647
  60.4 2.3 %collective-permute-done.10 = f32[144,128]{1,0:T(8,128)S(1)} collective-permute-done((f32[144,128]{1,0:T(8,128)S(1)}, f32[144,128]{1,0:T(8,128)S(1)}, u32[]{:S(2)}, u32[]{:S(2)}) %collective-permute-start.10) | collective-permute-done | bytes 73760 | tf_op jit(solution)/shard_map/ppermute | solution.py:647
  62.8 3.6 %collective-permute-start.11 = (f32[144,128]{1,0:T(8,128)S(1)}, f32[144,128]{1,0:T(8,128)S(1)}, u32[]{:S(2)}, u32[]{:S(2)}) collective-permute-start(f32[144,128]{1,0:T(8,128)S(1)} %add.15.mine), channel_id=1, source_target_pairs={{0,16},{4,20},{8,24},{12,28},{16,0},{20,4},{24,8},{28,12},{1,17},{... | collective-permute-start | bytes 221192 | tf_op jit(solution)/shard_map/ppermute | solution.py:647
  66.4 2.3 %collective-permute-done.11.other = f32[144,128]{1,0:T(8,128)S(1)} collective-permute-done((f32[144,128]{1,0:T(8,128)S(1)}, f32[144,128]{1,0:T(8,128)S(1)}, u32[]{:S(2)}, u32[]{:S(2)}) %collective-permute-start.11) | collective-permute-done | bytes 73760 | tf_op jit(solution)/shard_map/ppermute | solution.py:647
  68.7 0.9 %shard_map.91 = (f32[9,32,32]{2,1,0:T(8,128)}, f32[9,32,32]{2,1,0:T(8,128)}) custom-call(f32[144,128]{1,0:T(8,128)S(1)} %add.15.mine, f32[144,128]{1,0:T(8,128)S(1)} %collective-permute-done.11.other), custom_call_target="tpu_custom_call" | custom-call | bytes 4194304 | tf_op jit(solution)/shard_map/pallas_call | solution.py:659
  (24 shorter events, 1.2 us)
Async XLA Ops:
  0.6 1.0 %copy-start = (bf16[1,32,32,256]{3,2,1,0:T(8,128)(2,1)S(1)}, bf16[1,32,32,256]{3,2,1,0:T(8,128)(2,1)}, u32[]{:S(2)}) copy-start(bf16[1,32,32,256]{3,2,1,0:T(8,128)(2,1)} %param.6) | copy-start | bytes 1572868
  1.7 6.6 %copy-start.3 = (bf16[1,32,32,256]{3,2,1,0:T(8,128)(2,1)S(1)}, bf16[1,32,32,256]{3,2,1,0:T(8,128)(2,1)}, u32[]{:S(2)}) copy-start(bf16[1,32,32,256]{3,2,1,0:T(8,128)(2,1)} %param.11) | copy-start | bytes 1572868
  2.0 32.1 %collective-permute-start = (bf16[800,256]{1,0:T(8,128)(2,1)S(1)}, bf16[800,256]{1,0:T(8,128)(2,1)S(1)}, u32[]{:S(2)}, u32[]{:S(2)}) collective-permute-start(bf16[800,256]{1,0:T(8,128)(2,1)S(1)} %get-tuple-element.29), channel_id=1, source_target_pairs={{0,4},{4,8},{8,12},{12,16},{16,20},{20,24},{24,28},{1,5},{5,9},{9,... | collective-permute-start | bytes 1228808 | tf_op jit(solution)/shard_map/ppermute | solution.py:558
  7.0 27.2 %collective-permute-start.1 = (bf16[800,256]{1,0:T(8,128)(2,1)S(1)}, bf16[800,256]{1,0:T(8,128)(2,1)S(1)}, u32[]{:S(2)}, u32[]{:S(2)}) collective-permute-start(bf16[800,256]{1,0:T(8,128)(2,1)S(1)} %get-tuple-element.30), channel_id=1, source_target_pairs={{4,0},{8,4},{12,8},{16,12},{20,16},{24,20},{28,24},{5,1},{9,5},{13... | collective-permute-start | bytes 1228808 | tf_op jit(solution)/shard_map/ppermute | solution.py:559
  8.3 22.3 %copy-start.1 = (bf16[9,32,32]{2,1,0:T(8,128)(2,1)S(1)}, bf16[9,32,32]{2,1,0:T(8,128)(2,1)}, u32[]{:S(2)}) copy-start(bf16[9,32,32]{2,1,0:T(8,128)(2,1)} %bottle.3) | copy-start | bytes 55300
  8.3 22.3 %copy-start.2 = (bf16[9,32,32]{2,1,0:T(8,128)(2,1)S(1)}, bf16[9,32,32]{2,1,0:T(8,128)(2,1)}, u32[]{:S(2)}) copy-start(bf16[9,32,32]{2,1,0:T(8,128)(2,1)} %second.5) | copy-start | bytes 55300
  9.6 20.9 %collective-permute-start.2 = (bf16[1024,128]{1,0:T(8,128)(2,1)}, bf16[1024,128]{1,0:T(8,128)(2,1)S(1)}, u32[]{:S(2)}, u32[]{:S(2)}) collective-permute-start(bf16[1024,128]{1,0:T(8,128)(2,1)} %get-tuple-element.31), channel_id=1, source_target_pairs={{0,2},{2,0},{1,3},{3,1},{4,6},{6,4},{5,7},{7,5},{8,10},{10,8},{9,1... | collective-permute-start | bytes 786440 | tf_op jit(solution)/shard_map/ppermute | solution.py:580
  11.1 6.9 %collective-permute-start.3 = (bf16[256,128]{1,0:T(8,128)(2,1)S(1)}, bf16[256,128]{1,0:T(8,128)(2,1)S(1)}, u32[]{:S(2)}, u32[]{:S(2)}) collective-permute-start(bf16[256,128]{1,0:T(8,128)(2,1)S(1)} %get-tuple-element.32), channel_id=1, source_target_pairs={{0,6},{2,4},{4,10},{6,8},{8,14},{10,12},{12,18},{14,16},{16,22},{1... | collective-permute-start | bytes 196616 | tf_op jit(solution)/shard_map/ppermute | solution.py:549
  15.6 8.0 %collective-permute-start.4 = (bf16[256,128]{1,0:T(8,128)(2,1)S(1)}, bf16[256,128]{1,0:T(8,128)(2,1)S(1)}, u32[]{:S(2)}, u32[]{:S(2)}) collective-permute-start(bf16[256,128]{1,0:T(8,128)(2,1)S(1)} %get-tuple-element.33), channel_id=1, source_target_pairs={{4,2},{6,0},{8,6},{10,4},{12,10},{14,8},{16,14},{18,12},{20,18},{2... | collective-permute-start | bytes 196616 | tf_op jit(solution)/shard_map/ppermute | solution.py:549
  18.0 11.9 %collective-permute-start.5 = (bf16[160,256]{1,0:T(8,128)(2,1)}, bf16[160,256]{1,0:T(8,128)(2,1)S(1)}, u32[]{:S(2)}, u32[]{:S(2)}) collective-permute-start(bf16[160,256]{1,0:T(8,128)(2,1)} %get-tuple-element.35), channel_id=1, source_target_pairs={{0,4},{4,8},{8,12},{12,16},{16,20},{20,24},{24,28},{1,5},{5,9},{9,... | collective-permute-start | bytes 245768 | tf_op jit(solution)/shard_map/ppermute | solution.py:575
  23.6 1.3 %copy-start.5 = (s32[1,32,2]{1,2,0:T(2,128)S(1)}, s32[1,32,2]{1,2,0:T(2,128)}, u32[]{:S(2)}) copy-start(s32[1,32,2]{1,2,0:T(2,128)} %param.7) | copy-start | bytes 772
  23.6 6.9 %collective-permute-start.6 = (bf16[160,256]{1,0:T(8,128)(2,1)S(1)}, bf16[160,256]{1,0:T(8,128)(2,1)S(1)}, u32[]{:S(2)}, u32[]{:S(2)}) collective-permute-start(bf16[160,256]{1,0:T(8,128)(2,1)S(1)} %get-tuple-element.36), channel_id=1, source_target_pairs={{4,0},{8,4},{12,8},{16,12},{20,16},{24,20},{28,24},{5,1},{9,5},{13... | collective-permute-start | bytes 245768 | tf_op jit(solution)/shard_map/ppermute | solution.py:576
  30.5 3.6 %copy-start.4 = (bf16[9,32,32]{2,1,0:T(8,128)(2,1)S(1)}, bf16[9,32,32]{2,1,0:T(8,128)(2,1)}, u32[]{:S(2)}) copy-start(bf16[9,32,32]{2,1,0:T(8,128)(2,1)} %first.1) | copy-start | bytes 55300
  46.5 1.3 %collective-permute-start.7 = (f32[144,128]{1,0:T(8,128)S(1)}, f32[144,128]{1,0:T(8,128)S(1)}, u32[]{:S(2)}, u32[]{:S(2)}) collective-permute-start(f32[144,128]{1,0:T(8,128)S(1)} %get-tuple-element.41), channel_id=1, source_target_pairs={{0,1},{1,0},{2,3},{3,2},{4,5},{5,4},{6,7},{7,6},{8,9},{9,8},{10,11... | collective-permute-start | bytes 221192 | tf_op jit(solution)/shard_map/ppermute | solution.py:647
  47.9 4.4 %collective-permute-start.8 = (f32[144,128]{1,0:T(8,128)S(1)}, f32[144,128]{1,0:T(8,128)S(1)}, u32[]{:S(2)}, u32[]{:S(2)}) collective-permute-start(f32[144,128]{1,0:T(8,128)S(1)} %add.12), channel_id=1, source_target_pairs={{0,2},{2,0},{1,3},{3,1},{4,6},{6,4},{5,7},{7,5},{8,10},{10,8},{9,1... | collective-permute-start | bytes 221192 | tf_op jit(solution)/shard_map/ppermute | solution.py:647
  52.3 5.3 %collective-permute-start.9 = (f32[144,128]{1,0:T(8,128)S(1)}, f32[144,128]{1,0:T(8,128)S(1)}, u32[]{:S(2)}, u32[]{:S(2)}) collective-permute-start(f32[144,128]{1,0:T(8,128)S(1)} %add.13), channel_id=1, source_target_pairs={{0,4},{4,0},{8,12},{12,8},{16,20},{20,16},{24,28},{28,24},{1,5},{5... | collective-permute-start | bytes 221192 | tf_op jit(solution)/shard_map/ppermute | solution.py:647
  57.6 5.2 %collective-permute-start.10 = (f32[144,128]{1,0:T(8,128)S(1)}, f32[144,128]{1,0:T(8,128)S(1)}, u32[]{:S(2)}, u32[]{:S(2)}) collective-permute-start(f32[144,128]{1,0:T(8,128)S(1)} %add.14), channel_id=1, source_target_pairs={{0,8},{4,12},{8,0},{12,4},{16,24},{20,28},{24,16},{28,20},{1,9},{5... | collective-permute-start | bytes 221192 | tf_op jit(solution)/shard_map/ppermute | solution.py:647
  62.8 5.9 %collective-permute-start.11 = (f32[144,128]{1,0:T(8,128)S(1)}, f32[144,128]{1,0:T(8,128)S(1)}, u32[]{:S(2)}, u32[]{:S(2)}) collective-permute-start(f32[144,128]{1,0:T(8,128)S(1)} %add.15.mine), channel_id=1, source_target_pairs={{0,16},{4,20},{8,24},{12,28},{16,0},{20,4},{24,8},{28,12},{1,17},{... | collective-permute-start | bytes 221192 | tf_op jit(solution)/shard_map/ppermute | solution.py:647

commit v4 on v3

--- a/solution.py
+++ b/solution.py
@@ -52,86 +52,112 @@
     return pl.ds(pl.multiple_of(r * chans, chans), count * chans)
 
 
-def by_rows(source, out):
-    chans, height, span = source.shape
-    for t in range(0, span, TILE):
-        part = jnp.transpose(source[:, :, t : t + TILE], (1, 0, 2))
-        out[:, t : t + TILE] = part.reshape(height * chans, TILE)
-
-
-def feature_kernel(feat, feat_rows, up_msg, down_msg):
-    chans, height = feat.shape[0], feat.shape[1]
-    by_rows(feat, feat_rows)
-    up_msg[...] = feat_rows[0 : FHALO * chans]
-    down_msg[...] = feat_rows[(height - FHALO) * chans :]
-
-
-def pack_kernel(edges, feat_rows, cot, cot_rows, up_msg, down_msg, col_msg, *corner_msgs):
-    chans, height, span = cot.shape
-    last = slice(span - TILE, span)
-    by_rows(cot, cot_rows)
-    up_msg[...] = cot_rows[0 : CHALO * chans]
-    down_msg[...] = cot_rows[(height - CHALO) * chans :]
-    lane = lanes_of((chans, TILE))
-    is_left = lax.axis_index("cols") == 0
-    for (vertical, edge), msg in zip(edges, corner_msgs):
-        f0 = 0 if vertical == "up" else height - FHALO
-        c0 = 0 if vertical == "up" else height - CHALO
-        pieces = [(feat_rows, f0 + j) for j in range(FHALO)]
-        pieces += [(cot_rows, c0 + j) for j in range(CHALO)]
-        for q in range(0, len(pieces), POOL):
-            total = jnp.zeros((chans, TILE), F32)
-            for k, (ref, r) in enumerate(pieces[q : q + POOL]):
-                at = rows_at(r, chans)
-                if edge == "left":
-                    piece = turn(ref[at, 0:TILE].astype(F32), k * SLOT)
-                elif edge == "right":
-                    piece = turn(ref[at, last].astype(F32), (k + 1) * SLOT)
-                else:
-                    piece = jnp.where(is_left, ref[at, last].astype(F32), ref[at, 0:TILE].astype(F32))
-                    piece = turn(piece, jnp.where(is_left, (k + 1) * SLOT % TILE, k * SLOT))
-                inside = (lane >= k * SLOT) & (lane < (k + 1) * SLOT)
-                total = jnp.where(inside, piece, total)
-            msg[rows_at(q // POOL, chans)] = total.astype(BF16)
-    for r in range(height):
-        at = rows_at(r, chans)
-        cots = jnp.where(
-            lane < 2 * SLOT,
-            turn(cot_rows[at, 0:TILE].astype(F32), SLOT),
-            turn(cot_rows[at, last].astype(F32), -SLOT),
-        )
-        feats = jnp.where(
-            lane < 2 * SLOT, feat_rows[at, 0:TILE].astype(F32), feat_rows[at, last].astype(F32)
-        )
-        outer = (lane < SLOT) | (lane >= TILE - SLOT)
-        col_msg[at] = jnp.where(outer, feats, cots).astype(BF16)
-
-
-class Halo:
-
-    def __init__(self, chans, single):
-        _, _, has_left, has_right = has_sides()
-        lane = lanes_of((chans, TILE))
-        self.chans, self.single, self.has_right = chans, single, has_right
-        self.right_lanes = (lane < SLOT) & has_right
-        self.left_lanes = (lane >= TILE - SLOT) & has_left
-
-    def tile(self, right, left):
-        return jnp.where(self.right_lanes, right, jnp.where(self.left_lanes, left, 0.0))
-
-    def turned(self, right_ref, left_ref, at, right_shift, left_shift):
-        if self.single:
-            both = right_ref[at].astype(F32)
-            shift = jnp.where(self.has_right, right_shift % TILE, left_shift % TILE)
-            both = turn(both, shift)
-            return self.tile(both, both)
-        return self.tile(
-            turn(right_ref[at].astype(F32), right_shift), turn(left_ref[at].astype(F32), left_shift)
-        )
-
-    def corner(self, right_ref, left_ref, slot):
-        at, k = rows_at(slot // POOL, self.chans), slot % POOL
-        return self.turned(right_ref, left_ref, at, -k * SLOT, TILE - SLOT - k * SLOT)
+def to_rows(block):
+    chans, height, span = block.shape
+    return jnp.transpose(block, (1, 0, 2)).reshape(height * chans, span)
+
+
+def to_planes(block, chans):
+    height = block.shape[0] // chans
+    return jnp.transpose(block.reshape(height, chans, block.shape[1]), (1, 0, 2))
+
+
+def tiles_of(span):
+    return [slice(t, t + TILE) for t in range(0, span, TILE)]
+
+
+def is_even(axis):
+    return lax.rem(lax.axis_index(axis), 2) == 0
+
+
+def swaps(size):
+    first = [(i, i ^ 1) for i in range(size)]
+    second = [(i, i + 1) for i in range(1, size - 1, 2)]
+    return [first, second + [(j, i) for i, j in second]]
+
+
+def feature_kernel(feat, msg_a, msg_b, rows):
+    chans, height, span = feat.shape
+    for part in tiles_of(span):
+        rows[:, part] = to_rows(feat[:, :, part])
+    edge = (height - FHALO) * chans
+    low = jnp.where(is_even("rows"), edge, 0)
+    msg_a[...] = rows[pl.ds(pl.multiple_of(low, chans), FHALO * chans), :]
+    msg_b[...] = rows[pl.ds(pl.multiple_of(edge - low, chans), FHALO * chans), :]
+
+
+def column_kernel(feat, cot, cot_rows, *col_msgs):
+    chans, height, span = feat.shape
+    first, last = tiles_of(span)[0], tiles_of(span)[-1]
+    for part in tiles_of(span):
+        cot_rows[:, part] = to_rows(cot[:, :, part])
+    count = TILE // SLOT
+    block = height // count
+    lane = lanes_of((chans, block, TILE))
+    for index, msg in enumerate(col_msgs):
+        sends_right = is_even("cols") if index == 0 else jnp.logical_not(is_even("cols"))
+        total = jnp.zeros((chans, block, TILE), F32)
+        inner = jnp.where(sends_right, TILE - 1 - lane, lane) < FHALO
+        for k in range(count):
+            at = slice(k * block, (k + 1) * block)
+            feats = jnp.where(sends_right, feat[:, at, last].astype(F32), feat[:, at, first].astype(F32))
+            cots = jnp.where(sends_right, cot[:, at, last].astype(F32), cot[:, at, first].astype(F32))
+            cots = turn(cots, jnp.where(sends_right, TILE - FHALO, FHALO))
+            piece = jnp.where(inner, feats, cots)
+            piece = turn(piece, jnp.where(sends_right, (k + 1) * SLOT % TILE, k * SLOT))
+            inside = (lane >= k * SLOT) & (lane < (k + 1) * SLOT)
+            total = jnp.where(inside, piece, total)
+        msg[...] = total.reshape(chans * block, TILE).astype(BF16)
+
+
+def edge_kernel(cot_rows, *rest):
+    cols, (msg_a, msg_b) = rest[:-2], rest[-2:]
+    span = cot_rows.shape[1]
+    size = msg_a.shape[0] - sum(c.shape[0] * TILE // span for c in cols)
+    edge = cot_rows.shape[0] - size
+    chans = size // CHALO
+    low = jnp.where(is_even("rows"), edge, 0)
+    msg_a[0:size] = cot_rows[pl.ds(pl.multiple_of(low, chans), size), :]
+    msg_b[0:size] = cot_rows[pl.ds(pl.multiple_of(edge - low, chans), size), :]
+    at = size
+    for col in cols:
+        count = col.shape[0] * TILE // span
+        for t, part in enumerate(tiles_of(span)):
+            block = col[t * count : (t + 1) * count]
+            msg_a[at : at + count, part] = block
+            msg_b[at : at + count, part] = block
+        at += count
+
+
+def corner_views(msg, size, cols):
+    span = msg.shape[1]
+    views, at = [], size
+    for col in cols:
+        count = col.shape[0] * TILE // span
+        views.append(
+            jnp.concatenate([msg[at : at + count, part] for part in tiles_of(span)], axis=0)
+        )
+        at += count
+    return views
+
+
+def halo_block(sources, k, chans, kind):
+    rows = sources[0].shape[0] // chans
+    lane = lanes_of((chans * rows, TILE))
+    total = jnp.zeros((chans * rows, TILE), F32)
+    if kind == "features":
+        count, shift_r, shift_l = FHALO, -k * SLOT, TILE - (k + 1) * SLOT
+    else:
+        count, shift_r, shift_l = CHALO, -k * SLOT - FHALO, TILE - (k + 1) * SLOT + FHALO
+    for index, source in enumerate(sources):
+        from_right = is_even("cols") if index == 0 else jnp.logical_not(is_even("cols"))
+        moved = turn(
+            source.astype(F32), jnp.where(from_right, shift_r % TILE, shift_l % TILE)
+        )
+        total = jnp.where(
+            jnp.where(from_right, lane, TILE - 1 - lane) < count, moved, total
+        )
+    return total.astype(BF16).reshape(chans, rows, TILE)
 
 
 def columns_seen(shape, span):
@@ -196,17 +222,18 @@
 
 
 def back_kernel(
-    single, cot, up, down, col_r, col_l, up_r, up_l, down_r, down_l, second, bottle,
-    act_grad, view_m, view_0, view_p,
-    cot_m, cot_0, cot_p, back, high, low, coarse, bands_f, bands, small_f, small,
+    ncols, cot, msg_a, msg_b, *rest,
 ):
+    cols, (
+        second, bottle, act_grad, view_m, view_0, view_p,
+        cot_m, cot_0, cot_p, back, high, low, coarse, bands_f, bands, small_f, small,
+    ) = rest[:ncols], rest[ncols:]
     chans = second.shape[1]
     full, span = cot.shape
     height = full // chans
     width = span + TILE
     groups = height // POOL
     has_up, has_down, _, _ = has_sides()
-    halo = Halo(chans, single)
     seen_cols = columns_seen((chans, width), span)
 
     fill_turned_bands(bands_f, second, POOL)
@@ -216,18 +243,27 @@
     for b in range(3):
         small[rows_at(b, chans)] = small_t[0:chans, 3 * b * chans : 3 * (b + 1) * chans].astype(BF16)
 
-    cot_0[rows_at(0, chans, CHALO), 0:span] = up[...]
+    size = CHALO * chans
+    count = TILE // SLOT
+    block = height // count
     cot_0[rows_at(CHALO, chans, height), 0:span] = cot[...]
-    cot_0[rows_at(CHALO + height, chans, CHALO), 0:span] = down[...]
-    for j in range(CHALO):
-        cot_0[rows_at(j, chans), span:width] = halo.corner(up_r, up_l, FHALO + j).astype(BF16)
-        cot_0[rows_at(CHALO + height + j, chans), span:width] = halo.corner(
-            down_r, down_l, FHALO + j
-        ).astype(BF16)
-    for r in range(height):
-        cot_0[rows_at(CHALO + r, chans), span:width] = halo.turned(
-            col_r, col_l, rows_at(r, chans), -SLOT, SLOT
-        ).astype(BF16)
+    for k in range(count):
+        cot_0[rows_at(CHALO + k * block, chans, block), span:width] = to_rows(
+            halo_block([c[...] for c in cols], k, chans, "cotangent")
+        )
+
+    def vertical(up, down):
+        cot_0[rows_at(0, chans, CHALO), 0:span] = up[0:size]
+        cot_0[rows_at(CHALO + height, chans, CHALO), 0:span] = down[0:size]
+        corner = to_rows(
+            halo_block(corner_views(up, size, cols), count - 1, chans, "cotangent")
+        )
+        cot_0[rows_at(0, chans, CHALO), span:width] = corner[(block - CHALO) * chans :]
+        corner = to_rows(halo_block(corner_views(down, size, cols), 0, chans, "cotangent"))
+        cot_0[rows_at(CHALO + height, chans, CHALO), span:width] = corner[0:size]
+
+    pl.when(is_even("rows"))(lambda: vertical(msg_b, msg_a))
+    pl.when(jnp.logical_not(is_even("rows")))(lambda: vertical(msg_a, msg_b))
     for j in range(height + 2 * CHALO):
         at = rows_at(j, chans)
         cot_m[at] = turn(cot_0[at], 1)
@@ -299,19 +335,18 @@
 
 
 def main_kernel(
-    single, shifts, feat, up, down, col_r, col_l, up_r, up_l, down_r, down_l,
-    act_grad, view_m, view_0, view_p, first, bottle,
-    grads, blended,
-    fs, ws, warp_m, warp_0, warp_p, act, high, low, pooled, pre_grad, acc, bands_f, bands, small_f, small,
+    ncols, shifts, feat, feat_a, feat_b, msg_a, msg_b, *rest,
 ):
-    chans = first.shape[1]
-    full, span = feat.shape
-    height = full // chans
+    cols, (
+        act_grad, view_m, view_0, view_p, first, bottle, grads, blended,
+        planes, moved, warp_m, warp_0, warp_p, act, high, low, pooled, pre_grad, acc,
+        bands_f, bands, small_f, small,
+    ) = rest[:ncols], rest[ncols:]
+    chans, height, span = feat.shape
     tiles = span // TILE
     width = span + TILE
     groups = height // POOL
-    has_up, has_down, _, _ = has_sides()
-    halo = Halo(chans, single)
+    has_up, has_down, has_left, has_right = has_sides()
     seen_cols = columns_seen((chans, width), span)
 
     fill_bands(bands_f, first, POOL)
@@ -320,51 +355,71 @@
     for b in range(3):
         small[rows_at(b, chans)] = small_f[:, 3 * b * chans : 3 * (b + 1) * chans].astype(BF16)
 
-    for t in range(tiles):
-        part = slice(t * TILE, (t + 1) * TILE)
-        fs[t, rows_at(0, chans, FHALO)] = up[:, part].astype(F32)
-        fs[t, rows_at(FHALO, chans, height)] = feat[:, part].astype(F32)
-        fs[t, rows_at(FHALO + height, chans, FHALO)] = down[:, part].astype(F32)
-    for j in range(FHALO):
-        fs[tiles, rows_at(j, chans)] = halo.corner(up_r, up_l, j)
-        fs[tiles, rows_at(FHALO + height + j, chans)] = halo.corner(down_r, down_l, j)
-    for r in range(height):
-        at = rows_at(r, chans)
-        fs[tiles, rows_at(FHALO + r, chans)] = halo.tile(
-            col_r[at].astype(F32), col_l[at].astype(F32)
-        )
-
-    tall = height + 2 * EXT
+    size = CHALO * chans
+    count = TILE // SLOT
+    block = height // count
+    halo = slice(span, width)
+
+    def halo_columns(sources, at):
+        for k in range(count):
+            planes[:, at + k * block : at + (k + 1) * block, halo] = halo_block(
+                sources, k, chans, "features"
+            )
+
+    planes[:, height : 2 * height, 0:span] = feat[...]
+    halo_columns([c[...] for c in cols], height)
+    fill = (height - FHALO) * chans
+
+    def vertical(up, up_msg, down, down_msg):
+        for part in tiles_of(span):
+            none = jnp.zeros((fill, TILE), BF16)
+            planes[:, 0:height, part] = to_planes(
+                jnp.concatenate([none, up[:, part]], axis=0), chans
+            )
+            planes[:, 2 * height : 3 * height, part] = to_planes(
+                jnp.concatenate([down[:, part], none], axis=0), chans
+            )
+        halo_columns(corner_views(up_msg, size, cols), 0)
+        halo_columns(corner_views(down_msg, size, cols), 2 * height)
+
+    pl.when(is_even("rows"))(lambda: vertical(feat_b, msg_b, feat_a, msg_a))
+    pl.when(jnp.logical_not(is_even("rows")))(lambda: vertical(feat_a, msg_a, feat_b, msg_b))
+
+    tall = moved.shape[1]
     lane = lanes_of((tall, TILE))
+    seen_halo = ((lane < TILE // 2) & has_right) | ((lane >= TILE // 2) & has_left)
+    step = lanes_of((tall, 3 * height)) - lax.broadcasted_iota(jnp.int32, (tall, 3 * height), 0)
 
     def warp(c, _):
-        start = (MAXSHIFT + shifts[c, 0]) * chans + c
+        pick = jnp.where(step == height - EXT + shifts[c, 0], 1.0, 0.0).astype(BF16)
+        plane = jnp.dot(pick, planes[c], preferred_element_type=F32)
         move = shifts[c, 1]
-        planes = [
-            turn(fs[t, pl.ds(start, tall, stride=chans), :], jnp.where(move > 0, TILE - move, -move))
-            for t in range(tiles + 1)
-        ]
+        amount = jnp.where(move > 0, TILE - move, -move)
+        parts = [turn(plane[:, part], amount) for part in tiles_of(width)]
         inside = jnp.where(move > 0, lane, TILE - 1 - lane) < TILE - jnp.abs(move)
-        for t in range(tiles + 1):
-            after, before = planes[(t + 1) % (tiles + 1)], planes[t - 1]
-            ws[t, pl.ds(c, tall, stride=chans), :] = jnp.where(
-                inside, planes[t], jnp.where(move > 0, after, before)
-            )
+        for t, part in enumerate(tiles_of(width)):
+            after, before = parts[(t + 1) % (tiles + 1)], parts[t - 1]
+            result = jnp.where(inside, parts[t], jnp.where(move > 0, after, before))
+            if t == tiles:
+                result = jnp.where(seen_halo, result, 0.0)
+            moved[c, :, part] = result.astype(BF16)
         return 0
 
     lax.fori_loop(0, chans, warp, 0, unroll=4)
-    for j in range(tall):
-        row = jnp.concatenate([ws[t, rows_at(j, chans)] for t in range(tiles + 1)], axis=1)
-        seen = seen_cols
-        if j < EXT:
-            seen = seen & has_up
-        elif j >= EXT + height:
-            seen = seen & has_down
-        row = jnp.where(seen, row, 0.0).astype(BF16)
+    chunk = 16
+    for r in range(0, tall, chunk):
+        for part in tiles_of(width):
+            warp_0[rows_at(r, chans, chunk), part] = to_rows(moved[:, r : r + chunk, part])
+
+    def clear(r, count):
+        warp_0[rows_at(r, chans, count)] = jnp.zeros((count * chans, width), BF16)
+
+    pl.when(jnp.logical_not(has_up))(lambda: clear(0, EXT))
+    pl.when(jnp.logical_not(has_down))(lambda: clear(EXT + height, EXT))
+    for j in range(height + 2 * EXT):
         at = rows_at(j, chans)
-        warp_0[at] = row
-        warp_m[at] = turn(row, 1)
-        warp_p[at] = turn(row, -1)
+        warp_m[at] = turn(warp_0[at], 1)
+        warp_p[at] = turn(warp_0[at], -1)
 
     def first_group(g, own):
         at = rows_at(g * POOL, chans, POOL + 2)
@@ -429,9 +484,8 @@
 
 
 def predict_kernel(part, blended, second, *rest):
-    out, scratch, bands_f, bands = rest[-4:]
+    out, rows, bands_f, bands = rest[-4:]
     chans, height, span = out.shape
-    tiles = span // TILE
     bands_f[...] = jnp.zeros(bands_f.shape, F32)
     for k in range(POOL):
         for b in range(3):
@@ -446,18 +500,12 @@
         parts = jnp.dot(bands[...], blended[at, :], preferred_element_type=F32)
         for k in range(POOL):
             row = conv_sum(parts[3 * k * chans : 3 * (k + 1) * chans], chans, 1)
-            for t in range(tiles):
-                scratch[t, pl.ds(g * POOL + k, chans, stride=height), :] = row[
-                    :, t * TILE : (t + 1) * TILE
-                ]
+            rows[rows_at(g * POOL + k, chans), :] = row[:, 0:span].astype(BF16)
         return 0
 
-    lax.fori_loop(0, height // POOL, group, 0)
-    for c in range(chans):
-        for t in range(tiles):
-            out[c, :, t * TILE : (t + 1) * TILE] = scratch[
-                t, c * height : (c + 1) * height
-            ].astype(BF16)
+    lax.fori_loop(0, height // POOL, group, 0, unroll=2)
+    for part in tiles_of(span):
+        out[:, :, part] = to_planes(rows[:, part], chans)
 
 
 def final_kernel(factor, mine, other, first, second):
@@ -496,7 +544,6 @@
 def predict(blended, second, shape, parts, part, before):
     chans, height, span = shape
     rows = height // parts
-    tiles = span // TILE
     block = pl.BlockSpec((chans, rows, span), lambda i: (0, part, 0))
     whole = lambda a: pl.BlockSpec(a.shape, lambda i: (0,) * a.ndim)
     args = (blended, second)
@@ -510,7 +557,7 @@
         functools.partial(predict_kernel, part),
         jax.ShapeDtypeStruct(shape, BF16),
         [
-            pltpu.VMEM((tiles, chans * rows, TILE), F32),
+            pltpu.VMEM((chans * rows, span), BF16),
             pltpu.VMEM((3 * POOL * chans, (POOL + 2) * chans), F32),
             pltpu.VMEM((3 * POOL * chans, (POOL + 2) * chans), BF16),
         ],
@@ -531,66 +578,39 @@
     width = span + TILE
     full = height * chans
     groups = height // POOL
-    single = cols == 2
 
     def bf(*shape):
         return jax.ShapeDtypeStruct(shape, BF16)
 
-    ahead = [(i, i + 1) for i in range(rows - 1)]
-    astern = [(i + 1, i) for i in range(rows - 1)]
-
-    def diagonal(message, step, turns):
-        pairs = []
-        for i in range(rows):
-            for j in range(cols):
-                for move in turns:
-                    if 0 <= i + step < rows and 0 <= j + move < cols:
-                        pairs.append((i * cols + j, (i + step) * cols + j + move))
-        return lax.ppermute(message, ("rows", "cols"), pairs)
-
-    feat_rows, up_feat, down_feat = call(
-        feature_kernel,
-        (bf(full, span), bf(FHALO * chans, span), bf(FHALO * chans, span)),
-        [],
-        1,
-        8,
+    def swapped(messages, axis):
+        pairs = [p for p in swaps(lax.axis_size(axis)) if p]
+        return [lax.ppermute(m, axis, p) for m, p in zip(messages, pairs)]
+
+    halo = bf(FHALO * chans, span)
+    messages = call(
+        feature_kernel, (halo, halo), [pltpu.VMEM((full, span), BF16)], 1, 8
     )(features[0])
-    up_f = lax.ppermute(down_feat, "rows", ahead)
-    down_f = lax.ppermute(up_feat, "rows", astern)
-
-    if single:
-        edges = (("up", "single"), ("down", "single"))
-    else:
-        edges = tuple((v, e) for v in ("up", "down") for e in ("left", "right"))
-    packed = pl.cdiv(FHALO + CHALO, POOL) * chans
-    cot_rows, up_cot, down_cot, col_msg, *corner_msgs = call(
-        functools.partial(pack_kernel, edges),
-        (bf(full, span), bf(CHALO * chans, span), bf(CHALO * chans, span), bf(full, TILE))
-        + tuple(bf(packed, TILE) for _ in edges),
+    feat_msgs = swapped(messages, "rows")
+    packed = chans * (height * SLOT // TILE)
+    cot_rows, *messages = call(
+        column_kernel,
+        (bf(full, span),) + (bf(packed, TILE),) * (1 if cols == 2 else 2),
         [],
         2,
         8,
         flops=2 * 10**10,
-    )(feat_rows, cotangent[0])
-    up_c = lax.ppermute(down_cot, "rows", ahead)
-    down_c = lax.ppermute(up_cot, "rows", astern)
-    if single:
-        up_r = up_l = diagonal(corner_msgs[1], 1, (-1, 1))
-        down_r = down_l = diagonal(corner_msgs[0], -1, (-1, 1))
-        col_r = col_l = lax.ppermute(col_msg, "cols", [(0, 1), (1, 0)])
-    else:
-        up_r = diagonal(corner_msgs[2], 1, (-1,))
-        up_l = diagonal(corner_msgs[3], 1, (1,))
-        down_r = diagonal(corner_msgs[0], -1, (-1,))
-        down_l = diagonal(corner_msgs[1], -1, (1,))
-        col_r = lax.ppermute(col_msg, "cols", [(i + 1, i) for i in range(cols - 1)])
-        col_l = lax.ppermute(col_msg, "cols", [(i, i + 1) for i in range(cols - 1)])
+    )(features[0], cotangent[0])
+    col_msgs = swapped(messages, "cols")
+    ncols = len(col_msgs)
+    halo = bf(CHALO * chans + ncols * packed * TILE // span, span)
+    messages = call(edge_kernel, (halo, halo), [], 1 + ncols, 8)(cot_rows, *col_msgs)
+    row_msgs = swapped(messages, "rows")
 
     tall_c = (height + 2 * CHALO) * chans
     view = bf((height + 2) * chans, span)
     band = 3 * (POOL + 2) * chans
     act_grad, *views = call(
-        functools.partial(back_kernel, single),
+        functools.partial(back_kernel, ncols),
         (jax.ShapeDtypeStruct((full, span), F32), view, view, view),
         [pltpu.VMEM((tall_c, width), BF16)] * 3
         + [pltpu.VMEM(((height + 2 * POOL) * chans, span), BF16)]
@@ -601,22 +621,19 @@
             pltpu.VMEM((9 * chans, TILE), F32),
             pltpu.VMEM((3 * chans, 3 * chans), BF16),
         ],
-        11,
+        5 + ncols,
         16,
-    )(
-        cot_rows, up_c, down_c, col_r, col_l, up_r, up_l, down_r, down_l,
-        second_kernel, bottle_kernel,
-    )
-
-    tall = (height + 2 * EXT) * chans
+    )(cot_rows, *row_msgs, *col_msgs, second_kernel, bottle_kernel)
+
+    tall = pl.cdiv(height + 2 * EXT, 16) * 16
     grads, blended = call(
-        functools.partial(main_kernel, single),
+        functools.partial(main_kernel, ncols),
         (jax.ShapeDtypeStruct((9 * chans // 2, TILE), F32), bf((height + 2) * chans, width)),
         [
-            pltpu.VMEM((tiles + 1, (height + 2 * FHALO) * chans, TILE), F32),
-            pltpu.VMEM((tiles + 1, tall, TILE), F32),
+            pltpu.VMEM((chans, 3 * height, width), BF16),
+            pltpu.VMEM((chans, tall, width), BF16),
         ]
-        + [pltpu.VMEM((tall, width), BF16)] * 3
+        + [pltpu.VMEM((tall * chans, width), BF16)] * 3
         + [pltpu.VMEM(((height + 4 * POOL) * chans, width), BF16)]
         + [pltpu.VMEM(((groups + 4) * chans, width), BF16)] * 3
         + [
@@ -627,12 +644,12 @@
             pltpu.VMEM((chans, 9 * chans), F32),
             pltpu.VMEM((3 * chans, 3 * chans), BF16),
         ],
-        16,
+        12 + ncols,
         32,
         flops=10**10,
         smem_first=True,
     )(
-        shifts[0], feat_rows, up_f, down_f, col_r, col_l, up_r, up_l, down_r, down_l,
+        shifts[0], features[0], *feat_msgs, *row_msgs, *col_msgs,
         act_grad, *views, first_kernel, bottle_kernel,
     )
 

time: 69.9 us -> 66.9 us (0.957)
  waiting for transfers between devices: 13.1 us -> 24 us
  starting transfers between devices: 31.4 us -> 20.5 us
  Pallas kernels: 23.1 us -> 20.2 us
    ppermute x7 -> x5, starting transfers between devices: 20.3 us -> 10.4 us  [swapped(): return [lax.ppermute(m, axis, p) for m, p in zip(messages, pairs)]]
    ppermute x7 -> x5, waiting for transfers between devices: 6.59 us -> 15.8 us  [swapped(): return [lax.ppermute(m, axis, p) for m, p in zip(messages, pairs)]]
    pallas_call x4 -> x5, Pallas kernels: 17.6 us -> 15.6 us  [the longest x1 10.8 us: shards(): call(functools.partial(main_kernel, ncols), (jax.ShapeDtypeStruct((9 * ch...]
    ppermute x5, waiting for transfers between devices: 6.48 us -> 8.26 us  [shards(): other = lax.ppermute(grads, axis, pairs)]
    pallas_call x2, Pallas kernels: 4.61 us -> 3.63 us  [predict(): call(functools.partial(predict_kernel, part), jax.ShapeDtypeStruct(shape,...]
    ppermute x5, starting transfers between devices: 11.1 us -> 10.2 us  [shards(): other = lax.ppermute(grads, axis, pairs)]
  transfers between devices with their start and end apart: 12 -> 10, of which waited for: 7 -> 7; matrix products, arithmetic and copies ran while one was open for 0% -> 0% of each run, Pallas kernels for 14% -> 12%
where the time goes in v4:
time: 66.9 us; the launch traced here: 66.7 us
  waiting for transfers between devices  24 us (36%)
  starting transfers between devices  20.5 us (31%)
  Pallas kernels  20.2 us (30%)
  local copies, waits for them, and re-layouts  1.15 us (2%)
  between operations  0.79 us (1%)
    ppermute x5, waiting for transfers between devices, swapped(): return [lax.ppermute(m, axis, p) for m, p in zip(messages, pairs)]  15.8 us
    pallas_call x1, Pallas kernels, shards(): call(functools.partial(main_kernel, ncols), (jax.ShapeDtypeStruct((9 * ch...  10.8 us
    ppermute x5, starting transfers between devices, swapped(): return [lax.ppermute(m, axis, p) for m, p in zip(messages, pairs)]  10.4 us
    ppermute x5, starting transfers between devices, shards(): other = lax.ppermute(grads, axis, pairs)  10.2 us
    ppermute x5, waiting for transfers between devices, shards(): other = lax.ppermute(grads, axis, pairs)  8.26 us
    pallas_call x1, Pallas kernels, shards(): call(functools.partial(back_kernel, ncols), (jax.ShapeDtypeStruct((full,...  3.82 us
    pallas_call x2, Pallas kernels, predict(): call(functools.partial(predict_kernel, part), jax.ShapeDtypeStruct(shape,...  3.63 us
  transfers between devices with their start and end apart: 10, of which 7 were waited for; matrix products, arithmetic and copies ran while one was open for 0% of the time, Pallas kernels for 12%

profile of v4, /device:TPU:0, one launch (start us, length us, event | category | flops | bytes accessed | tf_op | source)
XLA Modules:
  0.0 66.7 jit_solution(1070435057133766605)
XLA Ops:
  0.6 1.0 %copy-done = bf16[1,32,32,256]{3,2,1,0:T(8,128)(2,1)S(1)} copy-done((bf16[1,32,32,256]{3,2,1,0:T(8,128)(2,1)S(1)}, bf16[1,32,32,256]{3,2,1,0:T(8,128)(2,1)}, u32[]{:S(2)}) %copy-start) | copy-done | bytes 524312
  1.7 0.4 shard_map.85
  2.1 3.0 %collective-permute-start = (bf16[800,256]{1,0:T(8,128)(2,1)S(1)}, bf16[800,256]{1,0:T(8,128)(2,1)S(1)}, u32[]{:S(2)}, u32[]{:S(2)}) collective-permute-start(bf16[800,256]{1,0:T(8,128)(2,1)S(1)} %get-tuple-element.25), channel_id=1, source_target_pairs={{0,4},{4,0},{8,12},{12,8},{16,20},{20,16},{24,28},{28,24},{1,5},{5... | collective-permute-start | bytes 1228808 | tf_op jit(solution)/shard_map/ppermute | solution.py:587
  5.1 0.7 %collective-permute-start.1 = (bf16[800,256]{1,0:T(8,128)(2,1)S(1)}, bf16[800,256]{1,0:T(8,128)(2,1)S(1)}, u32[]{:S(2)}, u32[]{:S(2)}) collective-permute-start(bf16[800,256]{1,0:T(8,128)(2,1)S(1)} %get-tuple-element.26), channel_id=1, source_target_pairs={{4,8},{12,16},{20,24},{8,4},{16,12},{24,20},{5,9},{13,17},{21,25},... | collective-permute-start | bytes 1228808 | tf_op jit(solution)/shard_map/ppermute | solution.py:587
  5.8 0.5 shard_map.86
  6.4 1.6 %collective-permute-start.2 = (bf16[256,128]{1,0:T(8,128)(2,1)S(1)}, bf16[256,128]{1,0:T(8,128)(2,1)S(1)}, u32[]{:S(2)}, u32[]{:S(2)}) collective-permute-start(bf16[256,128]{1,0:T(8,128)(2,1)S(1)} %get-tuple-element.28), channel_id=1, source_target_pairs={{0,2},{2,0},{1,3},{3,1},{4,6},{6,4},{5,7},{7,5},{8,10},{10,8},{9,1... | collective-permute-start | bytes 196616 | tf_op jit(solution)/shard_map/ppermute | solution.py:587
  7.9 2.8 %collective-permute-done.2.rest_0_ = bf16[256,128]{1,0:T(8,128)(2,1)S(1)} collective-permute-done((bf16[256,128]{1,0:T(8,128)(2,1)S(1)}, bf16[256,128]{1,0:T(8,128)(2,1)S(1)}, u32[]{:S(2)}, u32[]{:S(2)}) %collective-permute-start.2) | collective-permute-done | bytes 65568 | tf_op jit(solution)/shard_map/ppermute | solution.py:587
  10.7 4.3 %collective-permute-start.3 = (bf16[288,256]{1,0:T(8,128)(2,1)S(1)}, bf16[288,256]{1,0:T(8,128)(2,1)S(1)}, u32[]{:S(2)}, u32[]{:S(2)}) collective-permute-start(bf16[288,256]{1,0:T(8,128)(2,1)S(1)} %get-tuple-element.29), channel_id=1, source_target_pairs={{0,4},{4,0},{8,12},{12,8},{16,20},{20,16},{24,28},{28,24},{1,5},{5... | collective-permute-start | bytes 442376 | tf_op jit(solution)/shard_map/ppermute | solution.py:587
  15.1 0.8 %collective-permute-start.4 = (bf16[288,256]{1,0:T(8,128)(2,1)S(1)}, bf16[288,256]{1,0:T(8,128)(2,1)S(1)}, u32[]{:S(2)}, u32[]{:S(2)}) collective-permute-start(bf16[288,256]{1,0:T(8,128)(2,1)S(1)} %get-tuple-element.30), channel_id=1, source_target_pairs={{4,8},{12,16},{20,24},{8,4},{16,12},{24,20},{5,9},{13,17},{21,25},... | collective-permute-start | bytes 442376 | tf_op jit(solution)/shard_map/ppermute | solution.py:587
  16.0 13.0 %collective-permute-done.3.msg_a = bf16[288,256]{1,0:T(8,128)(2,1)S(1)} collective-permute-done((bf16[288,256]{1,0:T(8,128)(2,1)S(1)}, bf16[288,256]{1,0:T(8,128)(2,1)S(1)}, u32[]{:S(2)}, u32[]{:S(2)}) %collective-permute-start.3) | collective-permute-done | bytes 147488 | tf_op jit(solution)/shard_map/ppermute | solution.py:587
  28.9 3.8 %shard_map.88 = (f32[1024,256]{1,0:T(8,128)S(1)}, bf16[1088,256]{1,0:T(8,128)(2,1)S(1)}, bf16[1088,256]{1,0:T(8,128)(2,1)S(1)}, bf16[1088,256]{1,0:T(8,128)(2,1)S(1)}) custom-call(bf16[1024,256]{1,0:T(8,128)(2,1)S(1)} %get-tuple-element.27.cot_rows.cot, bf16[288,256]{1,0:T(8,128)(2,1)S(1)} %collective-permute-done.3.msg_a, ...), custom_call_target="tpu_custom_call" | custom-call | bytes 4194304 | tf_op jit(solution)/shard_map/pallas_call | solution.py:612
  32.8 10.8 %shard_map.89 = (f32[144,128]{1,0:T(8,128)S(1)}, bf16[1088,384]{1,0:T(8,128)(2,1)S(1)}) custom-call(s32[32,2]{1,0:T(8,128)S(1)} %copy.10.shifts, bf16[32,32,256]{2,1,0:T(8,128)(2,1)S(1)} %bitcast.6, bf16[800,256]{1,0:T(8,128)(2,1)S(1)} %collective-permute-done.feat_a, bf16[800,256]{1,0:T(8,128)(2,1)S(1)} %collective-permute-done.1.feat_b, ...), custom_call_target="tpu_custom_call" | custom-call | flops 10000000000 | bytes 4194304 | tf_op jit(solution)/shard_map/pallas_call | solution.py:629
  43.7 1.3 %collective-permute-done.5 = f32[144,128]{1,0:T(8,128)S(1)} collective-permute-done((f32[144,128]{1,0:T(8,128)S(1)}, f32[144,128]{1,0:T(8,128)S(1)}, u32[]{:S(2)}, u32[]{:S(2)}) %collective-permute-start.5) | collective-permute-done | bytes 73760 | tf_op jit(solution)/shard_map/ppermute | solution.py:664
  45.0 1.6 %collective-permute-start.6 = (f32[144,128]{1,0:T(8,128)S(1)}, f32[144,128]{1,0:T(8,128)S(1)}, u32[]{:S(2)}, u32[]{:S(2)}) collective-permute-start(f32[144,128]{1,0:T(8,128)S(1)} %add.12), channel_id=1, source_target_pairs={{0,2},{2,0},{1,3},{3,1},{4,6},{6,4},{5,7},{7,5},{8,10},{10,8},{9,1... | collective-permute-start | bytes 221192 | tf_op jit(solution)/shard_map/ppermute | solution.py:664
  46.6 1.8 %shard_map.90.rest_0_ = bf16[32,32,256]{2,1,0:T(8,128)(2,1)} custom-call(bf16[1088,384]{1,0:T(8,128)(2,1)S(1)} %get-tuple-element.41.blended, bf16[9,32,32]{2,1,0:T(8,128)(2,1)S(1)} %copy-done.3), custom_call_target="tpu_custom_call" | custom-call | flops 1000000000 | bytes 4194304 | tf_op jit(solution)/shard_map/pallas_call | solution.py:556
  48.4 1.0 %collective-permute-done.6 = f32[144,128]{1,0:T(8,128)S(1)} collective-permute-done((f32[144,128]{1,0:T(8,128)S(1)}, f32[144,128]{1,0:T(8,128)S(1)}, u32[]{:S(2)}, u32[]{:S(2)}) %collective-permute-start.6) | collective-permute-done | bytes 73760 | tf_op jit(solution)/shard_map/ppermute | solution.py:664
  49.4 2.5 %collective-permute-start.7 = (f32[144,128]{1,0:T(8,128)S(1)}, f32[144,128]{1,0:T(8,128)S(1)}, u32[]{:S(2)}, u32[]{:S(2)}) collective-permute-start(f32[144,128]{1,0:T(8,128)S(1)} %add.13), channel_id=1, source_target_pairs={{0,4},{4,0},{8,12},{12,8},{16,20},{20,16},{24,28},{28,24},{1,5},{5... | collective-permute-start | bytes 221192 | tf_op jit(solution)/shard_map/ppermute | solution.py:664
  52.0 1.8 %shard_map.91 = bf16[32,32,256]{2,1,0:T(8,128)(2,1)} custom-call(bf16[1088,384]{1,0:T(8,128)(2,1)S(1)} %get-tuple-element.41.blended, bf16[9,32,32]{2,1,0:T(8,128)(2,1)S(1)} %copy-done.3, bf16[32,32,256]{2,1,0:T(8,128)(2,1)} %shard_map.90.rest_0_), custom_call_target="tpu_custom_call", output_to_operand_aliasing={{}: (2, {})} | custom-call | flops 1000000000 | bytes 4194304 | tf_op jit(solution)/shard_map/pallas_call | solution.py:556
  53.8 0.5 collective-permute-done.7
  54.3 2.1 %collective-permute-start.8 = (f32[144,128]{1,0:T(8,128)S(1)}, f32[144,128]{1,0:T(8,128)S(1)}, u32[]{:S(2)}, u32[]{:S(2)}) collective-permute-start(f32[144,128]{1,0:T(8,128)S(1)} %add.14), channel_id=1, source_target_pairs={{0,8},{4,12},{8,0},{12,4},{16,24},{20,28},{24,16},{28,20},{1,9},{5... | collective-permute-start | bytes 221192 | tf_op jit(solution)/shard_map/ppermute | solution.py:664
  56.5 2.3 %collective-permute-done.8 = f32[144,128]{1,0:T(8,128)S(1)} collective-permute-done((f32[144,128]{1,0:T(8,128)S(1)}, f32[144,128]{1,0:T(8,128)S(1)}, u32[]{:S(2)}, u32[]{:S(2)}) %collective-permute-start.8) | collective-permute-done | bytes 73760 | tf_op jit(solution)/shard_map/ppermute | solution.py:664
  58.8 3.8 %collective-permute-start.9 = (f32[144,128]{1,0:T(8,128)S(1)}, f32[144,128]{1,0:T(8,128)S(1)}, u32[]{:S(2)}, u32[]{:S(2)}) collective-permute-start(f32[144,128]{1,0:T(8,128)S(1)} %add.15.mine), channel_id=1, source_target_pairs={{0,16},{4,20},{8,24},{12,28},{16,0},{20,4},{24,8},{28,12},{1,17},{... | collective-permute-start | bytes 221192 | tf_op jit(solution)/shard_map/ppermute | solution.py:664
  62.6 3.1 %collective-permute-done.9.other = f32[144,128]{1,0:T(8,128)S(1)} collective-permute-done((f32[144,128]{1,0:T(8,128)S(1)}, f32[144,128]{1,0:T(8,128)S(1)}, u32[]{:S(2)}, u32[]{:S(2)}) %collective-permute-start.9) | collective-permute-done | bytes 73760 | tf_op jit(solution)/shard_map/ppermute | solution.py:664
  65.8 0.9 %shard_map.92 = (f32[9,32,32]{2,1,0:T(8,128)}, f32[9,32,32]{2,1,0:T(8,128)}) custom-call(f32[144,128]{1,0:T(8,128)S(1)} %add.15.mine, f32[144,128]{1,0:T(8,128)S(1)} %collective-permute-done.9.other), custom_call_target="tpu_custom_call" | custom-call | bytes 4194304 | tf_op jit(solution)/shard_map/pallas_call | solution.py:676
  (23 shorter events, 0.3 us)
Async XLA Ops:
  0.6 1.0 %copy-start = (bf16[1,32,32,256]{3,2,1,0:T(8,128)(2,1)S(1)}, bf16[1,32,32,256]{3,2,1,0:T(8,128)(2,1)}, u32[]{:S(2)}) copy-start(bf16[1,32,32,256]{3,2,1,0:T(8,128)(2,1)} %param.6) | copy-start | bytes 1572868
  1.7 4.1 %copy-start.4 = (bf16[1,32,32,256]{3,2,1,0:T(8,128)(2,1)S(1)}, bf16[1,32,32,256]{3,2,1,0:T(8,128)(2,1)}, u32[]{:S(2)}) copy-start(bf16[1,32,32,256]{3,2,1,0:T(8,128)(2,1)} %param.11) | copy-start | bytes 1572868
  2.1 30.7 %collective-permute-start = (bf16[800,256]{1,0:T(8,128)(2,1)S(1)}, bf16[800,256]{1,0:T(8,128)(2,1)S(1)}, u32[]{:S(2)}, u32[]{:S(2)}) collective-permute-start(bf16[800,256]{1,0:T(8,128)(2,1)S(1)} %get-tuple-element.25), channel_id=1, source_target_pairs={{0,4},{4,0},{8,12},{12,8},{16,20},{20,16},{24,28},{28,24},{1,5},{5... | collective-permute-start | bytes 1228808 | tf_op jit(solution)/shard_map/ppermute | solution.py:587
  5.1 27.7 %collective-permute-start.1 = (bf16[800,256]{1,0:T(8,128)(2,1)S(1)}, bf16[800,256]{1,0:T(8,128)(2,1)S(1)}, u32[]{:S(2)}, u32[]{:S(2)}) collective-permute-start(bf16[800,256]{1,0:T(8,128)(2,1)S(1)} %get-tuple-element.26), channel_id=1, source_target_pairs={{4,8},{12,16},{20,24},{8,4},{16,12},{24,20},{5,9},{13,17},{21,25},... | collective-permute-start | bytes 1228808 | tf_op jit(solution)/shard_map/ppermute | solution.py:587
  5.8 23.1 %copy-start.2 = (bf16[9,32,32]{2,1,0:T(8,128)(2,1)S(1)}, bf16[9,32,32]{2,1,0:T(8,128)(2,1)}, u32[]{:S(2)}) copy-start(bf16[9,32,32]{2,1,0:T(8,128)(2,1)} %rest_6_.1) | copy-start | bytes 55300
  5.8 23.1 %copy-start.3 = (bf16[9,32,32]{2,1,0:T(8,128)(2,1)S(1)}, bf16[9,32,32]{2,1,0:T(8,128)(2,1)}, u32[]{:S(2)}) copy-start(bf16[9,32,32]{2,1,0:T(8,128)(2,1)} %second.3) | copy-start | bytes 55300
  6.4 4.3 %collective-permute-start.2 = (bf16[256,128]{1,0:T(8,128)(2,1)S(1)}, bf16[256,128]{1,0:T(8,128)(2,1)S(1)}, u32[]{:S(2)}, u32[]{:S(2)}) collective-permute-start(bf16[256,128]{1,0:T(8,128)(2,1)S(1)} %get-tuple-element.28), channel_id=1, source_target_pairs={{0,2},{2,0},{1,3},{3,1},{4,6},{6,4},{5,7},{7,5},{8,10},{10,8},{9,1... | collective-permute-start | bytes 196616 | tf_op jit(solution)/shard_map/ppermute | solution.py:587
  10.7 18.2 %collective-permute-start.3 = (bf16[288,256]{1,0:T(8,128)(2,1)S(1)}, bf16[288,256]{1,0:T(8,128)(2,1)S(1)}, u32[]{:S(2)}, u32[]{:S(2)}) collective-permute-start(bf16[288,256]{1,0:T(8,128)(2,1)S(1)} %get-tuple-element.29), channel_id=1, source_target_pairs={{0,4},{4,0},{8,12},{12,8},{16,20},{20,16},{24,28},{28,24},{1,5},{5... | collective-permute-start | bytes 442376 | tf_op jit(solution)/shard_map/ppermute | solution.py:587
  15.1 0.8 %copy-start.6 = (s32[1,32,2]{1,2,0:T(2,128)S(1)}, s32[1,32,2]{1,2,0:T(2,128)}, u32[]{:S(2)}) copy-start(s32[1,32,2]{1,2,0:T(2,128)} %param.7) | copy-start | bytes 772
  15.1 13.9 %collective-permute-start.4 = (bf16[288,256]{1,0:T(8,128)(2,1)S(1)}, bf16[288,256]{1,0:T(8,128)(2,1)S(1)}, u32[]{:S(2)}, u32[]{:S(2)}) collective-permute-start(bf16[288,256]{1,0:T(8,128)(2,1)S(1)} %get-tuple-element.30), channel_id=1, source_target_pairs={{4,8},{12,16},{20,24},{8,4},{16,12},{24,20},{5,9},{13,17},{21,25},... | collective-permute-start | bytes 442376 | tf_op jit(solution)/shard_map/ppermute | solution.py:587
  15.9 16.8 %copy-start.1 = (bf16[1,32,32,256]{3,2,1,0:T(8,128)(2,1)S(1)}, bf16[1,32,32,256]{3,2,1,0:T(8,128)(2,1)}, u32[]{:S(2)}) copy-start(bf16[1,32,32,256]{3,2,1,0:T(8,128)(2,1)} %param.6) | copy-start | bytes 1572868
  16.0 16.8 %copy-start.5 = (bf16[9,32,32]{2,1,0:T(8,128)(2,1)S(1)}, bf16[9,32,32]{2,1,0:T(8,128)(2,1)}, u32[]{:S(2)}) copy-start(bf16[9,32,32]{2,1,0:T(8,128)(2,1)} %rest_5_.1) | copy-start | bytes 55300
  43.7 1.3 %collective-permute-start.5 = (f32[144,128]{1,0:T(8,128)S(1)}, f32[144,128]{1,0:T(8,128)S(1)}, u32[]{:S(2)}, u32[]{:S(2)}) collective-permute-start(f32[144,128]{1,0:T(8,128)S(1)} %get-tuple-element.35), channel_id=1, source_target_pairs={{0,1},{1,0},{2,3},{3,2},{4,5},{5,4},{6,7},{7,6},{8,9},{9,8},{10,11... | collective-permute-start | bytes 221192 | tf_op jit(solution)/shard_map/ppermute | solution.py:664
  45.0 4.4 %collective-permute-start.6 = (f32[144,128]{1,0:T(8,128)S(1)}, f32[144,128]{1,0:T(8,128)S(1)}, u32[]{:S(2)}, u32[]{:S(2)}) collective-permute-start(f32[144,128]{1,0:T(8,128)S(1)} %add.12), channel_id=1, source_target_pairs={{0,2},{2,0},{1,3},{3,1},{4,6},{6,4},{5,7},{7,5},{8,10},{10,8},{9,1... | collective-permute-start | bytes 221192 | tf_op jit(solution)/shard_map/ppermute | solution.py:664
  49.4 4.9 %collective-permute-start.7 = (f32[144,128]{1,0:T(8,128)S(1)}, f32[144,128]{1,0:T(8,128)S(1)}, u32[]{:S(2)}, u32[]{:S(2)}) collective-permute-start(f32[144,128]{1,0:T(8,128)S(1)} %add.13), channel_id=1, source_target_pairs={{0,4},{4,0},{8,12},{12,8},{16,20},{20,16},{24,28},{28,24},{1,5},{5... | collective-permute-start | bytes 221192 | tf_op jit(solution)/shard_map/ppermute | solution.py:664
  54.3 4.5 %collective-permute-start.8 = (f32[144,128]{1,0:T(8,128)S(1)}, f32[144,128]{1,0:T(8,128)S(1)}, u32[]{:S(2)}, u32[]{:S(2)}) collective-permute-start(f32[144,128]{1,0:T(8,128)S(1)} %add.14), channel_id=1, source_target_pairs={{0,8},{4,12},{8,0},{12,4},{16,24},{20,28},{24,16},{28,20},{1,9},{5... | collective-permute-start | bytes 221192 | tf_op jit(solution)/shard_map/ppermute | solution.py:664
  58.8 7.0 %collective-permute-start.9 = (f32[144,128]{1,0:T(8,128)S(1)}, f32[144,128]{1,0:T(8,128)S(1)}, u32[]{:S(2)}, u32[]{:S(2)}) collective-permute-start(f32[144,128]{1,0:T(8,128)S(1)} %add.15.mine), channel_id=1, source_target_pairs={{0,16},{4,20},{8,24},{12,28},{16,0},{20,4},{24,8},{28,12},{1,17},{... | collective-permute-start | bytes 221192 | tf_op jit(solution)/shard_map/ppermute | solution.py:664

commit v5 on v4

--- a/solution.py
+++ b/solution.py
@@ -225,8 +225,9 @@
     ncols, cot, msg_a, msg_b, *rest,
 ):
     cols, (
-        second, bottle, act_grad, view_m, view_0, view_p,
-        cot_m, cot_0, cot_p, back, high, low, coarse, bands_f, bands, small_f, small,
+        first, bottle, second,
+        act_grad, view_m, view_0, view_p, sides, first_bands, bottle_bands, second_bands,
+        cot_m, cot_0, cot_p, back, high, low, coarse, bands_f, bands, small_f, small, wide_f,
     ) = rest[:ncols], rest[ncols:]
     chans = second.shape[1]
     full, span = cot.shape
@@ -242,10 +243,31 @@
     small_t = small_f[...].T
     for b in range(3):
         small[rows_at(b, chans)] = small_t[0:chans, 3 * b * chans : 3 * (b + 1) * chans].astype(BF16)
+    fill_bands(first_bands, first, POOL)
+    fill_bands(wide_f, bottle, 1)
+    for b in range(3):
+        bottle_bands[rows_at(b, chans)] = wide_f[
+            0:chans, 3 * b * chans : 3 * (b + 1) * chans
+        ].astype(BF16)
+    second_bands[...] = jnp.zeros(second_bands.shape, BF16)
+    for k in range(POOL):
+        for b in range(3):
+            for a in range(3):
+                second_bands[
+                    rows_at(3 * k + b, chans), (k + a) * chans : (k + a + 1) * chans
+                ] = second[3 * a + b]
 
     size = CHALO * chans
     count = TILE // SLOT
     block = height // count
+
+    def halo_columns(sources, at):
+        for k in range(count):
+            sides[:, at + k * block : at + (k + 1) * block, :] = halo_block(
+                sources, k, chans, "features"
+            )
+
+    halo_columns([c[...] for c in cols], height)
     cot_0[rows_at(CHALO, chans, height), 0:span] = cot[...]
     for k in range(count):
         cot_0[rows_at(CHALO + k * block, chans, block), span:width] = to_rows(
@@ -261,6 +283,8 @@
         cot_0[rows_at(0, chans, CHALO), span:width] = corner[(block - CHALO) * chans :]
         corner = to_rows(halo_block(corner_views(down, size, cols), 0, chans, "cotangent"))
         cot_0[rows_at(CHALO + height, chans, CHALO), span:width] = corner[0:size]
+        halo_columns(corner_views(up, size, cols), 0)
+        halo_columns(corner_views(down, size, cols), 2 * height)
 
     pl.when(is_even("rows"))(lambda: vertical(msg_b, msg_a))
     pl.when(jnp.logical_not(is_even("rows")))(lambda: vertical(msg_a, msg_b))
@@ -335,13 +359,10 @@
 
 
 def main_kernel(
-    ncols, shifts, feat, feat_a, feat_b, msg_a, msg_b, *rest,
+    shifts, feat, feat_a, feat_b, sides, act_grad, view_m, view_0, view_p, bands, small,
+    grads, blended,
+    planes, moved, warp_m, warp_0, warp_p, act, high, low, pooled, pre_grad, acc,
 ):
-    cols, (
-        act_grad, view_m, view_0, view_p, first, bottle, grads, blended,
-        planes, moved, warp_m, warp_0, warp_p, act, high, low, pooled, pre_grad, acc,
-        bands_f, bands, small_f, small,
-    ) = rest[:ncols], rest[ncols:]
     chans, height, span = feat.shape
     tiles = span // TILE
     width = span + TILE
@@ -349,28 +370,11 @@
     has_up, has_down, has_left, has_right = has_sides()
     seen_cols = columns_seen((chans, width), span)
 
-    fill_bands(bands_f, first, POOL)
-    bands[...] = bands_f[...].astype(BF16)
-    fill_bands(small_f, bottle, 1)
-    for b in range(3):
-        small[rows_at(b, chans)] = small_f[:, 3 * b * chans : 3 * (b + 1) * chans].astype(BF16)
-
-    size = CHALO * chans
-    count = TILE // SLOT
-    block = height // count
-    halo = slice(span, width)
-
-    def halo_columns(sources, at):
-        for k in range(count):
-            planes[:, at + k * block : at + (k + 1) * block, halo] = halo_block(
-                sources, k, chans, "features"
-            )
-
     planes[:, height : 2 * height, 0:span] = feat[...]
-    halo_columns([c[...] for c in cols], height)
+    planes[:, :, span:width] = sides[...]
     fill = (height - FHALO) * chans
 
-    def vertical(up, up_msg, down, down_msg):
+    def vertical(up, down):
         for part in tiles_of(span):
             none = jnp.zeros((fill, TILE), BF16)
             planes[:, 0:height, part] = to_planes(
@@ -379,11 +383,9 @@
             planes[:, 2 * height : 3 * height, part] = to_planes(
                 jnp.concatenate([down[:, part], none], axis=0), chans
             )
-        halo_columns(corner_views(up_msg, size, cols), 0)
-        halo_columns(corner_views(down_msg, size, cols), 2 * height)
-
-    pl.when(is_even("rows"))(lambda: vertical(feat_b, msg_b, feat_a, msg_a))
-    pl.when(jnp.logical_not(is_even("rows")))(lambda: vertical(feat_a, msg_a, feat_b, msg_b))
+
+    pl.when(is_even("rows"))(lambda: vertical(feat_b, feat_a))
+    pl.when(jnp.logical_not(is_even("rows")))(lambda: vertical(feat_a, feat_b))
 
     tall = moved.shape[1]
     lane = lanes_of((tall, TILE))
@@ -483,17 +485,9 @@
     )
 
 
-def predict_kernel(part, blended, second, *rest):
-    out, rows, bands_f, bands = rest[-4:]
+def predict_kernel(part, blended, bands, *rest):
+    out, rows = rest[-2:]
     chans, height, span = out.shape
-    bands_f[...] = jnp.zeros(bands_f.shape, F32)
-    for k in range(POOL):
-        for b in range(3):
-            for a in range(3):
-                bands_f[rows_at(3 * k + b, chans), (k + a) * chans : (k + a + 1) * chans] = second[
-                    3 * a + b
-                ].astype(F32)
-    bands[...] = bands_f[...].astype(BF16)
 
     def group(g, _):
         at = rows_at(part * height + g * POOL, chans, POOL + 2)
@@ -541,12 +535,12 @@
     )
 
 
-def predict(blended, second, shape, parts, part, before):
+def predict(blended, bands, shape, parts, part, before):
     chans, height, span = shape
     rows = height // parts
     block = pl.BlockSpec((chans, rows, span), lambda i: (0, part, 0))
     whole = lambda a: pl.BlockSpec(a.shape, lambda i: (0,) * a.ndim)
-    args = (blended, second)
+    args = (blended, bands)
     specs = [whole(a) for a in args]
     more = {}
     if before is not None:
@@ -558,8 +552,6 @@
         jax.ShapeDtypeStruct(shape, BF16),
         [
             pltpu.VMEM((chans * rows, span), BF16),
-            pltpu.VMEM((3 * POOL * chans, (POOL + 2) * chans), F32),
-            pltpu.VMEM((3 * POOL * chans, (POOL + 2) * chans), BF16),
         ],
         len(args),
         12,
@@ -587,10 +579,11 @@
         return [lax.ppermute(m, axis, p) for m, p in zip(messages, pairs)]
 
     halo = bf(FHALO * chans, span)
-    messages = call(
+    feat_msgs = call(
         feature_kernel, (halo, halo), [pltpu.VMEM((full, span), BF16)], 1, 8
     )(features[0])
-    feat_msgs = swapped(messages, "rows")
+    row_pairs = swaps(rows)
+    feat_a = lax.ppermute(feat_msgs[0], "rows", row_pairs[0])
     packed = chans * (height * SLOT // TILE)
     cot_rows, *messages = call(
         column_kernel,
@@ -604,14 +597,20 @@
     ncols = len(col_msgs)
     halo = bf(CHALO * chans + ncols * packed * TILE // span, span)
     messages = call(edge_kernel, (halo, halo), [], 1 + ncols, 8)(cot_rows, *col_msgs)
+    messages, late = lax.optimization_barrier((messages, feat_msgs[1]))
     row_msgs = swapped(messages, "rows")
+    feat_b = lax.ppermute(late, "rows", row_pairs[1])
 
     tall_c = (height + 2 * CHALO) * chans
     view = bf((height + 2) * chans, span)
     band = 3 * (POOL + 2) * chans
-    act_grad, *views = call(
+    act_grad, *rest = call(
         functools.partial(back_kernel, ncols),
-        (jax.ShapeDtypeStruct((full, span), F32), view, view, view),
+        (
+            jax.ShapeDtypeStruct((full, span), F32), view, view, view,
+            bf(chans, 3 * height, TILE), bf(POOL * chans, band), bf(3 * chans, 3 * chans),
+            bf(3 * POOL * chans, (POOL + 2) * chans),
+        ),
         [pltpu.VMEM((tall_c, width), BF16)] * 3
         + [pltpu.VMEM(((height + 2 * POOL) * chans, span), BF16)]
         + [pltpu.VMEM(((groups + 2) * chans, width), BF16)] * 3
@@ -620,14 +619,17 @@
             pltpu.VMEM((POOL * chans, band), BF16),
             pltpu.VMEM((9 * chans, TILE), F32),
             pltpu.VMEM((3 * chans, 3 * chans), BF16),
+            pltpu.VMEM((chans, 9 * chans), F32),
         ],
-        5 + ncols,
+        6 + ncols,
         16,
-    )(cot_rows, *row_msgs, *col_msgs, second_kernel, bottle_kernel)
+        flops=8 * 10**9,
+    )(cot_rows, *row_msgs, *col_msgs, first_kernel, bottle_kernel, second_kernel)
+    views, sides, weights = rest[:3], rest[3], rest[4:]
 
     tall = pl.cdiv(height + 2 * EXT, 16) * 16
     grads, blended = call(
-        functools.partial(main_kernel, ncols),
+        main_kernel,
         (jax.ShapeDtypeStruct((9 * chans // 2, TILE), F32), bf((height + 2) * chans, width)),
         [
             pltpu.VMEM((chans, 3 * height, width), BF16),
@@ -639,18 +641,13 @@
         + [
             pltpu.VMEM((full, span), BF16),
             pltpu.VMEM((band, POOL * chans), F32),
-            pltpu.VMEM((POOL * chans, band), F32),
-            pltpu.VMEM((POOL * chans, band), BF16),
-            pltpu.VMEM((chans, 9 * chans), F32),
-            pltpu.VMEM((3 * chans, 3 * chans), BF16),
         ],
-        12 + ncols,
+        11,
         32,
         flops=10**10,
         smem_first=True,
     )(
-        shifts[0], features[0], *feat_msgs, *row_msgs, *col_msgs,
-        act_grad, *views, first_kernel, bottle_kernel,
+        shifts[0], features[0], feat_a, feat_b, sides, act_grad, *views, *weights[:2]
     )
 
     steps = []
@@ -664,7 +661,7 @@
         other = lax.ppermute(grads, axis, pairs)
         if 1 <= step <= parts:
             prediction = predict(
-                blended, second_kernel, (chans, height, span), parts, step - 1, prediction
+                blended, weights[2], (chans, height, span), parts, step - 1, prediction
             )
             other, prediction = lax.optimization_barrier((other, prediction))
         if step < len(steps) - 1:

time: 66.9 us -> 68 us (1.016)
  local copies, waits for them, and re-layouts: 1.15 us -> 2.19 us
  starting transfers between devices: 20.5 us -> 21.2 us
    ppermute x5 -> x3, waiting for transfers between devices: 15.8 us -> 2.54 us  [swapped(): return [lax.ppermute(m, axis, p) for m, p in zip(messages, pairs)]]
    ppermute x0 -> x2, waiting for transfers between devices: none -> 12.4 us  [the longest x1 12.4 us: shards(): feat_a = lax.ppermute(feat_msgs[0], 'rows', row_pairs[0])]
    ppermute x0 -> x2, starting transfers between devices: none -> 5.15 us  [the longest x1 4.34 us: shards(): feat_a = lax.ppermute(feat_msgs[0], 'rows', row_pairs[0])]
    ppermute x5 -> x3, starting transfers between devices: 10.4 us -> 5.78 us  [swapped(): return [lax.ppermute(m, axis, p) for m, p in zip(messages, pairs)]]
    unnamed x14, local copies, waits for them, and re-layouts: 1.06 us -> 2.1 us
  transfers between devices with their start and end apart: 10 -> 10, of which waited for: 7 -> 8; matrix products, arithmetic and copies ran while one was open for 0% -> 0% of each run, Pallas kernels for 12% -> 12%
where the time goes in v5:
time: 68 us; the launch traced here: 67.7 us
  waiting for transfers between devices  23.5 us (35%)
  starting transfers between devices  21.2 us (31%)
  Pallas kernels  20 us (29%)
  local copies, waits for them, and re-layouts  2.19 us (3%)
  between operations  0.74 us (1%)
    ppermute x1, waiting for transfers between devices, shards(): feat_a = lax.ppermute(feat_msgs[0], 'rows', row_pairs[0])  12.4 us
    pallas_call x1, Pallas kernels, shards(): call(main_kernel, (jax.ShapeDtypeStruct((9 * chans // 2, TILE), F32), bf(...  10.5 us
    ppermute x5, starting transfers between devices, shards(): other = lax.ppermute(grads, axis, pairs)  10.3 us
    ppermute x5, waiting for transfers between devices, shards(): other = lax.ppermute(grads, axis, pairs)  8.58 us
    ppermute x3, starting transfers between devices, swapped(): return [lax.ppermute(m, axis, p) for m, p in zip(messages, pairs)]  5.78 us
    ppermute x1, starting transfers between devices, shards(): feat_a = lax.ppermute(feat_msgs[0], 'rows', row_pairs[0])  4.34 us
    pallas_call x1, Pallas kernels, shards(): call(functools.partial(back_kernel, ncols), (jax.ShapeDtypeStruct((full,...  4.34 us
    pallas_call x2, Pallas kernels, predict(): call(functools.partial(predict_kernel, part), jax.ShapeDtypeStruct(shape,...  3.33 us
  transfers between devices with their start and end apart: 10, of which 8 were waited for; matrix products, arithmetic and copies ran while one was open for 0% of the time, Pallas kernels for 12%

profile of v5, /device:TPU:0, one launch (start us, length us, event | category | flops | bytes accessed | tf_op | source)
XLA Modules:
  0.0 67.7 jit_solution(11858612665200170967)
XLA Ops:
  0.6 1.0 %copy-done = bf16[1,32,32,256]{3,2,1,0:T(8,128)(2,1)S(1)} copy-done((bf16[1,32,32,256]{3,2,1,0:T(8,128)(2,1)S(1)}, bf16[1,32,32,256]{3,2,1,0:T(8,128)(2,1)}, u32[]{:S(2)}) %copy-start) | copy-done | bytes 524312
  1.7 1.0 %copy-done.2 = bf16[1,32,32,256]{3,2,1,0:T(8,128)(2,1)S(1)} copy-done((bf16[1,32,32,256]{3,2,1,0:T(8,128)(2,1)S(1)}, bf16[1,32,32,256]{3,2,1,0:T(8,128)(2,1)}, u32[]{:S(2)}) %copy-start.2) | copy-done | bytes 524312
  3.2 3.0 %collective-permute-start.1 = (bf16[256,128]{1,0:T(8,128)(2,1)S(1)}, bf16[256,128]{1,0:T(8,128)(2,1)S(1)}, u32[]{:S(2)}, u32[]{:S(2)}) collective-permute-start(bf16[256,128]{1,0:T(8,128)(2,1)S(1)} %get-tuple-element.34), channel_id=1, source_target_pairs={{0,2},{2,0},{1,3},{3,1},{4,6},{6,4},{5,7},{7,5},{8,10},{10,8},{9,1... | collective-permute-start | bytes 196616 | tf_op jit(solution)/shard_map/ppermute | solution.py:579
  6.6 1.9 %collective-permute-done.1.rest_0_ = bf16[256,128]{1,0:T(8,128)(2,1)S(1)} collective-permute-done((bf16[256,128]{1,0:T(8,128)(2,1)S(1)}, bf16[256,128]{1,0:T(8,128)(2,1)S(1)}, u32[]{:S(2)}, u32[]{:S(2)}) %collective-permute-start.1) | collective-permute-done | bytes 65568 | tf_op jit(solution)/shard_map/ppermute | solution.py:579
  8.5 2.1 %collective-permute-start.3 = (bf16[288,256]{1,0:T(8,128)(2,1)S(1)}, bf16[288,256]{1,0:T(8,128)(2,1)S(1)}, u32[]{:S(2)}, u32[]{:S(2)}) collective-permute-start(bf16[288,256]{1,0:T(8,128)(2,1)S(1)} %get-tuple-element.39), channel_id=1, source_target_pairs={{0,4},{4,0},{8,12},{12,8},{16,20},{20,16},{24,28},{28,24},{1,5},{5... | collective-permute-start | bytes 442376 | tf_op jit(solution)/shard_map/ppermute | solution.py:579
  10.7 0.7 collective-permute-start.4
  11.3 4.3 %collective-permute-start = (bf16[800,256]{1,0:T(8,128)(2,1)S(1)}, bf16[800,256]{1,0:T(8,128)(2,1)S(1)}, u32[]{:S(2)}, u32[]{:S(2)}) collective-permute-start(bf16[800,256]{1,0:T(8,128)(2,1)S(1)} %get-tuple-element.32), channel_id=1, source_target_pairs={{0,4},{4,0},{8,12},{12,8},{16,20},{20,16},{24,28},{28,24},{1,5},{5... | collective-permute-start | bytes 1228808 | tf_op jit(solution)/shard_map/ppermute | solution.py:586
  15.8 0.8 %collective-permute-start.2 = (bf16[800,256]{1,0:T(8,128)(2,1)S(1)}, bf16[800,256]{1,0:T(8,128)(2,1)S(1)}, u32[]{:S(2)}, u32[]{:S(2)}) collective-permute-start(bf16[800,256]{1,0:T(8,128)(2,1)S(1)} %get-tuple-element.38), channel_id=1, source_target_pairs={{4,8},{12,16},{20,24},{8,4},{16,12},{24,20},{5,9},{13,17},{21,25},... | collective-permute-start | bytes 1228808 | tf_op jit(solution)/shard_map/ppermute | solution.py:602
  16.6 0.7 %collective-permute-done.3.msg_a = bf16[288,256]{1,0:T(8,128)(2,1)S(1)} collective-permute-done((bf16[288,256]{1,0:T(8,128)(2,1)S(1)}, bf16[288,256]{1,0:T(8,128)(2,1)S(1)}, u32[]{:S(2)}, u32[]{:S(2)}) %collective-permute-start.3) | collective-permute-done | bytes 147488 | tf_op jit(solution)/shard_map/ppermute | solution.py:579
  17.3 4.3 %shard_map.88 = (f32[1024,256]{1,0:T(8,128)S(1)}, bf16[1088,256]{1,0:T(8,128)(2,1)S(1)}, bf16[1088,256]{1,0:T(8,128)(2,1)S(1)}, bf16[1088,256]{1,0:T(8,128)(2,1)...) custom-call(bf16[1024,256]{1,0:T(8,128)(2,1)S(1)} %get-tuple-element, ...), custom_call_target="tpu_custom_call" | custom-call | flops 8000000000 | bytes 4194304 | tf_op jit(solution)/shard_map/pallas_call | solution.py:607
  21.6 12.4 %collective-permute-done.feat_a = bf16[800,256]{1,0:T(8,128)(2,1)S(1)} collective-permute-done((bf16[800,256]{1,0:T(8,128)(2,1)S(1)}, bf16[800,256]{1,0:T(8,128)(2,1)S(1)}, u32[]{:S(2)}, u32[]{:S(2)}) %collective-permute-start) | collective-permute-done | bytes 409632 | tf_op jit(solution)/shard_map/ppermute | solution.py:586
  34.0 10.5 %shard_map.89 = (f32[144,128]{1,0:T(8,128)S(1)}, bf16[1088,384]{1,0:T(8,128)(2,1)S(1)}) custom-call(s32[32,2]{1,0:T(8,128)S(1)} %copy.10.shifts, bf16[32,32,256]{2,1,0:T(8,128)(2,1)S(1)} %bitcast.6, bf16[800,256]{1,0:T(8,128)(2,1)S(1)} %collective-permute-done.feat_a, bf16[800,256]{1,0:T(8,128)(2,1)S(1)} %collective-permute-done.2.feat_b, ...), custom_call_target="tpu_custom_call" | custom-call | flops 10000000000 | bytes 4194304 | tf_op jit(solution)/shard_map/pallas_call | solution.py:631
  44.6 1.3 %collective-permute-done.5 = f32[144,128]{1,0:T(8,128)S(1)} collective-permute-done((f32[144,128]{1,0:T(8,128)S(1)}, f32[144,128]{1,0:T(8,128)S(1)}, u32[]{:S(2)}, u32[]{:S(2)}) %collective-permute-start.5) | collective-permute-done | bytes 73760 | tf_op jit(solution)/shard_map/ppermute | solution.py:661
  45.9 1.6 %collective-permute-start.6 = (f32[144,128]{1,0:T(8,128)S(1)}, f32[144,128]{1,0:T(8,128)S(1)}, u32[]{:S(2)}, u32[]{:S(2)}) collective-permute-start(f32[144,128]{1,0:T(8,128)S(1)} %add.12), channel_id=1, source_target_pairs={{0,2},{2,0},{1,3},{3,1},{4,6},{6,4},{5,7},{7,5},{8,10},{10,8},{9,1... | collective-permute-start | bytes 221192 | tf_op jit(solution)/shard_map/ppermute | solution.py:661
  47.5 1.7 %shard_map.90.rest_0_ = bf16[32,32,256]{2,1,0:T(8,128)(2,1)} custom-call(bf16[1088,384]{1,0:T(8,128)(2,1)S(1)} %get-tuple-element.55.blended, bf16[384,192]{1,0:T(8,128)(2,1)S(1)} %get-tuple-element.52.bands), custom_call_target="tpu_custom_call" | custom-call | flops 1000000000 | bytes 4194304 | tf_op jit(solution)/shard_map/pallas_call | solution.py:550
  49.1 1.2 %collective-permute-done.6 = f32[144,128]{1,0:T(8,128)S(1)} collective-permute-done((f32[144,128]{1,0:T(8,128)S(1)}, f32[144,128]{1,0:T(8,128)S(1)}, u32[]{:S(2)}, u32[]{:S(2)}) %collective-permute-start.6) | collective-permute-done | bytes 73760 | tf_op jit(solution)/shard_map/ppermute | solution.py:661
  50.3 2.5 %collective-permute-start.7 = (f32[144,128]{1,0:T(8,128)S(1)}, f32[144,128]{1,0:T(8,128)S(1)}, u32[]{:S(2)}, u32[]{:S(2)}) collective-permute-start(f32[144,128]{1,0:T(8,128)S(1)} %add.13), channel_id=1, source_target_pairs={{0,4},{4,0},{8,12},{12,8},{16,20},{20,16},{24,28},{28,24},{1,5},{5... | collective-permute-start | bytes 221192 | tf_op jit(solution)/shard_map/ppermute | solution.py:661
  52.9 1.7 %shard_map.91 = bf16[32,32,256]{2,1,0:T(8,128)(2,1)} custom-call(bf16[1088,384]{1,0:T(8,128)(2,1)S(1)} %get-tuple-element.55.blended, bf16[384,192]{1,0:T(8,128)(2,1)S(1)} %get-tuple-element.52.bands, bf16[32,32,256]{2,1,0:T(8,128)(2,1)} %shard_map.90.rest_0_), custom_call_target="tpu_custom_call", output_to_operand_aliasing={{}: (2, {})} | custom-call | flops 1000000000 | bytes 4194304 | tf_op jit(solution)/shard_map/pallas_call | solution.py:550
  54.5 0.7 collective-permute-done.7
  55.2 2.3 %collective-permute-start.8 = (f32[144,128]{1,0:T(8,128)S(1)}, f32[144,128]{1,0:T(8,128)S(1)}, u32[]{:S(2)}, u32[]{:S(2)}) collective-permute-start(f32[144,128]{1,0:T(8,128)S(1)} %add.14), channel_id=1, source_target_pairs={{0,8},{4,12},{8,0},{12,4},{16,24},{20,28},{24,16},{28,20},{1,9},{5... | collective-permute-start | bytes 221192 | tf_op jit(solution)/shard_map/ppermute | solution.py:661
  57.5 2.3 %collective-permute-done.8 = f32[144,128]{1,0:T(8,128)S(1)} collective-permute-done((f32[144,128]{1,0:T(8,128)S(1)}, f32[144,128]{1,0:T(8,128)S(1)}, u32[]{:S(2)}, u32[]{:S(2)}) %collective-permute-start.8) | collective-permute-done | bytes 73760 | tf_op jit(solution)/shard_map/ppermute | solution.py:661
  59.9 3.8 %collective-permute-start.9 = (f32[144,128]{1,0:T(8,128)S(1)}, f32[144,128]{1,0:T(8,128)S(1)}, u32[]{:S(2)}, u32[]{:S(2)}) collective-permute-start(f32[144,128]{1,0:T(8,128)S(1)} %add.15.mine), channel_id=1, source_target_pairs={{0,16},{4,20},{8,24},{12,28},{16,0},{20,4},{24,8},{28,12},{1,17},{... | collective-permute-start | bytes 221192 | tf_op jit(solution)/shard_map/ppermute | solution.py:661
  63.7 3.1 %collective-permute-done.9.other = f32[144,128]{1,0:T(8,128)S(1)} collective-permute-done((f32[144,128]{1,0:T(8,128)S(1)}, f32[144,128]{1,0:T(8,128)S(1)}, u32[]{:S(2)}, u32[]{:S(2)}) %collective-permute-start.9) | collective-permute-done | bytes 73760 | tf_op jit(solution)/shard_map/ppermute | solution.py:661
  66.8 0.9 %shard_map.92 = (f32[9,32,32]{2,1,0:T(8,128)}, f32[9,32,32]{2,1,0:T(8,128)}) custom-call(f32[144,128]{1,0:T(8,128)S(1)} %add.15.mine, f32[144,128]{1,0:T(8,128)S(1)} %collective-permute-done.9.other), custom_call_target="tpu_custom_call" | custom-call | bytes 4194304 | tf_op jit(solution)/shard_map/pallas_call | solution.py:673
  (23 shorter events, 1.2 us)
Async XLA Ops:
  0.6 1.0 %copy-start = (bf16[1,32,32,256]{3,2,1,0:T(8,128)(2,1)S(1)}, bf16[1,32,32,256]{3,2,1,0:T(8,128)(2,1)}, u32[]{:S(2)}) copy-start(bf16[1,32,32,256]{3,2,1,0:T(8,128)(2,1)} %param.6) | copy-start | bytes 1572868
  1.7 1.0 %copy-start.2 = (bf16[1,32,32,256]{3,2,1,0:T(8,128)(2,1)S(1)}, bf16[1,32,32,256]{3,2,1,0:T(8,128)(2,1)}, u32[]{:S(2)}) copy-start(bf16[1,32,32,256]{3,2,1,0:T(8,128)(2,1)} %param.11) | copy-start | bytes 1572868
  3.2 5.2 %collective-permute-start.1 = (bf16[256,128]{1,0:T(8,128)(2,1)S(1)}, bf16[256,128]{1,0:T(8,128)(2,1)S(1)}, u32[]{:S(2)}, u32[]{:S(2)}) collective-permute-start(bf16[256,128]{1,0:T(8,128)(2,1)S(1)} %get-tuple-element.34), channel_id=1, source_target_pairs={{0,2},{2,0},{1,3},{3,1},{4,6},{6,4},{5,7},{7,5},{8,10},{10,8},{9,1... | collective-permute-start | bytes 196616 | tf_op jit(solution)/shard_map/ppermute | solution.py:579
  8.5 8.8 %copy-start.3 = (bf16[9,32,32]{2,1,0:T(8,128)(2,1)S(1)}, bf16[9,32,32]{2,1,0:T(8,128)(2,1)}, u32[]{:S(2)}) copy-start(bf16[9,32,32]{2,1,0:T(8,128)(2,1)} %rest_1_.1) | copy-start | bytes 55300
  8.5 8.8 %copy-start.4 = (bf16[9,32,32]{2,1,0:T(8,128)(2,1)S(1)}, bf16[9,32,32]{2,1,0:T(8,128)(2,1)}, u32[]{:S(2)}) copy-start(bf16[9,32,32]{2,1,0:T(8,128)(2,1)} %rest_2_.1) | copy-start | bytes 55300
  8.5 8.8 %copy-start.5 = (bf16[9,32,32]{2,1,0:T(8,128)(2,1)S(1)}, bf16[9,32,32]{2,1,0:T(8,128)(2,1)}, u32[]{:S(2)}) copy-start(bf16[9,32,32]{2,1,0:T(8,128)(2,1)} %rest_3_.1) | copy-start | bytes 55300
  8.5 8.7 %collective-permute-start.3 = (bf16[288,256]{1,0:T(8,128)(2,1)S(1)}, bf16[288,256]{1,0:T(8,128)(2,1)S(1)}, u32[]{:S(2)}, u32[]{:S(2)}) collective-permute-start(bf16[288,256]{1,0:T(8,128)(2,1)S(1)} %get-tuple-element.39), channel_id=1, source_target_pairs={{0,4},{4,0},{8,12},{12,8},{16,20},{20,16},{24,28},{28,24},{1,5},{5... | collective-permute-start | bytes 442376 | tf_op jit(solution)/shard_map/ppermute | solution.py:579
  10.7 6.6 %collective-permute-start.4 = (bf16[288,256]{1,0:T(8,128)(2,1)S(1)}, bf16[288,256]{1,0:T(8,128)(2,1)S(1)}, u32[]{:S(2)}, u32[]{:S(2)}) collective-permute-start(bf16[288,256]{1,0:T(8,128)(2,1)S(1)} %get-tuple-element.40), channel_id=1, source_target_pairs={{4,8},{12,16},{20,24},{8,4},{16,12},{24,20},{5,9},{13,17},{21,25},... | collective-permute-start | bytes 442376 | tf_op jit(solution)/shard_map/ppermute | solution.py:579
  11.3 4.4 %copy-start.6 = (s32[1,32,2]{1,2,0:T(2,128)S(1)}, s32[1,32,2]{1,2,0:T(2,128)}, u32[]{:S(2)}) copy-start(s32[1,32,2]{1,2,0:T(2,128)} %param.7) | copy-start | bytes 772
  11.3 22.7 %collective-permute-start = (bf16[800,256]{1,0:T(8,128)(2,1)S(1)}, bf16[800,256]{1,0:T(8,128)(2,1)S(1)}, u32[]{:S(2)}, u32[]{:S(2)}) collective-permute-start(bf16[800,256]{1,0:T(8,128)(2,1)S(1)} %get-tuple-element.32), channel_id=1, source_target_pairs={{0,4},{4,0},{8,12},{12,8},{16,20},{20,16},{24,28},{28,24},{1,5},{5... | collective-permute-start | bytes 1228808 | tf_op jit(solution)/shard_map/ppermute | solution.py:586
  15.8 18.3 %copy-start.1 = (bf16[1,32,32,256]{3,2,1,0:T(8,128)(2,1)S(1)}, bf16[1,32,32,256]{3,2,1,0:T(8,128)(2,1)}, u32[]{:S(2)}) copy-start(bf16[1,32,32,256]{3,2,1,0:T(8,128)(2,1)} %param.6) | copy-start | bytes 1572868
  15.8 18.3 %collective-permute-start.2 = (bf16[800,256]{1,0:T(8,128)(2,1)S(1)}, bf16[800,256]{1,0:T(8,128)(2,1)S(1)}, u32[]{:S(2)}, u32[]{:S(2)}) collective-permute-start(bf16[800,256]{1,0:T(8,128)(2,1)S(1)} %get-tuple-element.38), channel_id=1, source_target_pairs={{4,8},{12,16},{20,24},{8,4},{16,12},{24,20},{5,9},{13,17},{21,25},... | collective-permute-start | bytes 1228808 | tf_op jit(solution)/shard_map/ppermute | solution.py:602
  44.6 1.3 %collective-permute-start.5 = (f32[144,128]{1,0:T(8,128)S(1)}, f32[144,128]{1,0:T(8,128)S(1)}, u32[]{:S(2)}, u32[]{:S(2)}) collective-permute-start(f32[144,128]{1,0:T(8,128)S(1)} %get-tuple-element.48), channel_id=1, source_target_pairs={{0,1},{1,0},{2,3},{3,2},{4,5},{5,4},{6,7},{7,6},{8,9},{9,8},{10,11... | collective-permute-start | bytes 221192 | tf_op jit(solution)/shard_map/ppermute | solution.py:661
  45.9 4.4 %collective-permute-start.6 = (f32[144,128]{1,0:T(8,128)S(1)}, f32[144,128]{1,0:T(8,128)S(1)}, u32[]{:S(2)}, u32[]{:S(2)}) collective-permute-start(f32[144,128]{1,0:T(8,128)S(1)} %add.12), channel_id=1, source_target_pairs={{0,2},{2,0},{1,3},{3,1},{4,6},{6,4},{5,7},{7,5},{8,10},{10,8},{9,1... | collective-permute-start | bytes 221192 | tf_op jit(solution)/shard_map/ppermute | solution.py:661
  50.3 4.9 %collective-permute-start.7 = (f32[144,128]{1,0:T(8,128)S(1)}, f32[144,128]{1,0:T(8,128)S(1)}, u32[]{:S(2)}, u32[]{:S(2)}) collective-permute-start(f32[144,128]{1,0:T(8,128)S(1)} %add.13), channel_id=1, source_target_pairs={{0,4},{4,0},{8,12},{12,8},{16,20},{20,16},{24,28},{28,24},{1,5},{5... | collective-permute-start | bytes 221192 | tf_op jit(solution)/shard_map/ppermute | solution.py:661
  55.2 4.6 %collective-permute-start.8 = (f32[144,128]{1,0:T(8,128)S(1)}, f32[144,128]{1,0:T(8,128)S(1)}, u32[]{:S(2)}, u32[]{:S(2)}) collective-permute-start(f32[144,128]{1,0:T(8,128)S(1)} %add.14), channel_id=1, source_target_pairs={{0,8},{4,12},{8,0},{12,4},{16,24},{20,28},{24,16},{28,20},{1,9},{5... | collective-permute-start | bytes 221192 | tf_op jit(solution)/shard_map/ppermute | solution.py:661
  59.9 7.0 %collective-permute-start.9 = (f32[144,128]{1,0:T(8,128)S(1)}, f32[144,128]{1,0:T(8,128)S(1)}, u32[]{:S(2)}, u32[]{:S(2)}) collective-permute-start(f32[144,128]{1,0:T(8,128)S(1)} %add.15.mine), channel_id=1, source_target_pairs={{0,16},{4,20},{8,24},{12,28},{16,0},{20,4},{24,8},{28,12},{1,17},{... | collective-permute-start | bytes 221192 | tf_op jit(solution)/shard_map/ppermute | solution.py:661

commit v6 on v5

--- a/solution.py
+++ b/solution.py
@@ -15,6 +15,8 @@
 SLOT = 32
 EXT = 9
 FHALO = MAXSHIFT + EXT
+USUAL = 14
+LARGEST = FHALO + 1
 CHALO = 5
 F32 = jnp.float32
 BF16 = jnp.bfloat16
@@ -76,14 +78,32 @@
     return [first, second + [(j, i) for i, j in second]]
 
 
-def feature_kernel(feat, msg_a, msg_b, rows):
+def needed(shift, below):
+    return jnp.maximum(EXT + shift if below else EXT - shift, 0)
+
+
+def feature_kernel(shifts, feat, msg_a, msg_b):
     chans, height, span = feat.shape
-    for part in tiles_of(span):
-        rows[:, part] = to_rows(feat[:, :, part])
-    edge = (height - FHALO) * chans
-    low = jnp.where(is_even("rows"), edge, 0)
-    msg_a[...] = rows[pl.ds(pl.multiple_of(low, chans), FHALO * chans), :]
-    msg_b[...] = rows[pl.ds(pl.multiple_of(edge - low, chans), FHALO * chans), :]
+    full = chans * height
+    size = msg_a.shape[0]
+    chunk = size // 4
+    source = feat[...].reshape(full, span)
+    lane = lanes_of((8, full))
+    chan, row = lane // height, lane % height
+    for msg, to_below in ((msg_a, is_even("rows")), (msg_b, jnp.logical_not(is_even("rows")))):
+        target = jnp.full((8, full), -1, jnp.int32)
+        at = jnp.int32(0)
+        for c in range(chans):
+            shift = shifts[c, 0]
+            count = jnp.where(to_below, needed(shift, False), needed(shift, True))
+            first = jnp.where(to_below, height - count, 0)
+            mine = (chan == c) & (row >= first) & (row < first + count)
+            target = jnp.where(mine, row + (at - first), target)
+            at = at + count
+        for p in range(0, size, chunk):
+            place = lax.broadcasted_iota(jnp.int32, (chunk, full), 0) + p
+            pick = jnp.where(place == target[0:1], 1.0, 0.0).astype(BF16)
+            msg[p : p + chunk] = jnp.dot(pick, source, preferred_element_type=F32).astype(BF16)
 
 
 def column_kernel(feat, cot, cot_rows, *col_msgs):
@@ -361,7 +381,7 @@
 def main_kernel(
     shifts, feat, feat_a, feat_b, sides, act_grad, view_m, view_0, view_p, bands, small,
     grads, blended,
-    planes, moved, warp_m, warp_0, warp_p, act, high, low, pooled, pre_grad, acc,
+    lent, moved, warp_m, warp_0, warp_p, act, high, low, pooled, pre_grad, acc,
 ):
     chans, height, span = feat.shape
     tiles = span // TILE
@@ -370,34 +390,56 @@
     has_up, has_down, has_left, has_right = has_sides()
     seen_cols = columns_seen((chans, width), span)
 
-    planes[:, height : 2 * height, 0:span] = feat[...]
-    planes[:, :, span:width] = sides[...]
-    fill = (height - FHALO) * chans
-
-    def vertical(up, down):
-        for part in tiles_of(span):
-            none = jnp.zeros((fill, TILE), BF16)
-            planes[:, 0:height, part] = to_planes(
-                jnp.concatenate([none, up[:, part]], axis=0), chans
-            )
-            planes[:, 2 * height : 3 * height, part] = to_planes(
-                jnp.concatenate([down[:, part], none], axis=0), chans
-            )
-
-    pl.when(is_even("rows"))(lambda: vertical(feat_b, feat_a))
-    pl.when(jnp.logical_not(is_even("rows")))(lambda: vertical(feat_a, feat_b))
+    size = feat_a.shape[0]
+    window = lent.shape[1] - size
+    lent[:, size:, :] = jnp.zeros((2, window, span), BF16)
+
+    def borrow(up, down):
+        lent[0, 0:size] = up[...]
+        lent[1, 0:size] = down[...]
+
+    pl.when(is_even("rows"))(lambda: borrow(feat_b, feat_a))
+    pl.when(jnp.logical_not(is_even("rows")))(lambda: borrow(feat_a, feat_b))
 
     tall = moved.shape[1]
     lane = lanes_of((tall, TILE))
     seen_halo = ((lane < TILE // 2) & has_right) | ((lane >= TILE // 2) & has_left)
     step = lanes_of((tall, 3 * height)) - lax.broadcasted_iota(jnp.int32, (tall, 3 * height), 0)
-
-    def warp(c, _):
-        pick = jnp.where(step == height - EXT + shifts[c, 0], 1.0, 0.0).astype(BF16)
-        plane = jnp.dot(pick, planes[c], preferred_element_type=F32)
-        move = shifts[c, 1]
+    depth = 2 * window + height
+    source = lanes_of((1, depth))
+    apart = lax.broadcasted_iota(jnp.int32, (tall, depth), 0) - lanes_of((tall, depth))
+    align = 16
+
+    def warp(c, ats):
+        at_up, at_down = ats
+        shift, move = shifts[c, 0], shifts[c, 1]
+        n_up, n_down = needed(shift, False), needed(shift, True)
+        base_up, base_down = (
+            pl.multiple_of(lax.div(at, align) * align, align) for at in (at_up, at_down)
+        )
+        skip_up, skip_down = at_up - base_up, at_down - base_down
+        own = EXT - window - shift
+        below = own - skip_down
+        above = EXT - skip_up - n_up - shift
+        in_up = (source >= skip_up) & (source < skip_up + n_up)
+        first_down = window + height + skip_down
+        in_down = (source >= first_down) & (source < first_down + n_down)
+        none = 4 * depth
+        offset = jnp.where(
+            source < window,
+            jnp.where(in_up, above, none),
+            jnp.where(source < window + height, own, jnp.where(in_down, below, none)),
+        )
+        pick = jnp.where(apart == offset, 1.0, 0.0).astype(BF16)
+        rows = jnp.concatenate(
+            [lent[0, pl.ds(base_up, window), :], feat[c], lent[1, pl.ds(base_down, window), :]], axis=0
+        )
+        plane = jnp.dot(pick, rows, preferred_element_type=F32)
+        pick = jnp.where(step == height - EXT + shift, 1.0, 0.0).astype(BF16)
+        plane = [plane[:, part] for part in tiles_of(span)]
+        plane.append(jnp.dot(pick, sides[c], preferred_element_type=F32))
         amount = jnp.where(move > 0, TILE - move, -move)
-        parts = [turn(plane[:, part], amount) for part in tiles_of(width)]
+        parts = [turn(part, amount) for part in plane]
         inside = jnp.where(move > 0, lane, TILE - 1 - lane) < TILE - jnp.abs(move)
         for t, part in enumerate(tiles_of(width)):
             after, before = parts[(t + 1) % (tiles + 1)], parts[t - 1]
@@ -405,9 +447,9 @@
             if t == tiles:
                 result = jnp.where(seen_halo, result, 0.0)
             moved[c, :, part] = result.astype(BF16)
-        return 0
-
-    lax.fori_loop(0, chans, warp, 0, unroll=4)
+        return at_up + n_up, at_down + n_down
+
+    lax.fori_loop(0, chans, warp, (jnp.int32(0), jnp.int32(0)), unroll=4)
     chunk = 16
     for r in range(0, tall, chunk):
         for part in tiles_of(width):
@@ -563,43 +605,30 @@
     )(*args)
 
 
-def shards(features, shifts, first_kernel, bottle_kernel, second_kernel, cotangent):
-    imgs, chans, height, span = features.shape
-    rows, cols, dp = (lax.axis_size(a) for a in ("rows", "cols", "dp"))
-    tiles = span // TILE
+def bf(*shape):
+    return jax.ShapeDtypeStruct(shape, BF16)
+
+
+def swapped(messages, axis):
+    pairs = [p for p in swaps(lax.axis_size(axis)) if p]
+    return [lax.ppermute(m, axis, p) for m, p in zip(messages, pairs)]
+
+
+def both_passes(size, feat, shifts, cot_rows, col_msgs, first_kernel, bottle_kernel, second_kernel):
+    chans, height, span = feat.shape
     width = span + TILE
     full = height * chans
     groups = height // POOL
-
-    def bf(*shape):
-        return jax.ShapeDtypeStruct(shape, BF16)
-
-    def swapped(messages, axis):
-        pairs = [p for p in swaps(lax.axis_size(axis)) if p]
-        return [lax.ppermute(m, axis, p) for m, p in zip(messages, pairs)]
-
-    halo = bf(FHALO * chans, span)
-    feat_msgs = call(
-        feature_kernel, (halo, halo), [pltpu.VMEM((full, span), BF16)], 1, 8
-    )(features[0])
-    row_pairs = swaps(rows)
-    feat_a = lax.ppermute(feat_msgs[0], "rows", row_pairs[0])
-    packed = chans * (height * SLOT // TILE)
-    cot_rows, *messages = call(
-        column_kernel,
-        (bf(full, span),) + (bf(packed, TILE),) * (1 if cols == 2 else 2),
-        [],
-        2,
-        8,
-        flops=2 * 10**10,
-    )(features[0], cotangent[0])
-    col_msgs = swapped(messages, "cols")
     ncols = len(col_msgs)
+    packed = col_msgs[0].shape[0]
+
     halo = bf(CHALO * chans + ncols * packed * TILE // span, span)
     messages = call(edge_kernel, (halo, halo), [], 1 + ncols, 8)(cot_rows, *col_msgs)
-    messages, late = lax.optimization_barrier((messages, feat_msgs[1]))
     row_msgs = swapped(messages, "rows")
-    feat_b = lax.ppermute(late, "rows", row_pairs[1])
+    messages = call(
+        feature_kernel, (bf(size, span), bf(size, span)), [], 2, 16, smem_first=True
+    )(shifts, feat)
+    feat_msgs = swapped(messages, "rows")
 
     tall_c = (height + 2 * CHALO) * chans
     view = bf((height + 2) * chans, span)
@@ -632,7 +661,7 @@
         main_kernel,
         (jax.ShapeDtypeStruct((9 * chans // 2, TILE), F32), bf((height + 2) * chans, width)),
         [
-            pltpu.VMEM((chans, 3 * height, width), BF16),
+            pltpu.VMEM((2, size + 48, span), BF16),
             pltpu.VMEM((chans, tall, width), BF16),
         ]
         + [pltpu.VMEM((tall * chans, width), BF16)] * 3
@@ -647,7 +676,42 @@
         flops=10**10,
         smem_first=True,
     )(
-        shifts[0], features[0], feat_a, feat_b, sides, act_grad, *views, *weights[:2]
+        shifts, feat, *feat_msgs, sides, act_grad, *views, *weights[:2]
+    )
+
+    return grads, blended, weights[2]
+
+
+def shards(features, shifts, first_kernel, bottle_kernel, second_kernel, cotangent):
+    imgs, chans, height, span = features.shape
+    rows, cols, dp = (lax.axis_size(a) for a in ("rows", "cols", "dp"))
+    full = height * chans
+
+    packed = chans * (height * SLOT // TILE)
+    cot_rows, *messages = call(
+        column_kernel,
+        (bf(full, span),) + (bf(packed, TILE),) * (1 if cols == 2 else 2),
+        [],
+        2,
+        8,
+    )(features[0], cotangent[0])
+    col_msgs = swapped(messages, "cols")
+    ncols = len(col_msgs)
+    moves = shifts[0, :, 0]
+    total = jnp.maximum(jnp.sum(needed(moves, False)), jnp.sum(needed(moves, True)))
+    bit = 1
+    while bit < dp:
+        total = jnp.maximum(total, lax.ppermute(total, "dp", [(i, i ^ bit) for i in range(dp)]))
+        bit *= 2
+
+    def passes(size):
+        return functools.partial(both_passes, size)
+
+    grads, blended, second_bands = lax.cond(
+        total <= USUAL * chans,
+        passes(USUAL * chans),
+        passes(LARGEST * chans),
+        features[0], shifts[0], cot_rows, tuple(col_msgs), first_kernel, bottle_kernel, second_kernel,
     )
 
     steps = []
@@ -661,7 +725,7 @@
         other = lax.ppermute(grads, axis, pairs)
         if 1 <= step <= parts:
             prediction = predict(
-                blended, weights[2], (chans, height, span), parts, step - 1, prediction
+                blended, second_bands, (chans, height, span), parts, step - 1, prediction
             )
             other, prediction = lax.optimization_barrier((other, prediction))
         if step < len(steps) - 1:

time: 68 us -> 62.8 us (0.924)
  waiting for transfers between devices: 23.5 us -> 14.3 us
  Pallas kernels: 20 us -> 22.1 us
  between operations: 0.74 us -> 2.67 us
  local copies, waits for them, and re-layouts: 2.19 us -> 1.14 us
    ppermute x2 -> x1, waiting for transfers between devices: 12.4 us -> 0.29 us  [shards(): lax.ppermute(total, 'dp', [(i, i ^ bit) for i in range(dp)])]
    ppermute x3 -> x5, starting transfers between devices: 5.78 us -> 10.2 us  [swapped(): return [lax.ppermute(m, axis, p) for m, p in zip(messages, pairs)]]
    ppermute x2 -> x1, starting transfers between devices: 5.15 us -> 1.02 us  [shards(): lax.ppermute(total, 'dp', [(i, i ^ bit) for i in range(dp)])]
    ppermute x3 -> x5, waiting for transfers between devices: 2.54 us -> 4.55 us  [swapped(): return [lax.ppermute(m, axis, p) for m, p in zip(messages, pairs)]]
    pallas_call x1, Pallas kernels: 0.52 us -> 1.63 us  [shards(): call(column_kernel, (bf(full, span),) + (bf(packed, TILE),) * (1 if cols...]
    unnamed x14 -> x12, local copies, waits for them, and re-layouts: 2.1 us -> 1.06 us
    pallas_call x4, Pallas kernels: 15.3 us -> 16.3 us  [the longest x1 10.1 us: both_passes(): call(main_kernel, (jax.ShapeDtypeStruct((9 * chans // 2, TILE), F32), bf(...]
    ppermute x5, waiting for transfers between devices: 8.58 us -> 9.45 us  [shards(): other = lax.ppermute(grads, axis, pairs)]
  transfers between devices with their start and end apart: 10 -> 11, of which waited for: 8 -> 7; matrix products, arithmetic and copies ran while one was open for 0% -> 1% of each run, Pallas kernels for 12% -> 15%
where the time goes in v6:
time: 62.8 us; the launch traced here: 62.6 us
  Pallas kernels  22.1 us (35%)
  starting transfers between devices  21.4 us (34%)
  waiting for transfers between devices  14.3 us (23%)
  between operations  2.67 us (4%)
  local copies, waits for them, and re-layouts  1.14 us (2%)
  other arithmetic  0.68 us (1%)
    ppermute x5, starting transfers between devices, swapped(): return [lax.ppermute(m, axis, p) for m, p in zip(messages, pairs)]  10.2 us
    ppermute x5, starting transfers between devices, shards(): other = lax.ppermute(grads, axis, pairs)  10.1 us
    pallas_call x1, Pallas kernels, both_passes(): call(main_kernel, (jax.ShapeDtypeStruct((9 * chans // 2, TILE), F32), bf(...  10.1 us
    ppermute x5, waiting for transfers between devices, shards(): other = lax.ppermute(grads, axis, pairs)  9.45 us
    ppermute x5, waiting for transfers between devices, swapped(): return [lax.ppermute(m, axis, p) for m, p in zip(messages, pairs)]  4.55 us
    pallas_call x1, Pallas kernels, both_passes(): call(functools.partial(back_kernel, ncols), (jax.ShapeDtypeStruct((full,...  4.52 us
    pallas_call x2, Pallas kernels, predict(): call(functools.partial(predict_kernel, part), jax.ShapeDtypeStruct(shape,...  3.34 us
    pallas_call x1, Pallas kernels, both_passes(): call(feature_kernel, (bf(size, span), bf(size, span)), [], 2, 16, smem_fi...  1.63 us
  transfers between devices with their start and end apart: 11, of which 7 were waited for; matrix products, arithmetic and copies ran while one was open for 1% of the time, Pallas kernels for 15%

profile of v6, /device:TPU:0, one launch (start us, length us, event | category | flops | bytes accessed | tf_op | source)
XLA Modules:
  0.0 62.6 jit_solution(7051562877509888962)
XLA Ops:
  0.6 1.0 %copy-done = bf16[1,32,32,256]{3,2,1,0:T(8,128)(2,1)S(1)} copy-done((bf16[1,32,32,256]{3,2,1,0:T(8,128)(2,1)S(1)}, bf16[1,32,32,256]{3,2,1,0:T(8,128)(2,1)}, u32[]{:S(2)}) %copy-start) | copy-done | bytes 524312
  1.7 1.6 %shard_map.85 = (bf16[1024,256]{1,0:T(8,128)(2,1)S(1)}, bf16[256,128]{1,0:T(8,128)(2,1)S(1)}) custom-call(bf16[32,32,256]{2,1,0:T(8,128)(2,1)} %bitcast.5, bf16[32,32,256]{2,1,0:T(8,128)(2,1)S(1)} %bitcast.4), custom_call_target="tpu_custom_call" | custom-call | bytes 4194304 | tf_op jit(solution)/shard_map/pallas_call | solution.py:691
  3.3 3.0 %collective-permute-start.9 = (bf16[256,128]{1,0:T(8,128)(2,1)S(1)}, bf16[256,128]{1,0:T(8,128)(2,1)S(1)}, u32[]{:S(2)}, u32[]{:S(2)}) collective-permute-start(bf16[256,128]{1,0:T(8,128)(2,1)S(1)} %get-tuple-element.89), channel_id=1, source_target_pairs={{0,2},{2,0},{1,3},{3,1},{4,6},{6,4},{5,7},{7,5},{8,10},{10,8},{9,1... | collective-permute-start | bytes 196616 | tf_op jit(solution)/shard_map/ppermute | solution.py:614
  8.3 1.0 %collective-permute-start.8 = (s32[]{:T(128)}, s32[]{:T(128)}, u32[]{:S(2)}, u32[]{:S(2)}) collective-permute-start(s32[]{:T(128)} %max.16), channel_id=1, source_target_pairs={{0,1},{1,0},{2,3},{3,2},{4,5},{5,4},{6,7},{7,6},{8,9},{9,8},{10,11... | collective-permute-start | bytes 20 | tf_op jit(solution)/shard_map/ppermute | solution.py:704
  10.3 28.4 %conditional.1 = (f32[144,128]{1,0:T(8,128)S(1)}, bf16[1088,384]{1,0:T(8,128)(2,1)S(1)}, bf16[384,192]{1,0:T(8,128)(2,1)S(1)}) conditional(s32[]{:T(128)} %convert_element_type.3, (s32[32,2]{0,1:T(2,128)S(1)}, bf16[32,32,256]{2,1,0:T(8,128)(2,1)S(1)}, bf16[1024,256]{1,0:T(8,128)(2,1)S(1)}, bf16[256,128]{1,0:T(8,128)(2,1)S(1)}, ...), branch_computations={%region_2.0_spmd, %region_3.0_spmd} | conditional | flops 17999998976 | bytes 21365432 | solution.py:710
  10.4 1.6 %collective-permute-start.6 = (bf16[288,256]{1,0:T(8,128)(2,1)S(1)}, bf16[288,256]{1,0:T(8,128)(2,1)S(1)}, u32[]{:S(2)}, u32[]{:S(2)}) collective-permute-start(bf16[288,256]{1,0:T(8,128)(2,1)S(1)} %get-tuple-element.55), channel_id=1, source_target_pairs={{0,4},{4,0},{8,12},{12,8},{16,20},{20,16},{24,28},{28,24},{1,5},{5... | collective-permute-start | bytes 442376 | tf_op jit(solution)/shard_map/cond/branch_1_fun/ppermute | solution.py:614
  12.7 1.6 %branch_1_fun.4 = (bf16[448,256]{1,0:T(8,128)(2,1)S(1)}, bf16[448,256]{1,0:T(8,128)(2,1)S(1)}) custom-call(s32[32,2]{1,0:T(8,128)S(1)} %copy.11.shifts, bf16[32,32,256]{2,1,0:T(8,128)(2,1)S(1)} %get-tuple-element.50.feat), custom_call_target="tpu_custom_call" | custom-call | bytes 4194304 | tf_op jit(solution)/shard_map/cond/branch_1_fun/pallas_call | solution.py:628
  14.3 4.3 %collective-permute-start.4 = (bf16[448,256]{1,0:T(8,128)(2,1)S(1)}, bf16[448,256]{1,0:T(8,128)(2,1)S(1)}, u32[]{:S(2)}, u32[]{:S(2)}) collective-permute-start(bf16[448,256]{1,0:T(8,128)(2,1)S(1)} %get-tuple-element.51), channel_id=1, source_target_pairs={{0,4},{4,0},{8,12},{12,8},{16,20},{20,16},{24,28},{28,24},{1,5},{5... | collective-permute-start | bytes 688136 | tf_op jit(solution)/shard_map/cond/branch_1_fun/ppermute | solution.py:614
  18.7 0.7 %collective-permute-start.5 = (bf16[448,256]{1,0:T(8,128)(2,1)S(1)}, bf16[448,256]{1,0:T(8,128)(2,1)S(1)}, u32[]{:S(2)}, u32[]{:S(2)}) collective-permute-start(bf16[448,256]{1,0:T(8,128)(2,1)S(1)} %get-tuple-element.52), channel_id=1, source_target_pairs={{4,8},{12,16},{20,24},{8,4},{16,12},{24,20},{5,9},{13,17},{21,25},... | collective-permute-start | bytes 688136 | tf_op jit(solution)/shard_map/cond/branch_1_fun/ppermute | solution.py:614
  19.3 4.5 %branch_1_fun.6 = (f32[1024,256]{1,0:T(8,128)S(1)}, bf16[1088,256]{1,0:T(8,128)(2,1)S(1)}, bf16[1088,256]{1,0:T(8,128)(2,1)S(1)}, bf16[1088,256]{1,0:T(8,128)(2,...) custom-call(bf16[1024,256]{1,0:T(8,128)(2,1)S(1)} %get-tuple-element, ...), custom_call_target="tpu_custom_call" | custom-call | flops 8000000000 | bytes 4194304 | tf_op jit(solution)/shard_map/cond/branch_1_fun/pallas_call | solution.py:636
  23.9 4.5 %collective-permute-done.4.feat_a = bf16[448,256]{1,0:T(8,128)(2,1)S(1)} collective-permute-done((bf16[448,256]{1,0:T(8,128)(2,1)S(1)}, bf16[448,256]{1,0:T(8,128)(2,1)S(1)}, u32[]{:S(2)}, u32[]{:S(2)}) %collective-permute-start.4) | collective-permute-done | bytes 229408 | tf_op jit(solution)/shard_map/cond/branch_1_fun/ppermute | solution.py:614
  28.4 10.1 %branch_1_fun.7 = (f32[144,128]{1,0:T(8,128)S(1)}, bf16[1088,384]{1,0:T(8,128)(2,1)S(1)}) custom-call(s32[32,2]{1,0:T(8,128)S(1)} %copy.11.shifts, bf16[32,32,256]{2,1,0:T(8,128)(2,1)S(1)} %get-tuple-element.50.feat, bf16[448,256]{1,0:T(8,128)(2,1)S(1)} %collective-permute-done.4.feat_a, bf16[448,256]{1,0:T(8,128)(2,1)S(1)} %collective-permute-done.5.feat_b, ...), custom_call_target="tpu_custom_call" | custom-call | flops 10000000000 | bytes 4194304 | tf_op jit(solution)/shard_map/cond/branch_1_fun/pallas_call | solution.py:660
  38.8 1.3 %collective-permute-done.10 = f32[144,128]{1,0:T(8,128)S(1)} collective-permute-done((f32[144,128]{1,0:T(8,128)S(1)}, f32[144,128]{1,0:T(8,128)S(1)}, u32[]{:S(2)}, u32[]{:S(2)}) %collective-permute-start.10) | collective-permute-done | bytes 73760 | tf_op jit(solution)/shard_map/ppermute | solution.py:725
  40.1 0.7 %collective-permute-start.11 = (f32[144,128]{1,0:T(8,128)S(1)}, f32[144,128]{1,0:T(8,128)S(1)}, u32[]{:S(2)}, u32[]{:S(2)}) collective-permute-start(f32[144,128]{1,0:T(8,128)S(1)} %add.17), channel_id=1, source_target_pairs={{0,2},{2,0},{1,3},{3,1},{4,6},{6,4},{5,7},{7,5},{8,10},{10,8},{9,1... | collective-permute-start | bytes 221192 | tf_op jit(solution)/shard_map/ppermute | solution.py:725
  40.7 1.7 %shard_map.86.rest_0_ = bf16[32,32,256]{2,1,0:T(8,128)(2,1)} custom-call(bf16[1088,384]{1,0:T(8,128)(2,1)S(1)} %get-tuple-element.97.blended, bf16[384,192]{1,0:T(8,128)(2,1)S(1)} %get-tuple-element.94.bands), custom_call_target="tpu_custom_call" | custom-call | flops 1000000000 | bytes 4194304 | tf_op jit(solution)/shard_map/pallas_call | solution.py:592
  42.4 2.1 %collective-permute-done.11 = f32[144,128]{1,0:T(8,128)S(1)} collective-permute-done((f32[144,128]{1,0:T(8,128)S(1)}, f32[144,128]{1,0:T(8,128)S(1)}, u32[]{:S(2)}, u32[]{:S(2)}) %collective-permute-start.11) | collective-permute-done | bytes 73760 | tf_op jit(solution)/shard_map/ppermute | solution.py:725
  44.5 2.5 %collective-permute-start.12 = (f32[144,128]{1,0:T(8,128)S(1)}, f32[144,128]{1,0:T(8,128)S(1)}, u32[]{:S(2)}, u32[]{:S(2)}) collective-permute-start(f32[144,128]{1,0:T(8,128)S(1)} %add.18), channel_id=1, source_target_pairs={{0,4},{4,0},{8,12},{12,8},{16,20},{20,16},{24,28},{28,24},{1,5},{5... | collective-permute-start | bytes 221192 | tf_op jit(solution)/shard_map/ppermute | solution.py:725
  47.0 1.7 %shard_map.87 = bf16[32,32,256]{2,1,0:T(8,128)(2,1)} custom-call(bf16[1088,384]{1,0:T(8,128)(2,1)S(1)} %get-tuple-element.97.blended, bf16[384,192]{1,0:T(8,128)(2,1)S(1)} %get-tuple-element.94.bands, bf16[32,32,256]{2,1,0:T(8,128)(2,1)} %shard_map.86.rest_0_), custom_call_target="tpu_custom_call", output_to_operand_aliasing={{}: (2, {})} | custom-call | flops 1000000000 | bytes 4194304 | tf_op jit(solution)/shard_map/pallas_call | solution.py:592
  48.7 0.7 %collective-permute-done.12 = f32[144,128]{1,0:T(8,128)S(1)} collective-permute-done((f32[144,128]{1,0:T(8,128)S(1)}, f32[144,128]{1,0:T(8,128)S(1)}, u32[]{:S(2)}, u32[]{:S(2)}) %collective-permute-start.12) | collective-permute-done | bytes 73760 | tf_op jit(solution)/shard_map/ppermute | solution.py:725
  49.4 3.0 %collective-permute-start.13 = (f32[144,128]{1,0:T(8,128)S(1)}, f32[144,128]{1,0:T(8,128)S(1)}, u32[]{:S(2)}, u32[]{:S(2)}) collective-permute-start(f32[144,128]{1,0:T(8,128)S(1)} %add.19), channel_id=1, source_target_pairs={{0,8},{4,12},{8,0},{12,4},{16,24},{20,28},{24,16},{28,20},{1,9},{5... | collective-permute-start | bytes 221192 | tf_op jit(solution)/shard_map/ppermute | solution.py:725
  52.4 2.3 %collective-permute-done.13 = f32[144,128]{1,0:T(8,128)S(1)} collective-permute-done((f32[144,128]{1,0:T(8,128)S(1)}, f32[144,128]{1,0:T(8,128)S(1)}, u32[]{:S(2)}, u32[]{:S(2)}) %collective-permute-start.13) | collective-permute-done | bytes 73760 | tf_op jit(solution)/shard_map/ppermute | solution.py:725
  54.7 3.8 %collective-permute-start.14 = (f32[144,128]{1,0:T(8,128)S(1)}, f32[144,128]{1,0:T(8,128)S(1)}, u32[]{:S(2)}, u32[]{:S(2)}) collective-permute-start(f32[144,128]{1,0:T(8,128)S(1)} %add.20.mine), channel_id=1, source_target_pairs={{0,16},{4,20},{8,24},{12,28},{16,0},{20,4},{24,8},{28,12},{1,17},{... | collective-permute-start | bytes 221192 | tf_op jit(solution)/shard_map/ppermute | solution.py:725
  58.5 3.1 %collective-permute-done.14.other = f32[144,128]{1,0:T(8,128)S(1)} collective-permute-done((f32[144,128]{1,0:T(8,128)S(1)}, f32[144,128]{1,0:T(8,128)S(1)}, u32[]{:S(2)}, u32[]{:S(2)}) %collective-permute-start.14) | collective-permute-done | bytes 73760 | tf_op jit(solution)/shard_map/ppermute | solution.py:725
  61.7 0.9 %shard_map.88 = (f32[9,32,32]{2,1,0:T(8,128)}, f32[9,32,32]{2,1,0:T(8,128)}) custom-call(f32[144,128]{1,0:T(8,128)S(1)} %add.20.mine, f32[144,128]{1,0:T(8,128)S(1)} %collective-permute-done.14.other), custom_call_target="tpu_custom_call" | custom-call | bytes 4194304 | tf_op jit(solution)/shard_map/pallas_call | solution.py:737
  (25 shorter events, 1.9 us)
Async XLA Ops:
  0.6 1.0 %copy-start = (bf16[1,32,32,256]{3,2,1,0:T(8,128)(2,1)S(1)}, bf16[1,32,32,256]{3,2,1,0:T(8,128)(2,1)}, u32[]{:S(2)}) copy-start(bf16[1,32,32,256]{3,2,1,0:T(8,128)(2,1)} %param.13) | copy-start | bytes 1572868
  1.7 8.6 %copy-start.1 = (bf16[1,32,32,256]{3,2,1,0:T(8,128)(2,1)S(1)}, bf16[1,32,32,256]{3,2,1,0:T(8,128)(2,1)}, u32[]{:S(2)}) copy-start(bf16[1,32,32,256]{3,2,1,0:T(8,128)(2,1)} %param.8) | copy-start | bytes 1572868
  1.7 8.6 %copy-start.3 = (bf16[9,32,32]{2,1,0:T(8,128)(2,1)S(1)}, bf16[9,32,32]{2,1,0:T(8,128)(2,1)}, u32[]{:S(2)}) copy-start(bf16[9,32,32]{2,1,0:T(8,128)(2,1)} %param.10) | copy-start | bytes 55300
  1.7 8.6 %copy-start.4 = (bf16[9,32,32]{2,1,0:T(8,128)(2,1)S(1)}, bf16[9,32,32]{2,1,0:T(8,128)(2,1)}, u32[]{:S(2)}) copy-start(bf16[9,32,32]{2,1,0:T(8,128)(2,1)} %param.11) | copy-start | bytes 55300
  1.7 8.6 %copy-start.5 = (bf16[9,32,32]{2,1,0:T(8,128)(2,1)S(1)}, bf16[9,32,32]{2,1,0:T(8,128)(2,1)}, u32[]{:S(2)}) copy-start(bf16[9,32,32]{2,1,0:T(8,128)(2,1)} %param.12) | copy-start | bytes 55300
  3.3 3.0 %copy-start.2 = (s32[1,32,2]{1,2,0:T(2,128)S(1)}, s32[1,32,2]{1,2,0:T(2,128)}, u32[]{:S(2)}) copy-start(s32[1,32,2]{1,2,0:T(2,128)} %param.9) | copy-start | bytes 772
  3.3 6.9 %collective-permute-start.9 = (bf16[256,128]{1,0:T(8,128)(2,1)S(1)}, bf16[256,128]{1,0:T(8,128)(2,1)S(1)}, u32[]{:S(2)}, u32[]{:S(2)}) collective-permute-start(bf16[256,128]{1,0:T(8,128)(2,1)S(1)} %get-tuple-element.89), channel_id=1, source_target_pairs={{0,2},{2,0},{1,3},{3,1},{4,6},{6,4},{5,7},{7,5},{8,10},{10,8},{9,1... | collective-permute-start | bytes 196616 | tf_op jit(solution)/shard_map/ppermute | solution.py:614
  8.3 1.3 %collective-permute-start.8 = (s32[]{:T(128)}, s32[]{:T(128)}, u32[]{:S(2)}, u32[]{:S(2)}) collective-permute-start(s32[]{:T(128)} %max.16), channel_id=1, source_target_pairs={{0,1},{1,0},{2,3},{3,2},{4,5},{5,4},{6,7},{7,6},{8,9},{9,8},{10,11... | collective-permute-start | bytes 20 | tf_op jit(solution)/shard_map/ppermute | solution.py:704
  10.4 9.0 %collective-permute-start.6 = (bf16[288,256]{1,0:T(8,128)(2,1)S(1)}, bf16[288,256]{1,0:T(8,128)(2,1)S(1)}, u32[]{:S(2)}, u32[]{:S(2)}) collective-permute-start(bf16[288,256]{1,0:T(8,128)(2,1)S(1)} %get-tuple-element.55), channel_id=1, source_target_pairs={{0,4},{4,0},{8,12},{12,8},{16,20},{20,16},{24,28},{28,24},{1,5},{5... | collective-permute-start | bytes 442376 | tf_op jit(solution)/shard_map/cond/branch_1_fun/ppermute | solution.py:614
  11.9 7.4 %collective-permute-start.7 = (bf16[288,256]{1,0:T(8,128)(2,1)S(1)}, bf16[288,256]{1,0:T(8,128)(2,1)S(1)}, u32[]{:S(2)}, u32[]{:S(2)}) collective-permute-start(bf16[288,256]{1,0:T(8,128)(2,1)S(1)} %get-tuple-element.56), channel_id=1, source_target_pairs={{4,8},{12,16},{20,24},{8,4},{16,12},{24,20},{5,9},{13,17},{21,25},... | collective-permute-start | bytes 442376 | tf_op jit(solution)/shard_map/cond/branch_1_fun/ppermute | solution.py:614
  14.3 14.1 %collective-permute-start.4 = (bf16[448,256]{1,0:T(8,128)(2,1)S(1)}, bf16[448,256]{1,0:T(8,128)(2,1)S(1)}, u32[]{:S(2)}, u32[]{:S(2)}) collective-permute-start(bf16[448,256]{1,0:T(8,128)(2,1)S(1)} %get-tuple-element.51), channel_id=1, source_target_pairs={{0,4},{4,0},{8,12},{12,8},{16,20},{20,16},{24,28},{28,24},{1,5},{5... | collective-permute-start | bytes 688136 | tf_op jit(solution)/shard_map/cond/branch_1_fun/ppermute | solution.py:614
  18.7 9.8 %collective-permute-start.5 = (bf16[448,256]{1,0:T(8,128)(2,1)S(1)}, bf16[448,256]{1,0:T(8,128)(2,1)S(1)}, u32[]{:S(2)}, u32[]{:S(2)}) collective-permute-start(bf16[448,256]{1,0:T(8,128)(2,1)S(1)} %get-tuple-element.52), channel_id=1, source_target_pairs={{4,8},{12,16},{20,24},{8,4},{16,12},{24,20},{5,9},{13,17},{21,25},... | collective-permute-start | bytes 688136 | tf_op jit(solution)/shard_map/cond/branch_1_fun/ppermute | solution.py:614
  38.7 1.3 %collective-permute-start.10 = (f32[144,128]{1,0:T(8,128)S(1)}, f32[144,128]{1,0:T(8,128)S(1)}, u32[]{:S(2)}, u32[]{:S(2)}) collective-permute-start(f32[144,128]{1,0:T(8,128)S(1)} %get-tuple-element.90), channel_id=1, source_target_pairs={{0,1},{1,0},{2,3},{3,2},{4,5},{5,4},{6,7},{7,6},{8,9},{9,8},{10,11... | collective-permute-start | bytes 221192 | tf_op jit(solution)/shard_map/ppermute | solution.py:725
  40.1 4.4 %collective-permute-start.11 = (f32[144,128]{1,0:T(8,128)S(1)}, f32[144,128]{1,0:T(8,128)S(1)}, u32[]{:S(2)}, u32[]{:S(2)}) collective-permute-start(f32[144,128]{1,0:T(8,128)S(1)} %add.17), channel_id=1, source_target_pairs={{0,2},{2,0},{1,3},{3,1},{4,6},{6,4},{5,7},{7,5},{8,10},{10,8},{9,1... | collective-permute-start | bytes 221192 | tf_op jit(solution)/shard_map/ppermute | solution.py:725
  44.5 4.9 %collective-permute-start.12 = (f32[144,128]{1,0:T(8,128)S(1)}, f32[144,128]{1,0:T(8,128)S(1)}, u32[]{:S(2)}, u32[]{:S(2)}) collective-permute-start(f32[144,128]{1,0:T(8,128)S(1)} %add.18), channel_id=1, source_target_pairs={{0,4},{4,0},{8,12},{12,8},{16,20},{20,16},{24,28},{28,24},{1,5},{5... | collective-permute-start | bytes 221192 | tf_op jit(solution)/shard_map/ppermute | solution.py:725
  49.4 5.3 %collective-permute-start.13 = (f32[144,128]{1,0:T(8,128)S(1)}, f32[144,128]{1,0:T(8,128)S(1)}, u32[]{:S(2)}, u32[]{:S(2)}) collective-permute-start(f32[144,128]{1,0:T(8,128)S(1)} %add.19), channel_id=1, source_target_pairs={{0,8},{4,12},{8,0},{12,4},{16,24},{20,28},{24,16},{28,20},{1,9},{5... | collective-permute-start | bytes 221192 | tf_op jit(solution)/shard_map/ppermute | solution.py:725
  54.7 7.0 %collective-permute-start.14 = (f32[144,128]{1,0:T(8,128)S(1)}, f32[144,128]{1,0:T(8,128)S(1)}, u32[]{:S(2)}, u32[]{:S(2)}) collective-permute-start(f32[144,128]{1,0:T(8,128)S(1)} %add.20.mine), channel_id=1, source_target_pairs={{0,16},{4,20},{8,24},{12,28},{16,0},{20,4},{24,8},{28,12},{1,17},{... | collective-permute-start | bytes 221192 | tf_op jit(solution)/shard_map/ppermute | solution.py:725

commit v7 on v6

--- a/solution.py
+++ b/solution.py
@@ -106,11 +106,22 @@
             msg[p : p + chunk] = jnp.dot(pick, source, preferred_element_type=F32).astype(BF16)
 
 
-def column_kernel(feat, cot, cot_rows, *col_msgs):
+def rows_kernel(source, out):
+    for part in tiles_of(source.shape[2]):
+        out[:, part] = to_rows(source[:, :, part])
+
+
+def count_kernel(shifts, out):
+    down = up = jnp.int32(0)
+    for c in range(shifts.shape[0]):
+        up = up + needed(shifts[c, 0], False)
+        down = down + needed(shifts[c, 0], True)
+    out[...] = jnp.full(out.shape, jnp.maximum(up, down), jnp.int32)
+
+
+def column_kernel(feat, cot, *col_msgs):
     chans, height, span = feat.shape
     first, last = tiles_of(span)[0], tiles_of(span)[-1]
-    for part in tiles_of(span):
-        cot_rows[:, part] = to_rows(cot[:, :, part])
     count = TILE // SLOT
     block = height // count
     lane = lanes_of((chans, block, TILE))
@@ -349,19 +360,20 @@
 
 
 def correlate(u, u0, views, v0, acc, height, chans, span):
-    acc[...] = jnp.zeros(acc.shape, F32)
-
-    def group(g, _):
-        left = jnp.concatenate(
-            [view[rows_at(v0 + g * POOL, chans, POOL + 2), 0:span] for view in views], axis=0
-        )
-        right = u[rows_at(u0 + g * POOL, chans, POOL), 0:span]
-        acc[...] += lax.dot_general(
-            left, right, (((1,), (1,)), ((), ())), preferred_element_type=F32
-        )
-        return 0
-
-    lax.fori_loop(0, height // POOL, group, 0, unroll=2)
+    groups = range(0, height, POOL)
+    left = jnp.concatenate(
+        [
+            jnp.concatenate(
+                [view[rows_at(v0 + g, chans, POOL + 2), 0:span] for view in views], axis=0
+            )
+            for g in groups
+        ],
+        axis=1,
+    )
+    right = jnp.concatenate([u[rows_at(u0 + g, chans, POOL), 0:span] for g in groups], axis=1)
+    acc[...] = lax.dot_general(
+        left, right, (((1,), (1,)), ((), ())), preferred_element_type=F32
+    )
 
 
 def folded(acc, chans):
@@ -449,7 +461,7 @@
             moved[c, :, part] = result.astype(BF16)
         return at_up + n_up, at_down + n_down
 
-    lax.fori_loop(0, chans, warp, (jnp.int32(0), jnp.int32(0)), unroll=4)
+    lax.fori_loop(0, chans, warp, (jnp.int32(0), jnp.int32(0)), unroll=8)
     chunk = 16
     for r in range(0, tall, chunk):
         for part in tiles_of(width):
@@ -488,7 +500,7 @@
 
     for g in (0, 1, groups + 2, groups + 3):
         first_group(g, False)
-    lax.fori_loop(2, groups + 2, lambda g, _: first_group(g, True), 0, unroll=2)
+    lax.fori_loop(2, groups + 2, lambda g, _: first_group(g, True), 0, unroll=4)
     sums = block_sums(high, low, block_ones(width))
     for g in range(groups + 4):
         at = rows_at(g, chans)
@@ -614,7 +626,14 @@
     return [lax.ppermute(m, axis, p) for m, p in zip(messages, pairs)]
 
 
-def both_passes(size, feat, shifts, cot_rows, col_msgs, first_kernel, bottle_kernel, second_kernel):
+def pack_rows(size, shifts, feat):
+    message = bf(size, feat.shape[2])
+    return call(
+        feature_kernel, (message, message), [], 2, 16, flops=10**9, smem_first=True
+    )(shifts, feat)
+
+
+def both_passes(size, usual, feat, shifts, cot_rows, col_msgs, first_kernel, bottle_kernel, second_kernel):
     chans, height, span = feat.shape
     width = span + TILE
     full = height * chans
@@ -625,10 +644,9 @@
     halo = bf(CHALO * chans + ncols * packed * TILE // span, span)
     messages = call(edge_kernel, (halo, halo), [], 1 + ncols, 8)(cot_rows, *col_msgs)
     row_msgs = swapped(messages, "rows")
-    messages = call(
-        feature_kernel, (bf(size, span), bf(size, span)), [], 2, 16, smem_first=True
-    )(shifts, feat)
-    feat_msgs = swapped(messages, "rows")
+    if usual[0].shape[0] != size:
+        usual = pack_rows(size, shifts, feat)
+    feat_msgs = swapped(usual, "rows")
 
     tall_c = (height + 2 * CHALO) * chans
     view = bf((height + 2) * chans, span)
@@ -688,30 +706,30 @@
     full = height * chans
 
     packed = chans * (height * SLOT // TILE)
-    cot_rows, *messages = call(
-        column_kernel,
-        (bf(full, span),) + (bf(packed, TILE),) * (1 if cols == 2 else 2),
-        [],
-        2,
-        8,
-    )(features[0], cotangent[0])
-    col_msgs = swapped(messages, "cols")
-    ncols = len(col_msgs)
-    moves = shifts[0, :, 0]
-    total = jnp.maximum(jnp.sum(needed(moves, False)), jnp.sum(needed(moves, True)))
+    shifts = shifts[0]
+    total = call(
+        count_kernel, jax.ShapeDtypeStruct((8, TILE), jnp.int32), [], 1, 2, smem_first=True
+    )(shifts)
     bit = 1
     while bit < dp:
         total = jnp.maximum(total, lax.ppermute(total, "dp", [(i, i ^ bit) for i in range(dp)]))
         bit *= 2
+    messages = call(
+        column_kernel, (bf(packed, TILE),) * (1 if cols == 2 else 2), [], 2, 8, flops=10**9
+    )(features[0], cotangent[0])
+    col_msgs = swapped(messages, "cols")
+    ncols = len(col_msgs)
+    usual = pack_rows(USUAL * chans, shifts, features[0])
+    cot_rows = call(rows_kernel, bf(full, span), [], 1, 4, flops=10**9)(cotangent[0])
 
     def passes(size):
         return functools.partial(both_passes, size)
 
     grads, blended, second_bands = lax.cond(
-        total <= USUAL * chans,
+        total[0, 0] <= USUAL * chans,
         passes(USUAL * chans),
         passes(LARGEST * chans),
-        features[0], shifts[0], cot_rows, tuple(col_msgs), first_kernel, bottle_kernel, second_kernel,
+        usual, features[0], shifts, cot_rows, tuple(col_msgs), first_kernel, bottle_kernel, second_kernel,
     )
 
     steps = []

time: 62.8 us -> 59.9 us (0.954)
  waiting for transfers between devices: 14.3 us -> 11.3 us
  local copies, waits for them, and re-layouts: 1.14 us -> 2.43 us
  between operations: 2.67 us -> 1.43 us
  Pallas kernels: 22.1 us -> 23 us
  other arithmetic: 0.68 us -> 0.05 us
    ppermute x5, waiting for transfers between devices: 9.45 us -> 6.56 us  [shards(): other = lax.ppermute(grads, axis, pairs)]
    pallas_call x2, Pallas kernels: 3.34 us -> 5.64 us  [predict(): call(functools.partial(predict_kernel, part), jax.ShapeDtypeStruct(shape,...]
    pallas_call x1, Pallas kernels: 10.1 us -> 7.83 us  [both_passes(): call(main_kernel, (jax.ShapeDtypeStruct((9 * chans // 2, TILE), F32), bf(...]
    ppermute x5, starting transfers between devices: 10.2 us -> 11.5 us  [swapped(): return [lax.ppermute(m, axis, p) for m, p in zip(messages, pairs)]]
    pallas_call x2 -> x4, Pallas kernels: 3.27 us -> 4.09 us  [the longest x1 1.64 us: pack_rows(): call(feature_kernel, (message, message), [], 2, 16, flops=10 ** 9, smem_f...]
    ppermute x5, starting transfers between devices: 10.1 us -> 9.36 us  [shards(): other = lax.ppermute(grads, axis, pairs)]
    unnamed x12 -> x14, local copies, waits for them, and re-layouts: 1.06 us -> 1.74 us
    reduce_sum x1 -> x0, other arithmetic: 0.64 us -> none  [shards(): jnp.sum(needed(moves, True))]
  transfers between devices with their start and end apart: 11 -> 11, of which waited for: 7 -> 5; matrix products, arithmetic and copies ran while one was open for 1% -> 1% of each run, Pallas kernels for 15% -> 22%
where the time goes in v7:
time: 59.9 us; the launch traced here: 59.6 us
  Pallas kernels  23 us (38%)
  starting transfers between devices  21.3 us (36%)
  waiting for transfers between devices  11.3 us (19%)
  local copies, waits for them, and re-layouts  2.43 us (4%)
  between operations  1.43 us (2%)
    ppermute x5, starting transfers between devices, swapped(): return [lax.ppermute(m, axis, p) for m, p in zip(messages, pairs)]  11.5 us
    ppermute x5, starting transfers between devices, shards(): other = lax.ppermute(grads, axis, pairs)  9.36 us
    pallas_call x1, Pallas kernels, both_passes(): call(main_kernel, (jax.ShapeDtypeStruct((9 * chans // 2, TILE), F32), bf(...  7.83 us
    ppermute x5, waiting for transfers between devices, shards(): other = lax.ppermute(grads, axis, pairs)  6.56 us
    pallas_call x2, Pallas kernels, predict(): call(functools.partial(predict_kernel, part), jax.ShapeDtypeStruct(shape,...  5.64 us
    ppermute x5, waiting for transfers between devices, swapped(): return [lax.ppermute(m, axis, p) for m, p in zip(messages, pairs)]  4.7 us
    pallas_call x1, Pallas kernels, both_passes(): call(functools.partial(back_kernel, ncols), (jax.ShapeDtypeStruct((full,...  4.52 us
    unnamed x14, local copies, waits for them, and re-layouts  1.74 us
  transfers between devices with their start and end apart: 11, of which 5 were waited for; matrix products, arithmetic and copies ran while one was open for 1% of the time, Pallas kernels for 22%

profile of v7, /device:TPU:0, one launch (start us, length us, event | category | flops | bytes accessed | tf_op | source)
XLA Modules:
  0.0 59.6 jit_solution(8096041818875087954)
XLA Ops:
  0.6 0.7 %copy-done.2 = s32[1,32,2]{1,2,0:T(2,128)S(1)} copy-done((s32[1,32,2]{1,2,0:T(2,128)S(1)}, s32[1,32,2]{1,2,0:T(2,128)}, u32[]{:S(2)}) %copy-start.2) | copy-done | bytes 280
  1.4 0.9 %shard_map.85 = s32[8,128]{1,0:T(8,128)S(1)} custom-call(s32[32,2]{1,0:T(8,128)S(1)} %copy.10.shifts), custom_call_target="tpu_custom_call" | custom-call | bytes 4194304 | tf_op jit(solution)/shard_map/pallas_call | solution.py:710
  2.8 1.0 %copy-done = bf16[1,32,32,256]{3,2,1,0:T(8,128)(2,1)S(1)} copy-done((bf16[1,32,32,256]{3,2,1,0:T(8,128)(2,1)S(1)}, bf16[1,32,32,256]{3,2,1,0:T(8,128)(2,1)}, u32[]{:S(2)}) %copy-start) | copy-done | bytes 524312
  3.9 1.4 %shard_map.87 = bf16[256,128]{1,0:T(8,128)(2,1)S(1)} custom-call(bf16[32,32,256]{2,1,0:T(8,128)(2,1)} %bitcast.10, bf16[32,32,256]{2,1,0:T(8,128)(2,1)S(1)} %bitcast.5), custom_call_target="tpu_custom_call" | custom-call | flops 1000000000 | bytes 4194304 | tf_op jit(solution)/shard_map/pallas_call | solution.py:717
  5.3 2.6 %collective-permute-start.9 = (bf16[256,128]{1,0:T(8,128)(2,1)S(1)}, bf16[256,128]{1,0:T(8,128)(2,1)S(1)}, u32[]{:S(2)}, u32[]{:S(2)}) collective-permute-start(bf16[256,128]{1,0:T(8,128)(2,1)S(1)} %shard_map.87), channel_id=1, source_target_pairs={{0,2},{2,0},{1,3},{3,1},{4,6},{6,4},{5,7},{7,5},{8,10},{10,8},{9,1... | collective-permute-start | bytes 196616 | tf_op jit(solution)/shard_map/ppermute | solution.py:626
  7.8 1.6 %shard_map.88 = (bf16[448,256]{1,0:T(8,128)(2,1)S(1)}, bf16[448,256]{1,0:T(8,128)(2,1)S(1)}) custom-call(s32[32,2]{1,0:T(8,128)S(1)} %copy.10.shifts, bf16[32,32,256]{2,1,0:T(8,128)(2,1)S(1)} %bitcast.11), custom_call_target="tpu_custom_call" | custom-call | flops 1000000000 | bytes 4194304 | tf_op jit(solution)/shard_map/pallas_call | solution.py:631
  10.9 26.1 %conditional.1 = (f32[144,128]{1,0:T(8,128)S(1)}, bf16[1088,384]{1,0:T(8,128)(2,1)}, bf16[384,192]{1,0:T(8,128)(2,1)S(1)}) conditional(s32[]{:T(128)} %bitcast.1, (s32[32,2]{0,1:T(2,128)S(1)}, bf16[32,32,256]{2,1,0:T(8,128)(2,1)S(1)}, bf16[1024,256]{1,0:T(8,128)(2,1)S(1)}, bf16[256,128]{1,0:T(8,128)(2,1)S(1)}, bf16[9,32,32]{2,1,0:T(8,128)(2,1)S(1)}, ...), branch_computations={%region_0.0_spmd, %region_1.0_spmd} | conditional | flops 19000000512 | bytes 21365432 | solution.py:728
  11.0 1.6 %collective-permute-start.6 = (bf16[288,256]{1,0:T(8,128)(2,1)S(1)}, bf16[288,256]{1,0:T(8,128)(2,1)S(1)}, u32[]{:S(2)}, u32[]{:S(2)}) collective-permute-start(bf16[288,256]{1,0:T(8,128)(2,1)S(1)} %get-tuple-element.59), channel_id=1, source_target_pairs={{0,4},{4,0},{8,12},{12,8},{16,20},{20,16},{24,28},{28,24},{1,5},{5... | collective-permute-start | bytes 442376 | tf_op jit(solution)/shard_map/cond/branch_1_fun/ppermute | solution.py:626
  12.6 0.7 %collective-permute-start.7 = (bf16[288,256]{1,0:T(8,128)(2,1)S(1)}, bf16[288,256]{1,0:T(8,128)(2,1)S(1)}, u32[]{:S(2)}, u32[]{:S(2)}) collective-permute-start(bf16[288,256]{1,0:T(8,128)(2,1)S(1)} %get-tuple-element.60), channel_id=1, source_target_pairs={{4,8},{12,16},{20,24},{8,4},{16,12},{24,20},{5,9},{13,17},{21,25},... | collective-permute-start | bytes 442376 | tf_op jit(solution)/shard_map/cond/branch_1_fun/ppermute | solution.py:626
  13.3 0.7 %collective-permute-start.5 = (bf16[448,256]{1,0:T(8,128)(2,1)S(1)}, bf16[448,256]{1,0:T(8,128)(2,1)S(1)}, u32[]{:S(2)}, u32[]{:S(2)}) collective-permute-start(bf16[448,256]{1,0:T(8,128)(2,1)S(1)} %get-tuple-element.56), channel_id=1, source_target_pairs={{4,8},{12,16},{20,24},{8,4},{16,12},{24,20},{5,9},{13,17},{21,25},... | collective-permute-start | bytes 688136 | tf_op jit(solution)/shard_map/cond/branch_1_fun/ppermute | solution.py:626
  13.9 6.0 %collective-permute-start.4 = (bf16[448,256]{1,0:T(8,128)(2,1)S(1)}, bf16[448,256]{1,0:T(8,128)(2,1)S(1)}, u32[]{:S(2)}, u32[]{:S(2)}) collective-permute-start(bf16[448,256]{1,0:T(8,128)(2,1)S(1)} %get-tuple-element.55), channel_id=1, source_target_pairs={{0,4},{4,0},{8,12},{12,8},{16,20},{20,16},{24,28},{28,24},{1,5},{5... | collective-permute-start | bytes 688136 | tf_op jit(solution)/shard_map/cond/branch_1_fun/ppermute | solution.py:626
  20.0 4.5 %branch_1_fun.4 = (f32[1024,256]{1,0:T(8,128)S(1)}, bf16[1088,256]{1,0:T(8,128)(2,1)S(1)}, bf16[1088,256]{1,0:T(8,128)(2,1)S(1)}, bf16[1088,256]{1,0:T(8,128)(2,...) custom-call(bf16[1024,256]{1,0:T(8,128)(2,1)S(1)} %get-tuple-element, ...), custom_call_target="tpu_custom_call" | custom-call | flops 8000000000 | bytes 4194304 | tf_op jit(solution)/shard_map/cond/branch_1_fun/pallas_call | solution.py:654
  24.5 4.7 %collective-permute-done.4.feat_a = bf16[448,256]{1,0:T(8,128)(2,1)S(1)} collective-permute-done((bf16[448,256]{1,0:T(8,128)(2,1)S(1)}, bf16[448,256]{1,0:T(8,128)(2,1)S(1)}, u32[]{:S(2)}, u32[]{:S(2)}) %collective-permute-start.4) | collective-permute-done | bytes 229408 | tf_op jit(solution)/shard_map/cond/branch_1_fun/ppermute | solution.py:626
  29.2 7.8 %branch_1_fun.5 = (f32[144,128]{1,0:T(8,128)S(1)}, bf16[1088,384]{1,0:T(8,128)(2,1)}) custom-call(s32[32,2]{1,0:T(8,128)S(1)} %copy.13.shifts, bf16[32,32,256]{2,1,0:T(8,128)(2,1)S(1)} %get-tuple-element.54.feat, bf16[448,256]{1,0:T(8,128)(2,1)S(1)} %collective-permute-done.4.feat_a, bf16[448,256]{1,0:T(8,128)(2,1)S(1)} %collective-permute-done.5.feat_b, ...), custom_call_target="tpu_custom_call" | custom-call | flops 10000000000 | bytes 4194304 | tf_op jit(solution)/shard_map/cond/branch_1_fun/pallas_call | solution.py:678
  37.1 1.3 %collective-permute-done.10 = f32[144,128]{1,0:T(8,128)S(1)} collective-permute-done((f32[144,128]{1,0:T(8,128)S(1)}, f32[144,128]{1,0:T(8,128)S(1)}, u32[]{:S(2)}, u32[]{:S(2)}) %collective-permute-start.10) | collective-permute-done | bytes 73760 | tf_op jit(solution)/shard_map/ppermute | solution.py:743
  38.3 1.0 %collective-permute-start.11 = (f32[144,128]{1,0:T(8,128)S(1)}, f32[144,128]{1,0:T(8,128)S(1)}, u32[]{:S(2)}, u32[]{:S(2)}) collective-permute-start(f32[144,128]{1,0:T(8,128)S(1)} %add.12), channel_id=1, source_target_pairs={{0,2},{2,0},{1,3},{3,1},{4,6},{6,4},{5,7},{7,5},{8,10},{10,8},{9,1... | collective-permute-start | bytes 221192 | tf_op jit(solution)/shard_map/ppermute | solution.py:743
  39.3 2.8 %shard_map.89.rest_0_ = bf16[32,32,256]{2,1,0:T(8,128)(2,1)} custom-call(bf16[1088,384]{1,0:T(8,128)(2,1)} %get-tuple-element.101.blended, bf16[384,192]{1,0:T(8,128)(2,1)S(1)} %get-tuple-element.98.bands), custom_call_target="tpu_custom_call" | custom-call | flops 1000000000 | bytes 4194304 | tf_op jit(solution)/shard_map/pallas_call | solution.py:604
  42.8 2.5 %collective-permute-start.12 = (f32[144,128]{1,0:T(8,128)S(1)}, f32[144,128]{1,0:T(8,128)S(1)}, u32[]{:S(2)}, u32[]{:S(2)}) collective-permute-start(f32[144,128]{1,0:T(8,128)S(1)} %add.13), channel_id=1, source_target_pairs={{0,4},{4,0},{8,12},{12,8},{16,20},{20,16},{24,28},{28,24},{1,5},{5... | collective-permute-start | bytes 221192 | tf_op jit(solution)/shard_map/ppermute | solution.py:743
  45.3 2.8 %shard_map.90 = bf16[32,32,256]{2,1,0:T(8,128)(2,1)} custom-call(bf16[1088,384]{1,0:T(8,128)(2,1)} %get-tuple-element.101.blended, bf16[384,192]{1,0:T(8,128)(2,1)S(1)} %get-tuple-element.98.bands, bf16[32,32,256]{2,1,0:T(8,128)(2,1)} %shard_map.89.rest_0_), custom_call_target="tpu_custom_call", output_to_operand_aliasing={{}: (2, {})} | custom-call | flops 1000000000 | bytes 4194304 | tf_op jit(solution)/shard_map/pallas_call | solution.py:604
  48.1 2.4 %collective-permute-start.13 = (f32[144,128]{1,0:T(8,128)S(1)}, f32[144,128]{1,0:T(8,128)S(1)}, u32[]{:S(2)}, u32[]{:S(2)}) collective-permute-start(f32[144,128]{1,0:T(8,128)S(1)} %add.14), channel_id=1, source_target_pairs={{0,8},{4,12},{8,0},{12,4},{16,24},{20,28},{24,16},{28,20},{1,9},{5... | collective-permute-start | bytes 221192 | tf_op jit(solution)/shard_map/ppermute | solution.py:743
  50.5 2.3 %collective-permute-done.13 = f32[144,128]{1,0:T(8,128)S(1)} collective-permute-done((f32[144,128]{1,0:T(8,128)S(1)}, f32[144,128]{1,0:T(8,128)S(1)}, u32[]{:S(2)}, u32[]{:S(2)}) %collective-permute-start.13) | collective-permute-done | bytes 73760 | tf_op jit(solution)/shard_map/ppermute | solution.py:743
  52.8 3.5 %collective-permute-start.14 = (f32[144,128]{1,0:T(8,128)S(1)}, f32[144,128]{1,0:T(8,128)S(1)}, u32[]{:S(2)}, u32[]{:S(2)}) collective-permute-start(f32[144,128]{1,0:T(8,128)S(1)} %add.15.mine), channel_id=1, source_target_pairs={{0,16},{4,20},{8,24},{12,28},{16,0},{20,4},{24,8},{28,12},{1,17},{... | collective-permute-start | bytes 221192 | tf_op jit(solution)/shard_map/ppermute | solution.py:743
  56.3 2.3 %collective-permute-done.14.other = f32[144,128]{1,0:T(8,128)S(1)} collective-permute-done((f32[144,128]{1,0:T(8,128)S(1)}, f32[144,128]{1,0:T(8,128)S(1)}, u32[]{:S(2)}, u32[]{:S(2)}) %collective-permute-start.14) | collective-permute-done | bytes 73760 | tf_op jit(solution)/shard_map/ppermute | solution.py:743
  58.7 0.9 %shard_map.91 = (f32[9,32,32]{2,1,0:T(8,128)}, f32[9,32,32]{2,1,0:T(8,128)}) custom-call(f32[144,128]{1,0:T(8,128)S(1)} %add.15.mine, f32[144,128]{1,0:T(8,128)S(1)} %collective-permute-done.14.other), custom_call_target="tpu_custom_call" | custom-call | bytes 4194304 | tf_op jit(solution)/shard_map/pallas_call | solution.py:755
  (31 shorter events, 2.1 us)
Async XLA Ops:
  0.6 0.7 %copy-start.2 = (s32[1,32,2]{1,2,0:T(2,128)S(1)}, s32[1,32,2]{1,2,0:T(2,128)}, u32[]{:S(2)}) copy-start(s32[1,32,2]{1,2,0:T(2,128)} %param.9) | copy-start | bytes 772
  2.3 7.4 %collective-permute-start.8 = (s32[8,128]{1,0:T(8,128)S(1)}, s32[8,128]{1,0:T(8,128)S(1)}, u32[]{:S(2)}, u32[]{:S(2)}) collective-permute-start(s32[8,128]{1,0:T(8,128)S(1)} %shard_map.85), channel_id=1, source_target_pairs={{0,1},{1,0},{2,3},{3,2},{4,5},{5,4},{6,7},{7,6},{8,9},{9,8},{10,11... | collective-permute-start | bytes 12296 | tf_op jit(solution)/shard_map/ppermute | solution.py:715
  2.8 1.0 %copy-start = (bf16[1,32,32,256]{3,2,1,0:T(8,128)(2,1)S(1)}, bf16[1,32,32,256]{3,2,1,0:T(8,128)(2,1)}, u32[]{:S(2)}) copy-start(bf16[1,32,32,256]{3,2,1,0:T(8,128)(2,1)} %param.13) | copy-start | bytes 1572868
  3.8 4.0 %copy-start.3 = (bf16[1,32,32,256]{3,2,1,0:T(8,128)(2,1)S(1)}, bf16[1,32,32,256]{3,2,1,0:T(8,128)(2,1)}, u32[]{:S(2)}) copy-start(bf16[1,32,32,256]{3,2,1,0:T(8,128)(2,1)} %param.8) | copy-start | bytes 1572868
  5.3 4.2 %copy-start.1 = (bf16[1,32,32,256]{3,2,1,0:T(8,128)(2,1)S(1)}, bf16[1,32,32,256]{3,2,1,0:T(8,128)(2,1)}, u32[]{:S(2)}) copy-start(bf16[1,32,32,256]{3,2,1,0:T(8,128)(2,1)} %param.13) | copy-start | bytes 1572868
  5.3 5.6 %collective-permute-start.9 = (bf16[256,128]{1,0:T(8,128)(2,1)S(1)}, bf16[256,128]{1,0:T(8,128)(2,1)S(1)}, u32[]{:S(2)}, u32[]{:S(2)}) collective-permute-start(bf16[256,128]{1,0:T(8,128)(2,1)S(1)} %shard_map.87), channel_id=1, source_target_pairs={{0,2},{2,0},{1,3},{3,1},{4,6},{6,4},{5,7},{7,5},{8,10},{10,8},{9,1... | collective-permute-start | bytes 196616 | tf_op jit(solution)/shard_map/ppermute | solution.py:626
  9.5 1.4 %copy-start.4 = (bf16[9,32,32]{2,1,0:T(8,128)(2,1)S(1)}, bf16[9,32,32]{2,1,0:T(8,128)(2,1)}, u32[]{:S(2)}) copy-start(bf16[9,32,32]{2,1,0:T(8,128)(2,1)} %param.10) | copy-start | bytes 55300
  9.5 1.4 %copy-start.5 = (bf16[9,32,32]{2,1,0:T(8,128)(2,1)S(1)}, bf16[9,32,32]{2,1,0:T(8,128)(2,1)}, u32[]{:S(2)}) copy-start(bf16[9,32,32]{2,1,0:T(8,128)(2,1)} %param.11) | copy-start | bytes 55300
  9.5 1.4 %copy-start.6 = (bf16[9,32,32]{2,1,0:T(8,128)(2,1)S(1)}, bf16[9,32,32]{2,1,0:T(8,128)(2,1)}, u32[]{:S(2)}) copy-start(bf16[9,32,32]{2,1,0:T(8,128)(2,1)} %param.12) | copy-start | bytes 55300
  11.0 9.0 %collective-permute-start.6 = (bf16[288,256]{1,0:T(8,128)(2,1)S(1)}, bf16[288,256]{1,0:T(8,128)(2,1)S(1)}, u32[]{:S(2)}, u32[]{:S(2)}) collective-permute-start(bf16[288,256]{1,0:T(8,128)(2,1)S(1)} %get-tuple-element.59), channel_id=1, source_target_pairs={{0,4},{4,0},{8,12},{12,8},{16,20},{20,16},{24,28},{28,24},{1,5},{5... | collective-permute-start | bytes 442376 | tf_op jit(solution)/shard_map/cond/branch_1_fun/ppermute | solution.py:626
  12.6 7.4 %collective-permute-start.7 = (bf16[288,256]{1,0:T(8,128)(2,1)S(1)}, bf16[288,256]{1,0:T(8,128)(2,1)S(1)}, u32[]{:S(2)}, u32[]{:S(2)}) collective-permute-start(bf16[288,256]{1,0:T(8,128)(2,1)S(1)} %get-tuple-element.60), channel_id=1, source_target_pairs={{4,8},{12,16},{20,24},{8,4},{16,12},{24,20},{5,9},{13,17},{21,25},... | collective-permute-start | bytes 442376 | tf_op jit(solution)/shard_map/cond/branch_1_fun/ppermute | solution.py:626
  13.3 11.3 %collective-permute-start.5 = (bf16[448,256]{1,0:T(8,128)(2,1)S(1)}, bf16[448,256]{1,0:T(8,128)(2,1)S(1)}, u32[]{:S(2)}, u32[]{:S(2)}) collective-permute-start(bf16[448,256]{1,0:T(8,128)(2,1)S(1)} %get-tuple-element.56), channel_id=1, source_target_pairs={{4,8},{12,16},{20,24},{8,4},{16,12},{24,20},{5,9},{13,17},{21,25},... | collective-permute-start | bytes 688136 | tf_op jit(solution)/shard_map/cond/branch_1_fun/ppermute | solution.py:626
  13.9 15.3 %collective-permute-start.4 = (bf16[448,256]{1,0:T(8,128)(2,1)S(1)}, bf16[448,256]{1,0:T(8,128)(2,1)S(1)}, u32[]{:S(2)}, u32[]{:S(2)}) collective-permute-start(bf16[448,256]{1,0:T(8,128)(2,1)S(1)} %get-tuple-element.55), channel_id=1, source_target_pairs={{0,4},{4,0},{8,12},{12,8},{16,20},{20,16},{24,28},{28,24},{1,5},{5... | collective-permute-start | bytes 688136 | tf_op jit(solution)/shard_map/cond/branch_1_fun/ppermute | solution.py:626
  37.0 1.3 %collective-permute-start.10 = (f32[144,128]{1,0:T(8,128)S(1)}, f32[144,128]{1,0:T(8,128)S(1)}, u32[]{:S(2)}, u32[]{:S(2)}) collective-permute-start(f32[144,128]{1,0:T(8,128)S(1)} %get-tuple-element.94), channel_id=1, source_target_pairs={{0,1},{1,0},{2,3},{3,2},{4,5},{5,4},{6,7},{7,6},{8,9},{9,8},{10,11... | collective-permute-start | bytes 221192 | tf_op jit(solution)/shard_map/ppermute | solution.py:743
  38.3 4.4 %collective-permute-start.11 = (f32[144,128]{1,0:T(8,128)S(1)}, f32[144,128]{1,0:T(8,128)S(1)}, u32[]{:S(2)}, u32[]{:S(2)}) collective-permute-start(f32[144,128]{1,0:T(8,128)S(1)} %add.12), channel_id=1, source_target_pairs={{0,2},{2,0},{1,3},{3,1},{4,6},{6,4},{5,7},{7,5},{8,10},{10,8},{9,1... | collective-permute-start | bytes 221192 | tf_op jit(solution)/shard_map/ppermute | solution.py:743
  42.8 5.4 %collective-permute-start.12 = (f32[144,128]{1,0:T(8,128)S(1)}, f32[144,128]{1,0:T(8,128)S(1)}, u32[]{:S(2)}, u32[]{:S(2)}) collective-permute-start(f32[144,128]{1,0:T(8,128)S(1)} %add.13), channel_id=1, source_target_pairs={{0,4},{4,0},{8,12},{12,8},{16,20},{20,16},{24,28},{28,24},{1,5},{5... | collective-permute-start | bytes 221192 | tf_op jit(solution)/shard_map/ppermute | solution.py:743
  48.1 4.7 %collective-permute-start.13 = (f32[144,128]{1,0:T(8,128)S(1)}, f32[144,128]{1,0:T(8,128)S(1)}, u32[]{:S(2)}, u32[]{:S(2)}) collective-permute-start(f32[144,128]{1,0:T(8,128)S(1)} %add.14), channel_id=1, source_target_pairs={{0,8},{4,12},{8,0},{12,4},{16,24},{20,28},{24,16},{28,20},{1,9},{5... | collective-permute-start | bytes 221192 | tf_op jit(solution)/shard_map/ppermute | solution.py:743
  52.8 5.8 %collective-permute-start.14 = (f32[144,128]{1,0:T(8,128)S(1)}, f32[144,128]{1,0:T(8,128)S(1)}, u32[]{:S(2)}, u32[]{:S(2)}) collective-permute-start(f32[144,128]{1,0:T(8,128)S(1)} %add.15.mine), channel_id=1, source_target_pairs={{0,16},{4,20},{8,24},{12,28},{16,0},{20,4},{24,8},{28,12},{1,17},{... | collective-permute-start | bytes 221192 | tf_op jit(solution)/shard_map/ppermute | solution.py:743

commit v8 on v7

--- a/solution.py
+++ b/solution.py
@@ -82,41 +82,36 @@
     return jnp.maximum(EXT + shift if below else EXT - shift, 0)
 
 
-def feature_kernel(shifts, feat, msg_a, msg_b):
+def feature_kernel(index, skip, shifts, feat, msg, *counts):
     chans, height, span = feat.shape
     full = chans * height
-    size = msg_a.shape[0]
+    size = msg.shape[0]
     chunk = size // 4
     source = feat[...].reshape(full, span)
     lane = lanes_of((8, full))
     chan, row = lane // height, lane % height
-    for msg, to_below in ((msg_a, is_even("rows")), (msg_b, jnp.logical_not(is_even("rows")))):
-        target = jnp.full((8, full), -1, jnp.int32)
-        at = jnp.int32(0)
-        for c in range(chans):
-            shift = shifts[c, 0]
-            count = jnp.where(to_below, needed(shift, False), needed(shift, True))
-            first = jnp.where(to_below, height - count, 0)
-            mine = (chan == c) & (row >= first) & (row < first + count)
-            target = jnp.where(mine, row + (at - first), target)
-            at = at + count
-        for p in range(0, size, chunk):
-            place = lax.broadcasted_iota(jnp.int32, (chunk, full), 0) + p
-            pick = jnp.where(place == target[0:1], 1.0, 0.0).astype(BF16)
-            msg[p : p + chunk] = jnp.dot(pick, source, preferred_element_type=F32).astype(BF16)
+    to_below = is_even("rows") if index == 0 else jnp.logical_not(is_even("rows"))
+    target = jnp.full((8, full), -1, jnp.int32)
+    at, up, down = jnp.int32(-skip), jnp.int32(0), jnp.int32(0)
+    for c in range(chans):
+        shift = shifts[c, 0]
+        n_up, n_down = needed(shift, False), needed(shift, True)
+        count = jnp.where(to_below, n_up, n_down)
+        first = jnp.where(to_below, height - count, 0)
+        mine = (chan == c) & (row >= first) & (row < first + count)
+        target = jnp.where(mine, row + (at - first), target)
+        at, up, down = at + count, up + n_up, down + n_down
+    for out in counts:
+        out[...] = jnp.full(out.shape, jnp.maximum(up, down), jnp.int32)
+    for p in range(0, size, chunk):
+        place = lax.broadcasted_iota(jnp.int32, (chunk, full), 0) + p
+        pick = jnp.where(place == target[0:1], 1.0, 0.0).astype(BF16)
+        msg[p : p + chunk] = jnp.dot(pick, source, preferred_element_type=F32).astype(BF16)
 
 
 def rows_kernel(source, out):
     for part in tiles_of(source.shape[2]):
         out[:, part] = to_rows(source[:, :, part])
-
-
-def count_kernel(shifts, out):
-    down = up = jnp.int32(0)
-    for c in range(shifts.shape[0]):
-        up = up + needed(shifts[c, 0], False)
-        down = down + needed(shifts[c, 0], True)
-    out[...] = jnp.full(out.shape, jnp.maximum(up, down), jnp.int32)
 
 
 def column_kernel(feat, cot, *col_msgs):
@@ -626,27 +621,84 @@
     return [lax.ppermute(m, axis, p) for m, p in zip(messages, pairs)]
 
 
-def pack_rows(size, shifts, feat):
+def pack_rows(index, skip, size, shifts, feat, counted=False):
     message = bf(size, feat.shape[2])
+    if counted:
+        message = (message, jax.ShapeDtypeStruct((8, TILE), jnp.int32))
     return call(
-        feature_kernel, (message, message), [], 2, 16, flops=10**9, smem_first=True
+        functools.partial(feature_kernel, index, skip),
+        message, [], 2, 16, smem_first=True,
     )(shifts, feat)
 
 
-def both_passes(size, usual, feat, shifts, cot_rows, col_msgs, first_kernel, bottle_kernel, second_kernel):
+def main_pass(rest, lent, shifts, feat, sides, act_grad, views, bands):
     chans, height, span = feat.shape
     width = span + TILE
     full = height * chans
     groups = height // POOL
+    band = 3 * (POOL + 2) * chans
+    if rest:
+        size = lent[0].shape[0]
+        more = swapped([pack_rows(i, size, rest, shifts, feat) for i in (0, 1)], "rows")
+        lent = [jnp.concatenate(pair, axis=0) for pair in zip(lent, more)]
+    size = lent[0].shape[0]
+    tall = pl.cdiv(height + 2 * EXT, 16) * 16
+    grads, blended = call(
+        main_kernel,
+        (jax.ShapeDtypeStruct((9 * chans // 2, TILE), F32), bf((height + 2) * chans, width)),
+        [
+            pltpu.VMEM((2, size + 48, span), BF16),
+            pltpu.VMEM((chans, tall, width), BF16),
+        ]
+        + [pltpu.VMEM((tall * chans, width), BF16)] * 3
+        + [pltpu.VMEM(((height + 4 * POOL) * chans, width), BF16)]
+        + [pltpu.VMEM(((groups + 4) * chans, width), BF16)] * 3
+        + [
+            pltpu.VMEM((full, span), BF16),
+            pltpu.VMEM((band, POOL * chans), F32),
+        ],
+        11,
+        32,
+        flops=10**10,
+        smem_first=True,
+    )(
+        shifts, feat, *lent, sides, act_grad, *views, *bands
+    )
+
+    return grads, blended
+
+
+def shards(features, shifts, first_kernel, bottle_kernel, second_kernel, cotangent):
+    imgs, chans, height, span = features.shape
+    rows, cols, dp = (lax.axis_size(a) for a in ("rows", "cols", "dp"))
+    full = height * chans
+
+    width = span + TILE
+    groups = height // POOL
+    feat, cot, shifts = features[0], cotangent[0], shifts[0]
+    row_pairs = swaps(rows)
+
+    usual = USUAL * chans
+    message, total = pack_rows(0, 0, usual, shifts, feat, counted=True)
+    message, total, cot = lax.optimization_barrier((message, total, cot))
+    feat_a = lax.ppermute(message, "rows", row_pairs[0])
+    bit = 1
+    while bit < dp:
+        total = jnp.maximum(total, lax.ppermute(total, "dp", [(i, i ^ bit) for i in range(dp)]))
+        bit *= 2
+
+    packed = chans * (height * SLOT // TILE)
+    messages = call(
+        column_kernel, (bf(packed, TILE),) * (1 if cols == 2 else 2), [], 2, 8, flops=2 * 10**10
+    )(feat, cot)
+    col_msgs = swapped(messages, "cols")
     ncols = len(col_msgs)
-    packed = col_msgs[0].shape[0]
-
+    feat_b = lax.ppermute(pack_rows(1, 0, usual, shifts, feat), "rows", row_pairs[1])
+    cot_rows = call(rows_kernel, bf(full, span), [], 1, 4)(cot)
     halo = bf(CHALO * chans + ncols * packed * TILE // span, span)
     messages = call(edge_kernel, (halo, halo), [], 1 + ncols, 8)(cot_rows, *col_msgs)
     row_msgs = swapped(messages, "rows")
-    if usual[0].shape[0] != size:
-        usual = pack_rows(size, shifts, feat)
-    feat_msgs = swapped(usual, "rows")
+    row_msgs, feat_a = lax.optimization_barrier((row_msgs, feat_a))
 
     tall_c = (height + 2 * CHALO) * chans
     view = bf((height + 2) * chans, span)
@@ -674,62 +726,11 @@
     )(cot_rows, *row_msgs, *col_msgs, first_kernel, bottle_kernel, second_kernel)
     views, sides, weights = rest[:3], rest[3], rest[4:]
 
-    tall = pl.cdiv(height + 2 * EXT, 16) * 16
-    grads, blended = call(
-        main_kernel,
-        (jax.ShapeDtypeStruct((9 * chans // 2, TILE), F32), bf((height + 2) * chans, width)),
-        [
-            pltpu.VMEM((2, size + 48, span), BF16),
-            pltpu.VMEM((chans, tall, width), BF16),
-        ]
-        + [pltpu.VMEM((tall * chans, width), BF16)] * 3
-        + [pltpu.VMEM(((height + 4 * POOL) * chans, width), BF16)]
-        + [pltpu.VMEM(((groups + 4) * chans, width), BF16)] * 3
-        + [
-            pltpu.VMEM((full, span), BF16),
-            pltpu.VMEM((band, POOL * chans), F32),
-        ],
-        11,
-        32,
-        flops=10**10,
-        smem_first=True,
-    )(
-        shifts, feat, *feat_msgs, sides, act_grad, *views, *weights[:2]
-    )
-
-    return grads, blended, weights[2]
-
-
-def shards(features, shifts, first_kernel, bottle_kernel, second_kernel, cotangent):
-    imgs, chans, height, span = features.shape
-    rows, cols, dp = (lax.axis_size(a) for a in ("rows", "cols", "dp"))
-    full = height * chans
-
-    packed = chans * (height * SLOT // TILE)
-    shifts = shifts[0]
-    total = call(
-        count_kernel, jax.ShapeDtypeStruct((8, TILE), jnp.int32), [], 1, 2, smem_first=True
-    )(shifts)
-    bit = 1
-    while bit < dp:
-        total = jnp.maximum(total, lax.ppermute(total, "dp", [(i, i ^ bit) for i in range(dp)]))
-        bit *= 2
-    messages = call(
-        column_kernel, (bf(packed, TILE),) * (1 if cols == 2 else 2), [], 2, 8, flops=10**9
-    )(features[0], cotangent[0])
-    col_msgs = swapped(messages, "cols")
-    ncols = len(col_msgs)
-    usual = pack_rows(USUAL * chans, shifts, features[0])
-    cot_rows = call(rows_kernel, bf(full, span), [], 1, 4, flops=10**9)(cotangent[0])
-
-    def passes(size):
-        return functools.partial(both_passes, size)
-
-    grads, blended, second_bands = lax.cond(
-        total[0, 0] <= USUAL * chans,
-        passes(USUAL * chans),
-        passes(LARGEST * chans),
-        usual, features[0], shifts, cot_rows, tuple(col_msgs), first_kernel, bottle_kernel, second_kernel,
+    grads, blended = lax.cond(
+        total[0, 0] <= usual,
+        functools.partial(main_pass, 0),
+        functools.partial(main_pass, LARGEST * chans - usual),
+        (feat_a, feat_b), shifts, feat, sides, act_grad, tuple(views), tuple(weights[:2]),
     )
 
     steps = []
@@ -743,7 +744,7 @@
         other = lax.ppermute(grads, axis, pairs)
         if 1 <= step <= parts:
             prediction = predict(
-                blended, second_bands, (chans, height, span), parts, step - 1, prediction
+                blended, weights[2], (chans, height, span), parts, step - 1, prediction
             )
             other, prediction = lax.optimization_barrier((other, prediction))
         if step < len(steps) - 1:

time: 59.9 us -> 58.8 us (0.982)
  Pallas kernels: 23 us -> 21.9 us
  local copies, waits for them, and re-layouts: 2.43 us -> 1.38 us
  waiting for transfers between devices: 11.3 us -> 12.2 us
    ppermute x5 -> x3, starting transfers between devices: 11.5 us -> 2.44 us  [swapped(): return [lax.ppermute(m, axis, p) for m, p in zip(messages, pairs)]]
    ppermute x5, starting transfers between devices: 9.36 us -> 15.1 us  [shards(): other = lax.ppermute(grads, axis, pairs)]
    ppermute x0 -> x2, starting transfers between devices: none -> 3.71 us  [the longest x1 3.03 us: shards(): feat_a = lax.ppermute(message, 'rows', row_pairs[0])]
    pallas_call x2, Pallas kernels: 5.64 us -> 3.33 us  [predict(): call(functools.partial(predict_kernel, part), jax.ShapeDtypeStruct(shape,...]
    ppermute x5, waiting for transfers between devices: 6.56 us -> 8.62 us  [shards(): other = lax.ppermute(grads, axis, pairs)]
    pallas_call x6, Pallas kernels: 15.1 us -> 16.3 us  [the longest x1 8.18 us: main_pass(): call(main_kernel, (jax.ShapeDtypeStruct((9 * chans // 2, TILE), F32), bf(...]
    ppermute x5 -> x3, waiting for transfers between devices: 4.7 us -> 3.57 us  [swapped(): return [lax.ppermute(m, axis, p) for m, p in zip(messages, pairs)]]
    unnamed x14 -> x12, local copies, waits for them, and re-layouts: 1.74 us -> 0.69 us
  transfers between devices with their start and end apart: 11 -> 11, of which waited for: 5 -> 7; matrix products, arithmetic and copies ran while one was open for 1% -> 1% of each run, Pallas kernels for 22% -> 19%
where the time goes in v8:
time: 58.8 us; the launch traced here: 58.5 us
  Pallas kernels  21.9 us (37%)
  starting transfers between devices  21.3 us (36%)
  waiting for transfers between devices  12.2 us (21%)
  between operations  1.46 us (2%)
  local copies, waits for them, and re-layouts  1.38 us (2%)
    ppermute x5, starting transfers between devices, shards(): other = lax.ppermute(grads, axis, pairs)  15.1 us
    ppermute x5, waiting for transfers between devices, shards(): other = lax.ppermute(grads, axis, pairs)  8.62 us
    pallas_call x1, Pallas kernels, main_pass(): call(main_kernel, (jax.ShapeDtypeStruct((9 * chans // 2, TILE), F32), bf(...  8.18 us
    pallas_call x1, Pallas kernels, shards(): call(functools.partial(back_kernel, ncols), (jax.ShapeDtypeStruct((full,...  4.98 us
    ppermute x3, waiting for transfers between devices, swapped(): return [lax.ppermute(m, axis, p) for m, p in zip(messages, pairs)]  3.57 us
    pallas_call x2, Pallas kernels, predict(): call(functools.partial(predict_kernel, part), jax.ShapeDtypeStruct(shape,...  3.33 us
    ppermute x1, starting transfers between devices, shards(): feat_a = lax.ppermute(message, 'rows', row_pairs[0])  3.03 us
    pallas_call x2, Pallas kernels, pack_rows(): call(functools.partial(feature_kernel, index, skip), message, [], 2, 16,...  2.94 us
  transfers between devices with their start and end apart: 11, of which 7 were waited for; matrix products, arithmetic and copies ran while one was open for 1% of the time, Pallas kernels for 19%

profile of v8, /device:TPU:0, one launch (start us, length us, event | category | flops | bytes accessed | tf_op | source)
XLA Modules:
  0.0 58.5 jit_solution(2171528190516245388)
XLA Ops:
  1.4 1.6 %shard_map.85 = (bf16[448,256]{1,0:T(8,128)(2,1)S(1)}, s32[8,128]{1,0:T(8,128)S(1)}) custom-call(s32[32,2]{1,0:T(8,128)S(1)} %copy.10.shifts, bf16[32,32,256]{2,1,0:T(8,128)(2,1)} %bitcast.7), custom_call_target="tpu_custom_call" | custom-call | bytes 4194304 | tf_op jit(solution)/shard_map/pallas_call | solution.py:628
  3.0 3.0 %collective-permute-start.6 = (bf16[448,256]{1,0:T(8,128)(2,1)S(1)}, bf16[448,256]{1,0:T(8,128)(2,1)S(1)}, u32[]{:S(2)}, u32[]{:S(2)}) collective-permute-start(bf16[448,256]{1,0:T(8,128)(2,1)S(1)} %get-tuple-element.105), channel_id=1, source_target_pairs={{0,4},{4,0},{8,12},{12,8},{16,20},{20,16},{24,28},{28,24},{1,5},{5... | collective-permute-start | bytes 688136 | tf_op jit(solution)/shard_map/ppermute | solution.py:684
  6.0 1.3 %shard_map.87 = bf16[256,128]{1,0:T(8,128)(2,1)S(1)} custom-call(bf16[32,32,256]{2,1,0:T(8,128)(2,1)} %bitcast.8, bf16[32,32,256]{2,1,0:T(8,128)(2,1)S(1)} %bitcast.5), custom_call_target="tpu_custom_call" | custom-call | flops 20000000000 | bytes 4194304 | tf_op jit(solution)/shard_map/pallas_call | solution.py:691
  7.4 1.6 %collective-permute-start.3 = (bf16[256,128]{1,0:T(8,128)(2,1)S(1)}, bf16[256,128]{1,0:T(8,128)(2,1)S(1)}, u32[]{:S(2)}, u32[]{:S(2)}) collective-permute-start(bf16[256,128]{1,0:T(8,128)(2,1)S(1)} %shard_map.87), channel_id=1, source_target_pairs={{0,2},{2,0},{1,3},{3,1},{4,6},{6,4},{5,7},{7,5},{8,10},{10,8},{9,1... | collective-permute-start | bytes 196616 | tf_op jit(solution)/shard_map/ppermute | solution.py:621
  9.1 2.6 %collective-permute-done.3.rest_0_ = bf16[256,128]{1,0:T(8,128)(2,1)S(1)} collective-permute-done((bf16[256,128]{1,0:T(8,128)(2,1)S(1)}, bf16[256,128]{1,0:T(8,128)(2,1)S(1)}, u32[]{:S(2)}, u32[]{:S(2)}) %collective-permute-start.3) | collective-permute-done | bytes 65568 | tf_op jit(solution)/shard_map/ppermute | solution.py:621
  11.9 0.8 %collective-permute-start.5 = (bf16[288,256]{1,0:T(8,128)(2,1)S(1)}, bf16[288,256]{1,0:T(8,128)(2,1)S(1)}, u32[]{:S(2)}, u32[]{:S(2)}) collective-permute-start(bf16[288,256]{1,0:T(8,128)(2,1)S(1)} %get-tuple-element.104), channel_id=1, source_target_pairs={{4,8},{12,16},{20,24},{8,4},{16,12},{24,20},{5,9},{13,17},{21,25},... | collective-permute-start | bytes 442376 | tf_op jit(solution)/shard_map/ppermute | solution.py:621
  12.8 1.3 %shard_map.89 = bf16[448,256]{1,0:T(8,128)(2,1)S(1)} custom-call(s32[32,2]{1,0:T(8,128)S(1)} %copy.10.shifts, bf16[32,32,256]{2,1,0:T(8,128)(2,1)S(1)} %bitcast.9), custom_call_target="tpu_custom_call" | custom-call | bytes 4194304 | tf_op jit(solution)/shard_map/pallas_call | solution.py:628
  14.1 0.7 %collective-permute-start.7 = (bf16[448,256]{1,0:T(8,128)(2,1)S(1)}, bf16[448,256]{1,0:T(8,128)(2,1)S(1)}, u32[]{:S(2)}, u32[]{:S(2)}) collective-permute-start(bf16[448,256]{1,0:T(8,128)(2,1)S(1)} %shard_map.89), channel_id=1, source_target_pairs={{4,8},{12,16},{20,24},{8,4},{16,12},{24,20},{5,9},{13,17},{21,25},... | collective-permute-start | bytes 688136 | tf_op jit(solution)/shard_map/ppermute | solution.py:696
  16.0 1.0 %collective-permute-done.4.msg_a = bf16[288,256]{1,0:T(8,128)(2,1)S(1)} collective-permute-done((bf16[288,256]{1,0:T(8,128)(2,1)S(1)}, bf16[288,256]{1,0:T(8,128)(2,1)S(1)}, u32[]{:S(2)}, u32[]{:S(2)}) %collective-permute-start.4) | collective-permute-done | bytes 147488 | tf_op jit(solution)/shard_map/ppermute | solution.py:621
  17.0 5.0 %shard_map.90 = (f32[1024,256]{1,0:T(8,128)S(1)}, bf16[1088,256]{1,0:T(8,128)(2,1)}, bf16[1088,256]{1,0:T(8,128)(2,1)}, bf16[1088,256]{1,0:T(8,128)(2,1)}, bf16[...) custom-call(bf16[1024,256]{1,0:T(8,128)(2,1)S(1)} %shard_map.86.cot_, ...), custom_call_target="tpu_custom_call" | custom-call | flops 8000000000 | bytes 4194304 | tf_op jit(solution)/shard_map/pallas_call | solution.py:706
  22.0 8.5 %conditional.1 = ((f32[144,128]{1,0:T(8,128)S(1)}, bf16[1088,384]{1,0:T(8,128)(2,1)S(1)})) conditional(s32[]{:T(128)} %bitcast.3, (s32[32,2]{0,1:T(2,128)S(1)}, bf16[32,32,256]{2,1,0:T(8,128)(2,1)S(1)}, bf16[448,256]{1,0:T(8,128)(2,1)S(1)}, bf16[448,256]{1,0:T(8,128)(2,1)S(1)}, bf16[32,96,128]{2,1,0:T(8,128)(2,1)}, ...), branch_computations={%region_0.0_spmd, %region_1.0_spmd} | conditional | flops 10001703936 | bytes 25690824 | solution.py:729
  22.1 8.2 %branch_1_fun.1 = (f32[144,128]{1,0:T(8,128)S(1)}, bf16[1088,384]{1,0:T(8,128)(2,1)S(1)}) custom-call(s32[32,2]{1,0:T(8,128)S(1)} %copy.13.shifts, bf16[32,32,256]{2,1,0:T(8,128)(2,1)S(1)} %get-tuple-element.56.feat, bf16[448,256]{1,0:T(8,128)(2,1)S(1)} %get-tuple-element.57.feat_a, bf16[448,256]{1,0:T(8,128)(2,1)S(1)} %get-tuple-element.58.feat_b, ...), custom_call_target="tpu_custom_call" | custom-call | flops 10000000000 | bytes 4194304 | tf_op jit(solution)/shard_map/cond/branch_1_fun/pallas_call | solution.py:646
  30.6 1.3 %collective-permute-done.8 = f32[144,128]{1,0:T(8,128)S(1)} collective-permute-done((f32[144,128]{1,0:T(8,128)S(1)}, f32[144,128]{1,0:T(8,128)S(1)}, u32[]{:S(2)}, u32[]{:S(2)}) %collective-permute-start.8) | collective-permute-done | bytes 73760 | tf_op jit(solution)/shard_map/ppermute | solution.py:744
  31.8 1.6 %collective-permute-start.9 = (f32[144,128]{1,0:T(8,128)S(1)}, f32[144,128]{1,0:T(8,128)S(1)}, u32[]{:S(2)}, u32[]{:S(2)}) collective-permute-start(f32[144,128]{1,0:T(8,128)S(1)} %add.12), channel_id=1, source_target_pairs={{0,2},{2,0},{1,3},{3,1},{4,6},{6,4},{5,7},{7,5},{8,10},{10,8},{9,1... | collective-permute-start | bytes 221192 | tf_op jit(solution)/shard_map/ppermute | solution.py:744
  33.4 1.7 %shard_map.91.rest_0_ = bf16[32,32,256]{2,1,0:T(8,128)(2,1)} custom-call(bf16[1088,384]{1,0:T(8,128)(2,1)S(1)} %get-tuple-element.123.blended, bf16[384,192]{1,0:T(8,128)(2,1)S(1)} %get-tuple-element.120.bands), custom_call_target="tpu_custom_call" | custom-call | flops 1000000000 | bytes 4194304 | tf_op jit(solution)/shard_map/pallas_call | solution.py:599
  35.0 1.2 %collective-permute-done.9 = f32[144,128]{1,0:T(8,128)S(1)} collective-permute-done((f32[144,128]{1,0:T(8,128)S(1)}, f32[144,128]{1,0:T(8,128)S(1)}, u32[]{:S(2)}, u32[]{:S(2)}) %collective-permute-start.9) | collective-permute-done | bytes 73760 | tf_op jit(solution)/shard_map/ppermute | solution.py:744
  36.3 7.7 %collective-permute-start.10 = (f32[144,128]{1,0:T(8,128)S(1)}, f32[144,128]{1,0:T(8,128)S(1)}, u32[]{:S(2)}, u32[]{:S(2)}) collective-permute-start(f32[144,128]{1,0:T(8,128)S(1)} %add.13), channel_id=1, source_target_pairs={{0,4},{4,0},{8,12},{12,8},{16,20},{20,16},{24,28},{28,24},{1,5},{5... | collective-permute-start | bytes 221192 | tf_op jit(solution)/shard_map/ppermute | solution.py:744
  44.0 1.7 %shard_map.92 = bf16[32,32,256]{2,1,0:T(8,128)(2,1)} custom-call(bf16[1088,384]{1,0:T(8,128)(2,1)S(1)} %get-tuple-element.123.blended, bf16[384,192]{1,0:T(8,128)(2,1)S(1)} %get-tuple-element.120.bands, bf16[32,32,256]{2,1,0:T(8,128)(2,1)} %shard_map.91.rest_0_), custom_call_target="tpu_custom_call", output_to_operand_aliasing={{}: (2, {})} | custom-call | flops 1000000000 | bytes 4194304 | tf_op jit(solution)/shard_map/pallas_call | solution.py:599
  45.6 0.7 %collective-permute-done.10 = f32[144,128]{1,0:T(8,128)S(1)} collective-permute-done((f32[144,128]{1,0:T(8,128)S(1)}, f32[144,128]{1,0:T(8,128)S(1)}, u32[]{:S(2)}, u32[]{:S(2)}) %collective-permute-start.10) | collective-permute-done | bytes 73760 | tf_op jit(solution)/shard_map/ppermute | solution.py:744
  46.3 2.0 %collective-permute-start.11 = (f32[144,128]{1,0:T(8,128)S(1)}, f32[144,128]{1,0:T(8,128)S(1)}, u32[]{:S(2)}, u32[]{:S(2)}) collective-permute-start(f32[144,128]{1,0:T(8,128)S(1)} %add.14), channel_id=1, source_target_pairs={{0,8},{4,12},{8,0},{12,4},{16,24},{20,28},{24,16},{28,20},{1,9},{5... | collective-permute-start | bytes 221192 | tf_op jit(solution)/shard_map/ppermute | solution.py:744
  48.3 2.4 %collective-permute-done.11 = f32[144,128]{1,0:T(8,128)S(1)} collective-permute-done((f32[144,128]{1,0:T(8,128)S(1)}, f32[144,128]{1,0:T(8,128)S(1)}, u32[]{:S(2)}, u32[]{:S(2)}) %collective-permute-start.11) | collective-permute-done | bytes 73760 | tf_op jit(solution)/shard_map/ppermute | solution.py:744
  50.7 3.8 %collective-permute-start.12 = (f32[144,128]{1,0:T(8,128)S(1)}, f32[144,128]{1,0:T(8,128)S(1)}, u32[]{:S(2)}, u32[]{:S(2)}) collective-permute-start(f32[144,128]{1,0:T(8,128)S(1)} %add.15.mine), channel_id=1, source_target_pairs={{0,16},{4,20},{8,24},{12,28},{16,0},{20,4},{24,8},{28,12},{1,17},{... | collective-permute-start | bytes 221192 | tf_op jit(solution)/shard_map/ppermute | solution.py:744
  54.5 3.1 %collective-permute-done.12.other = f32[144,128]{1,0:T(8,128)S(1)} collective-permute-done((f32[144,128]{1,0:T(8,128)S(1)}, f32[144,128]{1,0:T(8,128)S(1)}, u32[]{:S(2)}, u32[]{:S(2)}) %collective-permute-start.12) | collective-permute-done | bytes 73760 | tf_op jit(solution)/shard_map/ppermute | solution.py:744
  57.6 0.9 %shard_map.93 = (f32[9,32,32]{2,1,0:T(8,128)}, f32[9,32,32]{2,1,0:T(8,128)}) custom-call(f32[144,128]{1,0:T(8,128)S(1)} %add.15.mine, f32[144,128]{1,0:T(8,128)S(1)} %collective-permute-done.12.other), custom_call_target="tpu_custom_call" | custom-call | bytes 4194304 | tf_op jit(solution)/shard_map/pallas_call | solution.py:756
  (29 shorter events, 1.9 us)
Async XLA Ops:
  0.6 0.7 %copy-start.5 = (s32[1,32,2]{1,2,0:T(2,128)S(1)}, s32[1,32,2]{1,2,0:T(2,128)}, u32[]{:S(2)}) copy-start(s32[1,32,2]{1,2,0:T(2,128)} %param.9) | copy-start | bytes 772
  0.6 5.4 %copy-start = (bf16[1,32,32,256]{3,2,1,0:T(8,128)(2,1)S(1)}, bf16[1,32,32,256]{3,2,1,0:T(8,128)(2,1)}, u32[]{:S(2)}) copy-start(bf16[1,32,32,256]{3,2,1,0:T(8,128)(2,1)} %param.13) | copy-start | bytes 1572868
  3.0 14.0 %collective-permute-start.6 = (bf16[448,256]{1,0:T(8,128)(2,1)S(1)}, bf16[448,256]{1,0:T(8,128)(2,1)S(1)}, u32[]{:S(2)}, u32[]{:S(2)}) collective-permute-start(bf16[448,256]{1,0:T(8,128)(2,1)S(1)} %get-tuple-element.105), channel_id=1, source_target_pairs={{0,4},{4,0},{8,12},{12,8},{16,20},{20,16},{24,28},{28,24},{1,5},{5... | collective-permute-start | bytes 688136 | tf_op jit(solution)/shard_map/ppermute | solution.py:684
  7.4 4.3 %collective-permute-start.3 = (bf16[256,128]{1,0:T(8,128)(2,1)S(1)}, bf16[256,128]{1,0:T(8,128)(2,1)S(1)}, u32[]{:S(2)}, u32[]{:S(2)}) collective-permute-start(bf16[256,128]{1,0:T(8,128)(2,1)S(1)} %shard_map.87), channel_id=1, source_target_pairs={{0,2},{2,0},{1,3},{3,1},{4,6},{6,4},{5,7},{7,5},{8,10},{10,8},{9,1... | collective-permute-start | bytes 196616 | tf_op jit(solution)/shard_map/ppermute | solution.py:621
  9.1 3.7 %copy-start.4 = (bf16[1,32,32,256]{3,2,1,0:T(8,128)(2,1)S(1)}, bf16[1,32,32,256]{3,2,1,0:T(8,128)(2,1)}, u32[]{:S(2)}) copy-start(bf16[1,32,32,256]{3,2,1,0:T(8,128)(2,1)} %param.8) | copy-start | bytes 1572868
  11.8 5.2 %collective-permute-start.4 = (bf16[288,256]{1,0:T(8,128)(2,1)S(1)}, bf16[288,256]{1,0:T(8,128)(2,1)S(1)}, u32[]{:S(2)}, u32[]{:S(2)}) collective-permute-start(bf16[288,256]{1,0:T(8,128)(2,1)S(1)} %get-tuple-element.103), channel_id=1, source_target_pairs={{0,4},{4,0},{8,12},{12,8},{16,20},{20,16},{24,28},{28,24},{1,5},{5... | collective-permute-start | bytes 442376 | tf_op jit(solution)/shard_map/ppermute | solution.py:621
  11.8 5.1 %copy-start.1 = (bf16[9,32,32]{2,1,0:T(8,128)(2,1)S(1)}, bf16[9,32,32]{2,1,0:T(8,128)(2,1)}, u32[]{:S(2)}) copy-start(bf16[9,32,32]{2,1,0:T(8,128)(2,1)} %rest_1_.1) | copy-start | bytes 55300
  11.8 5.1 %copy-start.2 = (bf16[9,32,32]{2,1,0:T(8,128)(2,1)S(1)}, bf16[9,32,32]{2,1,0:T(8,128)(2,1)}, u32[]{:S(2)}) copy-start(bf16[9,32,32]{2,1,0:T(8,128)(2,1)} %rest_2_.1) | copy-start | bytes 55300
  11.9 5.1 %copy-start.3 = (bf16[9,32,32]{2,1,0:T(8,128)(2,1)S(1)}, bf16[9,32,32]{2,1,0:T(8,128)(2,1)}, u32[]{:S(2)}) copy-start(bf16[9,32,32]{2,1,0:T(8,128)(2,1)} %rest_3_.1) | copy-start | bytes 55300
  11.9 5.1 %collective-permute-start.5 = (bf16[288,256]{1,0:T(8,128)(2,1)S(1)}, bf16[288,256]{1,0:T(8,128)(2,1)S(1)}, u32[]{:S(2)}, u32[]{:S(2)}) collective-permute-start(bf16[288,256]{1,0:T(8,128)(2,1)S(1)} %get-tuple-element.104), channel_id=1, source_target_pairs={{4,8},{12,16},{20,24},{8,4},{16,12},{24,20},{5,9},{13,17},{21,25},... | collective-permute-start | bytes 442376 | tf_op jit(solution)/shard_map/ppermute | solution.py:621
  12.7 2.1 %collective-permute-start.2 = (s32[8,128]{1,0:T(8,128)S(1)}, s32[8,128]{1,0:T(8,128)S(1)}, u32[]{:S(2)}, u32[]{:S(2)}) collective-permute-start(s32[8,128]{1,0:T(8,128)S(1)} %get-tuple-element.101), channel_id=1, source_target_pairs={{0,1},{1,0},{2,3},{3,2},{4,5},{5,4},{6,7},{7,6},{8,9},{9,8},{10,11... | collective-permute-start | bytes 12296 | tf_op jit(solution)/shard_map/ppermute | solution.py:687
  14.1 7.9 %collective-permute-start.7 = (bf16[448,256]{1,0:T(8,128)(2,1)S(1)}, bf16[448,256]{1,0:T(8,128)(2,1)S(1)}, u32[]{:S(2)}, u32[]{:S(2)}) collective-permute-start(bf16[448,256]{1,0:T(8,128)(2,1)S(1)} %shard_map.89), channel_id=1, source_target_pairs={{4,8},{12,16},{20,24},{8,4},{16,12},{24,20},{5,9},{13,17},{21,25},... | collective-permute-start | bytes 688136 | tf_op jit(solution)/shard_map/ppermute | solution.py:696
  30.5 1.3 %collective-permute-start.8 = (f32[144,128]{1,0:T(8,128)S(1)}, f32[144,128]{1,0:T(8,128)S(1)}, u32[]{:S(2)}, u32[]{:S(2)}) collective-permute-start(f32[144,128]{1,0:T(8,128)S(1)} %get-tuple-element.116), channel_id=1, source_target_pairs={{0,1},{1,0},{2,3},{3,2},{4,5},{5,4},{6,7},{7,6},{8,9},{9,8},{10,11... | collective-permute-start | bytes 221192 | tf_op jit(solution)/shard_map/ppermute | solution.py:744
  31.8 4.4 %collective-permute-start.9 = (f32[144,128]{1,0:T(8,128)S(1)}, f32[144,128]{1,0:T(8,128)S(1)}, u32[]{:S(2)}, u32[]{:S(2)}) collective-permute-start(f32[144,128]{1,0:T(8,128)S(1)} %add.12), channel_id=1, source_target_pairs={{0,2},{2,0},{1,3},{3,1},{4,6},{6,4},{5,7},{7,5},{8,10},{10,8},{9,1... | collective-permute-start | bytes 221192 | tf_op jit(solution)/shard_map/ppermute | solution.py:744
  36.3 10.0 %collective-permute-start.10 = (f32[144,128]{1,0:T(8,128)S(1)}, f32[144,128]{1,0:T(8,128)S(1)}, u32[]{:S(2)}, u32[]{:S(2)}) collective-permute-start(f32[144,128]{1,0:T(8,128)S(1)} %add.13), channel_id=1, source_target_pairs={{0,4},{4,0},{8,12},{12,8},{16,20},{20,16},{24,28},{28,24},{1,5},{5... | collective-permute-start | bytes 221192 | tf_op jit(solution)/shard_map/ppermute | solution.py:744
  46.3 4.4 %collective-permute-start.11 = (f32[144,128]{1,0:T(8,128)S(1)}, f32[144,128]{1,0:T(8,128)S(1)}, u32[]{:S(2)}, u32[]{:S(2)}) collective-permute-start(f32[144,128]{1,0:T(8,128)S(1)} %add.14), channel_id=1, source_target_pairs={{0,8},{4,12},{8,0},{12,4},{16,24},{20,28},{24,16},{28,20},{1,9},{5... | collective-permute-start | bytes 221192 | tf_op jit(solution)/shard_map/ppermute | solution.py:744
  50.7 6.9 %collective-permute-start.12 = (f32[144,128]{1,0:T(8,128)S(1)}, f32[144,128]{1,0:T(8,128)S(1)}, u32[]{:S(2)}, u32[]{:S(2)}) collective-permute-start(f32[144,128]{1,0:T(8,128)S(1)} %add.15.mine), channel_id=1, source_target_pairs={{0,16},{4,20},{8,24},{12,28},{16,0},{20,4},{24,8},{28,12},{1,17},{... | collective-permute-start | bytes 221192 | tf_op jit(solution)/shard_map/ppermute | solution.py:744

commit v9 on v8

--- a/solution.py
+++ b/solution.py
@@ -693,7 +693,9 @@
     )(feat, cot)
     col_msgs = swapped(messages, "cols")
     ncols = len(col_msgs)
-    feat_b = lax.ppermute(pack_rows(1, 0, usual, shifts, feat), "rows", row_pairs[1])
+    message = pack_rows(1, 0, usual, shifts, feat)
+    col_msgs, message, total = lax.optimization_barrier((col_msgs, message, total))
+    feat_b = lax.ppermute(message, "rows", row_pairs[1])
     cot_rows = call(rows_kernel, bf(full, span), [], 1, 4)(cot)
     halo = bf(CHALO * chans + ncols * packed * TILE // span, span)
     messages = call(edge_kernel, (halo, halo), [], 1 + ncols, 8)(cot_rows, *col_msgs)

time: 58.8 us -> 56.7 us (0.964)
  starting transfers between devices: 21.3 us -> 19.1 us
    ppermute x5, starting transfers between devices: 15.1 us -> 13 us  [shards(): other = lax.ppermute(grads, axis, pairs)]
  transfers between devices with their start and end apart: 11 -> 11, of which waited for: 7 -> 7; matrix products, arithmetic and copies ran while one was open for 1% -> 1% of each run, Pallas kernels for 19% -> 20%
where the time goes in v9:
time: 56.7 us; the launch traced here: 56.4 us
  Pallas kernels  21.9 us (39%)
  starting transfers between devices  19.1 us (34%)
  waiting for transfers between devices  12.4 us (22%)
  between operations  1.46 us (3%)
  local copies, waits for them, and re-layouts  1.38 us (2%)
    ppermute x5, starting transfers between devices, shards(): other = lax.ppermute(grads, axis, pairs)  13 us
    ppermute x5, waiting for transfers between devices, shards(): other = lax.ppermute(grads, axis, pairs)  8.63 us
    pallas_call x1, Pallas kernels, main_pass(): call(main_kernel, (jax.ShapeDtypeStruct((9 * chans // 2, TILE), F32), bf(...  8.18 us
    pallas_call x1, Pallas kernels, shards(): call(functools.partial(back_kernel, ncols), (jax.ShapeDtypeStruct((full,...  4.98 us
    ppermute x3, waiting for transfers between devices, swapped(): return [lax.ppermute(m, axis, p) for m, p in zip(messages, pairs)]  3.75 us
    pallas_call x2, Pallas kernels, predict(): call(functools.partial(predict_kernel, part), jax.ShapeDtypeStruct(shape,...  3.33 us
    ppermute x1, starting transfers between devices, shards(): feat_a = lax.ppermute(message, 'rows', row_pairs[0])  3.03 us
    pallas_call x2, Pallas kernels, pack_rows(): call(functools.partial(feature_kernel, index, skip), message, [], 2, 16,...  2.94 us
  transfers between devices with their start and end apart: 11, of which 7 were waited for; matrix products, arithmetic and copies ran while one was open for 1% of the time, Pallas kernels for 20%

profile of v9, /device:TPU:0, one launch (start us, length us, event | category | flops | bytes accessed | tf_op | source)
XLA Modules:
  0.0 56.4 jit_solution(2817565724972255336)
XLA Ops:
  0.7 0.7 %copy-done.5 = s32[1,32,2]{1,2,0:T(2,128)S(1)} copy-done((s32[1,32,2]{1,2,0:T(2,128)S(1)}, s32[1,32,2]{1,2,0:T(2,128)}, u32[]{:S(2)}) %copy-start.5) | copy-done | bytes 280
  1.4 1.6 %shard_map.85 = (bf16[448,256]{1,0:T(8,128)(2,1)S(1)}, s32[8,128]{1,0:T(8,128)S(1)}) custom-call(s32[32,2]{1,0:T(8,128)S(1)} %copy.10.shifts, bf16[32,32,256]{2,1,0:T(8,128)(2,1)} %bitcast.7), custom_call_target="tpu_custom_call" | custom-call | bytes 4194304 | tf_op jit(solution)/shard_map/pallas_call | solution.py:628
  3.0 3.0 %collective-permute-start.6 = (bf16[448,256]{1,0:T(8,128)(2,1)S(1)}, bf16[448,256]{1,0:T(8,128)(2,1)S(1)}, u32[]{:S(2)}, u32[]{:S(2)}) collective-permute-start(bf16[448,256]{1,0:T(8,128)(2,1)S(1)} %get-tuple-element.110), channel_id=1, source_target_pairs={{0,4},{4,0},{8,12},{12,8},{16,20},{20,16},{24,28},{28,24},{1,5},{5... | collective-permute-start | bytes 688136 | tf_op jit(solution)/shard_map/ppermute | solution.py:684
  6.1 1.3 %shard_map.86 = bf16[256,128]{1,0:T(8,128)(2,1)S(1)} custom-call(bf16[32,32,256]{2,1,0:T(8,128)(2,1)} %bitcast.8, bf16[32,32,256]{2,1,0:T(8,128)(2,1)S(1)} %bitcast.5), custom_call_target="tpu_custom_call" | custom-call | flops 20000000000 | bytes 4194304 | tf_op jit(solution)/shard_map/pallas_call | solution.py:691
  7.4 1.6 %collective-permute-start.2 = (bf16[256,128]{1,0:T(8,128)(2,1)S(1)}, bf16[256,128]{1,0:T(8,128)(2,1)S(1)}, u32[]{:S(2)}, u32[]{:S(2)}) collective-permute-start(bf16[256,128]{1,0:T(8,128)(2,1)S(1)} %shard_map.86), channel_id=1, source_target_pairs={{0,2},{2,0},{1,3},{3,1},{4,6},{6,4},{5,7},{7,5},{8,10},{10,8},{9,1... | collective-permute-start | bytes 196616 | tf_op jit(solution)/shard_map/ppermute | solution.py:621
  9.0 1.3 %shard_map.87 = bf16[448,256]{1,0:T(8,128)(2,1)S(1)} custom-call(s32[32,2]{1,0:T(8,128)S(1)} %copy.10.shifts, bf16[32,32,256]{2,1,0:T(8,128)(2,1)S(1)} %bitcast.9), custom_call_target="tpu_custom_call" | custom-call | bytes 4194304 | tf_op jit(solution)/shard_map/pallas_call | solution.py:628
  10.5 1.2 %collective-permute-done.2.rest_0_ = bf16[256,128]{1,0:T(8,128)(2,1)S(1)} collective-permute-done((bf16[256,128]{1,0:T(8,128)(2,1)S(1)}, bf16[256,128]{1,0:T(8,128)(2,1)S(1)}, u32[]{:S(2)}, u32[]{:S(2)}) %collective-permute-start.2) | collective-permute-done | bytes 65568 | tf_op jit(solution)/shard_map/ppermute | solution.py:621
  13.7 0.7 %collective-permute-start.7 = (bf16[448,256]{1,0:T(8,128)(2,1)S(1)}, bf16[448,256]{1,0:T(8,128)(2,1)S(1)}, u32[]{:S(2)}, u32[]{:S(2)}) collective-permute-start(bf16[448,256]{1,0:T(8,128)(2,1)S(1)} %shard_map.87), channel_id=1, source_target_pairs={{4,8},{12,16},{20,24},{8,4},{16,12},{24,20},{5,9},{13,17},{21,25},... | collective-permute-start | bytes 688136 | tf_op jit(solution)/shard_map/ppermute | solution.py:698
  14.4 2.6 %collective-permute-done.4.msg_a = bf16[288,256]{1,0:T(8,128)(2,1)S(1)} collective-permute-done((bf16[288,256]{1,0:T(8,128)(2,1)S(1)}, bf16[288,256]{1,0:T(8,128)(2,1)S(1)}, u32[]{:S(2)}, u32[]{:S(2)}) %collective-permute-start.4) | collective-permute-done | bytes 147488 | tf_op jit(solution)/shard_map/ppermute | solution.py:621
  17.0 5.0 %shard_map.90 = (f32[1024,256]{1,0:T(8,128)S(1)}, bf16[1088,256]{1,0:T(8,128)(2,1)}, bf16[1088,256]{1,0:T(8,128)(2,1)}, bf16[1088,256]{1,0:T(8,128)(2,1)}, bf16[...) custom-call(bf16[1024,256]{1,0:T(8,128)(2,1)S(1)} %shard_map.88.cot_, ...), custom_call_target="tpu_custom_call" | custom-call | flops 8000000000 | bytes 4194304 | tf_op jit(solution)/shard_map/pallas_call | solution.py:708
  22.0 8.5 %conditional.1 = ((f32[144,128]{1,0:T(8,128)S(1)}, bf16[1088,384]{1,0:T(8,128)(2,1)S(1)})) conditional(s32[]{:T(128)} %bitcast.3, (s32[32,2]{0,1:T(2,128)S(1)}, bf16[32,32,256]{2,1,0:T(8,128)(2,1)S(1)}, bf16[448,256]{1,0:T(8,128)(2,1)S(1)}, bf16[448,256]{1,0:T(8,128)(2,1)S(1)}, bf16[32,96,128]{2,1,0:T(8,128)(2,1)}, ...), branch_computations={%region_0.0_spmd, %region_1.0_spmd} | conditional | flops 10001703936 | bytes 25690824 | solution.py:731
  22.1 8.2 %branch_1_fun.1 = (f32[144,128]{1,0:T(8,128)S(1)}, bf16[1088,384]{1,0:T(8,128)(2,1)S(1)}) custom-call(s32[32,2]{1,0:T(8,128)S(1)} %copy.13.shifts, bf16[32,32,256]{2,1,0:T(8,128)(2,1)S(1)} %get-tuple-element.56.feat, bf16[448,256]{1,0:T(8,128)(2,1)S(1)} %get-tuple-element.57.feat_a, bf16[448,256]{1,0:T(8,128)(2,1)S(1)} %get-tuple-element.58.feat_b, ...), custom_call_target="tpu_custom_call" | custom-call | flops 10000000000 | bytes 4194304 | tf_op jit(solution)/shard_map/cond/branch_1_fun/pallas_call | solution.py:646
  30.6 1.3 %collective-permute-done.8 = f32[144,128]{1,0:T(8,128)S(1)} collective-permute-done((f32[144,128]{1,0:T(8,128)S(1)}, f32[144,128]{1,0:T(8,128)S(1)}, u32[]{:S(2)}, u32[]{:S(2)}) %collective-permute-start.8) | collective-permute-done | bytes 73760 | tf_op jit(solution)/shard_map/ppermute | solution.py:746
  31.8 1.6 %collective-permute-start.9 = (f32[144,128]{1,0:T(8,128)S(1)}, f32[144,128]{1,0:T(8,128)S(1)}, u32[]{:S(2)}, u32[]{:S(2)}) collective-permute-start(f32[144,128]{1,0:T(8,128)S(1)} %add.12), channel_id=1, source_target_pairs={{0,2},{2,0},{1,3},{3,1},{4,6},{6,4},{5,7},{7,5},{8,10},{10,8},{9,1... | collective-permute-start | bytes 221192 | tf_op jit(solution)/shard_map/ppermute | solution.py:746
  33.4 1.7 %shard_map.91.rest_0_ = bf16[32,32,256]{2,1,0:T(8,128)(2,1)} custom-call(bf16[1088,384]{1,0:T(8,128)(2,1)S(1)} %get-tuple-element.129.blended, bf16[384,192]{1,0:T(8,128)(2,1)S(1)} %get-tuple-element.126.bands), custom_call_target="tpu_custom_call" | custom-call | flops 1000000000 | bytes 4194304 | tf_op jit(solution)/shard_map/pallas_call | solution.py:599
  35.1 1.2 %collective-permute-done.9 = f32[144,128]{1,0:T(8,128)S(1)} collective-permute-done((f32[144,128]{1,0:T(8,128)S(1)}, f32[144,128]{1,0:T(8,128)S(1)}, u32[]{:S(2)}, u32[]{:S(2)}) %collective-permute-start.9) | collective-permute-done | bytes 73760 | tf_op jit(solution)/shard_map/ppermute | solution.py:746
  36.3 5.6 %collective-permute-start.10 = (f32[144,128]{1,0:T(8,128)S(1)}, f32[144,128]{1,0:T(8,128)S(1)}, u32[]{:S(2)}, u32[]{:S(2)}) collective-permute-start(f32[144,128]{1,0:T(8,128)S(1)} %add.13), channel_id=1, source_target_pairs={{0,4},{4,0},{8,12},{12,8},{16,20},{20,16},{24,28},{28,24},{1,5},{5... | collective-permute-start | bytes 221192 | tf_op jit(solution)/shard_map/ppermute | solution.py:746
  41.8 1.7 %shard_map.92 = bf16[32,32,256]{2,1,0:T(8,128)(2,1)} custom-call(bf16[1088,384]{1,0:T(8,128)(2,1)S(1)} %get-tuple-element.129.blended, bf16[384,192]{1,0:T(8,128)(2,1)S(1)} %get-tuple-element.126.bands, bf16[32,32,256]{2,1,0:T(8,128)(2,1)} %shard_map.91.rest_0_), custom_call_target="tpu_custom_call", output_to_operand_aliasing={{}: (2, {})} | custom-call | flops 1000000000 | bytes 4194304 | tf_op jit(solution)/shard_map/pallas_call | solution.py:599
  43.5 0.7 %collective-permute-done.10 = f32[144,128]{1,0:T(8,128)S(1)} collective-permute-done((f32[144,128]{1,0:T(8,128)S(1)}, f32[144,128]{1,0:T(8,128)S(1)}, u32[]{:S(2)}, u32[]{:S(2)}) %collective-permute-start.10) | collective-permute-done | bytes 73760 | tf_op jit(solution)/shard_map/ppermute | solution.py:746
  44.2 2.0 %collective-permute-start.11 = (f32[144,128]{1,0:T(8,128)S(1)}, f32[144,128]{1,0:T(8,128)S(1)}, u32[]{:S(2)}, u32[]{:S(2)}) collective-permute-start(f32[144,128]{1,0:T(8,128)S(1)} %add.14), channel_id=1, source_target_pairs={{0,8},{4,12},{8,0},{12,4},{16,24},{20,28},{24,16},{28,20},{1,9},{5... | collective-permute-start | bytes 221192 | tf_op jit(solution)/shard_map/ppermute | solution.py:746
  46.2 2.4 %collective-permute-done.11 = f32[144,128]{1,0:T(8,128)S(1)} collective-permute-done((f32[144,128]{1,0:T(8,128)S(1)}, f32[144,128]{1,0:T(8,128)S(1)}, u32[]{:S(2)}, u32[]{:S(2)}) %collective-permute-start.11) | collective-permute-done | bytes 73760 | tf_op jit(solution)/shard_map/ppermute | solution.py:746
  48.6 3.8 %collective-permute-start.12 = (f32[144,128]{1,0:T(8,128)S(1)}, f32[144,128]{1,0:T(8,128)S(1)}, u32[]{:S(2)}, u32[]{:S(2)}) collective-permute-start(f32[144,128]{1,0:T(8,128)S(1)} %add.15.mine), channel_id=1, source_target_pairs={{0,16},{4,20},{8,24},{12,28},{16,0},{20,4},{24,8},{28,12},{1,17},{... | collective-permute-start | bytes 221192 | tf_op jit(solution)/shard_map/ppermute | solution.py:746
  52.4 3.1 %collective-permute-done.12.other = f32[144,128]{1,0:T(8,128)S(1)} collective-permute-done((f32[144,128]{1,0:T(8,128)S(1)}, f32[144,128]{1,0:T(8,128)S(1)}, u32[]{:S(2)}, u32[]{:S(2)}) %collective-permute-start.12) | collective-permute-done | bytes 73760 | tf_op jit(solution)/shard_map/ppermute | solution.py:746
  55.5 0.9 %shard_map.93 = (f32[9,32,32]{2,1,0:T(8,128)}, f32[9,32,32]{2,1,0:T(8,128)}) custom-call(f32[144,128]{1,0:T(8,128)S(1)} %add.15.mine, f32[144,128]{1,0:T(8,128)S(1)} %collective-permute-done.12.other), custom_call_target="tpu_custom_call" | custom-call | bytes 4194304 | tf_op jit(solution)/shard_map/pallas_call | solution.py:758
  (29 shorter events, 1.8 us)
Async XLA Ops:
  0.6 0.7 %copy-start.5 = (s32[1,32,2]{1,2,0:T(2,128)S(1)}, s32[1,32,2]{1,2,0:T(2,128)}, u32[]{:S(2)}) copy-start(s32[1,32,2]{1,2,0:T(2,128)} %param.9) | copy-start | bytes 772
  0.6 5.4 %copy-start = (bf16[1,32,32,256]{3,2,1,0:T(8,128)(2,1)S(1)}, bf16[1,32,32,256]{3,2,1,0:T(8,128)(2,1)}, u32[]{:S(2)}) copy-start(bf16[1,32,32,256]{3,2,1,0:T(8,128)(2,1)} %param.13) | copy-start | bytes 1572868
  3.0 5.9 %copy-start.4 = (bf16[1,32,32,256]{3,2,1,0:T(8,128)(2,1)S(1)}, bf16[1,32,32,256]{3,2,1,0:T(8,128)(2,1)}, u32[]{:S(2)}) copy-start(bf16[1,32,32,256]{3,2,1,0:T(8,128)(2,1)} %param.8) | copy-start | bytes 1572868
  3.0 14.0 %collective-permute-start.6 = (bf16[448,256]{1,0:T(8,128)(2,1)S(1)}, bf16[448,256]{1,0:T(8,128)(2,1)S(1)}, u32[]{:S(2)}, u32[]{:S(2)}) collective-permute-start(bf16[448,256]{1,0:T(8,128)(2,1)S(1)} %get-tuple-element.110), channel_id=1, source_target_pairs={{0,4},{4,0},{8,12},{12,8},{16,20},{20,16},{24,28},{28,24},{1,5},{5... | collective-permute-start | bytes 688136 | tf_op jit(solution)/shard_map/ppermute | solution.py:684
  7.4 4.3 %collective-permute-start.2 = (bf16[256,128]{1,0:T(8,128)(2,1)S(1)}, bf16[256,128]{1,0:T(8,128)(2,1)S(1)}, u32[]{:S(2)}, u32[]{:S(2)}) collective-permute-start(bf16[256,128]{1,0:T(8,128)(2,1)S(1)} %shard_map.86), channel_id=1, source_target_pairs={{0,2},{2,0},{1,3},{3,1},{4,6},{6,4},{5,7},{7,5},{8,10},{10,8},{9,1... | collective-permute-start | bytes 196616 | tf_op jit(solution)/shard_map/ppermute | solution.py:621
  8.9 1.5 %collective-permute-start.3 = (s32[8,128]{1,0:T(8,128)S(1)}, s32[8,128]{1,0:T(8,128)S(1)}, u32[]{:S(2)}, u32[]{:S(2)}) collective-permute-start(s32[8,128]{1,0:T(8,128)S(1)} %get-tuple-element.105), channel_id=1, source_target_pairs={{0,1},{1,0},{2,3},{3,2},{4,5},{5,4},{6,7},{7,6},{8,9},{9,8},{10,11... | collective-permute-start | bytes 12296 | tf_op jit(solution)/shard_map/ppermute | solution.py:687
  10.5 6.5 %copy-start.1 = (bf16[9,32,32]{2,1,0:T(8,128)(2,1)S(1)}, bf16[9,32,32]{2,1,0:T(8,128)(2,1)}, u32[]{:S(2)}) copy-start(bf16[9,32,32]{2,1,0:T(8,128)(2,1)} %rest_1_.1) | copy-start | bytes 55300
  10.5 6.5 %copy-start.2 = (bf16[9,32,32]{2,1,0:T(8,128)(2,1)S(1)}, bf16[9,32,32]{2,1,0:T(8,128)(2,1)}, u32[]{:S(2)}) copy-start(bf16[9,32,32]{2,1,0:T(8,128)(2,1)} %rest_2_.1) | copy-start | bytes 55300
  10.5 6.5 %copy-start.3 = (bf16[9,32,32]{2,1,0:T(8,128)(2,1)S(1)}, bf16[9,32,32]{2,1,0:T(8,128)(2,1)}, u32[]{:S(2)}) copy-start(bf16[9,32,32]{2,1,0:T(8,128)(2,1)} %rest_3_.1) | copy-start | bytes 55300
  11.8 5.2 %collective-permute-start.4 = (bf16[288,256]{1,0:T(8,128)(2,1)S(1)}, bf16[288,256]{1,0:T(8,128)(2,1)S(1)}, u32[]{:S(2)}, u32[]{:S(2)}) collective-permute-start(bf16[288,256]{1,0:T(8,128)(2,1)S(1)} %get-tuple-element.108), channel_id=1, source_target_pairs={{0,4},{4,0},{8,12},{12,8},{16,20},{20,16},{24,28},{28,24},{1,5},{5... | collective-permute-start | bytes 442376 | tf_op jit(solution)/shard_map/ppermute | solution.py:621
  11.9 5.1 %collective-permute-start.5 = (bf16[288,256]{1,0:T(8,128)(2,1)S(1)}, bf16[288,256]{1,0:T(8,128)(2,1)S(1)}, u32[]{:S(2)}, u32[]{:S(2)}) collective-permute-start(bf16[288,256]{1,0:T(8,128)(2,1)S(1)} %get-tuple-element.109), channel_id=1, source_target_pairs={{4,8},{12,16},{20,24},{8,4},{16,12},{24,20},{5,9},{13,17},{21,25},... | collective-permute-start | bytes 442376 | tf_op jit(solution)/shard_map/ppermute | solution.py:621
  13.7 8.3 %collective-permute-start.7 = (bf16[448,256]{1,0:T(8,128)(2,1)S(1)}, bf16[448,256]{1,0:T(8,128)(2,1)S(1)}, u32[]{:S(2)}, u32[]{:S(2)}) collective-permute-start(bf16[448,256]{1,0:T(8,128)(2,1)S(1)} %shard_map.87), channel_id=1, source_target_pairs={{4,8},{12,16},{20,24},{8,4},{16,12},{24,20},{5,9},{13,17},{21,25},... | collective-permute-start | bytes 688136 | tf_op jit(solution)/shard_map/ppermute | solution.py:698
  30.5 1.3 %collective-permute-start.8 = (f32[144,128]{1,0:T(8,128)S(1)}, f32[144,128]{1,0:T(8,128)S(1)}, u32[]{:S(2)}, u32[]{:S(2)}) collective-permute-start(f32[144,128]{1,0:T(8,128)S(1)} %get-tuple-element.122), channel_id=1, source_target_pairs={{0,1},{1,0},{2,3},{3,2},{4,5},{5,4},{6,7},{7,6},{8,9},{9,8},{10,11... | collective-permute-start | bytes 221192 | tf_op jit(solution)/shard_map/ppermute | solution.py:746
  31.8 4.4 %collective-permute-start.9 = (f32[144,128]{1,0:T(8,128)S(1)}, f32[144,128]{1,0:T(8,128)S(1)}, u32[]{:S(2)}, u32[]{:S(2)}) collective-permute-start(f32[144,128]{1,0:T(8,128)S(1)} %add.12), channel_id=1, source_target_pairs={{0,2},{2,0},{1,3},{3,1},{4,6},{6,4},{5,7},{7,5},{8,10},{10,8},{9,1... | collective-permute-start | bytes 221192 | tf_op jit(solution)/shard_map/ppermute | solution.py:746
  36.3 7.9 %collective-permute-start.10 = (f32[144,128]{1,0:T(8,128)S(1)}, f32[144,128]{1,0:T(8,128)S(1)}, u32[]{:S(2)}, u32[]{:S(2)}) collective-permute-start(f32[144,128]{1,0:T(8,128)S(1)} %add.13), channel_id=1, source_target_pairs={{0,4},{4,0},{8,12},{12,8},{16,20},{20,16},{24,28},{28,24},{1,5},{5... | collective-permute-start | bytes 221192 | tf_op jit(solution)/shard_map/ppermute | solution.py:746
  44.2 4.4 %collective-permute-start.11 = (f32[144,128]{1,0:T(8,128)S(1)}, f32[144,128]{1,0:T(8,128)S(1)}, u32[]{:S(2)}, u32[]{:S(2)}) collective-permute-start(f32[144,128]{1,0:T(8,128)S(1)} %add.14), channel_id=1, source_target_pairs={{0,8},{4,12},{8,0},{12,4},{16,24},{20,28},{24,16},{28,20},{1,9},{5... | collective-permute-start | bytes 221192 | tf_op jit(solution)/shard_map/ppermute | solution.py:746
  48.6 6.9 %collective-permute-start.12 = (f32[144,128]{1,0:T(8,128)S(1)}, f32[144,128]{1,0:T(8,128)S(1)}, u32[]{:S(2)}, u32[]{:S(2)}) collective-permute-start(f32[144,128]{1,0:T(8,128)S(1)} %add.15.mine), channel_id=1, source_target_pairs={{0,16},{4,20},{8,24},{12,28},{16,0},{20,4},{24,8},{28,12},{1,17},{... | collective-permute-start | bytes 221192 | tf_op jit(solution)/shard_map/ppermute | solution.py:746

commit v10 on v9

--- a/solution.py
+++ b/solution.py
@@ -94,7 +94,7 @@
     target = jnp.full((8, full), -1, jnp.int32)
     at, up, down = jnp.int32(-skip), jnp.int32(0), jnp.int32(0)
     for c in range(chans):
-        shift = shifts[c, 0]
+        shift = shifts[0, c]
         n_up, n_down = needed(shift, False), needed(shift, True)
         count = jnp.where(to_below, n_up, n_down)
         first = jnp.where(to_below, height - count, 0)
@@ -114,26 +114,33 @@
         out[:, part] = to_rows(source[:, :, part])
 
 
+def edge_lanes(shape, right, count):
+    lane = lanes_of(shape)
+    return jnp.where(jnp.where(right, TILE - 1 - lane, lane) < count, 1.0, 0.0).astype(BF16)
+
+
+def slots(chans, height):
+    half, block = chans // 2, height // 2
+    for h in (0, 1):
+        for m in (0, 1):
+            yield 2 * h + m, slice(h * half, (h + 1) * half), slice(m * block, (m + 1) * block)
+
+
 def column_kernel(feat, cot, *col_msgs):
     chans, height, span = feat.shape
-    first, last = tiles_of(span)[0], tiles_of(span)[-1]
-    count = TILE // SLOT
-    block = height // count
-    lane = lanes_of((chans, block, TILE))
     for index, msg in enumerate(col_msgs):
-        sends_right = is_even("cols") if index == 0 else jnp.logical_not(is_even("cols"))
-        total = jnp.zeros((chans, block, TILE), F32)
-        inner = jnp.where(sends_right, TILE - 1 - lane, lane) < FHALO
-        for k in range(count):
-            at = slice(k * block, (k + 1) * block)
-            feats = jnp.where(sends_right, feat[:, at, last].astype(F32), feat[:, at, first].astype(F32))
-            cots = jnp.where(sends_right, cot[:, at, last].astype(F32), cot[:, at, first].astype(F32))
-            cots = turn(cots, jnp.where(sends_right, TILE - FHALO, FHALO))
-            piece = jnp.where(inner, feats, cots)
-            piece = turn(piece, jnp.where(sends_right, (k + 1) * SLOT % TILE, k * SLOT))
-            inside = (lane >= k * SLOT) & (lane < (k + 1) * SLOT)
-            total = jnp.where(inside, piece, total)
-        msg[...] = total.reshape(chans * block, TILE).astype(BF16)
+        right = is_even("cols") if index == 0 else jnp.logical_not(is_even("cols"))
+        part = pl.ds(pl.multiple_of(jnp.where(right, span - TILE, 0), TILE), TILE)
+        shape = (1, height // 2, TILE)
+        inner = edge_lanes(shape, right, FHALO)
+        outer = edge_lanes(shape, right, SLOT) - inner
+        total = None
+        for q, channels, rows in slots(chans, height):
+            cots = turn(cot[channels, rows, part], jnp.where(right, TILE - FHALO, FHALO))
+            piece = feat[channels, rows, part] * inner + cots * outer
+            piece = turn(piece, jnp.where(right, (q + 1) * SLOT % TILE, q * SLOT))
+            total = piece if total is None else total + piece
+        msg[...] = total.reshape(msg.shape)
 
 
 def edge_kernel(cot_rows, *rest):
@@ -167,23 +174,26 @@
     return views
 
 
-def halo_block(sources, k, chans, kind):
-    rows = sources[0].shape[0] // chans
-    lane = lanes_of((chans * rows, TILE))
-    total = jnp.zeros((chans * rows, TILE), F32)
+def halo_block(sources, slot, rows, kind):
+    total = None
     if kind == "features":
-        count, shift_r, shift_l = FHALO, -k * SLOT, TILE - (k + 1) * SLOT
+        count, shift_r, shift_l = FHALO, -slot * SLOT, TILE - (slot + 1) * SLOT
     else:
-        count, shift_r, shift_l = CHALO, -k * SLOT - FHALO, TILE - (k + 1) * SLOT + FHALO
+        count = CHALO
+        shift_r, shift_l = -slot * SLOT - FHALO, TILE - (slot + 1) * SLOT + FHALO
     for index, source in enumerate(sources):
         from_right = is_even("cols") if index == 0 else jnp.logical_not(is_even("cols"))
-        moved = turn(
-            source.astype(F32), jnp.where(from_right, shift_r % TILE, shift_l % TILE)
-        )
-        total = jnp.where(
-            jnp.where(from_right, lane, TILE - 1 - lane) < count, moved, total
-        )
-    return total.astype(BF16).reshape(chans, rows, TILE)
+        block = source.reshape(source.shape[0] // rows, rows, TILE)
+        block = turn(block, jnp.where(from_right, shift_r % TILE, shift_l % TILE))
+        block = block * edge_lanes((1, rows, TILE), jnp.logical_not(from_right), count)
+        total = block if total is None else total + block
+    return total
+
+
+def halo_rows(sources, m, rows, kind):
+    return to_rows(
+        jnp.concatenate([halo_block(sources, 2 * h + m, rows, kind) for h in (0, 1)], axis=0)
+    )
 
 
 def columns_seen(shape, span):
@@ -252,8 +262,8 @@
 ):
     cols, (
         first, bottle, second,
-        act_grad, view_m, view_0, view_p, sides, first_bands, bottle_bands, second_bands,
-        cot_m, cot_0, cot_p, back, high, low, coarse, bands_f, bands, small_f, small, wide_f,
+        act_grad, cot_m, cot_0, cot_p, sides, first_bands, bottle_bands, second_bands,
+        back, high, low, coarse, bands_f, bands, small_f, small, wide_f,
     ) = rest[:ncols], rest[ncols:]
     chans = second.shape[1]
     full, span = cot.shape
@@ -284,33 +294,34 @@
                 ] = second[3 * a + b]
 
     size = CHALO * chans
-    count = TILE // SLOT
-    block = height // count
+    block = height // 2
 
     def halo_columns(sources, at):
-        for k in range(count):
-            sides[:, at + k * block : at + (k + 1) * block, :] = halo_block(
-                sources, k, chans, "features"
+        for q, channels, rows in slots(chans, height):
+            sides[channels, at + rows.start : at + rows.stop, :] = halo_block(
+                sources, q, block, "features"
             )
 
-    halo_columns([c[...] for c in cols], height)
+    own = [c[...] for c in cols]
+    halo_columns(own, height)
     cot_0[rows_at(CHALO, chans, height), 0:span] = cot[...]
-    for k in range(count):
-        cot_0[rows_at(CHALO + k * block, chans, block), span:width] = to_rows(
-            halo_block([c[...] for c in cols], k, chans, "cotangent")
+    for m in (0, 1):
+        cot_0[rows_at(CHALO + m * block, chans, block), span:width] = halo_rows(
+            own, m, block, "cotangent"
         )
 
     def vertical(up, down):
         cot_0[rows_at(0, chans, CHALO), 0:span] = up[0:size]
         cot_0[rows_at(CHALO + height, chans, CHALO), 0:span] = down[0:size]
-        corner = to_rows(
-            halo_block(corner_views(up, size, cols), count - 1, chans, "cotangent")
-        )
-        cot_0[rows_at(0, chans, CHALO), span:width] = corner[(block - CHALO) * chans :]
-        corner = to_rows(halo_block(corner_views(down, size, cols), 0, chans, "cotangent"))
-        cot_0[rows_at(CHALO + height, chans, CHALO), span:width] = corner[0:size]
-        halo_columns(corner_views(up, size, cols), 0)
-        halo_columns(corner_views(down, size, cols), 2 * height)
+        above, below = corner_views(up, size, cols), corner_views(down, size, cols)
+        cot_0[rows_at(0, chans, CHALO), span:width] = halo_rows(above, 1, block, "cotangent")[
+            (block - CHALO) * chans :
+        ]
+        cot_0[rows_at(CHALO + height, chans, CHALO), span:width] = halo_rows(
+            below, 0, block, "cotangent"
+        )[0:size]
+        halo_columns(above, 0)
+        halo_columns(below, 2 * height)
 
     pl.when(is_even("rows"))(lambda: vertical(msg_b, msg_a))
     pl.when(jnp.logical_not(is_even("rows")))(lambda: vertical(msg_a, msg_b))
@@ -318,11 +329,6 @@
         at = rows_at(j, chans)
         cot_m[at] = turn(cot_0[at], 1)
         cot_p[at] = turn(cot_0[at], -1)
-    inner = rows_at(CHALO - 1, chans, height + 2)
-    view_m[...] = cot_m[inner, 0:span]
-    view_0[...] = cot_0[inner, 0:span]
-    view_p[...] = cot_p[inner, 0:span]
-
     def group(g, _):
         at = rows_at(g * POOL, chans, POOL + 2)
         rows = jnp.dot(
@@ -336,7 +342,7 @@
         store_split(high, low, rows_at(g, chans), total)
         return 0
 
-    lax.fori_loop(0, groups + 2, group, 0, unroll=2)
+    lax.fori_loop(0, groups + 2, group, 0, unroll=5)
     sums = block_sums(high, low, block_ones(width))
     for g in range(groups + 2):
         at = rows_at(g, chans)
@@ -419,7 +425,7 @@
 
     def warp(c, ats):
         at_up, at_down = ats
-        shift, move = shifts[c, 0], shifts[c, 1]
+        shift, move = shifts[0, c], shifts[1, c]
         n_up, n_down = needed(shift, False), needed(shift, True)
         base_up, base_down = (
             pl.multiple_of(lax.div(at, align) * align, align) for at in (at_up, at_down)
@@ -522,7 +528,7 @@
 
     correlate(pre_grad, 0, (warp_m, warp_0, warp_p), EXT - 1, acc, height, chans, span)
     first_part = folded(acc, chans)
-    correlate(blended, 1, (view_m, view_0, view_p), 0, acc, height, chans, span)
+    correlate(blended, 1, (view_m, view_0, view_p), CHALO - 1, acc, height, chans, span)
     second_part = folded(acc, chans)
     lane = lanes_of((3 * chans, TILE))
     grads[0 : 3 * chans] = jnp.where(lane < 3 * chans, first_part, turn(second_part, 3 * chans))
@@ -658,7 +664,7 @@
             pltpu.VMEM((band, POOL * chans), F32),
         ],
         11,
-        32,
+        20,
         flops=10**10,
         smem_first=True,
     )(
@@ -675,7 +681,7 @@
 
     width = span + TILE
     groups = height // POOL
-    feat, cot, shifts = features[0], cotangent[0], shifts[0]
+    feat, cot, shifts = features[0], cotangent[0], shifts[0].T
     row_pairs = swaps(rows)
 
     usual = USUAL * chans
@@ -703,7 +709,7 @@
     row_msgs, feat_a = lax.optimization_barrier((row_msgs, feat_a))
 
     tall_c = (height + 2 * CHALO) * chans
-    view = bf((height + 2) * chans, span)
+    view = bf(tall_c, width)
     band = 3 * (POOL + 2) * chans
     act_grad, *rest = call(
         functools.partial(back_kernel, ncols),
@@ -712,8 +718,7 @@
             bf(chans, 3 * height, TILE), bf(POOL * chans, band), bf(3 * chans, 3 * chans),
             bf(3 * POOL * chans, (POOL + 2) * chans),
         ),
-        [pltpu.VMEM((tall_c, width), BF16)] * 3
-        + [pltpu.VMEM(((height + 2 * POOL) * chans, span), BF16)]
+        [pltpu.VMEM(((height + 2 * POOL) * chans, span), BF16)]
         + [pltpu.VMEM(((groups + 2) * chans, width), BF16)] * 3
         + [
             pltpu.VMEM((band, POOL * chans), F32),

time: 56.7 us -> 54.4 us (0.959)
  Pallas kernels: 21.9 us -> 19.3 us
  local copies, waits for them, and re-layouts: 1.38 us -> 0.55 us
  starting transfers between devices: 19.1 us -> 19.9 us
    pallas_call x1, Pallas kernels: 4.98 us -> 3.83 us  [shards(): call(functools.partial(back_kernel, ncols), (jax.ShapeDtypeStruct((full,...]
    pallas_call x1, Pallas kernels: 8.18 us -> 7.07 us  [main_pass(): call(main_kernel, (jax.ShapeDtypeStruct((9 * chans // 2, TILE), F32), bf(...]
    ppermute x5, starting transfers between devices: 13 us -> 13.8 us  [shards(): other = lax.ppermute(grads, axis, pairs)]
    unnamed x12, local copies, waits for them, and re-layouts: 0.69 us -> 0.04 us
  transfers between devices with their start and end apart: 11 -> 11, of which waited for: 7 -> 7; matrix products, arithmetic and copies ran while one was open for 1% -> 1% of each run, Pallas kernels for 20% -> 18%
where the time goes in v10:
time: 54.4 us; the launch traced here: 54.2 us
  starting transfers between devices  19.9 us (37%)
  Pallas kernels  19.3 us (35%)
  waiting for transfers between devices  12.6 us (23%)
  between operations  1.48 us (3%)
  local copies, waits for them, and re-layouts  0.55 us (1%)
    ppermute x5, starting transfers between devices, shards(): other = lax.ppermute(grads, axis, pairs)  13.8 us
    ppermute x5, waiting for transfers between devices, shards(): other = lax.ppermute(grads, axis, pairs)  8.64 us
    pallas_call x1, Pallas kernels, main_pass(): call(main_kernel, (jax.ShapeDtypeStruct((9 * chans // 2, TILE), F32), bf(...  7.07 us
    ppermute x3, waiting for transfers between devices, swapped(): return [lax.ppermute(m, axis, p) for m, p in zip(messages, pairs)]  3.98 us
    pallas_call x1, Pallas kernels, shards(): call(functools.partial(back_kernel, ncols), (jax.ShapeDtypeStruct((full,...  3.83 us
    pallas_call x2, Pallas kernels, predict(): call(functools.partial(predict_kernel, part), jax.ShapeDtypeStruct(shape,...  3.34 us
    ppermute x1, starting transfers between devices, shards(): feat_a = lax.ppermute(message, 'rows', row_pairs[0])  3.03 us
    pallas_call x2, Pallas kernels, pack_rows(): call(functools.partial(feature_kernel, index, skip), message, [], 2, 16,...  2.75 us
  transfers between devices with their start and end apart: 11, of which 7 were waited for; matrix products, arithmetic and copies ran while one was open for 1% of the time, Pallas kernels for 18%

profile of v10, /device:TPU:0, one launch (start us, length us, event | category | flops | bytes accessed | tf_op | source)
XLA Modules:
  0.0 54.2 jit_solution(10979369346737666805)
XLA Ops:
  0.6 1.7 %shard_map.85 = (bf16[448,256]{1,0:T(8,128)(2,1)S(1)}, s32[8,128]{1,0:T(8,128)S(1)}) custom-call(s32[2,32]{1,0:T(2,128)} %bitcast.14, bf16[32,32,256]{2,1,0:T(8,128)(2,1)} %bitcast.9), custom_call_target="tpu_custom_call" | custom-call | bytes 4194304 | tf_op jit(solution)/shard_map/pallas_call | solution.py:634
  2.3 3.0 %collective-permute-start.6 = (bf16[448,256]{1,0:T(8,128)(2,1)S(1)}, bf16[448,256]{1,0:T(8,128)(2,1)S(1)}, u32[]{:S(2)}, u32[]{:S(2)}) collective-permute-start(bf16[448,256]{1,0:T(8,128)(2,1)S(1)} %get-tuple-element.110), channel_id=1, source_target_pairs={{0,4},{4,0},{8,12},{12,8},{16,20},{20,16},{24,28},{28,24},{1,5},{5... | collective-permute-start | bytes 688136 | tf_op jit(solution)/shard_map/ppermute | solution.py:690
  5.4 1.2 %shard_map.86 = bf16[256,128]{1,0:T(8,128)(2,1)S(1)} custom-call(bf16[32,32,256]{2,1,0:T(8,128)(2,1)} %bitcast.10, bf16[32,32,256]{2,1,0:T(8,128)(2,1)S(1)} %bitcast.7), custom_call_target="tpu_custom_call" | custom-call | flops 20000000000 | bytes 4194304 | tf_op jit(solution)/shard_map/pallas_call | solution.py:697
  6.6 1.6 %collective-permute-start.2 = (bf16[256,128]{1,0:T(8,128)(2,1)S(1)}, bf16[256,128]{1,0:T(8,128)(2,1)S(1)}, u32[]{:S(2)}, u32[]{:S(2)}) collective-permute-start(bf16[256,128]{1,0:T(8,128)(2,1)S(1)} %shard_map.86), channel_id=1, source_target_pairs={{0,2},{2,0},{1,3},{3,1},{4,6},{6,4},{5,7},{7,5},{8,10},{10,8},{9,1... | collective-permute-start | bytes 196616 | tf_op jit(solution)/shard_map/ppermute | solution.py:627
  8.2 1.1 %shard_map.87 = bf16[448,256]{1,0:T(8,128)(2,1)S(1)} custom-call(s32[2,32]{1,0:T(2,128)S(1)} %bitcast.15, bf16[32,32,256]{2,1,0:T(8,128)(2,1)S(1)} %bitcast.11), custom_call_target="tpu_custom_call" | custom-call | bytes 4194304 | tf_op jit(solution)/shard_map/pallas_call | solution.py:634
  9.5 1.4 %collective-permute-done.2.rest_0_ = bf16[256,128]{1,0:T(8,128)(2,1)S(1)} collective-permute-done((bf16[256,128]{1,0:T(8,128)(2,1)S(1)}, bf16[256,128]{1,0:T(8,128)(2,1)S(1)}, u32[]{:S(2)}, u32[]{:S(2)}) %collective-permute-start.2) | collective-permute-done | bytes 65568 | tf_op jit(solution)/shard_map/ppermute | solution.py:627
  11.2 0.7 %collective-permute-start.5 = (bf16[288,256]{1,0:T(8,128)(2,1)S(1)}, bf16[288,256]{1,0:T(8,128)(2,1)S(1)}, u32[]{:S(2)}, u32[]{:S(2)}) collective-permute-start(bf16[288,256]{1,0:T(8,128)(2,1)S(1)} %get-tuple-element.109), channel_id=1, source_target_pairs={{4,8},{12,16},{20,24},{8,4},{16,12},{24,20},{5,9},{13,17},{21,25},... | collective-permute-start | bytes 442376 | tf_op jit(solution)/shard_map/ppermute | solution.py:627
  13.0 0.7 %collective-permute-start.7 = (bf16[448,256]{1,0:T(8,128)(2,1)S(1)}, bf16[448,256]{1,0:T(8,128)(2,1)S(1)}, u32[]{:S(2)}, u32[]{:S(2)}) collective-permute-start(bf16[448,256]{1,0:T(8,128)(2,1)S(1)} %shard_map.87), channel_id=1, source_target_pairs={{4,8},{12,16},{20,24},{8,4},{16,12},{24,20},{5,9},{13,17},{21,25},... | collective-permute-start | bytes 688136 | tf_op jit(solution)/shard_map/ppermute | solution.py:704
  13.7 2.5 %collective-permute-done.4.msg_a = bf16[288,256]{1,0:T(8,128)(2,1)S(1)} collective-permute-done((bf16[288,256]{1,0:T(8,128)(2,1)S(1)}, bf16[288,256]{1,0:T(8,128)(2,1)S(1)}, u32[]{:S(2)}, u32[]{:S(2)}) %collective-permute-start.4) | collective-permute-done | bytes 147488 | tf_op jit(solution)/shard_map/ppermute | solution.py:627
  16.2 3.8 %shard_map.90 = (f32[1024,256]{1,0:T(8,128)S(1)}, bf16[1344,384]{1,0:T(8,128)(2,1)S(1)}, bf16[1344,384]{1,0:T(8,128)(2,1)S(1)}, bf16[1344,384]{1,0:T(8,128)(2,1)...) custom-call(bf16[1024,256]{1,0:T(8,128)(2,1)S(1)} %shard_map.88.cot_, ...), custom_call_target="tpu_custom_call" | custom-call | flops 8000000000 | bytes 4194304 | tf_op jit(solution)/shard_map/pallas_call | solution.py:714
  20.1 7.3 %conditional.1 = ((f32[144,128]{1,0:T(8,128)S(1)}, bf16[1088,384]{1,0:T(8,128)(2,1)S(1)})) conditional(s32[]{:T(128)} %bitcast.5, (s32[2,32]{1,0:T(2,128)S(1)}, bf16[32,32,256]{2,1,0:T(8,128)(2,1)S(1)}, bf16[448,256]{1,0:T(8,128)(2,1)S(1)}, bf16[448,256]{1,0:T(8,128)(2,1)S(1)}, bf16[32,96,128]{2,1,0:T(8,128)(2,1)S(1)}, ...), branch_computations={%region_0.0_spmd, %region_1.0_spmd} | conditional | flops 10001703936 | bytes 15859800 | solution.py:736
  20.1 7.1 %branch_1_fun.1 = (f32[144,128]{1,0:T(8,128)S(1)}, bf16[1088,384]{1,0:T(8,128)(2,1)S(1)}) custom-call(s32[2,32]{1,0:T(2,128)S(1)} %get-tuple-element.55.shifts, bf16[32,32,256]{2,1,0:T(8,128)(2,1)S(1)} %get-tuple-element.56.feat, bf16[448,256]{1,0:T(8,128)(2,1)S(1)} %get-tuple-element.57.feat_a, bf16[448,256]{1,0:T(8,128)(2,1)S(1)} %get-tuple-element.58.feat_b, ...), custom_call_target="tpu_custom_call" | custom-call | flops 10000000000 | bytes 4194304 | tf_op jit(solution)/shard_map/cond/branch_1_fun/pallas_call | solution.py:652
  27.5 1.3 %collective-permute-done.8 = f32[144,128]{1,0:T(8,128)S(1)} collective-permute-done((f32[144,128]{1,0:T(8,128)S(1)}, f32[144,128]{1,0:T(8,128)S(1)}, u32[]{:S(2)}, u32[]{:S(2)}) %collective-permute-start.8) | collective-permute-done | bytes 73760 | tf_op jit(solution)/shard_map/ppermute | solution.py:751
  28.8 1.5 %collective-permute-start.9 = (f32[144,128]{1,0:T(8,128)S(1)}, f32[144,128]{1,0:T(8,128)S(1)}, u32[]{:S(2)}, u32[]{:S(2)}) collective-permute-start(f32[144,128]{1,0:T(8,128)S(1)} %add.12), channel_id=1, source_target_pairs={{0,2},{2,0},{1,3},{3,1},{4,6},{6,4},{5,7},{7,5},{8,10},{10,8},{9,1... | collective-permute-start | bytes 221192 | tf_op jit(solution)/shard_map/ppermute | solution.py:751
  30.3 1.7 %shard_map.91.rest_0_ = bf16[32,32,256]{2,1,0:T(8,128)(2,1)} custom-call(bf16[1088,384]{1,0:T(8,128)(2,1)S(1)} %get-tuple-element.129.blended, bf16[384,192]{1,0:T(8,128)(2,1)S(1)} %get-tuple-element.126.bands), custom_call_target="tpu_custom_call" | custom-call | flops 1000000000 | bytes 4194304 | tf_op jit(solution)/shard_map/pallas_call | solution.py:605
  32.0 1.2 %collective-permute-done.9 = f32[144,128]{1,0:T(8,128)S(1)} collective-permute-done((f32[144,128]{1,0:T(8,128)S(1)}, f32[144,128]{1,0:T(8,128)S(1)}, u32[]{:S(2)}, u32[]{:S(2)}) %collective-permute-start.9) | collective-permute-done | bytes 73760 | tf_op jit(solution)/shard_map/ppermute | solution.py:751
  33.2 6.4 %collective-permute-start.10 = (f32[144,128]{1,0:T(8,128)S(1)}, f32[144,128]{1,0:T(8,128)S(1)}, u32[]{:S(2)}, u32[]{:S(2)}) collective-permute-start(f32[144,128]{1,0:T(8,128)S(1)} %add.13), channel_id=1, source_target_pairs={{0,4},{4,0},{8,12},{12,8},{16,20},{20,16},{24,28},{28,24},{1,5},{5... | collective-permute-start | bytes 221192 | tf_op jit(solution)/shard_map/ppermute | solution.py:751
  39.6 1.7 %shard_map.92 = bf16[32,32,256]{2,1,0:T(8,128)(2,1)} custom-call(bf16[1088,384]{1,0:T(8,128)(2,1)S(1)} %get-tuple-element.129.blended, bf16[384,192]{1,0:T(8,128)(2,1)S(1)} %get-tuple-element.126.bands, bf16[32,32,256]{2,1,0:T(8,128)(2,1)} %shard_map.91.rest_0_), custom_call_target="tpu_custom_call", output_to_operand_aliasing={{}: (2, {})} | custom-call | flops 1000000000 | bytes 4194304 | tf_op jit(solution)/shard_map/pallas_call | solution.py:605
  41.3 0.7 %collective-permute-done.10 = f32[144,128]{1,0:T(8,128)S(1)} collective-permute-done((f32[144,128]{1,0:T(8,128)S(1)}, f32[144,128]{1,0:T(8,128)S(1)}, u32[]{:S(2)}, u32[]{:S(2)}) %collective-permute-start.10) | collective-permute-done | bytes 73760 | tf_op jit(solution)/shard_map/ppermute | solution.py:751
  42.0 2.0 %collective-permute-start.11 = (f32[144,128]{1,0:T(8,128)S(1)}, f32[144,128]{1,0:T(8,128)S(1)}, u32[]{:S(2)}, u32[]{:S(2)}) collective-permute-start(f32[144,128]{1,0:T(8,128)S(1)} %add.14), channel_id=1, source_target_pairs={{0,8},{4,12},{8,0},{12,4},{16,24},{20,28},{24,16},{28,20},{1,9},{5... | collective-permute-start | bytes 221192 | tf_op jit(solution)/shard_map/ppermute | solution.py:751
  44.0 2.4 %collective-permute-done.11 = f32[144,128]{1,0:T(8,128)S(1)} collective-permute-done((f32[144,128]{1,0:T(8,128)S(1)}, f32[144,128]{1,0:T(8,128)S(1)}, u32[]{:S(2)}, u32[]{:S(2)}) %collective-permute-start.11) | collective-permute-done | bytes 73760 | tf_op jit(solution)/shard_map/ppermute | solution.py:751
  46.4 3.8 %collective-permute-start.12 = (f32[144,128]{1,0:T(8,128)S(1)}, f32[144,128]{1,0:T(8,128)S(1)}, u32[]{:S(2)}, u32[]{:S(2)}) collective-permute-start(f32[144,128]{1,0:T(8,128)S(1)} %add.15.mine), channel_id=1, source_target_pairs={{0,16},{4,20},{8,24},{12,28},{16,0},{20,4},{24,8},{28,12},{1,17},{... | collective-permute-start | bytes 221192 | tf_op jit(solution)/shard_map/ppermute | solution.py:751
  50.2 3.1 %collective-permute-done.12.other = f32[144,128]{1,0:T(8,128)S(1)} collective-permute-done((f32[144,128]{1,0:T(8,128)S(1)}, f32[144,128]{1,0:T(8,128)S(1)}, u32[]{:S(2)}, u32[]{:S(2)}) %collective-permute-start.12) | collective-permute-done | bytes 73760 | tf_op jit(solution)/shard_map/ppermute | solution.py:751
  53.3 0.9 %shard_map.93 = (f32[9,32,32]{2,1,0:T(8,128)}, f32[9,32,32]{2,1,0:T(8,128)}) custom-call(f32[144,128]{1,0:T(8,128)S(1)} %add.15.mine, f32[144,128]{1,0:T(8,128)S(1)} %collective-permute-done.12.other), custom_call_target="tpu_custom_call" | custom-call | bytes 4194304 | tf_op jit(solution)/shard_map/pallas_call | solution.py:763
  (27 shorter events, 1.0 us)
Async XLA Ops:
  0.6 4.7 %copy-start = (bf16[1,32,32,256]{3,2,1,0:T(8,128)(2,1)S(1)}, bf16[1,32,32,256]{3,2,1,0:T(8,128)(2,1)}, u32[]{:S(2)}) copy-start(bf16[1,32,32,256]{3,2,1,0:T(8,128)(2,1)} %param.13) | copy-start | bytes 1572868
  2.3 5.9 %copy-start.4 = (bf16[1,32,32,256]{3,2,1,0:T(8,128)(2,1)S(1)}, bf16[1,32,32,256]{3,2,1,0:T(8,128)(2,1)}, u32[]{:S(2)}) copy-start(bf16[1,32,32,256]{3,2,1,0:T(8,128)(2,1)} %param.8) | copy-start | bytes 1572868
  2.3 5.9 %copy-start.5 = (s32[1,32,2]{1,2,0:T(2,128)S(1)}, s32[1,32,2]{1,2,0:T(2,128)}, u32[]{:S(2)}) copy-start(s32[1,32,2]{1,2,0:T(2,128)} %param.9) | copy-start | bytes 772
  2.3 13.9 %collective-permute-start.6 = (bf16[448,256]{1,0:T(8,128)(2,1)S(1)}, bf16[448,256]{1,0:T(8,128)(2,1)S(1)}, u32[]{:S(2)}, u32[]{:S(2)}) collective-permute-start(bf16[448,256]{1,0:T(8,128)(2,1)S(1)} %get-tuple-element.110), channel_id=1, source_target_pairs={{0,4},{4,0},{8,12},{12,8},{16,20},{20,16},{24,28},{28,24},{1,5},{5... | collective-permute-start | bytes 688136 | tf_op jit(solution)/shard_map/ppermute | solution.py:690
  6.6 4.3 %collective-permute-start.2 = (bf16[256,128]{1,0:T(8,128)(2,1)S(1)}, bf16[256,128]{1,0:T(8,128)(2,1)S(1)}, u32[]{:S(2)}, u32[]{:S(2)}) collective-permute-start(bf16[256,128]{1,0:T(8,128)(2,1)S(1)} %shard_map.86), channel_id=1, source_target_pairs={{0,2},{2,0},{1,3},{3,1},{4,6},{6,4},{5,7},{7,5},{8,10},{10,8},{9,1... | collective-permute-start | bytes 196616 | tf_op jit(solution)/shard_map/ppermute | solution.py:627
  8.2 1.3 %collective-permute-start.3 = (s32[8,128]{1,0:T(8,128)S(1)}, s32[8,128]{1,0:T(8,128)S(1)}, u32[]{:S(2)}, u32[]{:S(2)}) collective-permute-start(s32[8,128]{1,0:T(8,128)S(1)} %get-tuple-element.105), channel_id=1, source_target_pairs={{0,1},{1,0},{2,3},{3,2},{4,5},{5,4},{6,7},{7,6},{8,9},{9,8},{10,11... | collective-permute-start | bytes 12296 | tf_op jit(solution)/shard_map/ppermute | solution.py:693
  9.5 6.7 %copy-start.1 = (bf16[9,32,32]{2,1,0:T(8,128)(2,1)S(1)}, bf16[9,32,32]{2,1,0:T(8,128)(2,1)}, u32[]{:S(2)}) copy-start(bf16[9,32,32]{2,1,0:T(8,128)(2,1)} %rest_1_.1) | copy-start | bytes 55300
  9.5 6.7 %copy-start.2 = (bf16[9,32,32]{2,1,0:T(8,128)(2,1)S(1)}, bf16[9,32,32]{2,1,0:T(8,128)(2,1)}, u32[]{:S(2)}) copy-start(bf16[9,32,32]{2,1,0:T(8,128)(2,1)} %rest_2_.1) | copy-start | bytes 55300
  9.5 6.7 %copy-start.3 = (bf16[9,32,32]{2,1,0:T(8,128)(2,1)S(1)}, bf16[9,32,32]{2,1,0:T(8,128)(2,1)}, u32[]{:S(2)}) copy-start(bf16[9,32,32]{2,1,0:T(8,128)(2,1)} %rest_3_.1) | copy-start | bytes 55300
  11.0 5.2 %collective-permute-start.4 = (bf16[288,256]{1,0:T(8,128)(2,1)S(1)}, bf16[288,256]{1,0:T(8,128)(2,1)S(1)}, u32[]{:S(2)}, u32[]{:S(2)}) collective-permute-start(bf16[288,256]{1,0:T(8,128)(2,1)S(1)} %get-tuple-element.108), channel_id=1, source_target_pairs={{0,4},{4,0},{8,12},{12,8},{16,20},{20,16},{24,28},{28,24},{1,5},{5... | collective-permute-start | bytes 442376 | tf_op jit(solution)/shard_map/ppermute | solution.py:627
  11.2 5.1 %collective-permute-start.5 = (bf16[288,256]{1,0:T(8,128)(2,1)S(1)}, bf16[288,256]{1,0:T(8,128)(2,1)S(1)}, u32[]{:S(2)}, u32[]{:S(2)}) collective-permute-start(bf16[288,256]{1,0:T(8,128)(2,1)S(1)} %get-tuple-element.109), channel_id=1, source_target_pairs={{4,8},{12,16},{20,24},{8,4},{16,12},{24,20},{5,9},{13,17},{21,25},... | collective-permute-start | bytes 442376 | tf_op jit(solution)/shard_map/ppermute | solution.py:627
  13.0 7.1 %collective-permute-start.7 = (bf16[448,256]{1,0:T(8,128)(2,1)S(1)}, bf16[448,256]{1,0:T(8,128)(2,1)S(1)}, u32[]{:S(2)}, u32[]{:S(2)}) collective-permute-start(bf16[448,256]{1,0:T(8,128)(2,1)S(1)} %shard_map.87), channel_id=1, source_target_pairs={{4,8},{12,16},{20,24},{8,4},{16,12},{24,20},{5,9},{13,17},{21,25},... | collective-permute-start | bytes 688136 | tf_op jit(solution)/shard_map/ppermute | solution.py:704
  27.4 1.3 %collective-permute-start.8 = (f32[144,128]{1,0:T(8,128)S(1)}, f32[144,128]{1,0:T(8,128)S(1)}, u32[]{:S(2)}, u32[]{:S(2)}) collective-permute-start(f32[144,128]{1,0:T(8,128)S(1)} %get-tuple-element.122), channel_id=1, source_target_pairs={{0,1},{1,0},{2,3},{3,2},{4,5},{5,4},{6,7},{7,6},{8,9},{9,8},{10,11... | collective-permute-start | bytes 221192 | tf_op jit(solution)/shard_map/ppermute | solution.py:751
  28.8 4.4 %collective-permute-start.9 = (f32[144,128]{1,0:T(8,128)S(1)}, f32[144,128]{1,0:T(8,128)S(1)}, u32[]{:S(2)}, u32[]{:S(2)}) collective-permute-start(f32[144,128]{1,0:T(8,128)S(1)} %add.12), channel_id=1, source_target_pairs={{0,2},{2,0},{1,3},{3,1},{4,6},{6,4},{5,7},{7,5},{8,10},{10,8},{9,1... | collective-permute-start | bytes 221192 | tf_op jit(solution)/shard_map/ppermute | solution.py:751
  33.2 8.8 %collective-permute-start.10 = (f32[144,128]{1,0:T(8,128)S(1)}, f32[144,128]{1,0:T(8,128)S(1)}, u32[]{:S(2)}, u32[]{:S(2)}) collective-permute-start(f32[144,128]{1,0:T(8,128)S(1)} %add.13), channel_id=1, source_target_pairs={{0,4},{4,0},{8,12},{12,8},{16,20},{20,16},{24,28},{28,24},{1,5},{5... | collective-permute-start | bytes 221192 | tf_op jit(solution)/shard_map/ppermute | solution.py:751
  42.0 4.4 %collective-permute-start.11 = (f32[144,128]{1,0:T(8,128)S(1)}, f32[144,128]{1,0:T(8,128)S(1)}, u32[]{:S(2)}, u32[]{:S(2)}) collective-permute-start(f32[144,128]{1,0:T(8,128)S(1)} %add.14), channel_id=1, source_target_pairs={{0,8},{4,12},{8,0},{12,4},{16,24},{20,28},{24,16},{28,20},{1,9},{5... | collective-permute-start | bytes 221192 | tf_op jit(solution)/shard_map/ppermute | solution.py:751
  46.4 6.9 %collective-permute-start.12 = (f32[144,128]{1,0:T(8,128)S(1)}, f32[144,128]{1,0:T(8,128)S(1)}, u32[]{:S(2)}, u32[]{:S(2)}) collective-permute-start(f32[144,128]{1,0:T(8,128)S(1)} %add.15.mine), channel_id=1, source_target_pairs={{0,16},{4,20},{8,24},{12,28},{16,0},{20,4},{24,8},{28,12},{1,17},{... | collective-permute-start | bytes 221192 | tf_op jit(solution)/shard_map/ppermute | solution.py:751

commit v11 on v10

--- a/solution.py
+++ b/solution.py
@@ -557,9 +557,9 @@
         out[:, :, part] = to_planes(rows[:, part], chans)
 
 
-def final_kernel(factor, mine, other, first, second):
+def final_kernel(factor, sums, first, second):
     chans = first.shape[1]
-    total = (mine[...] + other[...]) * factor
+    total = sums[...] * factor
     turned = total[0 : 3 * chans].T
     for b in range(3):
         for a in range(3):
@@ -740,29 +740,37 @@
         (feat_a, feat_b), shifts, feat, sides, act_grad, tuple(views), tuple(weights[:2]),
     )
 
+    lead = dp - 1
     steps = []
-    for axis, size in (("dp", dp), ("cols", cols), ("rows", rows)):
+    for axis, size in (("cols", cols), ("rows", rows)):
         bit = 1
         while bit < size:
-            steps.append((axis, [(i, i ^ bit) for i in range(size)]))
+            steps.append(
+                ((axis, "dp"), [(i * dp + lead, (i ^ bit) * dp + lead) for i in range(size)])
+            )
             bit *= 2
+    for i in range(lead):
+        grads = grads + lax.ppermute(grads, "dp", [(i, lead)])
     parts, prediction = 2, None
-    for step, (axis, pairs) in enumerate(steps):
-        other = lax.ppermute(grads, axis, pairs)
-        if 1 <= step <= parts:
+    for step, (axes, pairs) in enumerate(steps):
+        if step < parts:
+            grads, blended = lax.optimization_barrier((grads, blended))
+        other = lax.ppermute(grads, axes, pairs)
+        if step < parts:
             prediction = predict(
-                blended, weights[2], (chans, height, span), parts, step - 1, prediction
+                blended, weights[2], (chans, height, span), parts, step, prediction
             )
             other, prediction = lax.optimization_barrier((other, prediction))
-        if step < len(steps) - 1:
-            grads = grads + other
-            if step < parts:
-                grads, blended = lax.optimization_barrier((grads, blended))
+        grads = grads + other
+    result = grads
+    for i in range(lead):
+        back = lax.ppermute(grads, "dp", [(lead, i)])
+        result = jnp.where(lax.axis_index("dp") == i, back, result)
     factor = 1.0 / math.sqrt(imgs * dp * height * rows * span * cols)
     shape = jax.ShapeDtypeStruct((9, chans, chans), F32)
     first_grad, second_grad = call(
-        functools.partial(final_kernel, factor), (shape, shape), [], 2, 2
-    )(grads, other)
+        functools.partial(final_kernel, factor), (shape, shape), [], 1, 2
+    )(result)
     return (prediction[None], first_grad, second_grad)
 
 

time: 54.4 us -> 58.9 us (1.083)
  waiting for transfers between devices: 12.6 us -> 25.4 us
  starting transfers between devices: 19.9 us -> 11.3 us
    ppermute x5 -> x6, waiting for transfers between devices: 8.64 us -> 21.4 us  [the longest x1 20.5 us: shards(): back = lax.ppermute(grads, 'dp', [(lead, i)])]
    ppermute x5 -> x6, starting transfers between devices: 13.8 us -> 5.25 us  [the longest x4 2.66 us: shards(): other = lax.ppermute(grads, axes, pairs)]
  transfers between devices with their start and end apart: 11 -> 12, of which waited for: 7 -> 4; matrix products, arithmetic and copies ran while one was open for 1% -> 1% of each run, Pallas kernels for 18% -> 17%
where the time goes in v11:
time: 58.9 us; the launch traced here: 58.5 us
  waiting for transfers between devices  25.4 us (43%)
  Pallas kernels  19.3 us (33%)
  starting transfers between devices  11.3 us (19%)
  between operations  1.55 us (3%)
    ppermute x1, waiting for transfers between devices, shards(): back = lax.ppermute(grads, 'dp', [(lead, i)])  20.5 us
    pallas_call x1, Pallas kernels, main_pass(): call(main_kernel, (jax.ShapeDtypeStruct((9 * chans // 2, TILE), F32), bf(...  7.07 us
    ppermute x3, waiting for transfers between devices, swapped(): return [lax.ppermute(m, axis, p) for m, p in zip(messages, pairs)]  3.98 us
    pallas_call x1, Pallas kernels, shards(): call(functools.partial(back_kernel, ncols), (jax.ShapeDtypeStruct((full,...  3.83 us
    pallas_call x2, Pallas kernels, predict(): call(functools.partial(predict_kernel, part), jax.ShapeDtypeStruct(shape,...  3.35 us
    ppermute x1, starting transfers between devices, shards(): feat_a = lax.ppermute(message, 'rows', row_pairs[0])  3.03 us
    pallas_call x2, Pallas kernels, pack_rows(): call(functools.partial(feature_kernel, index, skip), message, [], 2, 16,...  2.75 us
    ppermute x4, starting transfers between devices, shards(): other = lax.ppermute(grads, axes, pairs)  2.66 us
  transfers between devices with their start and end apart: 12, of which 4 were waited for; matrix products, arithmetic and copies ran while one was open for 1% of the time, Pallas kernels for 17%

profile of v11, /device:TPU:0, one launch (start us, length us, event | category | flops | bytes accessed | tf_op | source)
XLA Modules:
  0.0 58.5 jit_solution(11878028335661541070)
XLA Ops:
  0.6 1.7 %shard_map.85 = (bf16[448,256]{1,0:T(8,128)(2,1)S(1)}, s32[8,128]{1,0:T(8,128)S(1)}) custom-call(s32[2,32]{1,0:T(2,128)} %bitcast.14, bf16[32,32,256]{2,1,0:T(8,128)(2,1)} %bitcast.9), custom_call_target="tpu_custom_call" | custom-call | bytes 4194304 | tf_op jit(solution)/shard_map/pallas_call | solution.py:634
  2.3 3.0 %collective-permute-start.6 = (bf16[448,256]{1,0:T(8,128)(2,1)S(1)}, bf16[448,256]{1,0:T(8,128)(2,1)S(1)}, u32[]{:S(2)}, u32[]{:S(2)}) collective-permute-start(bf16[448,256]{1,0:T(8,128)(2,1)S(1)} %get-tuple-element.110), channel_id=1, source_target_pairs={{0,4},{4,0},{8,12},{12,8},{16,20},{20,16},{24,28},{28,24},{1,5},{5... | collective-permute-start | bytes 688136 | tf_op jit(solution)/shard_map/ppermute | solution.py:690
  5.4 1.2 %shard_map.86 = bf16[256,128]{1,0:T(8,128)(2,1)S(1)} custom-call(bf16[32,32,256]{2,1,0:T(8,128)(2,1)} %bitcast.10, bf16[32,32,256]{2,1,0:T(8,128)(2,1)S(1)} %bitcast.7), custom_call_target="tpu_custom_call" | custom-call | flops 20000000000 | bytes 4194304 | tf_op jit(solution)/shard_map/pallas_call | solution.py:697
  6.6 1.6 %collective-permute-start.2 = (bf16[256,128]{1,0:T(8,128)(2,1)S(1)}, bf16[256,128]{1,0:T(8,128)(2,1)S(1)}, u32[]{:S(2)}, u32[]{:S(2)}) collective-permute-start(bf16[256,128]{1,0:T(8,128)(2,1)S(1)} %shard_map.86), channel_id=1, source_target_pairs={{0,2},{2,0},{1,3},{3,1},{4,6},{6,4},{5,7},{7,5},{8,10},{10,8},{9,1... | collective-permute-start | bytes 196616 | tf_op jit(solution)/shard_map/ppermute | solution.py:627
  8.2 1.1 %shard_map.87 = bf16[448,256]{1,0:T(8,128)(2,1)S(1)} custom-call(s32[2,32]{1,0:T(2,128)S(1)} %bitcast.15, bf16[32,32,256]{2,1,0:T(8,128)(2,1)S(1)} %bitcast.11), custom_call_target="tpu_custom_call" | custom-call | bytes 4194304 | tf_op jit(solution)/shard_map/pallas_call | solution.py:634
  9.5 1.4 %collective-permute-done.2.rest_0_ = bf16[256,128]{1,0:T(8,128)(2,1)S(1)} collective-permute-done((bf16[256,128]{1,0:T(8,128)(2,1)S(1)}, bf16[256,128]{1,0:T(8,128)(2,1)S(1)}, u32[]{:S(2)}, u32[]{:S(2)}) %collective-permute-start.2) | collective-permute-done | bytes 65568 | tf_op jit(solution)/shard_map/ppermute | solution.py:627
  11.2 0.7 %collective-permute-start.5 = (bf16[288,256]{1,0:T(8,128)(2,1)S(1)}, bf16[288,256]{1,0:T(8,128)(2,1)S(1)}, u32[]{:S(2)}, u32[]{:S(2)}) collective-permute-start(bf16[288,256]{1,0:T(8,128)(2,1)S(1)} %get-tuple-element.109), channel_id=1, source_target_pairs={{4,8},{12,16},{20,24},{8,4},{16,12},{24,20},{5,9},{13,17},{21,25},... | collective-permute-start | bytes 442376 | tf_op jit(solution)/shard_map/ppermute | solution.py:627
  11.8 0.7 %collective-permute-start.7 = (bf16[448,256]{1,0:T(8,128)(2,1)S(1)}, bf16[448,256]{1,0:T(8,128)(2,1)S(1)}, u32[]{:S(2)}, u32[]{:S(2)}) collective-permute-start(bf16[448,256]{1,0:T(8,128)(2,1)S(1)} %shard_map.87), channel_id=1, source_target_pairs={{4,8},{12,16},{20,24},{8,4},{16,12},{24,20},{5,9},{13,17},{21,25},... | collective-permute-start | bytes 688136 | tf_op jit(solution)/shard_map/ppermute | solution.py:704
  12.5 0.5 slice.3
  13.7 2.5 %collective-permute-done.4.msg_a = bf16[288,256]{1,0:T(8,128)(2,1)S(1)} collective-permute-done((bf16[288,256]{1,0:T(8,128)(2,1)S(1)}, bf16[288,256]{1,0:T(8,128)(2,1)S(1)}, u32[]{:S(2)}, u32[]{:S(2)}) %collective-permute-start.4) | collective-permute-done | bytes 147488 | tf_op jit(solution)/shard_map/ppermute | solution.py:627
  16.2 3.8 %shard_map.90 = (f32[1024,256]{1,0:T(8,128)S(1)}, bf16[1344,384]{1,0:T(8,128)(2,1)S(1)}, bf16[1344,384]{1,0:T(8,128)(2,1)S(1)}, bf16[1344,384]{1,0:T(8,128)(2,1)...) custom-call(bf16[1024,256]{1,0:T(8,128)(2,1)S(1)} %shard_map.88.cot_, ...), custom_call_target="tpu_custom_call" | custom-call | flops 8000000000 | bytes 4194304 | tf_op jit(solution)/shard_map/pallas_call | solution.py:714
  20.1 7.3 %conditional.1 = ((f32[144,128]{1,0:T(8,128)S(1)}, bf16[1088,384]{1,0:T(8,128)(2,1)S(1)})) conditional(s32[]{:T(128)} %bitcast.5, (s32[2,32]{1,0:T(2,128)S(1)}, bf16[32,32,256]{2,1,0:T(8,128)(2,1)S(1)}, bf16[448,256]{1,0:T(8,128)(2,1)S(1)}, bf16[448,256]{1,0:T(8,128)(2,1)S(1)}, bf16[32,96,128]{2,1,0:T(8,128)(2,1)S(1)}, ...), branch_computations={%region_0.0_spmd, %region_1.0_spmd} | conditional | flops 10001703936 | bytes 15859800 | solution.py:736
  20.1 7.1 %branch_1_fun.1 = (f32[144,128]{1,0:T(8,128)S(1)}, bf16[1088,384]{1,0:T(8,128)(2,1)S(1)}) custom-call(s32[2,32]{1,0:T(2,128)S(1)} %get-tuple-element.55.shifts, bf16[32,32,256]{2,1,0:T(8,128)(2,1)S(1)} %get-tuple-element.56.feat, bf16[448,256]{1,0:T(8,128)(2,1)S(1)} %get-tuple-element.57.feat_a, bf16[448,256]{1,0:T(8,128)(2,1)S(1)} %get-tuple-element.58.feat_b, ...), custom_call_target="tpu_custom_call" | custom-call | flops 10000000000 | bytes 4194304 | tf_op jit(solution)/shard_map/cond/branch_1_fun/pallas_call | solution.py:652
  27.4 1.3 %collective-permute-start.8 = (f32[144,128]{1,0:T(8,128)S(1)}, f32[144,128]{1,0:T(8,128)S(1)}, u32[]{:S(2)}, u32[]{:S(2)}) collective-permute-start(f32[144,128]{1,0:T(8,128)S(1)} %get-tuple-element.122), channel_id=1, source_target_pairs={{0,1},{2,3},{4,5},{6,7},{8,9},{10,11},{12,13},{14,15},{16,17},{18,... | collective-permute-start | bytes 221192 | tf_op jit(solution)/shard_map/ppermute | solution.py:753
  28.7 0.9 %collective-permute-done.8 = f32[144,128]{1,0:T(8,128)S(1)} collective-permute-done((f32[144,128]{1,0:T(8,128)S(1)}, f32[144,128]{1,0:T(8,128)S(1)}, u32[]{:S(2)}, u32[]{:S(2)}) %collective-permute-start.8) | collective-permute-done | bytes 73760 | tf_op jit(solution)/shard_map/ppermute | solution.py:753
  29.6 0.7 %collective-permute-start.9 = (f32[144,128]{1,0:T(8,128)S(1)}, f32[144,128]{1,0:T(8,128)S(1)}, u32[]{:S(2)}, u32[]{:S(2)}) collective-permute-start(f32[144,128]{1,0:T(8,128)S(1)} %add.15), channel_id=1, source_target_pairs={{1,3},{3,1},{5,7},{7,5},{9,11},{11,9},{13,15},{15,13},{17,19},{19,... | collective-permute-start | bytes 221192 | tf_op jit(solution)/shard_map/ppermute | solution.py:758
  30.3 1.7 %shard_map.91.rest_0_ = bf16[32,32,256]{2,1,0:T(8,128)(2,1)} custom-call(bf16[1088,384]{1,0:T(8,128)(2,1)S(1)} %get-tuple-element.129.blended, bf16[384,192]{1,0:T(8,128)(2,1)S(1)} %get-tuple-element.126.bands), custom_call_target="tpu_custom_call" | custom-call | flops 1000000000 | bytes 4194304 | tf_op jit(solution)/shard_map/pallas_call | solution.py:605
  32.0 0.7 %collective-permute-start.10 = (f32[144,128]{1,0:T(8,128)S(1)}, f32[144,128]{1,0:T(8,128)S(1)}, u32[]{:S(2)}, u32[]{:S(2)}) collective-permute-start(f32[144,128]{1,0:T(8,128)S(1)} %add.16), channel_id=1, source_target_pairs={{1,5},{5,1},{9,13},{13,9},{17,21},{21,17},{25,29},{29,25},{3,7},{7... | collective-permute-start | bytes 221192 | tf_op jit(solution)/shard_map/ppermute | solution.py:758
  32.6 1.7 %shard_map.92 = bf16[32,32,256]{2,1,0:T(8,128)(2,1)} custom-call(bf16[1088,384]{1,0:T(8,128)(2,1)S(1)} %get-tuple-element.129.blended, bf16[384,192]{1,0:T(8,128)(2,1)S(1)} %get-tuple-element.126.bands, bf16[32,32,256]{2,1,0:T(8,128)(2,1)} %shard_map.91.rest_0_), custom_call_target="tpu_custom_call", output_to_operand_aliasing={{}: (2, {})} | custom-call | flops 1000000000 | bytes 4194304 | tf_op jit(solution)/shard_map/pallas_call | solution.py:605
  34.3 0.7 %collective-permute-start.11 = (f32[144,128]{1,0:T(8,128)S(1)}, f32[144,128]{1,0:T(8,128)S(1)}, u32[]{:S(2)}, u32[]{:S(2)}) collective-permute-start(f32[144,128]{1,0:T(8,128)S(1)} %add.17), channel_id=1, source_target_pairs={{1,9},{5,13},{9,1},{13,5},{17,25},{21,29},{25,17},{29,21},{3,11},{... | collective-permute-start | bytes 221192 | tf_op jit(solution)/shard_map/ppermute | solution.py:758
  35.0 0.7 %collective-permute-start.12 = (f32[144,128]{1,0:T(8,128)S(1)}, f32[144,128]{1,0:T(8,128)S(1)}, u32[]{:S(2)}, u32[]{:S(2)}) collective-permute-start(f32[144,128]{1,0:T(8,128)S(1)} %add.18), channel_id=1, source_target_pairs={{1,17},{5,21},{9,25},{13,29},{17,1},{21,5},{25,9},{29,13},{3,19},{... | collective-permute-start | bytes 221192 | tf_op jit(solution)/shard_map/ppermute | solution.py:758
  35.7 1.3 %collective-permute-start.13 = (f32[144,128]{1,0:T(8,128)S(1)}, f32[144,128]{1,0:T(8,128)S(1)}, u32[]{:S(2)}, u32[]{:S(2)}) collective-permute-start(f32[144,128]{1,0:T(8,128)S(1)} %add.19), channel_id=1, source_target_pairs={{1,0},{3,2},{5,4},{7,6},{9,8},{11,10},{13,12},{15,14},{17,16},{19,... | collective-permute-start | bytes 221192 | tf_op jit(solution)/shard_map/ppermute | solution.py:767
  37.1 20.5 %collective-permute-done.13 = f32[144,128]{1,0:T(8,128)S(1)} collective-permute-done((f32[144,128]{1,0:T(8,128)S(1)}, f32[144,128]{1,0:T(8,128)S(1)}, u32[]{:S(2)}, u32[]{:S(2)}) %collective-permute-start.13) | collective-permute-done | bytes 73760 | tf_op jit(solution)/shard_map/ppermute | solution.py:767
  57.6 0.9 %shard_map.93 = (f32[9,32,32]{2,1,0:T(8,128)}, f32[9,32,32]{2,1,0:T(8,128)}) custom-call(f32[144,128]{1,0:T(8,128)S(1)} %broadcast_select_fusion.sums), custom_call_target="tpu_custom_call" | custom-call | bytes 4194304 | tf_op jit(solution)/shard_map/pallas_call | solution.py:771
  (31 shorter events, 0.5 us)
Async XLA Ops:
  0.6 4.7 %copy-start = (bf16[1,32,32,256]{3,2,1,0:T(8,128)(2,1)S(1)}, bf16[1,32,32,256]{3,2,1,0:T(8,128)(2,1)}, u32[]{:S(2)}) copy-start(bf16[1,32,32,256]{3,2,1,0:T(8,128)(2,1)} %param.13) | copy-start | bytes 1572868
  2.3 5.9 %copy-start.4 = (bf16[1,32,32,256]{3,2,1,0:T(8,128)(2,1)S(1)}, bf16[1,32,32,256]{3,2,1,0:T(8,128)(2,1)}, u32[]{:S(2)}) copy-start(bf16[1,32,32,256]{3,2,1,0:T(8,128)(2,1)} %param.8) | copy-start | bytes 1572868
  2.3 5.9 %copy-start.5 = (s32[1,32,2]{1,2,0:T(2,128)S(1)}, s32[1,32,2]{1,2,0:T(2,128)}, u32[]{:S(2)}) copy-start(s32[1,32,2]{1,2,0:T(2,128)} %param.9) | copy-start | bytes 772
  2.3 13.9 %collective-permute-start.6 = (bf16[448,256]{1,0:T(8,128)(2,1)S(1)}, bf16[448,256]{1,0:T(8,128)(2,1)S(1)}, u32[]{:S(2)}, u32[]{:S(2)}) collective-permute-start(bf16[448,256]{1,0:T(8,128)(2,1)S(1)} %get-tuple-element.110), channel_id=1, source_target_pairs={{0,4},{4,0},{8,12},{12,8},{16,20},{20,16},{24,28},{28,24},{1,5},{5... | collective-permute-start | bytes 688136 | tf_op jit(solution)/shard_map/ppermute | solution.py:690
  6.6 4.3 %collective-permute-start.2 = (bf16[256,128]{1,0:T(8,128)(2,1)S(1)}, bf16[256,128]{1,0:T(8,128)(2,1)S(1)}, u32[]{:S(2)}, u32[]{:S(2)}) collective-permute-start(bf16[256,128]{1,0:T(8,128)(2,1)S(1)} %shard_map.86), channel_id=1, source_target_pairs={{0,2},{2,0},{1,3},{3,1},{4,6},{6,4},{5,7},{7,5},{8,10},{10,8},{9,1... | collective-permute-start | bytes 196616 | tf_op jit(solution)/shard_map/ppermute | solution.py:627
  8.2 1.3 %collective-permute-start.3 = (s32[8,128]{1,0:T(8,128)S(1)}, s32[8,128]{1,0:T(8,128)S(1)}, u32[]{:S(2)}, u32[]{:S(2)}) collective-permute-start(s32[8,128]{1,0:T(8,128)S(1)} %get-tuple-element.105), channel_id=1, source_target_pairs={{0,1},{1,0},{2,3},{3,2},{4,5},{5,4},{6,7},{7,6},{8,9},{9,8},{10,11... | collective-permute-start | bytes 12296 | tf_op jit(solution)/shard_map/ppermute | solution.py:693
  9.5 6.7 %copy-start.1 = (bf16[9,32,32]{2,1,0:T(8,128)(2,1)S(1)}, bf16[9,32,32]{2,1,0:T(8,128)(2,1)}, u32[]{:S(2)}) copy-start(bf16[9,32,32]{2,1,0:T(8,128)(2,1)} %rest_1_.1) | copy-start | bytes 55300
  9.5 6.7 %copy-start.2 = (bf16[9,32,32]{2,1,0:T(8,128)(2,1)S(1)}, bf16[9,32,32]{2,1,0:T(8,128)(2,1)}, u32[]{:S(2)}) copy-start(bf16[9,32,32]{2,1,0:T(8,128)(2,1)} %rest_2_.1) | copy-start | bytes 55300
  9.5 6.7 %copy-start.3 = (bf16[9,32,32]{2,1,0:T(8,128)(2,1)S(1)}, bf16[9,32,32]{2,1,0:T(8,128)(2,1)}, u32[]{:S(2)}) copy-start(bf16[9,32,32]{2,1,0:T(8,128)(2,1)} %rest_3_.1) | copy-start | bytes 55300
  11.0 5.2 %collective-permute-start.4 = (bf16[288,256]{1,0:T(8,128)(2,1)S(1)}, bf16[288,256]{1,0:T(8,128)(2,1)S(1)}, u32[]{:S(2)}, u32[]{:S(2)}) collective-permute-start(bf16[288,256]{1,0:T(8,128)(2,1)S(1)} %get-tuple-element.108), channel_id=1, source_target_pairs={{0,4},{4,0},{8,12},{12,8},{16,20},{20,16},{24,28},{28,24},{1,5},{5... | collective-permute-start | bytes 442376 | tf_op jit(solution)/shard_map/ppermute | solution.py:627
  11.2 5.1 %collective-permute-start.5 = (bf16[288,256]{1,0:T(8,128)(2,1)S(1)}, bf16[288,256]{1,0:T(8,128)(2,1)S(1)}, u32[]{:S(2)}, u32[]{:S(2)}) collective-permute-start(bf16[288,256]{1,0:T(8,128)(2,1)S(1)} %get-tuple-element.109), channel_id=1, source_target_pairs={{4,8},{12,16},{20,24},{8,4},{16,12},{24,20},{5,9},{13,17},{21,25},... | collective-permute-start | bytes 442376 | tf_op jit(solution)/shard_map/ppermute | solution.py:627
  11.8 8.3 %collective-permute-start.7 = (bf16[448,256]{1,0:T(8,128)(2,1)S(1)}, bf16[448,256]{1,0:T(8,128)(2,1)S(1)}, u32[]{:S(2)}, u32[]{:S(2)}) collective-permute-start(bf16[448,256]{1,0:T(8,128)(2,1)S(1)} %shard_map.87), channel_id=1, source_target_pairs={{4,8},{12,16},{20,24},{8,4},{16,12},{24,20},{5,9},{13,17},{21,25},... | collective-permute-start | bytes 688136 | tf_op jit(solution)/shard_map/ppermute | solution.py:704
  27.4 2.2 %collective-permute-start.8 = (f32[144,128]{1,0:T(8,128)S(1)}, f32[144,128]{1,0:T(8,128)S(1)}, u32[]{:S(2)}, u32[]{:S(2)}) collective-permute-start(f32[144,128]{1,0:T(8,128)S(1)} %get-tuple-element.122), channel_id=1, source_target_pairs={{0,1},{2,3},{4,5},{6,7},{8,9},{10,11},{12,13},{14,15},{16,17},{18,... | collective-permute-start | bytes 221192 | tf_op jit(solution)/shard_map/ppermute | solution.py:753
  29.6 2.3 %collective-permute-start.9 = (f32[144,128]{1,0:T(8,128)S(1)}, f32[144,128]{1,0:T(8,128)S(1)}, u32[]{:S(2)}, u32[]{:S(2)}) collective-permute-start(f32[144,128]{1,0:T(8,128)S(1)} %add.15), channel_id=1, source_target_pairs={{1,3},{3,1},{5,7},{7,5},{9,11},{11,9},{13,15},{15,13},{17,19},{19,... | collective-permute-start | bytes 221192 | tf_op jit(solution)/shard_map/ppermute | solution.py:758
  32.0 2.4 %collective-permute-start.10 = (f32[144,128]{1,0:T(8,128)S(1)}, f32[144,128]{1,0:T(8,128)S(1)}, u32[]{:S(2)}, u32[]{:S(2)}) collective-permute-start(f32[144,128]{1,0:T(8,128)S(1)} %add.16), channel_id=1, source_target_pairs={{1,5},{5,1},{9,13},{13,9},{17,21},{21,17},{25,29},{29,25},{3,7},{7... | collective-permute-start | bytes 221192 | tf_op jit(solution)/shard_map/ppermute | solution.py:758
  34.3 0.7 %collective-permute-start.11 = (f32[144,128]{1,0:T(8,128)S(1)}, f32[144,128]{1,0:T(8,128)S(1)}, u32[]{:S(2)}, u32[]{:S(2)}) collective-permute-start(f32[144,128]{1,0:T(8,128)S(1)} %add.17), channel_id=1, source_target_pairs={{1,9},{5,13},{9,1},{13,5},{17,25},{21,29},{25,17},{29,21},{3,11},{... | collective-permute-start | bytes 221192 | tf_op jit(solution)/shard_map/ppermute | solution.py:758
  35.0 0.7 %collective-permute-start.12 = (f32[144,128]{1,0:T(8,128)S(1)}, f32[144,128]{1,0:T(8,128)S(1)}, u32[]{:S(2)}, u32[]{:S(2)}) collective-permute-start(f32[144,128]{1,0:T(8,128)S(1)} %add.18), channel_id=1, source_target_pairs={{1,17},{5,21},{9,25},{13,29},{17,1},{21,5},{25,9},{29,13},{3,19},{... | collective-permute-start | bytes 221192 | tf_op jit(solution)/shard_map/ppermute | solution.py:758
  35.7 21.8 %collective-permute-start.13 = (f32[144,128]{1,0:T(8,128)S(1)}, f32[144,128]{1,0:T(8,128)S(1)}, u32[]{:S(2)}, u32[]{:S(2)}) collective-permute-start(f32[144,128]{1,0:T(8,128)S(1)} %add.19), channel_id=1, source_target_pairs={{1,0},{3,2},{5,4},{7,6},{9,8},{11,10},{13,12},{15,14},{17,16},{19,... | collective-permute-start | bytes 221192 | tf_op jit(solution)/shard_map/ppermute | solution.py:767

commit v12 on v10

--- a/solution.py
+++ b/solution.py
@@ -559,7 +559,7 @@
 
 def final_kernel(factor, mine, other, first, second):
     chans = first.shape[1]
-    total = (mine[...] + other[...]) * factor
+    total = (mine[...].astype(F32) + other[...].astype(F32)) * factor
     turned = total[0 : 3 * chans].T
     for b in range(3):
         for a in range(3):
@@ -706,7 +706,7 @@
     halo = bf(CHALO * chans + ncols * packed * TILE // span, span)
     messages = call(edge_kernel, (halo, halo), [], 1 + ncols, 8)(cot_rows, *col_msgs)
     row_msgs = swapped(messages, "rows")
-    row_msgs, feat_a = lax.optimization_barrier((row_msgs, feat_a))
+    row_msgs, feat_a, total = lax.optimization_barrier((row_msgs, feat_a, total))
 
     tall_c = (height + 2 * CHALO) * chans
     view = bf(tall_c, width)
@@ -748,6 +748,8 @@
             bit *= 2
     parts, prediction = 2, None
     for step, (axis, pairs) in enumerate(steps):
+        if axis != "dp":
+            grads = lax.optimization_barrier(grads.astype(BF16))
         other = lax.ppermute(grads, axis, pairs)
         if 1 <= step <= parts:
             prediction = predict(
@@ -755,7 +757,7 @@
             )
             other, prediction = lax.optimization_barrier((other, prediction))
         if step < len(steps) - 1:
-            grads = grads + other
+            grads = grads.astype(F32) + other.astype(F32)
             if step < parts:
                 grads, blended = lax.optimization_barrier((grads, blended))
     factor = 1.0 / math.sqrt(imgs * dp * height * rows * span * cols)

time: 54.4 us -> 52 us (0.956)
  starting transfers between devices: 19.9 us -> 18.7 us
  waiting for transfers between devices: 12.6 us -> 11.4 us
    ppermute x5, waiting for transfers between devices: 8.64 us -> 6.21 us  [shards(): other = lax.ppermute(grads, axis, pairs)]
    ppermute x5, starting transfers between devices: 13.8 us -> 12.7 us  [shards(): other = lax.ppermute(grads, axis, pairs)]
    ppermute x3, waiting for transfers between devices: 3.98 us -> 5.15 us  [swapped(): return [lax.ppermute(m, axis, p) for m, p in zip(messages, pairs)]]
  transfers between devices with their start and end apart: 11 -> 11, of which waited for: 7 -> 7; matrix products, arithmetic and copies ran while one was open for 1% -> 1% of each run, Pallas kernels for 18% -> 19%
where the time goes in v12:
time: 52 us; the launch traced here: 51.8 us
  Pallas kernels  19.3 us (37%)
  starting transfers between devices  18.7 us (36%)
  waiting for transfers between devices  11.4 us (22%)
  between operations  1.48 us (3%)
  local copies, waits for them, and re-layouts  0.55 us (1%)
    ppermute x5, starting transfers between devices, shards(): other = lax.ppermute(grads, axis, pairs)  12.7 us
    pallas_call x1, Pallas kernels, main_pass(): call(main_kernel, (jax.ShapeDtypeStruct((9 * chans // 2, TILE), F32), bf(...  7.07 us
    ppermute x5, waiting for transfers between devices, shards(): other = lax.ppermute(grads, axis, pairs)  6.21 us
    ppermute x3, waiting for transfers between devices, swapped(): return [lax.ppermute(m, axis, p) for m, p in zip(messages, pairs)]  5.15 us
    pallas_call x1, Pallas kernels, shards(): call(functools.partial(back_kernel, ncols), (jax.ShapeDtypeStruct((full,...  3.83 us
    pallas_call x2, Pallas kernels, predict(): call(functools.partial(predict_kernel, part), jax.ShapeDtypeStruct(shape,...  3.34 us
    ppermute x1, starting transfers between devices, shards(): feat_a = lax.ppermute(message, 'rows', row_pairs[0])  3.03 us
    pallas_call x2, Pallas kernels, pack_rows(): call(functools.partial(feature_kernel, index, skip), message, [], 2, 16,...  2.75 us
  transfers between devices with their start and end apart: 11, of which 7 were waited for; matrix products, arithmetic and copies ran while one was open for 1% of the time, Pallas kernels for 19%

profile of v12, /device:TPU:0, one launch (start us, length us, event | category | flops | bytes accessed | tf_op | source)
XLA Modules:
  0.0 51.8 jit_solution(15529055518720383584)
XLA Ops:
  0.6 1.7 %shard_map.85 = (bf16[448,256]{1,0:T(8,128)(2,1)S(1)}, s32[8,128]{1,0:T(8,128)S(1)}) custom-call(s32[2,32]{1,0:T(2,128)} %bitcast.14, bf16[32,32,256]{2,1,0:T(8,128)(2,1)} %bitcast.9), custom_call_target="tpu_custom_call" | custom-call | bytes 4194304 | tf_op jit(solution)/shard_map/pallas_call | solution.py:634
  2.3 3.0 %collective-permute-start.6 = (bf16[448,256]{1,0:T(8,128)(2,1)S(1)}, bf16[448,256]{1,0:T(8,128)(2,1)S(1)}, u32[]{:S(2)}, u32[]{:S(2)}) collective-permute-start(bf16[448,256]{1,0:T(8,128)(2,1)S(1)} %get-tuple-element.110), channel_id=1, source_target_pairs={{0,4},{4,0},{8,12},{12,8},{16,20},{20,16},{24,28},{28,24},{1,5},{5... | collective-permute-start | bytes 688136 | tf_op jit(solution)/shard_map/ppermute | solution.py:690
  5.4 1.2 %shard_map.87 = bf16[256,128]{1,0:T(8,128)(2,1)S(1)} custom-call(bf16[32,32,256]{2,1,0:T(8,128)(2,1)} %bitcast.10, bf16[32,32,256]{2,1,0:T(8,128)(2,1)S(1)} %bitcast.7), custom_call_target="tpu_custom_call" | custom-call | flops 20000000000 | bytes 4194304 | tf_op jit(solution)/shard_map/pallas_call | solution.py:697
  6.6 1.6 %collective-permute-start.2 = (bf16[256,128]{1,0:T(8,128)(2,1)S(1)}, bf16[256,128]{1,0:T(8,128)(2,1)S(1)}, u32[]{:S(2)}, u32[]{:S(2)}) collective-permute-start(bf16[256,128]{1,0:T(8,128)(2,1)S(1)} %shard_map.87), channel_id=1, source_target_pairs={{0,2},{2,0},{1,3},{3,1},{4,6},{6,4},{5,7},{7,5},{8,10},{10,8},{9,1... | collective-permute-start | bytes 196616 | tf_op jit(solution)/shard_map/ppermute | solution.py:627
  8.2 1.1 %shard_map.88 = bf16[448,256]{1,0:T(8,128)(2,1)S(1)} custom-call(s32[2,32]{1,0:T(2,128)S(1)} %bitcast.15, bf16[32,32,256]{2,1,0:T(8,128)(2,1)S(1)} %bitcast.11), custom_call_target="tpu_custom_call" | custom-call | bytes 4194304 | tf_op jit(solution)/shard_map/pallas_call | solution.py:634
  9.5 1.4 %collective-permute-done.2.rest_0_ = bf16[256,128]{1,0:T(8,128)(2,1)S(1)} collective-permute-done((bf16[256,128]{1,0:T(8,128)(2,1)S(1)}, bf16[256,128]{1,0:T(8,128)(2,1)S(1)}, u32[]{:S(2)}, u32[]{:S(2)}) %collective-permute-start.2) | collective-permute-done | bytes 65568 | tf_op jit(solution)/shard_map/ppermute | solution.py:627
  11.2 0.7 %collective-permute-start.5 = (bf16[288,256]{1,0:T(8,128)(2,1)S(1)}, bf16[288,256]{1,0:T(8,128)(2,1)S(1)}, u32[]{:S(2)}, u32[]{:S(2)}) collective-permute-start(bf16[288,256]{1,0:T(8,128)(2,1)S(1)} %get-tuple-element.109), channel_id=1, source_target_pairs={{4,8},{12,16},{20,24},{8,4},{16,12},{24,20},{5,9},{13,17},{21,25},... | collective-permute-start | bytes 442376 | tf_op jit(solution)/shard_map/ppermute | solution.py:627
  11.8 0.7 %collective-permute-start.7 = (bf16[448,256]{1,0:T(8,128)(2,1)S(1)}, bf16[448,256]{1,0:T(8,128)(2,1)S(1)}, u32[]{:S(2)}, u32[]{:S(2)}) collective-permute-start(bf16[448,256]{1,0:T(8,128)(2,1)S(1)} %shard_map.88), channel_id=1, source_target_pairs={{4,8},{12,16},{20,24},{8,4},{16,12},{24,20},{5,9},{13,17},{21,25},... | collective-permute-start | bytes 688136 | tf_op jit(solution)/shard_map/ppermute | solution.py:704
  12.5 3.7 %collective-permute-done.4.msg_a = bf16[288,256]{1,0:T(8,128)(2,1)S(1)} collective-permute-done((bf16[288,256]{1,0:T(8,128)(2,1)S(1)}, bf16[288,256]{1,0:T(8,128)(2,1)S(1)}, u32[]{:S(2)}, u32[]{:S(2)}) %collective-permute-start.4) | collective-permute-done | bytes 147488 | tf_op jit(solution)/shard_map/ppermute | solution.py:627
  16.2 3.8 %shard_map.90 = (f32[1024,256]{1,0:T(8,128)S(1)}, bf16[1344,384]{1,0:T(8,128)(2,1)S(1)}, bf16[1344,384]{1,0:T(8,128)(2,1)S(1)}, bf16[1344,384]{1,0:T(8,128)(2,1)...) custom-call(bf16[1024,256]{1,0:T(8,128)(2,1)S(1)} %shard_map.86.cot_, ...), custom_call_target="tpu_custom_call" | custom-call | flops 8000000000 | bytes 4194304 | tf_op jit(solution)/shard_map/pallas_call | solution.py:714
  20.1 0.5 slice.3
  21.3 7.3 %conditional.1 = ((f32[144,128]{1,0:T(8,128)S(1)}, bf16[1088,384]{1,0:T(8,128)(2,1)S(1)})) conditional(s32[]{:T(128)} %bitcast.5, (s32[2,32]{1,0:T(2,128)S(1)}, bf16[32,32,256]{2,1,0:T(8,128)(2,1)S(1)}, bf16[448,256]{1,0:T(8,128)(2,1)S(1)}, bf16[448,256]{1,0:T(8,128)(2,1)S(1)}, bf16[32,96,128]{2,1,0:T(8,128)(2,1)S(1)}, ...), branch_computations={%region_0.0_spmd, %region_1.0_spmd} | conditional | flops 10001703936 | bytes 15859800 | solution.py:736
  21.3 7.1 %branch_1_fun.1 = (f32[144,128]{1,0:T(8,128)S(1)}, bf16[1088,384]{1,0:T(8,128)(2,1)S(1)}) custom-call(s32[2,32]{1,0:T(2,128)S(1)} %get-tuple-element.55.shifts, bf16[32,32,256]{2,1,0:T(8,128)(2,1)S(1)} %get-tuple-element.56.feat, bf16[448,256]{1,0:T(8,128)(2,1)S(1)} %get-tuple-element.57.feat_a, bf16[448,256]{1,0:T(8,128)(2,1)S(1)} %get-tuple-element.58.feat_b, ...), custom_call_target="tpu_custom_call" | custom-call | flops 10000000000 | bytes 4194304 | tf_op jit(solution)/shard_map/cond/branch_1_fun/pallas_call | solution.py:652
  28.7 1.3 %collective-permute-done.8 = f32[144,128]{1,0:T(8,128)S(1)} collective-permute-done((f32[144,128]{1,0:T(8,128)S(1)}, f32[144,128]{1,0:T(8,128)S(1)}, u32[]{:S(2)}, u32[]{:S(2)}) %collective-permute-start.8) | collective-permute-done | bytes 73760 | tf_op jit(solution)/shard_map/ppermute | solution.py:753
  29.9 1.5 %collective-permute-start.9 = (bf16[144,128]{1,0:T(8,128)(2,1)S(1)}, bf16[144,128]{1,0:T(8,128)(2,1)S(1)}, u32[]{:S(2)}, u32[]{:S(2)}) collective-permute-start(bf16[144,128]{1,0:T(8,128)(2,1)S(1)} %add.12), channel_id=1, source_target_pairs={{0,2},{2,0},{1,3},{3,1},{4,6},{6,4},{5,7},{7,5},{8,10},{10,8},{9,1... | collective-permute-start | bytes 110600 | tf_op jit(solution)/shard_map/ppermute | solution.py:753
  31.5 1.7 %shard_map.91.rest_0_ = bf16[32,32,256]{2,1,0:T(8,128)(2,1)} custom-call(bf16[1088,384]{1,0:T(8,128)(2,1)S(1)} %get-tuple-element.131.blended, bf16[384,192]{1,0:T(8,128)(2,1)S(1)} %get-tuple-element.128.bands), custom_call_target="tpu_custom_call" | custom-call | flops 1000000000 | bytes 4194304 | tf_op jit(solution)/shard_map/pallas_call | solution.py:605
  33.1 0.8 %collective-permute-done.9 = bf16[144,128]{1,0:T(8,128)(2,1)S(1)} collective-permute-done((bf16[144,128]{1,0:T(8,128)(2,1)S(1)}, bf16[144,128]{1,0:T(8,128)(2,1)S(1)}, u32[]{:S(2)}, u32[]{:S(2)}) %collective-permute-start.9) | collective-permute-done | bytes 36896 | tf_op jit(solution)/shard_map/ppermute | solution.py:753
  34.0 5.4 %collective-permute-start.10 = (bf16[144,128]{1,0:T(8,128)(2,1)S(1)}, bf16[144,128]{1,0:T(8,128)(2,1)S(1)}, u32[]{:S(2)}, u32[]{:S(2)}) collective-permute-start(bf16[144,128]{1,0:T(8,128)(2,1)S(1)} %convert_add_fusion), channel_id=1, source_target_pairs={{0,4},{4,0},{8,12},{12,8},{16,20},{20,16},{24,28},{28,24},{1,5},{5... | collective-permute-start | bytes 110600 | tf_op jit(solution)/shard_map/ppermute | solution.py:753
  39.4 1.7 %shard_map.92 = bf16[32,32,256]{2,1,0:T(8,128)(2,1)} custom-call(bf16[1088,384]{1,0:T(8,128)(2,1)S(1)} %get-tuple-element.131.blended, bf16[384,192]{1,0:T(8,128)(2,1)S(1)} %get-tuple-element.128.bands, bf16[32,32,256]{2,1,0:T(8,128)(2,1)} %shard_map.91.rest_0_), custom_call_target="tpu_custom_call", output_to_operand_aliasing={{}: (2, {})} | custom-call | flops 1000000000 | bytes 4194304 | tf_op jit(solution)/shard_map/pallas_call | solution.py:605
  41.4 2.3 %collective-permute-start.11 = (bf16[144,128]{1,0:T(8,128)(2,1)S(1)}, bf16[144,128]{1,0:T(8,128)(2,1)S(1)}, u32[]{:S(2)}, u32[]{:S(2)}) collective-permute-start(bf16[144,128]{1,0:T(8,128)(2,1)S(1)} %add_convert_fusion.1), channel_id=1, source_target_pairs={{0,8},{4,12},{8,0},{12,4},{16,24},{20,28},{24,16},{28,20},{1,9},{5... | collective-permute-start | bytes 110600 | tf_op jit(solution)/shard_map/ppermute | solution.py:753
  43.6 1.9 %collective-permute-done.11 = bf16[144,128]{1,0:T(8,128)(2,1)S(1)} collective-permute-done((bf16[144,128]{1,0:T(8,128)(2,1)S(1)}, bf16[144,128]{1,0:T(8,128)(2,1)S(1)}, u32[]{:S(2)}, u32[]{:S(2)}) %collective-permute-start.11) | collective-permute-done | bytes 36896 | tf_op jit(solution)/shard_map/ppermute | solution.py:753
  45.6 3.3 %collective-permute-start.12 = (bf16[144,128]{1,0:T(8,128)(2,1)S(1)}, bf16[144,128]{1,0:T(8,128)(2,1)S(1)}, u32[]{:S(2)}, u32[]{:S(2)}) collective-permute-start(bf16[144,128]{1,0:T(8,128)(2,1)S(1)} %add_convert_fusion.mine), channel_id=1, source_target_pairs={{0,16},{4,20},{8,24},{12,28},{16,0},{20,4},{24,8},{28,12},{1,17},{... | collective-permute-start | bytes 110600 | tf_op jit(solution)/shard_map/ppermute | solution.py:753
  48.9 1.9 %collective-permute-done.12.other = bf16[144,128]{1,0:T(8,128)(2,1)S(1)} collective-permute-done((bf16[144,128]{1,0:T(8,128)(2,1)S(1)}, bf16[144,128]{1,0:T(8,128)(2,1)S(1)}, u32[]{:S(2)}, u32[]{:S(2)}) %collective-permute-start.12) | collective-permute-done | bytes 36896 | tf_op jit(solution)/shard_map/ppermute | solution.py:753
  50.8 0.9 %shard_map.93 = (f32[9,32,32]{2,1,0:T(8,128)}, f32[9,32,32]{2,1,0:T(8,128)}) custom-call(bf16[144,128]{1,0:T(8,128)(2,1)S(1)} %add_convert_fusion.mine, bf16[144,128]{1,0:T(8,128)(2,1)S(1)} %collective-permute-done.12.other), custom_call_target="tpu_custom_call" | custom-call | bytes 4194304 | tf_op jit(solution)/shard_map/pallas_call | solution.py:765
  (27 shorter events, 0.8 us)
Async XLA Ops:
  0.6 4.7 %copy-start = (bf16[1,32,32,256]{3,2,1,0:T(8,128)(2,1)S(1)}, bf16[1,32,32,256]{3,2,1,0:T(8,128)(2,1)}, u32[]{:S(2)}) copy-start(bf16[1,32,32,256]{3,2,1,0:T(8,128)(2,1)} %param.13) | copy-start | bytes 1572868
  2.3 5.9 %copy-start.4 = (bf16[1,32,32,256]{3,2,1,0:T(8,128)(2,1)S(1)}, bf16[1,32,32,256]{3,2,1,0:T(8,128)(2,1)}, u32[]{:S(2)}) copy-start(bf16[1,32,32,256]{3,2,1,0:T(8,128)(2,1)} %param.8) | copy-start | bytes 1572868
  2.3 5.9 %copy-start.5 = (s32[1,32,2]{1,2,0:T(2,128)S(1)}, s32[1,32,2]{1,2,0:T(2,128)}, u32[]{:S(2)}) copy-start(s32[1,32,2]{1,2,0:T(2,128)} %param.9) | copy-start | bytes 772
  2.3 13.9 %collective-permute-start.6 = (bf16[448,256]{1,0:T(8,128)(2,1)S(1)}, bf16[448,256]{1,0:T(8,128)(2,1)S(1)}, u32[]{:S(2)}, u32[]{:S(2)}) collective-permute-start(bf16[448,256]{1,0:T(8,128)(2,1)S(1)} %get-tuple-element.110), channel_id=1, source_target_pairs={{0,4},{4,0},{8,12},{12,8},{16,20},{20,16},{24,28},{28,24},{1,5},{5... | collective-permute-start | bytes 688136 | tf_op jit(solution)/shard_map/ppermute | solution.py:690
  6.6 4.3 %collective-permute-start.2 = (bf16[256,128]{1,0:T(8,128)(2,1)S(1)}, bf16[256,128]{1,0:T(8,128)(2,1)S(1)}, u32[]{:S(2)}, u32[]{:S(2)}) collective-permute-start(bf16[256,128]{1,0:T(8,128)(2,1)S(1)} %shard_map.87), channel_id=1, source_target_pairs={{0,2},{2,0},{1,3},{3,1},{4,6},{6,4},{5,7},{7,5},{8,10},{10,8},{9,1... | collective-permute-start | bytes 196616 | tf_op jit(solution)/shard_map/ppermute | solution.py:627
  8.2 1.3 %collective-permute-start.3 = (s32[8,128]{1,0:T(8,128)S(1)}, s32[8,128]{1,0:T(8,128)S(1)}, u32[]{:S(2)}, u32[]{:S(2)}) collective-permute-start(s32[8,128]{1,0:T(8,128)S(1)} %get-tuple-element.106), channel_id=1, source_target_pairs={{0,1},{1,0},{2,3},{3,2},{4,5},{5,4},{6,7},{7,6},{8,9},{9,8},{10,11... | collective-permute-start | bytes 12296 | tf_op jit(solution)/shard_map/ppermute | solution.py:693
  9.5 6.7 %copy-start.1 = (bf16[9,32,32]{2,1,0:T(8,128)(2,1)S(1)}, bf16[9,32,32]{2,1,0:T(8,128)(2,1)}, u32[]{:S(2)}) copy-start(bf16[9,32,32]{2,1,0:T(8,128)(2,1)} %rest_1_.1) | copy-start | bytes 55300
  9.5 6.7 %copy-start.2 = (bf16[9,32,32]{2,1,0:T(8,128)(2,1)S(1)}, bf16[9,32,32]{2,1,0:T(8,128)(2,1)}, u32[]{:S(2)}) copy-start(bf16[9,32,32]{2,1,0:T(8,128)(2,1)} %rest_2_.1) | copy-start | bytes 55300
  9.5 6.7 %copy-start.3 = (bf16[9,32,32]{2,1,0:T(8,128)(2,1)S(1)}, bf16[9,32,32]{2,1,0:T(8,128)(2,1)}, u32[]{:S(2)}) copy-start(bf16[9,32,32]{2,1,0:T(8,128)(2,1)} %rest_3_.1) | copy-start | bytes 55300
  11.0 5.2 %collective-permute-start.4 = (bf16[288,256]{1,0:T(8,128)(2,1)S(1)}, bf16[288,256]{1,0:T(8,128)(2,1)S(1)}, u32[]{:S(2)}, u32[]{:S(2)}) collective-permute-start(bf16[288,256]{1,0:T(8,128)(2,1)S(1)} %get-tuple-element.108), channel_id=1, source_target_pairs={{0,4},{4,0},{8,12},{12,8},{16,20},{20,16},{24,28},{28,24},{1,5},{5... | collective-permute-start | bytes 442376 | tf_op jit(solution)/shard_map/ppermute | solution.py:627
  11.2 5.1 %collective-permute-start.5 = (bf16[288,256]{1,0:T(8,128)(2,1)S(1)}, bf16[288,256]{1,0:T(8,128)(2,1)S(1)}, u32[]{:S(2)}, u32[]{:S(2)}) collective-permute-start(bf16[288,256]{1,0:T(8,128)(2,1)S(1)} %get-tuple-element.109), channel_id=1, source_target_pairs={{4,8},{12,16},{20,24},{8,4},{16,12},{24,20},{5,9},{13,17},{21,25},... | collective-permute-start | bytes 442376 | tf_op jit(solution)/shard_map/ppermute | solution.py:627
  11.8 9.4 %collective-permute-start.7 = (bf16[448,256]{1,0:T(8,128)(2,1)S(1)}, bf16[448,256]{1,0:T(8,128)(2,1)S(1)}, u32[]{:S(2)}, u32[]{:S(2)}) collective-permute-start(bf16[448,256]{1,0:T(8,128)(2,1)S(1)} %shard_map.88), channel_id=1, source_target_pairs={{4,8},{12,16},{20,24},{8,4},{16,12},{24,20},{5,9},{13,17},{21,25},... | collective-permute-start | bytes 688136 | tf_op jit(solution)/shard_map/ppermute | solution.py:704
  28.6 1.3 %collective-permute-start.8 = (f32[144,128]{1,0:T(8,128)S(1)}, f32[144,128]{1,0:T(8,128)S(1)}, u32[]{:S(2)}, u32[]{:S(2)}) collective-permute-start(f32[144,128]{1,0:T(8,128)S(1)} %get-tuple-element.124), channel_id=1, source_target_pairs={{0,1},{1,0},{2,3},{3,2},{4,5},{5,4},{6,7},{7,6},{8,9},{9,8},{10,11... | collective-permute-start | bytes 221192 | tf_op jit(solution)/shard_map/ppermute | solution.py:753
  29.9 4.0 %collective-permute-start.9 = (bf16[144,128]{1,0:T(8,128)(2,1)S(1)}, bf16[144,128]{1,0:T(8,128)(2,1)S(1)}, u32[]{:S(2)}, u32[]{:S(2)}) collective-permute-start(bf16[144,128]{1,0:T(8,128)(2,1)S(1)} %add.12), channel_id=1, source_target_pairs={{0,2},{2,0},{1,3},{3,1},{4,6},{6,4},{5,7},{7,5},{8,10},{10,8},{9,1... | collective-permute-start | bytes 110600 | tf_op jit(solution)/shard_map/ppermute | solution.py:753
  34.0 7.4 %collective-permute-start.10 = (bf16[144,128]{1,0:T(8,128)(2,1)S(1)}, bf16[144,128]{1,0:T(8,128)(2,1)S(1)}, u32[]{:S(2)}, u32[]{:S(2)}) collective-permute-start(bf16[144,128]{1,0:T(8,128)(2,1)S(1)} %convert_add_fusion), channel_id=1, source_target_pairs={{0,4},{4,0},{8,12},{12,8},{16,20},{20,16},{24,28},{28,24},{1,5},{5... | collective-permute-start | bytes 110600 | tf_op jit(solution)/shard_map/ppermute | solution.py:753
  41.4 4.2 %collective-permute-start.11 = (bf16[144,128]{1,0:T(8,128)(2,1)S(1)}, bf16[144,128]{1,0:T(8,128)(2,1)S(1)}, u32[]{:S(2)}, u32[]{:S(2)}) collective-permute-start(bf16[144,128]{1,0:T(8,128)(2,1)S(1)} %add_convert_fusion.1), channel_id=1, source_target_pairs={{0,8},{4,12},{8,0},{12,4},{16,24},{20,28},{24,16},{28,20},{1,9},{5... | collective-permute-start | bytes 110600 | tf_op jit(solution)/shard_map/ppermute | solution.py:753
  45.6 5.3 %collective-permute-start.12 = (bf16[144,128]{1,0:T(8,128)(2,1)S(1)}, bf16[144,128]{1,0:T(8,128)(2,1)S(1)}, u32[]{:S(2)}, u32[]{:S(2)}) collective-permute-start(bf16[144,128]{1,0:T(8,128)(2,1)S(1)} %add_convert_fusion.mine), channel_id=1, source_target_pairs={{0,16},{4,20},{8,24},{12,28},{16,0},{20,4},{24,8},{28,12},{1,17},{... | collective-permute-start | bytes 110600 | tf_op jit(solution)/shard_map/ppermute | solution.py:753

commit v13 on v10

--- a/solution.py
+++ b/solution.py
@@ -203,10 +203,20 @@
     return (lane < span) | ((lane < middle) & has_right) | ((lane >= middle) & has_left)
 
 
-def block_ones(width):
-    row = lax.broadcasted_iota(jnp.int32, (width, width), 0) // POOL
-    col = lax.broadcasted_iota(jnp.int32, (width, width), 1) // POOL
-    return jnp.where(row == col, 1.0, 0.0).astype(BF16)
+def cell_matrix(width, by_cell):
+    shape = (TILE, width) if by_cell else (width, TILE)
+    lane = lax.broadcasted_iota(jnp.int32, shape, 1 if by_cell else 0)
+    cell = lax.broadcasted_iota(jnp.int32, shape, 0 if by_cell else 1)
+    place = lane // POOL + jnp.where(lane >= width - TILE // 2, TILE - width // POOL, 0)
+    return jnp.where(place == cell, 1.0, 0.0).astype(BF16)
+
+
+def cells_seen(shape, span):
+    _, _, has_left, has_right = has_sides()
+    lane = lanes_of(shape)
+    count = span // POOL
+    middle = (count + TILE) // 2
+    return (lane < count) | ((lane < middle) & has_right) | ((lane >= middle) & has_left)
 
 
 def store_split(high, low, at, total):
@@ -215,9 +225,22 @@
     low[at, :] = (total - top.astype(F32)).astype(BF16)
 
 
-def block_sums(high, low, ones):
-    return jnp.dot(high[...], ones, preferred_element_type=F32) + jnp.dot(
-        low[...], ones, preferred_element_type=F32
+def block_sums(high, low):
+    matrix = cell_matrix(high.shape[1], False)
+    return jnp.dot(high[...], matrix, preferred_element_type=F32) + jnp.dot(
+        low[...], matrix, preferred_element_type=F32
+    )
+
+
+def spread(rows, width, count):
+    values = jnp.concatenate(rows, axis=0)
+    top = values.astype(BF16)
+    rest = (values - top.astype(F32)).astype(BF16)
+    matrix = cell_matrix(width, True)[:, 0:count]
+    return jnp.dot(
+        jnp.concatenate([top, rest], axis=1),
+        jnp.concatenate([matrix, matrix], axis=0),
+        preferred_element_type=F32,
     )
 
 
@@ -271,7 +294,6 @@
     width = span + TILE
     groups = height // POOL
     has_up, has_down, _, _ = has_sides()
-    seen_cols = columns_seen((chans, width), span)
 
     fill_turned_bands(bands_f, second, POOL)
     bands[...] = bands_f[...].T.astype(BF16)
@@ -343,21 +365,25 @@
         return 0
 
     lax.fori_loop(0, groups + 2, group, 0, unroll=5)
-    sums = block_sums(high, low, block_ones(width))
+    sums = block_sums(high, low)
+    seen_cells = cells_seen((chans, TILE), span)
     for g in range(groups + 2):
         at = rows_at(g, chans)
-        seen = seen_cols
+        seen = seen_cells
         if g == 0:
             seen = seen & has_up
         elif g == groups + 1:
             seen = seen & has_down
         coarse[at] = jnp.where(seen, sums[at], 0.0).astype(BF16)
+    means = []
     for g in range(groups):
         parts = jnp.dot(small[...], coarse[rows_at(g, chans, 3), :], preferred_element_type=F32)
-        mean = conv_sum(parts, chans, POOL)[:, 0:span] * (1.0 / POOL**2)
-        for k in range(POOL):
-            r = g * POOL + k
-            act_grad[rows_at(r, chans), :] = back[rows_at(r + POOL, chans), :].astype(F32) + mean
+        means.append(conv_sum(parts, chans, 1) * (1.0 / POOL**2))
+    mean = spread(means, width, span)
+    for r in range(height):
+        act_grad[rows_at(r, chans), :] = (
+            back[rows_at(r + POOL, chans), :].astype(F32) + mean[rows_at(r // POOL, chans)]
+        )
 
 
 def correlate(u, u0, views, v0, acc, height, chans, span):
@@ -502,26 +528,30 @@
     for g in (0, 1, groups + 2, groups + 3):
         first_group(g, False)
     lax.fori_loop(2, groups + 2, lambda g, _: first_group(g, True), 0, unroll=4)
-    sums = block_sums(high, low, block_ones(width))
+    sums = block_sums(high, low)
+    seen_cells = cells_seen((chans, TILE), span)
     for g in range(groups + 4):
         at = rows_at(g, chans)
-        seen = seen_cols
+        seen = seen_cells
         if g < 2:
             seen = seen & has_up
         elif g >= groups + 2:
             seen = seen & has_down
         pooled[at] = jnp.where(seen, sums[at] * (1.0 / POOL**2), 0.0).astype(BF16)
 
+    bottles = []
     for g in range(groups + 2):
         parts = jnp.dot(small[...], pooled[rows_at(g, chans, 3), :], preferred_element_type=F32)
-        bottle_row = conv_sum(parts, chans, POOL)
+        bottles.append(conv_sum(parts, chans, 1))
+    bottle = spread(bottles, width, width)
+    for g in range(groups + 2):
         rows, seen = range(POOL), seen_cols
         if g == 0:
             rows, seen = (POOL - 1,), seen & has_up
         elif g == groups + 1:
             rows, seen = (0,), seen & has_down
         for k in rows:
-            row = act[rows_at((g + 1) * POOL + k, chans), :].astype(F32) + bottle_row
+            row = act[rows_at((g + 1) * POOL + k, chans), :].astype(F32) + bottle[rows_at(g, chans)]
             blended[rows_at(g * POOL + k - POOL + 1, chans), :] = jnp.where(seen, row, 0.0).astype(
                 BF16
             )
@@ -559,7 +589,7 @@
 
 def final_kernel(factor, mine, other, first, second):
     chans = first.shape[1]
-    total = (mine[...] + other[...]) * factor
+    total = (mine[...].astype(F32) + other[...].astype(F32)) * factor
     turned = total[0 : 3 * chans].T
     for b in range(3):
         for a in range(3):
@@ -658,7 +688,8 @@
         ]
         + [pltpu.VMEM((tall * chans, width), BF16)] * 3
         + [pltpu.VMEM(((height + 4 * POOL) * chans, width), BF16)]
-        + [pltpu.VMEM(((groups + 4) * chans, width), BF16)] * 3
+        + [pltpu.VMEM(((groups + 4) * chans, width), BF16)] * 2
+        + [pltpu.VMEM(((groups + 4) * chans, TILE), BF16)]
         + [
             pltpu.VMEM((full, span), BF16),
             pltpu.VMEM((band, POOL * chans), F32),
@@ -707,6 +738,7 @@
     messages = call(edge_kernel, (halo, halo), [], 1 + ncols, 8)(cot_rows, *col_msgs)
     row_msgs = swapped(messages, "rows")
     row_msgs, feat_a = lax.optimization_barrier((row_msgs, feat_a))
+    row_msgs[0], total = lax.optimization_barrier((row_msgs[0], total))
 
     tall_c = (height + 2 * CHALO) * chans
     view = bf(tall_c, width)
@@ -719,7 +751,8 @@
             bf(3 * POOL * chans, (POOL + 2) * chans),
         ),
         [pltpu.VMEM(((height + 2 * POOL) * chans, span), BF16)]
-        + [pltpu.VMEM(((groups + 2) * chans, width), BF16)] * 3
+        + [pltpu.VMEM(((groups + 2) * chans, width), BF16)] * 2
+        + [pltpu.VMEM(((groups + 2) * chans, TILE), BF16)]
         + [
             pltpu.VMEM((band, POOL * chans), F32),
             pltpu.VMEM((POOL * chans, band), BF16),
@@ -748,6 +781,8 @@
             bit *= 2
     parts, prediction = 2, None
     for step, (axis, pairs) in enumerate(steps):
+        if step == len(steps) - 1:
+            grads = lax.optimization_barrier(grads.astype(BF16))
         other = lax.ppermute(grads, axis, pairs)
         if 1 <= step <= parts:
             prediction = predict(

time: 54.4 us -> 53.2 us (0.978)
  starting transfers between devices: 19.9 us -> 18.9 us
    ppermute x5, waiting for transfers between devices: 8.64 us -> 7.38 us  [shards(): other = lax.ppermute(grads, axis, pairs)]
    ppermute x3, waiting for transfers between devices: 3.98 us -> 5.15 us  [swapped(): return [lax.ppermute(m, axis, p) for m, p in zip(messages, pairs)]]
    ppermute x5, starting transfers between devices: 13.8 us -> 12.8 us  [shards(): other = lax.ppermute(grads, axis, pairs)]
where the time goes in v13:
time: 53.2 us; the launch traced here: 53 us
  Pallas kernels  19.2 us (36%)
  starting transfers between devices  18.9 us (36%)
  waiting for transfers between devices  12.5 us (23%)
  between operations  1.48 us (3%)
  local copies, waits for them, and re-layouts  0.55 us (1%)
    ppermute x5, starting transfers between devices, shards(): other = lax.ppermute(grads, axis, pairs)  12.8 us
    ppermute x5, waiting for transfers between devices, shards(): other = lax.ppermute(grads, axis, pairs)  7.38 us
    pallas_call x1, Pallas kernels, main_pass(): call(main_kernel, (jax.ShapeDtypeStruct((9 * chans // 2, TILE), F32), bf(...  7.05 us
    ppermute x3, waiting for transfers between devices, swapped(): return [lax.ppermute(m, axis, p) for m, p in zip(messages, pairs)]  5.15 us
    pallas_call x1, Pallas kernels, shards(): call(functools.partial(back_kernel, ncols), (jax.ShapeDtypeStruct((full,...  3.73 us
    pallas_call x2, Pallas kernels, predict(): call(functools.partial(predict_kernel, part), jax.ShapeDtypeStruct(shape,...  3.34 us
    ppermute x1, starting transfers between devices, shards(): feat_a = lax.ppermute(message, 'rows', row_pairs[0])  3.03 us
    pallas_call x2, Pallas kernels, pack_rows(): call(functools.partial(feature_kernel, index, skip), message, [], 2, 16,...  2.75 us
  transfers between devices with their start and end apart: 11, of which 7 were waited for; matrix products, arithmetic and copies ran while one was open for 1% of the time, Pallas kernels for 18%

profile of v13, /device:TPU:0, one launch (start us, length us, event | category | flops | bytes accessed | tf_op | source)
XLA Modules:
  0.0 53.0 jit_solution(9873712489901677289)
XLA Ops:
  0.6 1.7 %shard_map.85 = (bf16[448,256]{1,0:T(8,128)(2,1)S(1)}, s32[8,128]{1,0:T(8,128)S(1)}) custom-call(s32[2,32]{1,0:T(2,128)} %bitcast.14, bf16[32,32,256]{2,1,0:T(8,128)(2,1)} %bitcast.9), custom_call_target="tpu_custom_call" | custom-call | bytes 4194304 | tf_op jit(solution)/shard_map/pallas_call | solution.py:664
  2.3 3.0 %collective-permute-start.6 = (bf16[448,256]{1,0:T(8,128)(2,1)S(1)}, bf16[448,256]{1,0:T(8,128)(2,1)S(1)}, u32[]{:S(2)}, u32[]{:S(2)}) collective-permute-start(bf16[448,256]{1,0:T(8,128)(2,1)S(1)} %get-tuple-element.111), channel_id=1, source_target_pairs={{0,4},{4,0},{8,12},{12,8},{16,20},{20,16},{24,28},{28,24},{1,5},{5... | collective-permute-start | bytes 688136 | tf_op jit(solution)/shard_map/ppermute | solution.py:721
  5.4 1.2 %shard_map.87 = bf16[256,128]{1,0:T(8,128)(2,1)S(1)} custom-call(bf16[32,32,256]{2,1,0:T(8,128)(2,1)} %bitcast.10, bf16[32,32,256]{2,1,0:T(8,128)(2,1)S(1)} %bitcast.7), custom_call_target="tpu_custom_call" | custom-call | flops 20000000000 | bytes 4194304 | tf_op jit(solution)/shard_map/pallas_call | solution.py:728
  6.6 1.6 %collective-permute-start.2 = (bf16[256,128]{1,0:T(8,128)(2,1)S(1)}, bf16[256,128]{1,0:T(8,128)(2,1)S(1)}, u32[]{:S(2)}, u32[]{:S(2)}) collective-permute-start(bf16[256,128]{1,0:T(8,128)(2,1)S(1)} %shard_map.87), channel_id=1, source_target_pairs={{0,2},{2,0},{1,3},{3,1},{4,6},{6,4},{5,7},{7,5},{8,10},{10,8},{9,1... | collective-permute-start | bytes 196616 | tf_op jit(solution)/shard_map/ppermute | solution.py:657
  8.2 1.1 %shard_map.88 = bf16[448,256]{1,0:T(8,128)(2,1)S(1)} custom-call(s32[2,32]{1,0:T(2,128)S(1)} %bitcast.15, bf16[32,32,256]{2,1,0:T(8,128)(2,1)S(1)} %bitcast.11), custom_call_target="tpu_custom_call" | custom-call | bytes 4194304 | tf_op jit(solution)/shard_map/pallas_call | solution.py:664
  9.5 1.4 %collective-permute-done.2.rest_0_ = bf16[256,128]{1,0:T(8,128)(2,1)S(1)} collective-permute-done((bf16[256,128]{1,0:T(8,128)(2,1)S(1)}, bf16[256,128]{1,0:T(8,128)(2,1)S(1)}, u32[]{:S(2)}, u32[]{:S(2)}) %collective-permute-start.2) | collective-permute-done | bytes 65568 | tf_op jit(solution)/shard_map/ppermute | solution.py:657
  11.2 0.7 %collective-permute-start.5 = (bf16[288,256]{1,0:T(8,128)(2,1)S(1)}, bf16[288,256]{1,0:T(8,128)(2,1)S(1)}, u32[]{:S(2)}, u32[]{:S(2)}) collective-permute-start(bf16[288,256]{1,0:T(8,128)(2,1)S(1)} %get-tuple-element.110), channel_id=1, source_target_pairs={{4,8},{12,16},{20,24},{8,4},{16,12},{24,20},{5,9},{13,17},{21,25},... | collective-permute-start | bytes 442376 | tf_op jit(solution)/shard_map/ppermute | solution.py:657
  11.8 0.7 %collective-permute-start.7 = (bf16[448,256]{1,0:T(8,128)(2,1)S(1)}, bf16[448,256]{1,0:T(8,128)(2,1)S(1)}, u32[]{:S(2)}, u32[]{:S(2)}) collective-permute-start(bf16[448,256]{1,0:T(8,128)(2,1)S(1)} %shard_map.88), channel_id=1, source_target_pairs={{4,8},{12,16},{20,24},{8,4},{16,12},{24,20},{5,9},{13,17},{21,25},... | collective-permute-start | bytes 688136 | tf_op jit(solution)/shard_map/ppermute | solution.py:735
  12.5 3.7 %collective-permute-done.4.msg_a = bf16[288,256]{1,0:T(8,128)(2,1)S(1)} collective-permute-done((bf16[288,256]{1,0:T(8,128)(2,1)S(1)}, bf16[288,256]{1,0:T(8,128)(2,1)S(1)}, u32[]{:S(2)}, u32[]{:S(2)}) %collective-permute-start.4) | collective-permute-done | bytes 147488 | tf_op jit(solution)/shard_map/ppermute | solution.py:657
  16.2 3.7 %shard_map.90 = (f32[1024,256]{1,0:T(8,128)S(1)}, bf16[1344,384]{1,0:T(8,128)(2,1)S(1)}, bf16[1344,384]{1,0:T(8,128)(2,1)S(1)}, bf16[1344,384]{1,0:T(8,128)(2,1)...) custom-call(bf16[1024,256]{1,0:T(8,128)(2,1)S(1)} %shard_map.86.cot_, ...), custom_call_target="tpu_custom_call" | custom-call | flops 8000000000 | bytes 4194304 | tf_op jit(solution)/shard_map/pallas_call | solution.py:746
  21.2 7.3 %conditional.1 = ((f32[144,128]{1,0:T(8,128)S(1)}, bf16[1088,384]{1,0:T(8,128)(2,1)S(1)})) conditional(s32[]{:T(128)} %bitcast.5, (s32[2,32]{1,0:T(2,128)S(1)}, bf16[32,32,256]{2,1,0:T(8,128)(2,1)S(1)}, bf16[448,256]{1,0:T(8,128)(2,1)S(1)}, bf16[448,256]{1,0:T(8,128)(2,1)S(1)}, bf16[32,96,128]{2,1,0:T(8,128)(2,1)S(1)}, ...), branch_computations={%region_0.0_spmd, %region_1.0_spmd} | conditional | flops 10001703936 | bytes 15859800 | solution.py:769
  21.2 7.1 %branch_1_fun.1 = (f32[144,128]{1,0:T(8,128)S(1)}, bf16[1088,384]{1,0:T(8,128)(2,1)S(1)}) custom-call(s32[2,32]{1,0:T(2,128)S(1)} %get-tuple-element.55.shifts, bf16[32,32,256]{2,1,0:T(8,128)(2,1)S(1)} %get-tuple-element.56.feat, bf16[448,256]{1,0:T(8,128)(2,1)S(1)} %get-tuple-element.57.feat_a, bf16[448,256]{1,0:T(8,128)(2,1)S(1)} %get-tuple-element.58.feat_b, ...), custom_call_target="tpu_custom_call" | custom-call | flops 10000000000 | bytes 4194304 | tf_op jit(solution)/shard_map/cond/branch_1_fun/pallas_call | solution.py:682
  28.5 1.3 %collective-permute-done.8 = f32[144,128]{1,0:T(8,128)S(1)} collective-permute-done((f32[144,128]{1,0:T(8,128)S(1)}, f32[144,128]{1,0:T(8,128)S(1)}, u32[]{:S(2)}, u32[]{:S(2)}) %collective-permute-start.8) | collective-permute-done | bytes 73760 | tf_op jit(solution)/shard_map/ppermute | solution.py:786
  29.8 1.6 %collective-permute-start.9 = (f32[144,128]{1,0:T(8,128)S(1)}, f32[144,128]{1,0:T(8,128)S(1)}, u32[]{:S(2)}, u32[]{:S(2)}) collective-permute-start(f32[144,128]{1,0:T(8,128)S(1)} %add.12), channel_id=1, source_target_pairs={{0,2},{2,0},{1,3},{3,1},{4,6},{6,4},{5,7},{7,5},{8,10},{10,8},{9,1... | collective-permute-start | bytes 221192 | tf_op jit(solution)/shard_map/ppermute | solution.py:786
  31.4 1.7 %shard_map.91.rest_0_ = bf16[32,32,256]{2,1,0:T(8,128)(2,1)} custom-call(bf16[1088,384]{1,0:T(8,128)(2,1)S(1)} %get-tuple-element.133.blended, bf16[384,192]{1,0:T(8,128)(2,1)S(1)} %get-tuple-element.130.bands), custom_call_target="tpu_custom_call" | custom-call | flops 1000000000 | bytes 4194304 | tf_op jit(solution)/shard_map/pallas_call | solution.py:635
  33.0 1.2 %collective-permute-done.9 = f32[144,128]{1,0:T(8,128)S(1)} collective-permute-done((f32[144,128]{1,0:T(8,128)S(1)}, f32[144,128]{1,0:T(8,128)S(1)}, u32[]{:S(2)}, u32[]{:S(2)}) %collective-permute-start.9) | collective-permute-done | bytes 73760 | tf_op jit(solution)/shard_map/ppermute | solution.py:786
  34.2 5.6 %collective-permute-start.10 = (f32[144,128]{1,0:T(8,128)S(1)}, f32[144,128]{1,0:T(8,128)S(1)}, u32[]{:S(2)}, u32[]{:S(2)}) collective-permute-start(f32[144,128]{1,0:T(8,128)S(1)} %add.13), channel_id=1, source_target_pairs={{0,4},{4,0},{8,12},{12,8},{16,20},{20,16},{24,28},{28,24},{1,5},{5... | collective-permute-start | bytes 221192 | tf_op jit(solution)/shard_map/ppermute | solution.py:786
  39.8 1.7 %shard_map.92 = bf16[32,32,256]{2,1,0:T(8,128)(2,1)} custom-call(bf16[1088,384]{1,0:T(8,128)(2,1)S(1)} %get-tuple-element.133.blended, bf16[384,192]{1,0:T(8,128)(2,1)S(1)} %get-tuple-element.130.bands, bf16[32,32,256]{2,1,0:T(8,128)(2,1)} %shard_map.91.rest_0_), custom_call_target="tpu_custom_call", output_to_operand_aliasing={{}: (2, {})} | custom-call | flops 1000000000 | bytes 4194304 | tf_op jit(solution)/shard_map/pallas_call | solution.py:635
  41.5 0.7 %collective-permute-done.10 = f32[144,128]{1,0:T(8,128)S(1)} collective-permute-done((f32[144,128]{1,0:T(8,128)S(1)}, f32[144,128]{1,0:T(8,128)S(1)}, u32[]{:S(2)}, u32[]{:S(2)}) %collective-permute-start.10) | collective-permute-done | bytes 73760 | tf_op jit(solution)/shard_map/ppermute | solution.py:786
  42.2 2.3 %collective-permute-start.11 = (f32[144,128]{1,0:T(8,128)S(1)}, f32[144,128]{1,0:T(8,128)S(1)}, u32[]{:S(2)}, u32[]{:S(2)}) collective-permute-start(f32[144,128]{1,0:T(8,128)S(1)} %add.14), channel_id=1, source_target_pairs={{0,8},{4,12},{8,0},{12,4},{16,24},{20,28},{24,16},{28,20},{1,9},{5... | collective-permute-start | bytes 221192 | tf_op jit(solution)/shard_map/ppermute | solution.py:786
  44.5 2.3 %collective-permute-done.11 = f32[144,128]{1,0:T(8,128)S(1)} collective-permute-done((f32[144,128]{1,0:T(8,128)S(1)}, f32[144,128]{1,0:T(8,128)S(1)}, u32[]{:S(2)}, u32[]{:S(2)}) %collective-permute-start.11) | collective-permute-done | bytes 73760 | tf_op jit(solution)/shard_map/ppermute | solution.py:786
  46.8 3.3 %collective-permute-start.12 = (bf16[144,128]{1,0:T(8,128)(2,1)S(1)}, bf16[144,128]{1,0:T(8,128)(2,1)S(1)}, u32[]{:S(2)}, u32[]{:S(2)}) collective-permute-start(bf16[144,128]{1,0:T(8,128)(2,1)S(1)} %add_convert_fusion.mine), channel_id=1, source_target_pairs={{0,16},{4,20},{8,24},{12,28},{16,0},{20,4},{24,8},{28,12},{1,17},{... | collective-permute-start | bytes 110600 | tf_op jit(solution)/shard_map/ppermute | solution.py:786
  50.1 1.9 %collective-permute-done.12.other = bf16[144,128]{1,0:T(8,128)(2,1)S(1)} collective-permute-done((bf16[144,128]{1,0:T(8,128)(2,1)S(1)}, bf16[144,128]{1,0:T(8,128)(2,1)S(1)}, u32[]{:S(2)}, u32[]{:S(2)}) %collective-permute-start.12) | collective-permute-done | bytes 36896 | tf_op jit(solution)/shard_map/ppermute | solution.py:786
  52.1 0.9 %shard_map.93 = (f32[9,32,32]{2,1,0:T(8,128)}, f32[9,32,32]{2,1,0:T(8,128)}) custom-call(bf16[144,128]{1,0:T(8,128)(2,1)S(1)} %add_convert_fusion.mine, bf16[144,128]{1,0:T(8,128)(2,1)S(1)} %collective-permute-done.12.other), custom_call_target="tpu_custom_call" | custom-call | bytes 4194304 | tf_op jit(solution)/shard_map/pallas_call | solution.py:798
  (27 shorter events, 1.0 us)
Async XLA Ops:
  0.6 4.7 %copy-start = (bf16[1,32,32,256]{3,2,1,0:T(8,128)(2,1)S(1)}, bf16[1,32,32,256]{3,2,1,0:T(8,128)(2,1)}, u32[]{:S(2)}) copy-start(bf16[1,32,32,256]{3,2,1,0:T(8,128)(2,1)} %param.13) | copy-start | bytes 1572868
  2.3 5.9 %copy-start.4 = (bf16[1,32,32,256]{3,2,1,0:T(8,128)(2,1)S(1)}, bf16[1,32,32,256]{3,2,1,0:T(8,128)(2,1)}, u32[]{:S(2)}) copy-start(bf16[1,32,32,256]{3,2,1,0:T(8,128)(2,1)} %param.8) | copy-start | bytes 1572868
  2.3 5.9 %copy-start.5 = (s32[1,32,2]{1,2,0:T(2,128)S(1)}, s32[1,32,2]{1,2,0:T(2,128)}, u32[]{:S(2)}) copy-start(s32[1,32,2]{1,2,0:T(2,128)} %param.9) | copy-start | bytes 772
  2.3 13.9 %collective-permute-start.6 = (bf16[448,256]{1,0:T(8,128)(2,1)S(1)}, bf16[448,256]{1,0:T(8,128)(2,1)S(1)}, u32[]{:S(2)}, u32[]{:S(2)}) collective-permute-start(bf16[448,256]{1,0:T(8,128)(2,1)S(1)} %get-tuple-element.111), channel_id=1, source_target_pairs={{0,4},{4,0},{8,12},{12,8},{16,20},{20,16},{24,28},{28,24},{1,5},{5... | collective-permute-start | bytes 688136 | tf_op jit(solution)/shard_map/ppermute | solution.py:721
  6.6 4.3 %collective-permute-start.2 = (bf16[256,128]{1,0:T(8,128)(2,1)S(1)}, bf16[256,128]{1,0:T(8,128)(2,1)S(1)}, u32[]{:S(2)}, u32[]{:S(2)}) collective-permute-start(bf16[256,128]{1,0:T(8,128)(2,1)S(1)} %shard_map.87), channel_id=1, source_target_pairs={{0,2},{2,0},{1,3},{3,1},{4,6},{6,4},{5,7},{7,5},{8,10},{10,8},{9,1... | collective-permute-start | bytes 196616 | tf_op jit(solution)/shard_map/ppermute | solution.py:657
  8.2 1.3 %collective-permute-start.3 = (s32[8,128]{1,0:T(8,128)S(1)}, s32[8,128]{1,0:T(8,128)S(1)}, u32[]{:S(2)}, u32[]{:S(2)}) collective-permute-start(s32[8,128]{1,0:T(8,128)S(1)} %get-tuple-element.107), channel_id=1, source_target_pairs={{0,1},{1,0},{2,3},{3,2},{4,5},{5,4},{6,7},{7,6},{8,9},{9,8},{10,11... | collective-permute-start | bytes 12296 | tf_op jit(solution)/shard_map/ppermute | solution.py:724
  9.5 6.7 %copy-start.1 = (bf16[9,32,32]{2,1,0:T(8,128)(2,1)S(1)}, bf16[9,32,32]{2,1,0:T(8,128)(2,1)}, u32[]{:S(2)}) copy-start(bf16[9,32,32]{2,1,0:T(8,128)(2,1)} %rest_1_.1) | copy-start | bytes 55300
  9.5 6.7 %copy-start.2 = (bf16[9,32,32]{2,1,0:T(8,128)(2,1)S(1)}, bf16[9,32,32]{2,1,0:T(8,128)(2,1)}, u32[]{:S(2)}) copy-start(bf16[9,32,32]{2,1,0:T(8,128)(2,1)} %rest_2_.1) | copy-start | bytes 55300
  9.5 6.7 %copy-start.3 = (bf16[9,32,32]{2,1,0:T(8,128)(2,1)S(1)}, bf16[9,32,32]{2,1,0:T(8,128)(2,1)}, u32[]{:S(2)}) copy-start(bf16[9,32,32]{2,1,0:T(8,128)(2,1)} %rest_3_.1) | copy-start | bytes 55300
  11.0 5.2 %collective-permute-start.4 = (bf16[288,256]{1,0:T(8,128)(2,1)S(1)}, bf16[288,256]{1,0:T(8,128)(2,1)S(1)}, u32[]{:S(2)}, u32[]{:S(2)}) collective-permute-start(bf16[288,256]{1,0:T(8,128)(2,1)S(1)} %get-tuple-element.109), channel_id=1, source_target_pairs={{0,4},{4,0},{8,12},{12,8},{16,20},{20,16},{24,28},{28,24},{1,5},{5... | collective-permute-start | bytes 442376 | tf_op jit(solution)/shard_map/ppermute | solution.py:657
  11.2 5.1 %collective-permute-start.5 = (bf16[288,256]{1,0:T(8,128)(2,1)S(1)}, bf16[288,256]{1,0:T(8,128)(2,1)S(1)}, u32[]{:S(2)}, u32[]{:S(2)}) collective-permute-start(bf16[288,256]{1,0:T(8,128)(2,1)S(1)} %get-tuple-element.110), channel_id=1, source_target_pairs={{4,8},{12,16},{20,24},{8,4},{16,12},{24,20},{5,9},{13,17},{21,25},... | collective-permute-start | bytes 442376 | tf_op jit(solution)/shard_map/ppermute | solution.py:657
  11.8 9.3 %collective-permute-start.7 = (bf16[448,256]{1,0:T(8,128)(2,1)S(1)}, bf16[448,256]{1,0:T(8,128)(2,1)S(1)}, u32[]{:S(2)}, u32[]{:S(2)}) collective-permute-start(bf16[448,256]{1,0:T(8,128)(2,1)S(1)} %shard_map.88), channel_id=1, source_target_pairs={{4,8},{12,16},{20,24},{8,4},{16,12},{24,20},{5,9},{13,17},{21,25},... | collective-permute-start | bytes 688136 | tf_op jit(solution)/shard_map/ppermute | solution.py:735
  28.5 1.3 %collective-permute-start.8 = (f32[144,128]{1,0:T(8,128)S(1)}, f32[144,128]{1,0:T(8,128)S(1)}, u32[]{:S(2)}, u32[]{:S(2)}) collective-permute-start(f32[144,128]{1,0:T(8,128)S(1)} %get-tuple-element.126), channel_id=1, source_target_pairs={{0,1},{1,0},{2,3},{3,2},{4,5},{5,4},{6,7},{7,6},{8,9},{9,8},{10,11... | collective-permute-start | bytes 221192 | tf_op jit(solution)/shard_map/ppermute | solution.py:786
  29.8 4.4 %collective-permute-start.9 = (f32[144,128]{1,0:T(8,128)S(1)}, f32[144,128]{1,0:T(8,128)S(1)}, u32[]{:S(2)}, u32[]{:S(2)}) collective-permute-start(f32[144,128]{1,0:T(8,128)S(1)} %add.12), channel_id=1, source_target_pairs={{0,2},{2,0},{1,3},{3,1},{4,6},{6,4},{5,7},{7,5},{8,10},{10,8},{9,1... | collective-permute-start | bytes 221192 | tf_op jit(solution)/shard_map/ppermute | solution.py:786
  34.2 7.9 %collective-permute-start.10 = (f32[144,128]{1,0:T(8,128)S(1)}, f32[144,128]{1,0:T(8,128)S(1)}, u32[]{:S(2)}, u32[]{:S(2)}) collective-permute-start(f32[144,128]{1,0:T(8,128)S(1)} %add.13), channel_id=1, source_target_pairs={{0,4},{4,0},{8,12},{12,8},{16,20},{20,16},{24,28},{28,24},{1,5},{5... | collective-permute-start | bytes 221192 | tf_op jit(solution)/shard_map/ppermute | solution.py:786
  42.2 4.6 %collective-permute-start.11 = (f32[144,128]{1,0:T(8,128)S(1)}, f32[144,128]{1,0:T(8,128)S(1)}, u32[]{:S(2)}, u32[]{:S(2)}) collective-permute-start(f32[144,128]{1,0:T(8,128)S(1)} %add.14), channel_id=1, source_target_pairs={{0,8},{4,12},{8,0},{12,4},{16,24},{20,28},{24,16},{28,20},{1,9},{5... | collective-permute-start | bytes 221192 | tf_op jit(solution)/shard_map/ppermute | solution.py:786
  46.8 5.3 %collective-permute-start.12 = (bf16[144,128]{1,0:T(8,128)(2,1)S(1)}, bf16[144,128]{1,0:T(8,128)(2,1)S(1)}, u32[]{:S(2)}, u32[]{:S(2)}) collective-permute-start(bf16[144,128]{1,0:T(8,128)(2,1)S(1)} %add_convert_fusion.mine), channel_id=1, source_target_pairs={{0,16},{4,20},{8,24},{12,28},{16,0},{20,4},{24,8},{28,12},{1,17},{... | collective-permute-start | bytes 110600 | tf_op jit(solution)/shard_map/ppermute | solution.py:786

commit v14 on v13

--- a/solution.py
+++ b/solution.py
@@ -46,6 +46,14 @@
         col > 0,
         col < lax.axis_size("cols") - 1,
     )
+
+
+def as_bf(values):
+    return values.astype(F32).astype(BF16)
+
+
+def one_hot(mask):
+    return jnp.where(mask, jnp.ones((), BF16), jnp.zeros((), BF16))
 
 
 def rows_at(r, chans, count=1):
@@ -103,9 +111,9 @@
         at, up, down = at + count, up + n_up, down + n_down
     for out in counts:
         out[...] = jnp.full(out.shape, jnp.maximum(up, down), jnp.int32)
+    place = as_bf(lax.broadcasted_iota(jnp.int32, (chunk, full), 0))
     for p in range(0, size, chunk):
-        place = lax.broadcasted_iota(jnp.int32, (chunk, full), 0) + p
-        pick = jnp.where(place == target[0:1], 1.0, 0.0).astype(BF16)
+        pick = one_hot(place == as_bf(target[0:1] - p))
         msg[p : p + chunk] = jnp.dot(pick, source, preferred_element_type=F32).astype(BF16)
 
 
@@ -442,11 +450,14 @@
 
     tall = moved.shape[1]
     lane = lanes_of((tall, TILE))
-    seen_halo = ((lane < TILE // 2) & has_right) | ((lane >= TILE // 2) & has_left)
-    step = lanes_of((tall, 3 * height)) - lax.broadcasted_iota(jnp.int32, (tall, 3 * height), 0)
+    seen_halo = one_hot(((lane < TILE // 2) & has_right) | ((lane >= TILE // 2) & has_left))
+    lane, mirrored = as_bf(lane), as_bf(TILE - 1 - lane)
+    step = as_bf(
+        lanes_of((tall, 3 * height)) - lax.broadcasted_iota(jnp.int32, (tall, 3 * height), 0)
+    )
     depth = 2 * window + height
     source = lanes_of((1, depth))
-    apart = lax.broadcasted_iota(jnp.int32, (tall, depth), 0) - lanes_of((tall, depth))
+    apart = as_bf(lax.broadcasted_iota(jnp.int32, (tall, depth), 0) - lanes_of((tall, depth)))
     align = 16
 
     def warp(c, ats):
@@ -469,23 +480,21 @@
             jnp.where(in_up, above, none),
             jnp.where(source < window + height, own, jnp.where(in_down, below, none)),
         )
-        pick = jnp.where(apart == offset, 1.0, 0.0).astype(BF16)
+        pick = one_hot(apart == as_bf(offset))
         rows = jnp.concatenate(
             [lent[0, pl.ds(base_up, window), :], feat[c], lent[1, pl.ds(base_down, window), :]], axis=0
         )
-        plane = jnp.dot(pick, rows, preferred_element_type=F32)
-        pick = jnp.where(step == height - EXT + shift, 1.0, 0.0).astype(BF16)
+        plane = jnp.dot(pick, rows, preferred_element_type=F32).astype(BF16)
+        pick = one_hot(step == as_bf(height - EXT + shift))
         plane = [plane[:, part] for part in tiles_of(span)]
-        plane.append(jnp.dot(pick, sides[c], preferred_element_type=F32))
+        plane.append(jnp.dot(pick, sides[c], preferred_element_type=F32).astype(BF16))
         amount = jnp.where(move > 0, TILE - move, -move)
         parts = [turn(part, amount) for part in plane]
-        inside = jnp.where(move > 0, lane, TILE - 1 - lane) < TILE - jnp.abs(move)
+        inside = jnp.where(move > 0, lane, mirrored) < as_bf(TILE - jnp.abs(move))
         for t, part in enumerate(tiles_of(width)):
             after, before = parts[(t + 1) % (tiles + 1)], parts[t - 1]
             result = jnp.where(inside, parts[t], jnp.where(move > 0, after, before))
-            if t == tiles:
-                result = jnp.where(seen_halo, result, 0.0)
-            moved[c, :, part] = result.astype(BF16)
+            moved[c, :, part] = result * seen_halo if t == tiles else result
         return at_up + n_up, at_down + n_down
 
     lax.fori_loop(0, chans, warp, (jnp.int32(0), jnp.int32(0)), unroll=8)
@@ -737,8 +746,9 @@
     halo = bf(CHALO * chans + ncols * packed * TILE // span, span)
     messages = call(edge_kernel, (halo, halo), [], 1 + ncols, 8)(cot_rows, *col_msgs)
     row_msgs = swapped(messages, "rows")
-    row_msgs, feat_a = lax.optimization_barrier((row_msgs, feat_a))
     row_msgs[0], total = lax.optimization_barrier((row_msgs[0], total))
+    fits = total[0, 0] <= usual
+    row_msgs, feat_a, fits = lax.optimization_barrier((row_msgs, feat_a, fits))
 
     tall_c = (height + 2 * CHALO) * chans
     view = bf(tall_c, width)
@@ -767,7 +777,7 @@
     views, sides, weights = rest[:3], rest[3], rest[4:]
 
     grads, blended = lax.cond(
-        total[0, 0] <= usual,
+        fits,
         functools.partial(main_pass, 0),
         functools.partial(main_pass, LARGEST * chans - usual),
         (feat_a, feat_b), shifts, feat, sides, act_grad, tuple(views), tuple(weights[:2]),

time: 53.2 us -> 54.8 us (1.030)
  Pallas kernels: 19.2 us -> 22 us
  starting transfers between devices: 18.9 us -> 17.8 us
    pallas_call x1, Pallas kernels: 7.05 us -> 8.61 us  [main_pass(): call(main_kernel, (jax.ShapeDtypeStruct((9 * chans // 2, TILE), F32), bf(...]
    pallas_call x1, Pallas kernels: 3.73 us -> 4.91 us  [shards(): call(functools.partial(back_kernel, ncols), (jax.ShapeDtypeStruct((full,...]
    ppermute x5, starting transfers between devices: 12.8 us -> 11.7 us  [shards(): other = lax.ppermute(grads, axis, pairs)]
  transfers between devices with their start and end apart: 11 -> 11, of which waited for: 7 -> 7; matrix products, arithmetic and copies ran while one was open for 1% -> 1% of each run, Pallas kernels for 18% -> 20%
where the time goes in v14:
time: 54.8 us; the launch traced here: 54.6 us
  Pallas kernels  22 us (40%)
  starting transfers between devices  17.8 us (32%)
  waiting for transfers between devices  12.5 us (23%)
  between operations  1.48 us (3%)
  local copies, waits for them, and re-layouts  0.55 us (1%)
    ppermute x5, starting transfers between devices, shards(): other = lax.ppermute(grads, axis, pairs)  11.7 us
    pallas_call x1, Pallas kernels, main_pass(): call(main_kernel, (jax.ShapeDtypeStruct((9 * chans // 2, TILE), F32), bf(...  8.61 us
    ppermute x5, waiting for transfers between devices, shards(): other = lax.ppermute(grads, axis, pairs)  7.38 us
    ppermute x3, waiting for transfers between devices, swapped(): return [lax.ppermute(m, axis, p) for m, p in zip(messages, pairs)]  5.15 us
    pallas_call x1, Pallas kernels, shards(): call(functools.partial(back_kernel, ncols), (jax.ShapeDtypeStruct((full,...  4.91 us
    pallas_call x2, Pallas kernels, predict(): call(functools.partial(predict_kernel, part), jax.ShapeDtypeStruct(shape,...  3.33 us
    ppermute x1, starting transfers between devices, shards(): feat_a = lax.ppermute(message, 'rows', row_pairs[0])  3.03 us
    pallas_call x2, Pallas kernels, pack_rows(): call(functools.partial(feature_kernel, index, skip), message, [], 2, 16,...  2.75 us
  transfers between devices with their start and end apart: 11, of which 7 were waited for; matrix products, arithmetic and copies ran while one was open for 1% of the time, Pallas kernels for 20%

profile of v14, /device:TPU:0, one launch (start us, length us, event | category | flops | bytes accessed | tf_op | source)
XLA Modules:
  0.0 54.6 jit_solution(12679214624321158406)
XLA Ops:
  0.6 1.7 %shard_map.85 = (bf16[448,256]{1,0:T(8,128)(2,1)S(1)}, s32[8,128]{1,0:T(8,128)S(1)}) custom-call(s32[2,32]{1,0:T(2,128)} %bitcast.14, bf16[32,32,256]{2,1,0:T(8,128)(2,1)} %bitcast.9), custom_call_target="tpu_custom_call" | custom-call | bytes 4194304 | tf_op jit(solution)/shard_map/pallas_call | solution.py:673
  2.3 3.0 %collective-permute-start.6 = (bf16[448,256]{1,0:T(8,128)(2,1)S(1)}, bf16[448,256]{1,0:T(8,128)(2,1)S(1)}, u32[]{:S(2)}, u32[]{:S(2)}) collective-permute-start(bf16[448,256]{1,0:T(8,128)(2,1)S(1)} %get-tuple-element.114), channel_id=1, source_target_pairs={{0,4},{4,0},{8,12},{12,8},{16,20},{20,16},{24,28},{28,24},{1,5},{5... | collective-permute-start | bytes 688136 | tf_op jit(solution)/shard_map/ppermute | solution.py:730
  5.4 1.2 %shard_map.87 = bf16[256,128]{1,0:T(8,128)(2,1)S(1)} custom-call(bf16[32,32,256]{2,1,0:T(8,128)(2,1)} %bitcast.10, bf16[32,32,256]{2,1,0:T(8,128)(2,1)S(1)} %bitcast.7), custom_call_target="tpu_custom_call" | custom-call | flops 20000000000 | bytes 4194304 | tf_op jit(solution)/shard_map/pallas_call | solution.py:737
  6.6 1.6 %collective-permute-start.2 = (bf16[256,128]{1,0:T(8,128)(2,1)S(1)}, bf16[256,128]{1,0:T(8,128)(2,1)S(1)}, u32[]{:S(2)}, u32[]{:S(2)}) collective-permute-start(bf16[256,128]{1,0:T(8,128)(2,1)S(1)} %shard_map.87), channel_id=1, source_target_pairs={{0,2},{2,0},{1,3},{3,1},{4,6},{6,4},{5,7},{7,5},{8,10},{10,8},{9,1... | collective-permute-start | bytes 196616 | tf_op jit(solution)/shard_map/ppermute | solution.py:666
  8.2 1.1 %shard_map.88 = bf16[448,256]{1,0:T(8,128)(2,1)S(1)} custom-call(s32[2,32]{1,0:T(2,128)S(1)} %bitcast.15, bf16[32,32,256]{2,1,0:T(8,128)(2,1)S(1)} %bitcast.11), custom_call_target="tpu_custom_call" | custom-call | bytes 4194304 | tf_op jit(solution)/shard_map/pallas_call | solution.py:673
  9.5 1.4 %collective-permute-done.2.rest_0_ = bf16[256,128]{1,0:T(8,128)(2,1)S(1)} collective-permute-done((bf16[256,128]{1,0:T(8,128)(2,1)S(1)}, bf16[256,128]{1,0:T(8,128)(2,1)S(1)}, u32[]{:S(2)}, u32[]{:S(2)}) %collective-permute-start.2) | collective-permute-done | bytes 65568 | tf_op jit(solution)/shard_map/ppermute | solution.py:666
  11.2 0.7 %collective-permute-start.5 = (bf16[288,256]{1,0:T(8,128)(2,1)S(1)}, bf16[288,256]{1,0:T(8,128)(2,1)S(1)}, u32[]{:S(2)}, u32[]{:S(2)}) collective-permute-start(bf16[288,256]{1,0:T(8,128)(2,1)S(1)} %get-tuple-element.113), channel_id=1, source_target_pairs={{4,8},{12,16},{20,24},{8,4},{16,12},{24,20},{5,9},{13,17},{21,25},... | collective-permute-start | bytes 442376 | tf_op jit(solution)/shard_map/ppermute | solution.py:666
  11.8 0.7 %collective-permute-start.7 = (bf16[448,256]{1,0:T(8,128)(2,1)S(1)}, bf16[448,256]{1,0:T(8,128)(2,1)S(1)}, u32[]{:S(2)}, u32[]{:S(2)}) collective-permute-start(bf16[448,256]{1,0:T(8,128)(2,1)S(1)} %shard_map.88), channel_id=1, source_target_pairs={{4,8},{12,16},{20,24},{8,4},{16,12},{24,20},{5,9},{13,17},{21,25},... | collective-permute-start | bytes 688136 | tf_op jit(solution)/shard_map/ppermute | solution.py:744
  12.5 3.7 %collective-permute-done.4.msg_a = bf16[288,256]{1,0:T(8,128)(2,1)S(1)} collective-permute-done((bf16[288,256]{1,0:T(8,128)(2,1)S(1)}, bf16[288,256]{1,0:T(8,128)(2,1)S(1)}, u32[]{:S(2)}, u32[]{:S(2)}) %collective-permute-start.4) | collective-permute-done | bytes 147488 | tf_op jit(solution)/shard_map/ppermute | solution.py:666
  17.4 4.9 %shard_map.90 = (f32[1024,256]{1,0:T(8,128)S(1)}, bf16[1344,384]{1,0:T(8,128)(2,1)}, bf16[1344,384]{1,0:T(8,128)(2,1)}, bf16[1344,384]{1,0:T(8,128)(2,1)}, bf16[...) custom-call(bf16[1024,256]{1,0:T(8,128)(2,1)S(1)} %shard_map.86.cot_, ...), custom_call_target="tpu_custom_call" | custom-call | flops 8000000000 | bytes 4194304 | tf_op jit(solution)/shard_map/pallas_call | solution.py:756
  22.3 8.8 %conditional.1 = ((f32[144,128]{1,0:T(8,128)S(1)}, bf16[1088,384]{1,0:T(8,128)(2,1)S(1)})) conditional(s32[]{:T(128)} %convert_element_type.6, (s32[2,32]{1,0:T(2,128)S(1)}, bf16[32,32,256]{2,1,0:T(8,128)(2,1)S(1)}, bf16[448,256]{1,0:T(8,128)(2,1)S(1)}, bf16[448,256]{1,0:T(8,128)(2,1)S(1)}, bf16[32,96,128]{2,1,0:T(8,128)(2,1)}, ...), branch_computations={%region_0.0_spmd, %region_1.0_spmd} | conditional | flops 10001703936 | bytes 28246188 | solution.py:779
  22.3 8.6 %branch_1_fun.1 = (f32[144,128]{1,0:T(8,128)S(1)}, bf16[1088,384]{1,0:T(8,128)(2,1)S(1)}) custom-call(s32[2,32]{1,0:T(2,128)S(1)} %get-tuple-element.55.shifts, bf16[32,32,256]{2,1,0:T(8,128)(2,1)S(1)} %get-tuple-element.56.feat, bf16[448,256]{1,0:T(8,128)(2,1)S(1)} %get-tuple-element.57.feat_a, bf16[448,256]{1,0:T(8,128)(2,1)S(1)} %get-tuple-element.58.feat_b, ...), custom_call_target="tpu_custom_call" | custom-call | flops 10000000000 | bytes 4194304 | tf_op jit(solution)/shard_map/cond/branch_1_fun/pallas_call | solution.py:691
  31.3 1.3 %collective-permute-done.8 = f32[144,128]{1,0:T(8,128)S(1)} collective-permute-done((f32[144,128]{1,0:T(8,128)S(1)}, f32[144,128]{1,0:T(8,128)S(1)}, u32[]{:S(2)}, u32[]{:S(2)}) %collective-permute-start.8) | collective-permute-done | bytes 73760 | tf_op jit(solution)/shard_map/ppermute | solution.py:796
  32.5 1.6 %collective-permute-start.9 = (f32[144,128]{1,0:T(8,128)S(1)}, f32[144,128]{1,0:T(8,128)S(1)}, u32[]{:S(2)}, u32[]{:S(2)}) collective-permute-start(f32[144,128]{1,0:T(8,128)S(1)} %add.12), channel_id=1, source_target_pairs={{0,2},{2,0},{1,3},{3,1},{4,6},{6,4},{5,7},{7,5},{8,10},{10,8},{9,1... | collective-permute-start | bytes 221192 | tf_op jit(solution)/shard_map/ppermute | solution.py:796
  34.1 1.7 %shard_map.91.rest_0_ = bf16[32,32,256]{2,1,0:T(8,128)(2,1)} custom-call(bf16[1088,384]{1,0:T(8,128)(2,1)S(1)} %get-tuple-element.135.blended, bf16[384,192]{1,0:T(8,128)(2,1)S(1)} %get-tuple-element.132.bands), custom_call_target="tpu_custom_call" | custom-call | flops 1000000000 | bytes 4194304 | tf_op jit(solution)/shard_map/pallas_call | solution.py:644
  35.8 1.2 %collective-permute-done.9 = f32[144,128]{1,0:T(8,128)S(1)} collective-permute-done((f32[144,128]{1,0:T(8,128)S(1)}, f32[144,128]{1,0:T(8,128)S(1)}, u32[]{:S(2)}, u32[]{:S(2)}) %collective-permute-start.9) | collective-permute-done | bytes 73760 | tf_op jit(solution)/shard_map/ppermute | solution.py:796
  37.0 4.4 %collective-permute-start.10 = (f32[144,128]{1,0:T(8,128)S(1)}, f32[144,128]{1,0:T(8,128)S(1)}, u32[]{:S(2)}, u32[]{:S(2)}) collective-permute-start(f32[144,128]{1,0:T(8,128)S(1)} %add.13), channel_id=1, source_target_pairs={{0,4},{4,0},{8,12},{12,8},{16,20},{20,16},{24,28},{28,24},{1,5},{5... | collective-permute-start | bytes 221192 | tf_op jit(solution)/shard_map/ppermute | solution.py:796
  41.4 1.7 %shard_map.92 = bf16[32,32,256]{2,1,0:T(8,128)(2,1)} custom-call(bf16[1088,384]{1,0:T(8,128)(2,1)S(1)} %get-tuple-element.135.blended, bf16[384,192]{1,0:T(8,128)(2,1)S(1)} %get-tuple-element.132.bands, bf16[32,32,256]{2,1,0:T(8,128)(2,1)} %shard_map.91.rest_0_), custom_call_target="tpu_custom_call", output_to_operand_aliasing={{}: (2, {})} | custom-call | flops 1000000000 | bytes 4194304 | tf_op jit(solution)/shard_map/pallas_call | solution.py:644
  43.1 0.7 %collective-permute-done.10 = f32[144,128]{1,0:T(8,128)S(1)} collective-permute-done((f32[144,128]{1,0:T(8,128)S(1)}, f32[144,128]{1,0:T(8,128)S(1)}, u32[]{:S(2)}, u32[]{:S(2)}) %collective-permute-start.10) | collective-permute-done | bytes 73760 | tf_op jit(solution)/shard_map/ppermute | solution.py:796
  43.7 2.3 %collective-permute-start.11 = (f32[144,128]{1,0:T(8,128)S(1)}, f32[144,128]{1,0:T(8,128)S(1)}, u32[]{:S(2)}, u32[]{:S(2)}) collective-permute-start(f32[144,128]{1,0:T(8,128)S(1)} %add.14), channel_id=1, source_target_pairs={{0,8},{4,12},{8,0},{12,4},{16,24},{20,28},{24,16},{28,20},{1,9},{5... | collective-permute-start | bytes 221192 | tf_op jit(solution)/shard_map/ppermute | solution.py:796
  46.0 2.3 %collective-permute-done.11 = f32[144,128]{1,0:T(8,128)S(1)} collective-permute-done((f32[144,128]{1,0:T(8,128)S(1)}, f32[144,128]{1,0:T(8,128)S(1)}, u32[]{:S(2)}, u32[]{:S(2)}) %collective-permute-start.11) | collective-permute-done | bytes 73760 | tf_op jit(solution)/shard_map/ppermute | solution.py:796
  48.3 3.4 %collective-permute-start.12 = (bf16[144,128]{1,0:T(8,128)(2,1)S(1)}, bf16[144,128]{1,0:T(8,128)(2,1)S(1)}, u32[]{:S(2)}, u32[]{:S(2)}) collective-permute-start(bf16[144,128]{1,0:T(8,128)(2,1)S(1)} %add_convert_fusion.mine), channel_id=1, source_target_pairs={{0,16},{4,20},{8,24},{12,28},{16,0},{20,4},{24,8},{28,12},{1,17},{... | collective-permute-start | bytes 110600 | tf_op jit(solution)/shard_map/ppermute | solution.py:796
  51.7 1.9 %collective-permute-done.12.other = bf16[144,128]{1,0:T(8,128)(2,1)S(1)} collective-permute-done((bf16[144,128]{1,0:T(8,128)(2,1)S(1)}, bf16[144,128]{1,0:T(8,128)(2,1)S(1)}, u32[]{:S(2)}, u32[]{:S(2)}) %collective-permute-start.12) | collective-permute-done | bytes 36896 | tf_op jit(solution)/shard_map/ppermute | solution.py:796
  53.7 0.9 %shard_map.93 = (f32[9,32,32]{2,1,0:T(8,128)}, f32[9,32,32]{2,1,0:T(8,128)}) custom-call(bf16[144,128]{1,0:T(8,128)(2,1)S(1)} %add_convert_fusion.mine, bf16[144,128]{1,0:T(8,128)(2,1)S(1)} %collective-permute-done.12.other), custom_call_target="tpu_custom_call" | custom-call | bytes 4194304 | tf_op jit(solution)/shard_map/pallas_call | solution.py:808
  (27 shorter events, 1.0 us)
Async XLA Ops:
  0.6 4.7 %copy-start = (bf16[1,32,32,256]{3,2,1,0:T(8,128)(2,1)S(1)}, bf16[1,32,32,256]{3,2,1,0:T(8,128)(2,1)}, u32[]{:S(2)}) copy-start(bf16[1,32,32,256]{3,2,1,0:T(8,128)(2,1)} %param.13) | copy-start | bytes 1572868
  2.3 5.9 %copy-start.4 = (bf16[1,32,32,256]{3,2,1,0:T(8,128)(2,1)S(1)}, bf16[1,32,32,256]{3,2,1,0:T(8,128)(2,1)}, u32[]{:S(2)}) copy-start(bf16[1,32,32,256]{3,2,1,0:T(8,128)(2,1)} %param.8) | copy-start | bytes 1572868
  2.3 5.9 %copy-start.5 = (s32[1,32,2]{1,2,0:T(2,128)S(1)}, s32[1,32,2]{1,2,0:T(2,128)}, u32[]{:S(2)}) copy-start(s32[1,32,2]{1,2,0:T(2,128)} %param.9) | copy-start | bytes 772
  2.3 15.1 %collective-permute-start.6 = (bf16[448,256]{1,0:T(8,128)(2,1)S(1)}, bf16[448,256]{1,0:T(8,128)(2,1)S(1)}, u32[]{:S(2)}, u32[]{:S(2)}) collective-permute-start(bf16[448,256]{1,0:T(8,128)(2,1)S(1)} %get-tuple-element.114), channel_id=1, source_target_pairs={{0,4},{4,0},{8,12},{12,8},{16,20},{20,16},{24,28},{28,24},{1,5},{5... | collective-permute-start | bytes 688136 | tf_op jit(solution)/shard_map/ppermute | solution.py:730
  6.6 4.3 %collective-permute-start.2 = (bf16[256,128]{1,0:T(8,128)(2,1)S(1)}, bf16[256,128]{1,0:T(8,128)(2,1)S(1)}, u32[]{:S(2)}, u32[]{:S(2)}) collective-permute-start(bf16[256,128]{1,0:T(8,128)(2,1)S(1)} %shard_map.87), channel_id=1, source_target_pairs={{0,2},{2,0},{1,3},{3,1},{4,6},{6,4},{5,7},{7,5},{8,10},{10,8},{9,1... | collective-permute-start | bytes 196616 | tf_op jit(solution)/shard_map/ppermute | solution.py:666
  8.2 1.3 %collective-permute-start.3 = (s32[8,128]{1,0:T(8,128)S(1)}, s32[8,128]{1,0:T(8,128)S(1)}, u32[]{:S(2)}, u32[]{:S(2)}) collective-permute-start(s32[8,128]{1,0:T(8,128)S(1)} %get-tuple-element.108), channel_id=1, source_target_pairs={{0,1},{1,0},{2,3},{3,2},{4,5},{5,4},{6,7},{7,6},{8,9},{9,8},{10,11... | collective-permute-start | bytes 12296 | tf_op jit(solution)/shard_map/ppermute | solution.py:733
  9.5 7.9 %copy-start.1 = (bf16[9,32,32]{2,1,0:T(8,128)(2,1)S(1)}, bf16[9,32,32]{2,1,0:T(8,128)(2,1)}, u32[]{:S(2)}) copy-start(bf16[9,32,32]{2,1,0:T(8,128)(2,1)} %rest_1_.1) | copy-start | bytes 55300
  9.5 7.9 %copy-start.2 = (bf16[9,32,32]{2,1,0:T(8,128)(2,1)S(1)}, bf16[9,32,32]{2,1,0:T(8,128)(2,1)}, u32[]{:S(2)}) copy-start(bf16[9,32,32]{2,1,0:T(8,128)(2,1)} %rest_2_.1) | copy-start | bytes 55300
  9.5 7.9 %copy-start.3 = (bf16[9,32,32]{2,1,0:T(8,128)(2,1)S(1)}, bf16[9,32,32]{2,1,0:T(8,128)(2,1)}, u32[]{:S(2)}) copy-start(bf16[9,32,32]{2,1,0:T(8,128)(2,1)} %rest_3_.1) | copy-start | bytes 55300
  11.0 5.2 %collective-permute-start.4 = (bf16[288,256]{1,0:T(8,128)(2,1)S(1)}, bf16[288,256]{1,0:T(8,128)(2,1)S(1)}, u32[]{:S(2)}, u32[]{:S(2)}) collective-permute-start(bf16[288,256]{1,0:T(8,128)(2,1)S(1)} %get-tuple-element.110), channel_id=1, source_target_pairs={{0,4},{4,0},{8,12},{12,8},{16,20},{20,16},{24,28},{28,24},{1,5},{5... | collective-permute-start | bytes 442376 | tf_op jit(solution)/shard_map/ppermute | solution.py:666
  11.2 6.2 %collective-permute-start.5 = (bf16[288,256]{1,0:T(8,128)(2,1)S(1)}, bf16[288,256]{1,0:T(8,128)(2,1)S(1)}, u32[]{:S(2)}, u32[]{:S(2)}) collective-permute-start(bf16[288,256]{1,0:T(8,128)(2,1)S(1)} %get-tuple-element.113), channel_id=1, source_target_pairs={{4,8},{12,16},{20,24},{8,4},{16,12},{24,20},{5,9},{13,17},{21,25},... | collective-permute-start | bytes 442376 | tf_op jit(solution)/shard_map/ppermute | solution.py:666
  11.8 10.5 %collective-permute-start.7 = (bf16[448,256]{1,0:T(8,128)(2,1)S(1)}, bf16[448,256]{1,0:T(8,128)(2,1)S(1)}, u32[]{:S(2)}, u32[]{:S(2)}) collective-permute-start(bf16[448,256]{1,0:T(8,128)(2,1)S(1)} %shard_map.88), channel_id=1, source_target_pairs={{4,8},{12,16},{20,24},{8,4},{16,12},{24,20},{5,9},{13,17},{21,25},... | collective-permute-start | bytes 688136 | tf_op jit(solution)/shard_map/ppermute | solution.py:744
  31.2 1.3 %collective-permute-start.8 = (f32[144,128]{1,0:T(8,128)S(1)}, f32[144,128]{1,0:T(8,128)S(1)}, u32[]{:S(2)}, u32[]{:S(2)}) collective-permute-start(f32[144,128]{1,0:T(8,128)S(1)} %get-tuple-element.128), channel_id=1, source_target_pairs={{0,1},{1,0},{2,3},{3,2},{4,5},{5,4},{6,7},{7,6},{8,9},{9,8},{10,11... | collective-permute-start | bytes 221192 | tf_op jit(solution)/shard_map/ppermute | solution.py:796
  32.5 4.4 %collective-permute-start.9 = (f32[144,128]{1,0:T(8,128)S(1)}, f32[144,128]{1,0:T(8,128)S(1)}, u32[]{:S(2)}, u32[]{:S(2)}) collective-permute-start(f32[144,128]{1,0:T(8,128)S(1)} %add.12), channel_id=1, source_target_pairs={{0,2},{2,0},{1,3},{3,1},{4,6},{6,4},{5,7},{7,5},{8,10},{10,8},{9,1... | collective-permute-start | bytes 221192 | tf_op jit(solution)/shard_map/ppermute | solution.py:796
  37.0 6.8 %collective-permute-start.10 = (f32[144,128]{1,0:T(8,128)S(1)}, f32[144,128]{1,0:T(8,128)S(1)}, u32[]{:S(2)}, u32[]{:S(2)}) collective-permute-start(f32[144,128]{1,0:T(8,128)S(1)} %add.13), channel_id=1, source_target_pairs={{0,4},{4,0},{8,12},{12,8},{16,20},{20,16},{24,28},{28,24},{1,5},{5... | collective-permute-start | bytes 221192 | tf_op jit(solution)/shard_map/ppermute | solution.py:796
  43.7 4.6 %collective-permute-start.11 = (f32[144,128]{1,0:T(8,128)S(1)}, f32[144,128]{1,0:T(8,128)S(1)}, u32[]{:S(2)}, u32[]{:S(2)}) collective-permute-start(f32[144,128]{1,0:T(8,128)S(1)} %add.14), channel_id=1, source_target_pairs={{0,8},{4,12},{8,0},{12,4},{16,24},{20,28},{24,16},{28,20},{1,9},{5... | collective-permute-start | bytes 221192 | tf_op jit(solution)/shard_map/ppermute | solution.py:796
  48.3 5.3 %collective-permute-start.12 = (bf16[144,128]{1,0:T(8,128)(2,1)S(1)}, bf16[144,128]{1,0:T(8,128)(2,1)S(1)}, u32[]{:S(2)}, u32[]{:S(2)}) collective-permute-start(bf16[144,128]{1,0:T(8,128)(2,1)S(1)} %add_convert_fusion.mine), channel_id=1, source_target_pairs={{0,16},{4,20},{8,24},{12,28},{16,0},{20,4},{24,8},{28,12},{1,17},{... | collective-permute-start | bytes 110600 | tf_op jit(solution)/shard_map/ppermute | solution.py:796

commit v15 on v14

--- a/solution.py
+++ b/solution.py
@@ -648,7 +648,7 @@
             pltpu.VMEM((chans * rows, span), BF16),
         ],
         len(args),
-        12,
+        6,
         flops=10**9,
         grid=(1,),
         in_specs=specs,
@@ -672,7 +672,7 @@
         message = (message, jax.ShapeDtypeStruct((8, TILE), jnp.int32))
     return call(
         functools.partial(feature_kernel, index, skip),
-        message, [], 2, 16, smem_first=True,
+        message, [], 2, 6, smem_first=True,
     )(shifts, feat)
 
 
@@ -704,7 +704,7 @@
             pltpu.VMEM((band, POOL * chans), F32),
         ],
         11,
-        20,
+        14,
         flops=10**10,
         smem_first=True,
     )(
@@ -735,7 +735,7 @@
 
     packed = chans * (height * SLOT // TILE)
     messages = call(
-        column_kernel, (bf(packed, TILE),) * (1 if cols == 2 else 2), [], 2, 8, flops=2 * 10**10
+        column_kernel, (bf(packed, TILE),) * (1 if cols == 2 else 2), [], 2, 4, flops=2 * 10**10
     )(feat, cot)
     col_msgs = swapped(messages, "cols")
     ncols = len(col_msgs)
@@ -744,7 +744,7 @@
     feat_b = lax.ppermute(message, "rows", row_pairs[1])
     cot_rows = call(rows_kernel, bf(full, span), [], 1, 4)(cot)
     halo = bf(CHALO * chans + ncols * packed * TILE // span, span)
-    messages = call(edge_kernel, (halo, halo), [], 1 + ncols, 8)(cot_rows, *col_msgs)
+    messages = call(edge_kernel, (halo, halo), [], 1 + ncols, 4)(cot_rows, *col_msgs)
     row_msgs = swapped(messages, "rows")
     row_msgs[0], total = lax.optimization_barrier((row_msgs[0], total))
     fits = total[0, 0] <= usual
@@ -771,7 +771,7 @@
             pltpu.VMEM((chans, 9 * chans), F32),
         ],
         6 + ncols,
-        16,
+        8,
         flops=8 * 10**9,
     )(cot_rows, *row_msgs, *col_msgs, first_kernel, bottle_kernel, second_kernel)
     views, sides, weights = rest[:3], rest[3], rest[4:]

time: 54.8 us -> 54.8 us (level)
  no operation moved by 1% of the time
where the time goes in v15:
time: 54.8 us; the launch traced here: 54.6 us
  Pallas kernels  22 us (40%)
  starting transfers between devices  17.8 us (32%)
  waiting for transfers between devices  12.5 us (23%)
  between operations  1.48 us (3%)
  local copies, waits for them, and re-layouts  0.55 us (1%)
    ppermute x5, starting transfers between devices, shards(): other = lax.ppermute(grads, axis, pairs)  11.7 us
    pallas_call x1, Pallas kernels, main_pass(): call(main_kernel, (jax.ShapeDtypeStruct((9 * chans // 2, TILE), F32), bf(...  8.61 us
    ppermute x5, waiting for transfers between devices, shards(): other = lax.ppermute(grads, axis, pairs)  7.38 us
    ppermute x3, waiting for transfers between devices, swapped(): return [lax.ppermute(m, axis, p) for m, p in zip(messages, pairs)]  5.15 us
    pallas_call x1, Pallas kernels, shards(): call(functools.partial(back_kernel, ncols), (jax.ShapeDtypeStruct((full,...  4.91 us
    pallas_call x2, Pallas kernels, predict(): call(functools.partial(predict_kernel, part), jax.ShapeDtypeStruct(shape,...  3.33 us
    ppermute x1, starting transfers between devices, shards(): feat_a = lax.ppermute(message, 'rows', row_pairs[0])  3.03 us
    pallas_call x2, Pallas kernels, pack_rows(): call(functools.partial(feature_kernel, index, skip), message, [], 2, 6, s...  2.75 us
  transfers between devices with their start and end apart: 11, of which 7 were waited for; matrix products, arithmetic and copies ran while one was open for 1% of the time, Pallas kernels for 20%

profile of v15, /device:TPU:0, one launch (start us, length us, event | category | flops | bytes accessed | tf_op | source)
XLA Modules:
  0.0 54.6 jit_solution(16284390698533252411)
XLA Ops:
  0.6 1.7 %shard_map.85 = (bf16[448,256]{1,0:T(8,128)(2,1)S(1)}, s32[8,128]{1,0:T(8,128)S(1)}) custom-call(s32[2,32]{1,0:T(2,128)} %bitcast.14, bf16[32,32,256]{2,1,0:T(8,128)(2,1)} %bitcast.9), custom_call_target="tpu_custom_call" | custom-call | bytes 4194304 | tf_op jit(solution)/shard_map/pallas_call | solution.py:673
  2.3 3.0 %collective-permute-start.6 = (bf16[448,256]{1,0:T(8,128)(2,1)S(1)}, bf16[448,256]{1,0:T(8,128)(2,1)S(1)}, u32[]{:S(2)}, u32[]{:S(2)}) collective-permute-start(bf16[448,256]{1,0:T(8,128)(2,1)S(1)} %get-tuple-element.114), channel_id=1, source_target_pairs={{0,4},{4,0},{8,12},{12,8},{16,20},{20,16},{24,28},{28,24},{1,5},{5... | collective-permute-start | bytes 688136 | tf_op jit(solution)/shard_map/ppermute | solution.py:730
  5.4 1.2 %shard_map.87 = bf16[256,128]{1,0:T(8,128)(2,1)S(1)} custom-call(bf16[32,32,256]{2,1,0:T(8,128)(2,1)} %bitcast.10, bf16[32,32,256]{2,1,0:T(8,128)(2,1)S(1)} %bitcast.7), custom_call_target="tpu_custom_call" | custom-call | flops 20000000000 | bytes 4194304 | tf_op jit(solution)/shard_map/pallas_call | solution.py:737
  6.6 1.6 %collective-permute-start.2 = (bf16[256,128]{1,0:T(8,128)(2,1)S(1)}, bf16[256,128]{1,0:T(8,128)(2,1)S(1)}, u32[]{:S(2)}, u32[]{:S(2)}) collective-permute-start(bf16[256,128]{1,0:T(8,128)(2,1)S(1)} %shard_map.87), channel_id=1, source_target_pairs={{0,2},{2,0},{1,3},{3,1},{4,6},{6,4},{5,7},{7,5},{8,10},{10,8},{9,1... | collective-permute-start | bytes 196616 | tf_op jit(solution)/shard_map/ppermute | solution.py:666
  8.2 1.1 %shard_map.88 = bf16[448,256]{1,0:T(8,128)(2,1)S(1)} custom-call(s32[2,32]{1,0:T(2,128)S(1)} %bitcast.15, bf16[32,32,256]{2,1,0:T(8,128)(2,1)S(1)} %bitcast.11), custom_call_target="tpu_custom_call" | custom-call | bytes 4194304 | tf_op jit(solution)/shard_map/pallas_call | solution.py:673
  9.5 1.4 %collective-permute-done.2.rest_0_ = bf16[256,128]{1,0:T(8,128)(2,1)S(1)} collective-permute-done((bf16[256,128]{1,0:T(8,128)(2,1)S(1)}, bf16[256,128]{1,0:T(8,128)(2,1)S(1)}, u32[]{:S(2)}, u32[]{:S(2)}) %collective-permute-start.2) | collective-permute-done | bytes 65568 | tf_op jit(solution)/shard_map/ppermute | solution.py:666
  11.2 0.7 %collective-permute-start.5 = (bf16[288,256]{1,0:T(8,128)(2,1)S(1)}, bf16[288,256]{1,0:T(8,128)(2,1)S(1)}, u32[]{:S(2)}, u32[]{:S(2)}) collective-permute-start(bf16[288,256]{1,0:T(8,128)(2,1)S(1)} %get-tuple-element.113), channel_id=1, source_target_pairs={{4,8},{12,16},{20,24},{8,4},{16,12},{24,20},{5,9},{13,17},{21,25},... | collective-permute-start | bytes 442376 | tf_op jit(solution)/shard_map/ppermute | solution.py:666
  11.8 0.7 %collective-permute-start.7 = (bf16[448,256]{1,0:T(8,128)(2,1)S(1)}, bf16[448,256]{1,0:T(8,128)(2,1)S(1)}, u32[]{:S(2)}, u32[]{:S(2)}) collective-permute-start(bf16[448,256]{1,0:T(8,128)(2,1)S(1)} %shard_map.88), channel_id=1, source_target_pairs={{4,8},{12,16},{20,24},{8,4},{16,12},{24,20},{5,9},{13,17},{21,25},... | collective-permute-start | bytes 688136 | tf_op jit(solution)/shard_map/ppermute | solution.py:744
  12.5 3.7 %collective-permute-done.4.msg_a = bf16[288,256]{1,0:T(8,128)(2,1)S(1)} collective-permute-done((bf16[288,256]{1,0:T(8,128)(2,1)S(1)}, bf16[288,256]{1,0:T(8,128)(2,1)S(1)}, u32[]{:S(2)}, u32[]{:S(2)}) %collective-permute-start.4) | collective-permute-done | bytes 147488 | tf_op jit(solution)/shard_map/ppermute | solution.py:666
  17.4 4.9 %shard_map.90 = (f32[1024,256]{1,0:T(8,128)S(1)}, bf16[1344,384]{1,0:T(8,128)(2,1)}, bf16[1344,384]{1,0:T(8,128)(2,1)}, bf16[1344,384]{1,0:T(8,128)(2,1)}, bf16[...) custom-call(bf16[1024,256]{1,0:T(8,128)(2,1)S(1)} %shard_map.86.cot_, ...), custom_call_target="tpu_custom_call" | custom-call | flops 8000000000 | bytes 4194304 | tf_op jit(solution)/shard_map/pallas_call | solution.py:756
  22.3 8.8 %conditional.1 = ((f32[144,128]{1,0:T(8,128)S(1)}, bf16[1088,384]{1,0:T(8,128)(2,1)S(1)})) conditional(s32[]{:T(128)} %convert_element_type.6, (s32[2,32]{1,0:T(2,128)S(1)}, bf16[32,32,256]{2,1,0:T(8,128)(2,1)S(1)}, bf16[448,256]{1,0:T(8,128)(2,1)S(1)}, bf16[448,256]{1,0:T(8,128)(2,1)S(1)}, bf16[32,96,128]{2,1,0:T(8,128)(2,1)}, ...), branch_computations={%region_0.0_spmd, %region_1.0_spmd} | conditional | flops 10001703936 | bytes 28246188 | solution.py:779
  22.3 8.6 %branch_1_fun.1 = (f32[144,128]{1,0:T(8,128)S(1)}, bf16[1088,384]{1,0:T(8,128)(2,1)S(1)}) custom-call(s32[2,32]{1,0:T(2,128)S(1)} %get-tuple-element.55.shifts, bf16[32,32,256]{2,1,0:T(8,128)(2,1)S(1)} %get-tuple-element.56.feat, bf16[448,256]{1,0:T(8,128)(2,1)S(1)} %get-tuple-element.57.feat_a, bf16[448,256]{1,0:T(8,128)(2,1)S(1)} %get-tuple-element.58.feat_b, ...), custom_call_target="tpu_custom_call" | custom-call | flops 10000000000 | bytes 4194304 | tf_op jit(solution)/shard_map/cond/branch_1_fun/pallas_call | solution.py:691
  31.3 1.3 %collective-permute-done.8 = f32[144,128]{1,0:T(8,128)S(1)} collective-permute-done((f32[144,128]{1,0:T(8,128)S(1)}, f32[144,128]{1,0:T(8,128)S(1)}, u32[]{:S(2)}, u32[]{:S(2)}) %collective-permute-start.8) | collective-permute-done | bytes 73760 | tf_op jit(solution)/shard_map/ppermute | solution.py:796
  32.5 1.6 %collective-permute-start.9 = (f32[144,128]{1,0:T(8,128)S(1)}, f32[144,128]{1,0:T(8,128)S(1)}, u32[]{:S(2)}, u32[]{:S(2)}) collective-permute-start(f32[144,128]{1,0:T(8,128)S(1)} %add.12), channel_id=1, source_target_pairs={{0,2},{2,0},{1,3},{3,1},{4,6},{6,4},{5,7},{7,5},{8,10},{10,8},{9,1... | collective-permute-start | bytes 221192 | tf_op jit(solution)/shard_map/ppermute | solution.py:796
  34.1 1.7 %shard_map.91.rest_0_ = bf16[32,32,256]{2,1,0:T(8,128)(2,1)} custom-call(bf16[1088,384]{1,0:T(8,128)(2,1)S(1)} %get-tuple-element.135.blended, bf16[384,192]{1,0:T(8,128)(2,1)S(1)} %get-tuple-element.132.bands), custom_call_target="tpu_custom_call" | custom-call | flops 1000000000 | bytes 4194304 | tf_op jit(solution)/shard_map/pallas_call | solution.py:644
  35.8 1.2 %collective-permute-done.9 = f32[144,128]{1,0:T(8,128)S(1)} collective-permute-done((f32[144,128]{1,0:T(8,128)S(1)}, f32[144,128]{1,0:T(8,128)S(1)}, u32[]{:S(2)}, u32[]{:S(2)}) %collective-permute-start.9) | collective-permute-done | bytes 73760 | tf_op jit(solution)/shard_map/ppermute | solution.py:796
  37.0 4.4 %collective-permute-start.10 = (f32[144,128]{1,0:T(8,128)S(1)}, f32[144,128]{1,0:T(8,128)S(1)}, u32[]{:S(2)}, u32[]{:S(2)}) collective-permute-start(f32[144,128]{1,0:T(8,128)S(1)} %add.13), channel_id=1, source_target_pairs={{0,4},{4,0},{8,12},{12,8},{16,20},{20,16},{24,28},{28,24},{1,5},{5... | collective-permute-start | bytes 221192 | tf_op jit(solution)/shard_map/ppermute | solution.py:796
  41.4 1.7 %shard_map.92 = bf16[32,32,256]{2,1,0:T(8,128)(2,1)} custom-call(bf16[1088,384]{1,0:T(8,128)(2,1)S(1)} %get-tuple-element.135.blended, bf16[384,192]{1,0:T(8,128)(2,1)S(1)} %get-tuple-element.132.bands, bf16[32,32,256]{2,1,0:T(8,128)(2,1)} %shard_map.91.rest_0_), custom_call_target="tpu_custom_call", output_to_operand_aliasing={{}: (2, {})} | custom-call | flops 1000000000 | bytes 4194304 | tf_op jit(solution)/shard_map/pallas_call | solution.py:644
  43.1 0.7 %collective-permute-done.10 = f32[144,128]{1,0:T(8,128)S(1)} collective-permute-done((f32[144,128]{1,0:T(8,128)S(1)}, f32[144,128]{1,0:T(8,128)S(1)}, u32[]{:S(2)}, u32[]{:S(2)}) %collective-permute-start.10) | collective-permute-done | bytes 73760 | tf_op jit(solution)/shard_map/ppermute | solution.py:796
  43.7 2.3 %collective-permute-start.11 = (f32[144,128]{1,0:T(8,128)S(1)}, f32[144,128]{1,0:T(8,128)S(1)}, u32[]{:S(2)}, u32[]{:S(2)}) collective-permute-start(f32[144,128]{1,0:T(8,128)S(1)} %add.14), channel_id=1, source_target_pairs={{0,8},{4,12},{8,0},{12,4},{16,24},{20,28},{24,16},{28,20},{1,9},{5... | collective-permute-start | bytes 221192 | tf_op jit(solution)/shard_map/ppermute | solution.py:796
  46.0 2.3 %collective-permute-done.11 = f32[144,128]{1,0:T(8,128)S(1)} collective-permute-done((f32[144,128]{1,0:T(8,128)S(1)}, f32[144,128]{1,0:T(8,128)S(1)}, u32[]{:S(2)}, u32[]{:S(2)}) %collective-permute-start.11) | collective-permute-done | bytes 73760 | tf_op jit(solution)/shard_map/ppermute | solution.py:796
  48.3 3.4 %collective-permute-start.12 = (bf16[144,128]{1,0:T(8,128)(2,1)S(1)}, bf16[144,128]{1,0:T(8,128)(2,1)S(1)}, u32[]{:S(2)}, u32[]{:S(2)}) collective-permute-start(bf16[144,128]{1,0:T(8,128)(2,1)S(1)} %add_convert_fusion.mine), channel_id=1, source_target_pairs={{0,16},{4,20},{8,24},{12,28},{16,0},{20,4},{24,8},{28,12},{1,17},{... | collective-permute-start | bytes 110600 | tf_op jit(solution)/shard_map/ppermute | solution.py:796
  51.7 1.9 %collective-permute-done.12.other = bf16[144,128]{1,0:T(8,128)(2,1)S(1)} collective-permute-done((bf16[144,128]{1,0:T(8,128)(2,1)S(1)}, bf16[144,128]{1,0:T(8,128)(2,1)S(1)}, u32[]{:S(2)}, u32[]{:S(2)}) %collective-permute-start.12) | collective-permute-done | bytes 36896 | tf_op jit(solution)/shard_map/ppermute | solution.py:796
  53.7 0.9 %shard_map.93 = (f32[9,32,32]{2,1,0:T(8,128)}, f32[9,32,32]{2,1,0:T(8,128)}) custom-call(bf16[144,128]{1,0:T(8,128)(2,1)S(1)} %add_convert_fusion.mine, bf16[144,128]{1,0:T(8,128)(2,1)S(1)} %collective-permute-done.12.other), custom_call_target="tpu_custom_call" | custom-call | bytes 4194304 | tf_op jit(solution)/shard_map/pallas_call | solution.py:808
  (27 shorter events, 1.0 us)
Async XLA Ops:
  0.6 4.7 %copy-start = (bf16[1,32,32,256]{3,2,1,0:T(8,128)(2,1)S(1)}, bf16[1,32,32,256]{3,2,1,0:T(8,128)(2,1)}, u32[]{:S(2)}) copy-start(bf16[1,32,32,256]{3,2,1,0:T(8,128)(2,1)} %param.13) | copy-start | bytes 1572868
  2.3 5.9 %copy-start.4 = (bf16[1,32,32,256]{3,2,1,0:T(8,128)(2,1)S(1)}, bf16[1,32,32,256]{3,2,1,0:T(8,128)(2,1)}, u32[]{:S(2)}) copy-start(bf16[1,32,32,256]{3,2,1,0:T(8,128)(2,1)} %param.8) | copy-start | bytes 1572868
  2.3 5.9 %copy-start.5 = (s32[1,32,2]{1,2,0:T(2,128)S(1)}, s32[1,32,2]{1,2,0:T(2,128)}, u32[]{:S(2)}) copy-start(s32[1,32,2]{1,2,0:T(2,128)} %param.9) | copy-start | bytes 772
  2.3 15.1 %collective-permute-start.6 = (bf16[448,256]{1,0:T(8,128)(2,1)S(1)}, bf16[448,256]{1,0:T(8,128)(2,1)S(1)}, u32[]{:S(2)}, u32[]{:S(2)}) collective-permute-start(bf16[448,256]{1,0:T(8,128)(2,1)S(1)} %get-tuple-element.114), channel_id=1, source_target_pairs={{0,4},{4,0},{8,12},{12,8},{16,20},{20,16},{24,28},{28,24},{1,5},{5... | collective-permute-start | bytes 688136 | tf_op jit(solution)/shard_map/ppermute | solution.py:730
  6.6 4.3 %collective-permute-start.2 = (bf16[256,128]{1,0:T(8,128)(2,1)S(1)}, bf16[256,128]{1,0:T(8,128)(2,1)S(1)}, u32[]{:S(2)}, u32[]{:S(2)}) collective-permute-start(bf16[256,128]{1,0:T(8,128)(2,1)S(1)} %shard_map.87), channel_id=1, source_target_pairs={{0,2},{2,0},{1,3},{3,1},{4,6},{6,4},{5,7},{7,5},{8,10},{10,8},{9,1... | collective-permute-start | bytes 196616 | tf_op jit(solution)/shard_map/ppermute | solution.py:666
  8.2 1.3 %collective-permute-start.3 = (s32[8,128]{1,0:T(8,128)S(1)}, s32[8,128]{1,0:T(8,128)S(1)}, u32[]{:S(2)}, u32[]{:S(2)}) collective-permute-start(s32[8,128]{1,0:T(8,128)S(1)} %get-tuple-element.108), channel_id=1, source_target_pairs={{0,1},{1,0},{2,3},{3,2},{4,5},{5,4},{6,7},{7,6},{8,9},{9,8},{10,11... | collective-permute-start | bytes 12296 | tf_op jit(solution)/shard_map/ppermute | solution.py:733
  9.5 7.9 %copy-start.1 = (bf16[9,32,32]{2,1,0:T(8,128)(2,1)S(1)}, bf16[9,32,32]{2,1,0:T(8,128)(2,1)}, u32[]{:S(2)}) copy-start(bf16[9,32,32]{2,1,0:T(8,128)(2,1)} %rest_1_.1) | copy-start | bytes 55300
  9.5 7.9 %copy-start.2 = (bf16[9,32,32]{2,1,0:T(8,128)(2,1)S(1)}, bf16[9,32,32]{2,1,0:T(8,128)(2,1)}, u32[]{:S(2)}) copy-start(bf16[9,32,32]{2,1,0:T(8,128)(2,1)} %rest_2_.1) | copy-start | bytes 55300
  9.5 7.9 %copy-start.3 = (bf16[9,32,32]{2,1,0:T(8,128)(2,1)S(1)}, bf16[9,32,32]{2,1,0:T(8,128)(2,1)}, u32[]{:S(2)}) copy-start(bf16[9,32,32]{2,1,0:T(8,128)(2,1)} %rest_3_.1) | copy-start | bytes 55300
  11.0 5.2 %collective-permute-start.4 = (bf16[288,256]{1,0:T(8,128)(2,1)S(1)}, bf16[288,256]{1,0:T(8,128)(2,1)S(1)}, u32[]{:S(2)}, u32[]{:S(2)}) collective-permute-start(bf16[288,256]{1,0:T(8,128)(2,1)S(1)} %get-tuple-element.110), channel_id=1, source_target_pairs={{0,4},{4,0},{8,12},{12,8},{16,20},{20,16},{24,28},{28,24},{1,5},{5... | collective-permute-start | bytes 442376 | tf_op jit(solution)/shard_map/ppermute | solution.py:666
  11.2 6.2 %collective-permute-start.5 = (bf16[288,256]{1,0:T(8,128)(2,1)S(1)}, bf16[288,256]{1,0:T(8,128)(2,1)S(1)}, u32[]{:S(2)}, u32[]{:S(2)}) collective-permute-start(bf16[288,256]{1,0:T(8,128)(2,1)S(1)} %get-tuple-element.113), channel_id=1, source_target_pairs={{4,8},{12,16},{20,24},{8,4},{16,12},{24,20},{5,9},{13,17},{21,25},... | collective-permute-start | bytes 442376 | tf_op jit(solution)/shard_map/ppermute | solution.py:666
  11.8 10.5 %collective-permute-start.7 = (bf16[448,256]{1,0:T(8,128)(2,1)S(1)}, bf16[448,256]{1,0:T(8,128)(2,1)S(1)}, u32[]{:S(2)}, u32[]{:S(2)}) collective-permute-start(bf16[448,256]{1,0:T(8,128)(2,1)S(1)} %shard_map.88), channel_id=1, source_target_pairs={{4,8},{12,16},{20,24},{8,4},{16,12},{24,20},{5,9},{13,17},{21,25},... | collective-permute-start | bytes 688136 | tf_op jit(solution)/shard_map/ppermute | solution.py:744
  31.2 1.3 %collective-permute-start.8 = (f32[144,128]{1,0:T(8,128)S(1)}, f32[144,128]{1,0:T(8,128)S(1)}, u32[]{:S(2)}, u32[]{:S(2)}) collective-permute-start(f32[144,128]{1,0:T(8,128)S(1)} %get-tuple-element.128), channel_id=1, source_target_pairs={{0,1},{1,0},{2,3},{3,2},{4,5},{5,4},{6,7},{7,6},{8,9},{9,8},{10,11... | collective-permute-start | bytes 221192 | tf_op jit(solution)/shard_map/ppermute | solution.py:796
  32.5 4.4 %collective-permute-start.9 = (f32[144,128]{1,0:T(8,128)S(1)}, f32[144,128]{1,0:T(8,128)S(1)}, u32[]{:S(2)}, u32[]{:S(2)}) collective-permute-start(f32[144,128]{1,0:T(8,128)S(1)} %add.12), channel_id=1, source_target_pairs={{0,2},{2,0},{1,3},{3,1},{4,6},{6,4},{5,7},{7,5},{8,10},{10,8},{9,1... | collective-permute-start | bytes 221192 | tf_op jit(solution)/shard_map/ppermute | solution.py:796
  37.0 6.8 %collective-permute-start.10 = (f32[144,128]{1,0:T(8,128)S(1)}, f32[144,128]{1,0:T(8,128)S(1)}, u32[]{:S(2)}, u32[]{:S(2)}) collective-permute-start(f32[144,128]{1,0:T(8,128)S(1)} %add.13), channel_id=1, source_target_pairs={{0,4},{4,0},{8,12},{12,8},{16,20},{20,16},{24,28},{28,24},{1,5},{5... | collective-permute-start | bytes 221192 | tf_op jit(solution)/shard_map/ppermute | solution.py:796
  43.7 4.6 %collective-permute-start.11 = (f32[144,128]{1,0:T(8,128)S(1)}, f32[144,128]{1,0:T(8,128)S(1)}, u32[]{:S(2)}, u32[]{:S(2)}) collective-permute-start(f32[144,128]{1,0:T(8,128)S(1)} %add.14), channel_id=1, source_target_pairs={{0,8},{4,12},{8,0},{12,4},{16,24},{20,28},{24,16},{28,20},{1,9},{5... | collective-permute-start | bytes 221192 | tf_op jit(solution)/shard_map/ppermute | solution.py:796
  48.3 5.3 %collective-permute-start.12 = (bf16[144,128]{1,0:T(8,128)(2,1)S(1)}, bf16[144,128]{1,0:T(8,128)(2,1)S(1)}, u32[]{:S(2)}, u32[]{:S(2)}) collective-permute-start(bf16[144,128]{1,0:T(8,128)(2,1)S(1)} %add_convert_fusion.mine), channel_id=1, source_target_pairs={{0,16},{4,20},{8,24},{12,28},{16,0},{20,4},{24,8},{28,12},{1,17},{... | collective-permute-start | bytes 110600 | tf_op jit(solution)/shard_map/ppermute | solution.py:796

commit v16 on v14

--- a/solution.py
+++ b/solution.py
@@ -747,8 +747,7 @@
     messages = call(edge_kernel, (halo, halo), [], 1 + ncols, 8)(cot_rows, *col_msgs)
     row_msgs = swapped(messages, "rows")
     row_msgs[0], total = lax.optimization_barrier((row_msgs[0], total))
-    fits = total[0, 0] <= usual
-    row_msgs, feat_a, fits = lax.optimization_barrier((row_msgs, feat_a, fits))
+    row_msgs, feat_a = lax.optimization_barrier((row_msgs, feat_a))
 
     tall_c = (height + 2 * CHALO) * chans
     view = bf(tall_c, width)
@@ -777,7 +776,7 @@
     views, sides, weights = rest[:3], rest[3], rest[4:]
 
     grads, blended = lax.cond(
-        fits,
+        total[0, 0] <= usual,
         functools.partial(main_pass, 0),
         functools.partial(main_pass, LARGEST * chans - usual),
         (feat_a, feat_b), shifts, feat, sides, act_grad, tuple(views), tuple(weights[:2]),
@@ -791,7 +790,7 @@
             bit *= 2
     parts, prediction = 2, None
     for step, (axis, pairs) in enumerate(steps):
-        if step == len(steps) - 1:
+        if step >= len(steps) - 2:
             grads = lax.optimization_barrier(grads.astype(BF16))
         other = lax.ppermute(grads, axis, pairs)
         if 1 <= step <= parts:
@@ -800,7 +799,7 @@
             )
             other, prediction = lax.optimization_barrier((other, prediction))
         if step < len(steps) - 1:
-            grads = grads + other
+            grads = grads.astype(F32) + other.astype(F32)
             if step < parts:
                 grads, blended = lax.optimization_barrier((grads, blended))
     factor = 1.0 / math.sqrt(imgs * dp * height * rows * span * cols)

time: 54.8 us -> 51.8 us (0.945)
  Pallas kernels: 22 us -> 19.3 us
    pallas_call x1, Pallas kernels: 8.61 us -> 7.09 us  [main_pass(): call(main_kernel, (jax.ShapeDtypeStruct((9 * chans // 2, TILE), F32), bf(...]
    pallas_call x1, Pallas kernels: 4.91 us -> 3.74 us  [shards(): call(functools.partial(back_kernel, ncols), (jax.ShapeDtypeStruct((full,...]
  transfers between devices with their start and end apart: 11 -> 11, of which waited for: 7 -> 7; matrix products, arithmetic and copies ran while one was open for 1% -> 1% of each run, Pallas kernels for 20% -> 19%
where the time goes in v16:
time: 51.8 us; the launch traced here: 51.5 us
  Pallas kernels  19.3 us (37%)
  starting transfers between devices  17.8 us (34%)
  waiting for transfers between devices  12.2 us (24%)
  between operations  1.5 us (3%)
  local copies, waits for them, and re-layouts  0.55 us (1%)
    ppermute x5, starting transfers between devices, shards(): other = lax.ppermute(grads, axis, pairs)  11.7 us
    pallas_call x1, Pallas kernels, main_pass(): call(main_kernel, (jax.ShapeDtypeStruct((9 * chans // 2, TILE), F32), bf(...  7.09 us
    ppermute x5, waiting for transfers between devices, shards(): other = lax.ppermute(grads, axis, pairs)  7 us
    ppermute x3, waiting for transfers between devices, swapped(): return [lax.ppermute(m, axis, p) for m, p in zip(messages, pairs)]  5.15 us
    pallas_call x1, Pallas kernels, shards(): call(functools.partial(back_kernel, ncols), (jax.ShapeDtypeStruct((full,...  3.74 us
    pallas_call x2, Pallas kernels, predict(): call(functools.partial(predict_kernel, part), jax.ShapeDtypeStruct(shape,...  3.33 us
    ppermute x1, starting transfers between devices, shards(): feat_a = lax.ppermute(message, 'rows', row_pairs[0])  3.03 us
    pallas_call x2, Pallas kernels, pack_rows(): call(functools.partial(feature_kernel, index, skip), message, [], 2, 16,...  2.75 us
  transfers between devices with their start and end apart: 11, of which 7 were waited for; matrix products, arithmetic and copies ran while one was open for 1% of the time, Pallas kernels for 19%

profile of v16, /device:TPU:0, one launch (start us, length us, event | category | flops | bytes accessed | tf_op | source)
XLA Modules:
  0.0 51.5 jit_solution(781944779936464468)
XLA Ops:
  0.6 1.7 %shard_map.85 = (bf16[448,256]{1,0:T(8,128)(2,1)S(1)}, s32[8,128]{1,0:T(8,128)S(1)}) custom-call(s32[2,32]{1,0:T(2,128)} %bitcast.14, bf16[32,32,256]{2,1,0:T(8,128)(2,1)} %bitcast.9), custom_call_target="tpu_custom_call" | custom-call | bytes 4194304 | tf_op jit(solution)/shard_map/pallas_call | solution.py:673
  2.3 3.0 %collective-permute-start.6 = (bf16[448,256]{1,0:T(8,128)(2,1)S(1)}, bf16[448,256]{1,0:T(8,128)(2,1)S(1)}, u32[]{:S(2)}, u32[]{:S(2)}) collective-permute-start(bf16[448,256]{1,0:T(8,128)(2,1)S(1)} %get-tuple-element.114), channel_id=1, source_target_pairs={{0,4},{4,0},{8,12},{12,8},{16,20},{20,16},{24,28},{28,24},{1,5},{5... | collective-permute-start | bytes 688136 | tf_op jit(solution)/shard_map/ppermute | solution.py:730
  5.4 1.2 %shard_map.87 = bf16[256,128]{1,0:T(8,128)(2,1)S(1)} custom-call(bf16[32,32,256]{2,1,0:T(8,128)(2,1)} %bitcast.10, bf16[32,32,256]{2,1,0:T(8,128)(2,1)S(1)} %bitcast.7), custom_call_target="tpu_custom_call" | custom-call | flops 20000000000 | bytes 4194304 | tf_op jit(solution)/shard_map/pallas_call | solution.py:737
  6.6 1.6 %collective-permute-start.2 = (bf16[256,128]{1,0:T(8,128)(2,1)S(1)}, bf16[256,128]{1,0:T(8,128)(2,1)S(1)}, u32[]{:S(2)}, u32[]{:S(2)}) collective-permute-start(bf16[256,128]{1,0:T(8,128)(2,1)S(1)} %shard_map.87), channel_id=1, source_target_pairs={{0,2},{2,0},{1,3},{3,1},{4,6},{6,4},{5,7},{7,5},{8,10},{10,8},{9,1... | collective-permute-start | bytes 196616 | tf_op jit(solution)/shard_map/ppermute | solution.py:666
  8.2 1.1 %shard_map.88 = bf16[448,256]{1,0:T(8,128)(2,1)S(1)} custom-call(s32[2,32]{1,0:T(2,128)S(1)} %bitcast.15, bf16[32,32,256]{2,1,0:T(8,128)(2,1)S(1)} %bitcast.11), custom_call_target="tpu_custom_call" | custom-call | bytes 4194304 | tf_op jit(solution)/shard_map/pallas_call | solution.py:673
  9.5 1.4 %collective-permute-done.2.rest_0_ = bf16[256,128]{1,0:T(8,128)(2,1)S(1)} collective-permute-done((bf16[256,128]{1,0:T(8,128)(2,1)S(1)}, bf16[256,128]{1,0:T(8,128)(2,1)S(1)}, u32[]{:S(2)}, u32[]{:S(2)}) %collective-permute-start.2) | collective-permute-done | bytes 65568 | tf_op jit(solution)/shard_map/ppermute | solution.py:666
  11.2 0.7 %collective-permute-start.5 = (bf16[288,256]{1,0:T(8,128)(2,1)S(1)}, bf16[288,256]{1,0:T(8,128)(2,1)S(1)}, u32[]{:S(2)}, u32[]{:S(2)}) collective-permute-start(bf16[288,256]{1,0:T(8,128)(2,1)S(1)} %get-tuple-element.113), channel_id=1, source_target_pairs={{4,8},{12,16},{20,24},{8,4},{16,12},{24,20},{5,9},{13,17},{21,25},... | collective-permute-start | bytes 442376 | tf_op jit(solution)/shard_map/ppermute | solution.py:666
  11.8 0.7 %collective-permute-start.7 = (bf16[448,256]{1,0:T(8,128)(2,1)S(1)}, bf16[448,256]{1,0:T(8,128)(2,1)S(1)}, u32[]{:S(2)}, u32[]{:S(2)}) collective-permute-start(bf16[448,256]{1,0:T(8,128)(2,1)S(1)} %shard_map.88), channel_id=1, source_target_pairs={{4,8},{12,16},{20,24},{8,4},{16,12},{24,20},{5,9},{13,17},{21,25},... | collective-permute-start | bytes 688136 | tf_op jit(solution)/shard_map/ppermute | solution.py:744
  12.5 3.7 %collective-permute-done.4.msg_a = bf16[288,256]{1,0:T(8,128)(2,1)S(1)} collective-permute-done((bf16[288,256]{1,0:T(8,128)(2,1)S(1)}, bf16[288,256]{1,0:T(8,128)(2,1)S(1)}, u32[]{:S(2)}, u32[]{:S(2)}) %collective-permute-start.4) | collective-permute-done | bytes 147488 | tf_op jit(solution)/shard_map/ppermute | solution.py:666
  17.4 3.7 %shard_map.90 = (f32[1024,256]{1,0:T(8,128)S(1)}, bf16[1344,384]{1,0:T(8,128)(2,1)S(1)}, bf16[1344,384]{1,0:T(8,128)(2,1)S(1)}, bf16[1344,384]{1,0:T(8,128)(2,1)...) custom-call(bf16[1024,256]{1,0:T(8,128)(2,1)S(1)} %shard_map.86.cot_, ...), custom_call_target="tpu_custom_call" | custom-call | flops 8000000000 | bytes 4194304 | tf_op jit(solution)/shard_map/pallas_call | solution.py:755
  21.2 7.3 %conditional.1 = ((f32[144,128]{1,0:T(8,128)S(1)}, bf16[1088,384]{1,0:T(8,128)(2,1)S(1)})) conditional(s32[]{:T(128)} %bitcast.5, (s32[2,32]{1,0:T(2,128)S(1)}, bf16[32,32,256]{2,1,0:T(8,128)(2,1)S(1)}, bf16[448,256]{1,0:T(8,128)(2,1)S(1)}, bf16[448,256]{1,0:T(8,128)(2,1)S(1)}, bf16[32,96,128]{2,1,0:T(8,128)(2,1)S(1)}, ...), branch_computations={%region_0.0_spmd, %region_1.0_spmd} | conditional | flops 10001703936 | bytes 15859800 | solution.py:778
  21.2 7.1 %branch_1_fun.1 = (f32[144,128]{1,0:T(8,128)S(1)}, bf16[1088,384]{1,0:T(8,128)(2,1)S(1)}) custom-call(s32[2,32]{1,0:T(2,128)S(1)} %get-tuple-element.55.shifts, bf16[32,32,256]{2,1,0:T(8,128)(2,1)S(1)} %get-tuple-element.56.feat, bf16[448,256]{1,0:T(8,128)(2,1)S(1)} %get-tuple-element.57.feat_a, bf16[448,256]{1,0:T(8,128)(2,1)S(1)} %get-tuple-element.58.feat_b, ...), custom_call_target="tpu_custom_call" | custom-call | flops 10000000000 | bytes 4194304 | tf_op jit(solution)/shard_map/cond/branch_1_fun/pallas_call | solution.py:691
  28.6 1.3 %collective-permute-done.8 = f32[144,128]{1,0:T(8,128)S(1)} collective-permute-done((f32[144,128]{1,0:T(8,128)S(1)}, f32[144,128]{1,0:T(8,128)S(1)}, u32[]{:S(2)}, u32[]{:S(2)}) %collective-permute-start.8) | collective-permute-done | bytes 73760 | tf_op jit(solution)/shard_map/ppermute | solution.py:795
  29.9 1.5 %collective-permute-start.9 = (f32[144,128]{1,0:T(8,128)S(1)}, f32[144,128]{1,0:T(8,128)S(1)}, u32[]{:S(2)}, u32[]{:S(2)}) collective-permute-start(f32[144,128]{1,0:T(8,128)S(1)} %add.12), channel_id=1, source_target_pairs={{0,2},{2,0},{1,3},{3,1},{4,6},{6,4},{5,7},{7,5},{8,10},{10,8},{9,1... | collective-permute-start | bytes 221192 | tf_op jit(solution)/shard_map/ppermute | solution.py:795
  31.4 1.7 %shard_map.91.rest_0_ = bf16[32,32,256]{2,1,0:T(8,128)(2,1)} custom-call(bf16[1088,384]{1,0:T(8,128)(2,1)S(1)} %get-tuple-element.133.blended, bf16[384,192]{1,0:T(8,128)(2,1)S(1)} %get-tuple-element.130.bands), custom_call_target="tpu_custom_call" | custom-call | flops 1000000000 | bytes 4194304 | tf_op jit(solution)/shard_map/pallas_call | solution.py:644
  33.1 1.2 %collective-permute-done.9 = f32[144,128]{1,0:T(8,128)S(1)} collective-permute-done((f32[144,128]{1,0:T(8,128)S(1)}, f32[144,128]{1,0:T(8,128)S(1)}, u32[]{:S(2)}, u32[]{:S(2)}) %collective-permute-start.9) | collective-permute-done | bytes 73760 | tf_op jit(solution)/shard_map/ppermute | solution.py:795
  34.3 4.8 %collective-permute-start.10 = (f32[144,128]{1,0:T(8,128)S(1)}, f32[144,128]{1,0:T(8,128)S(1)}, u32[]{:S(2)}, u32[]{:S(2)}) collective-permute-start(f32[144,128]{1,0:T(8,128)S(1)} %add.13), channel_id=1, source_target_pairs={{0,4},{4,0},{8,12},{12,8},{16,20},{20,16},{24,28},{28,24},{1,5},{5... | collective-permute-start | bytes 221192 | tf_op jit(solution)/shard_map/ppermute | solution.py:795
  39.1 1.7 %shard_map.92 = bf16[32,32,256]{2,1,0:T(8,128)(2,1)} custom-call(bf16[1088,384]{1,0:T(8,128)(2,1)S(1)} %get-tuple-element.133.blended, bf16[384,192]{1,0:T(8,128)(2,1)S(1)} %get-tuple-element.130.bands, bf16[32,32,256]{2,1,0:T(8,128)(2,1)} %shard_map.91.rest_0_), custom_call_target="tpu_custom_call", output_to_operand_aliasing={{}: (2, {})} | custom-call | flops 1000000000 | bytes 4194304 | tf_op jit(solution)/shard_map/pallas_call | solution.py:644
  40.7 0.7 %collective-permute-done.10 = f32[144,128]{1,0:T(8,128)S(1)} collective-permute-done((f32[144,128]{1,0:T(8,128)S(1)}, f32[144,128]{1,0:T(8,128)S(1)}, u32[]{:S(2)}, u32[]{:S(2)}) %collective-permute-start.10) | collective-permute-done | bytes 73760 | tf_op jit(solution)/shard_map/ppermute | solution.py:795
  41.4 2.1 %collective-permute-start.11 = (bf16[144,128]{1,0:T(8,128)(2,1)S(1)}, bf16[144,128]{1,0:T(8,128)(2,1)S(1)}, u32[]{:S(2)}, u32[]{:S(2)}) collective-permute-start(bf16[144,128]{1,0:T(8,128)(2,1)S(1)} %add_convert_fusion.1), channel_id=1, source_target_pairs={{0,8},{4,12},{8,0},{12,4},{16,24},{20,28},{24,16},{28,20},{1,9},{5... | collective-permute-start | bytes 110600 | tf_op jit(solution)/shard_map/ppermute | solution.py:795
  43.6 1.9 %collective-permute-done.11 = bf16[144,128]{1,0:T(8,128)(2,1)S(1)} collective-permute-done((bf16[144,128]{1,0:T(8,128)(2,1)S(1)}, bf16[144,128]{1,0:T(8,128)(2,1)S(1)}, u32[]{:S(2)}, u32[]{:S(2)}) %collective-permute-start.11) | collective-permute-done | bytes 36896 | tf_op jit(solution)/shard_map/ppermute | solution.py:795
  45.5 3.2 %collective-permute-start.12 = (bf16[144,128]{1,0:T(8,128)(2,1)S(1)}, bf16[144,128]{1,0:T(8,128)(2,1)S(1)}, u32[]{:S(2)}, u32[]{:S(2)}) collective-permute-start(bf16[144,128]{1,0:T(8,128)(2,1)S(1)} %add_convert_fusion.mine), channel_id=1, source_target_pairs={{0,16},{4,20},{8,24},{12,28},{16,0},{20,4},{24,8},{28,12},{1,17},{... | collective-permute-start | bytes 110600 | tf_op jit(solution)/shard_map/ppermute | solution.py:795
  48.7 1.9 %collective-permute-done.12.other = bf16[144,128]{1,0:T(8,128)(2,1)S(1)} collective-permute-done((bf16[144,128]{1,0:T(8,128)(2,1)S(1)}, bf16[144,128]{1,0:T(8,128)(2,1)S(1)}, u32[]{:S(2)}, u32[]{:S(2)}) %collective-permute-start.12) | collective-permute-done | bytes 36896 | tf_op jit(solution)/shard_map/ppermute | solution.py:795
  50.6 0.9 %shard_map.93 = (f32[9,32,32]{2,1,0:T(8,128)}, f32[9,32,32]{2,1,0:T(8,128)}) custom-call(bf16[144,128]{1,0:T(8,128)(2,1)S(1)} %add_convert_fusion.mine, bf16[144,128]{1,0:T(8,128)(2,1)S(1)} %collective-permute-done.12.other), custom_call_target="tpu_custom_call" | custom-call | bytes 4194304 | tf_op jit(solution)/shard_map/pallas_call | solution.py:807
  (27 shorter events, 1.0 us)
Async XLA Ops:
  0.6 4.7 %copy-start = (bf16[1,32,32,256]{3,2,1,0:T(8,128)(2,1)S(1)}, bf16[1,32,32,256]{3,2,1,0:T(8,128)(2,1)}, u32[]{:S(2)}) copy-start(bf16[1,32,32,256]{3,2,1,0:T(8,128)(2,1)} %param.13) | copy-start | bytes 1572868
  2.3 5.9 %copy-start.4 = (bf16[1,32,32,256]{3,2,1,0:T(8,128)(2,1)S(1)}, bf16[1,32,32,256]{3,2,1,0:T(8,128)(2,1)}, u32[]{:S(2)}) copy-start(bf16[1,32,32,256]{3,2,1,0:T(8,128)(2,1)} %param.8) | copy-start | bytes 1572868
  2.3 5.9 %copy-start.5 = (s32[1,32,2]{1,2,0:T(2,128)S(1)}, s32[1,32,2]{1,2,0:T(2,128)}, u32[]{:S(2)}) copy-start(s32[1,32,2]{1,2,0:T(2,128)} %param.9) | copy-start | bytes 772
  2.3 15.1 %collective-permute-start.6 = (bf16[448,256]{1,0:T(8,128)(2,1)S(1)}, bf16[448,256]{1,0:T(8,128)(2,1)S(1)}, u32[]{:S(2)}, u32[]{:S(2)}) collective-permute-start(bf16[448,256]{1,0:T(8,128)(2,1)S(1)} %get-tuple-element.114), channel_id=1, source_target_pairs={{0,4},{4,0},{8,12},{12,8},{16,20},{20,16},{24,28},{28,24},{1,5},{5... | collective-permute-start | bytes 688136 | tf_op jit(solution)/shard_map/ppermute | solution.py:730
  6.6 4.3 %collective-permute-start.2 = (bf16[256,128]{1,0:T(8,128)(2,1)S(1)}, bf16[256,128]{1,0:T(8,128)(2,1)S(1)}, u32[]{:S(2)}, u32[]{:S(2)}) collective-permute-start(bf16[256,128]{1,0:T(8,128)(2,1)S(1)} %shard_map.87), channel_id=1, source_target_pairs={{0,2},{2,0},{1,3},{3,1},{4,6},{6,4},{5,7},{7,5},{8,10},{10,8},{9,1... | collective-permute-start | bytes 196616 | tf_op jit(solution)/shard_map/ppermute | solution.py:666
  8.2 1.3 %collective-permute-start.3 = (s32[8,128]{1,0:T(8,128)S(1)}, s32[8,128]{1,0:T(8,128)S(1)}, u32[]{:S(2)}, u32[]{:S(2)}) collective-permute-start(s32[8,128]{1,0:T(8,128)S(1)} %get-tuple-element.107), channel_id=1, source_target_pairs={{0,1},{1,0},{2,3},{3,2},{4,5},{5,4},{6,7},{7,6},{8,9},{9,8},{10,11... | collective-permute-start | bytes 12296 | tf_op jit(solution)/shard_map/ppermute | solution.py:733
  9.5 7.9 %copy-start.1 = (bf16[9,32,32]{2,1,0:T(8,128)(2,1)S(1)}, bf16[9,32,32]{2,1,0:T(8,128)(2,1)}, u32[]{:S(2)}) copy-start(bf16[9,32,32]{2,1,0:T(8,128)(2,1)} %rest_1_.1) | copy-start | bytes 55300
  9.5 7.9 %copy-start.2 = (bf16[9,32,32]{2,1,0:T(8,128)(2,1)S(1)}, bf16[9,32,32]{2,1,0:T(8,128)(2,1)}, u32[]{:S(2)}) copy-start(bf16[9,32,32]{2,1,0:T(8,128)(2,1)} %rest_2_.1) | copy-start | bytes 55300
  9.5 7.9 %copy-start.3 = (bf16[9,32,32]{2,1,0:T(8,128)(2,1)S(1)}, bf16[9,32,32]{2,1,0:T(8,128)(2,1)}, u32[]{:S(2)}) copy-start(bf16[9,32,32]{2,1,0:T(8,128)(2,1)} %rest_3_.1) | copy-start | bytes 55300
  11.0 5.2 %collective-permute-start.4 = (bf16[288,256]{1,0:T(8,128)(2,1)S(1)}, bf16[288,256]{1,0:T(8,128)(2,1)S(1)}, u32[]{:S(2)}, u32[]{:S(2)}) collective-permute-start(bf16[288,256]{1,0:T(8,128)(2,1)S(1)} %get-tuple-element.109), channel_id=1, source_target_pairs={{0,4},{4,0},{8,12},{12,8},{16,20},{20,16},{24,28},{28,24},{1,5},{5... | collective-permute-start | bytes 442376 | tf_op jit(solution)/shard_map/ppermute | solution.py:666
  11.2 6.2 %collective-permute-start.5 = (bf16[288,256]{1,0:T(8,128)(2,1)S(1)}, bf16[288,256]{1,0:T(8,128)(2,1)S(1)}, u32[]{:S(2)}, u32[]{:S(2)}) collective-permute-start(bf16[288,256]{1,0:T(8,128)(2,1)S(1)} %get-tuple-element.113), channel_id=1, source_target_pairs={{4,8},{12,16},{20,24},{8,4},{16,12},{24,20},{5,9},{13,17},{21,25},... | collective-permute-start | bytes 442376 | tf_op jit(solution)/shard_map/ppermute | solution.py:666
  11.8 9.4 %collective-permute-start.7 = (bf16[448,256]{1,0:T(8,128)(2,1)S(1)}, bf16[448,256]{1,0:T(8,128)(2,1)S(1)}, u32[]{:S(2)}, u32[]{:S(2)}) collective-permute-start(bf16[448,256]{1,0:T(8,128)(2,1)S(1)} %shard_map.88), channel_id=1, source_target_pairs={{4,8},{12,16},{20,24},{8,4},{16,12},{24,20},{5,9},{13,17},{21,25},... | collective-permute-start | bytes 688136 | tf_op jit(solution)/shard_map/ppermute | solution.py:744
  28.5 1.3 %collective-permute-start.8 = (f32[144,128]{1,0:T(8,128)S(1)}, f32[144,128]{1,0:T(8,128)S(1)}, u32[]{:S(2)}, u32[]{:S(2)}) collective-permute-start(f32[144,128]{1,0:T(8,128)S(1)} %get-tuple-element.126), channel_id=1, source_target_pairs={{0,1},{1,0},{2,3},{3,2},{4,5},{5,4},{6,7},{7,6},{8,9},{9,8},{10,11... | collective-permute-start | bytes 221192 | tf_op jit(solution)/shard_map/ppermute | solution.py:795
  29.9 4.4 %collective-permute-start.9 = (f32[144,128]{1,0:T(8,128)S(1)}, f32[144,128]{1,0:T(8,128)S(1)}, u32[]{:S(2)}, u32[]{:S(2)}) collective-permute-start(f32[144,128]{1,0:T(8,128)S(1)} %add.12), channel_id=1, source_target_pairs={{0,2},{2,0},{1,3},{3,1},{4,6},{6,4},{5,7},{7,5},{8,10},{10,8},{9,1... | collective-permute-start | bytes 221192 | tf_op jit(solution)/shard_map/ppermute | solution.py:795
  34.3 7.1 %collective-permute-start.10 = (f32[144,128]{1,0:T(8,128)S(1)}, f32[144,128]{1,0:T(8,128)S(1)}, u32[]{:S(2)}, u32[]{:S(2)}) collective-permute-start(f32[144,128]{1,0:T(8,128)S(1)} %add.13), channel_id=1, source_target_pairs={{0,4},{4,0},{8,12},{12,8},{16,20},{20,16},{24,28},{28,24},{1,5},{5... | collective-permute-start | bytes 221192 | tf_op jit(solution)/shard_map/ppermute | solution.py:795
  41.4 4.1 %collective-permute-start.11 = (bf16[144,128]{1,0:T(8,128)(2,1)S(1)}, bf16[144,128]{1,0:T(8,128)(2,1)S(1)}, u32[]{:S(2)}, u32[]{:S(2)}) collective-permute-start(bf16[144,128]{1,0:T(8,128)(2,1)S(1)} %add_convert_fusion.1), channel_id=1, source_target_pairs={{0,8},{4,12},{8,0},{12,4},{16,24},{20,28},{24,16},{28,20},{1,9},{5... | collective-permute-start | bytes 110600 | tf_op jit(solution)/shard_map/ppermute | solution.py:795
  45.5 5.1 %collective-permute-start.12 = (bf16[144,128]{1,0:T(8,128)(2,1)S(1)}, bf16[144,128]{1,0:T(8,128)(2,1)S(1)}, u32[]{:S(2)}, u32[]{:S(2)}) collective-permute-start(bf16[144,128]{1,0:T(8,128)(2,1)S(1)} %add_convert_fusion.mine), channel_id=1, source_target_pairs={{0,16},{4,20},{8,24},{12,28},{16,0},{20,4},{24,8},{28,12},{1,17},{... | collective-permute-start | bytes 110600 | tf_op jit(solution)/shard_map/ppermute | solution.py:795

commit v17 on v16

--- a/solution.py
+++ b/solution.py
@@ -11,6 +11,7 @@
 
 MAXSHIFT = 16
 POOL = 4
+BATCH = 8
 TILE = 128
 SLOT = 32
 EXT = 9
@@ -395,17 +396,17 @@
 
 
 def correlate(u, u0, views, v0, acc, height, chans, span):
-    groups = range(0, height, POOL)
+    groups = range(0, height, BATCH)
     left = jnp.concatenate(
         [
             jnp.concatenate(
-                [view[rows_at(v0 + g, chans, POOL + 2), 0:span] for view in views], axis=0
+                [view[rows_at(v0 + g, chans, BATCH + 2), 0:span] for view in views], axis=0
             )
             for g in groups
         ],
         axis=1,
     )
-    right = jnp.concatenate([u[rows_at(u0 + g, chans, POOL), 0:span] for g in groups], axis=1)
+    right = jnp.concatenate([u[rows_at(u0 + g, chans, BATCH), 0:span] for g in groups], axis=1)
     acc[...] = lax.dot_general(
         left, right, (((1,), (1,)), ((), ())), preferred_element_type=F32
     )
@@ -414,13 +415,17 @@
 def folded(acc, chans):
     lane = lanes_of((3 * chans, TILE))
     result = jnp.zeros((3 * chans, TILE), F32)
+    per_tile = TILE // chans
     for b in range(3):
         total = None
-        for k in range(POOL):
-            block = turn(
-                acc[rows_at(b * (POOL + 2) + k, chans, 3), 0:TILE], (b - k) * chans
-            )
-            total = block if total is None else total + block
+        for place in range(per_tile):
+            column = None
+            for k in range(place, BATCH, per_tile):
+                part = slice(k // per_tile * TILE, (k // per_tile + 1) * TILE)
+                block = acc[rows_at(b * (BATCH + 2) + k, chans, 3), part]
+                column = block if column is None else column + block
+            column = turn(column, (b - place) * chans)
+            total = column if total is None else total + column
         result = jnp.where((lane >= b * chans) & (lane < (b + 1) * chans), total, result)
     return result
 
@@ -536,7 +541,7 @@
 
     for g in (0, 1, groups + 2, groups + 3):
         first_group(g, False)
-    lax.fori_loop(2, groups + 2, lambda g, _: first_group(g, True), 0, unroll=4)
+    lax.fori_loop(2, groups + 2, lambda g, _: first_group(g, True), 0, unroll=8)
     sums = block_sums(high, low)
     seen_cells = cells_seen((chans, TILE), span)
     for g in range(groups + 4):
@@ -701,7 +706,7 @@
         + [pltpu.VMEM(((groups + 4) * chans, TILE), BF16)]
         + [
             pltpu.VMEM((full, span), BF16),
-            pltpu.VMEM((band, POOL * chans), F32),
+            pltpu.VMEM((3 * (BATCH + 2) * chans, BATCH * chans), F32),
         ],
         11,
         20,

time: 51.8 us -> 51.1 us (0.986)
  Pallas kernels: 19.3 us -> 18.6 us
    pallas_call x1, Pallas kernels: 7.09 us -> 6.41 us  [main_pass(): call(main_kernel, (jax.ShapeDtypeStruct((9 * chans // 2, TILE), F32), bf(...]
where the time goes in v17:
time: 51.1 us; the launch traced here: 50.9 us
  Pallas kernels  18.6 us (36%)
  starting transfers between devices  17.8 us (35%)
  waiting for transfers between devices  12.2 us (24%)
  between operations  1.5 us (3%)
  local copies, waits for them, and re-layouts  0.55 us (1%)
    ppermute x5, starting transfers between devices, shards(): other = lax.ppermute(grads, axis, pairs)  11.7 us
    ppermute x5, waiting for transfers between devices, shards(): other = lax.ppermute(grads, axis, pairs)  7 us
    pallas_call x1, Pallas kernels, main_pass(): call(main_kernel, (jax.ShapeDtypeStruct((9 * chans // 2, TILE), F32), bf(...  6.41 us
    ppermute x3, waiting for transfers between devices, swapped(): return [lax.ppermute(m, axis, p) for m, p in zip(messages, pairs)]  5.15 us
    pallas_call x1, Pallas kernels, shards(): call(functools.partial(back_kernel, ncols), (jax.ShapeDtypeStruct((full,...  3.74 us
    pallas_call x2, Pallas kernels, predict(): call(functools.partial(predict_kernel, part), jax.ShapeDtypeStruct(shape,...  3.34 us
    ppermute x1, starting transfers between devices, shards(): feat_a = lax.ppermute(message, 'rows', row_pairs[0])  3.03 us
    pallas_call x2, Pallas kernels, pack_rows(): call(functools.partial(feature_kernel, index, skip), message, [], 2, 16,...  2.75 us
  transfers between devices with their start and end apart: 11, of which 7 were waited for; matrix products, arithmetic and copies ran while one was open for 1% of the time, Pallas kernels for 19%

profile of v17, /device:TPU:0, one launch (start us, length us, event | category | flops | bytes accessed | tf_op | source)
XLA Modules:
  0.0 50.9 jit_solution(1988566036159097471)
XLA Ops:
  0.6 1.7 %shard_map.85 = (bf16[448,256]{1,0:T(8,128)(2,1)S(1)}, s32[8,128]{1,0:T(8,128)S(1)}) custom-call(s32[2,32]{1,0:T(2,128)} %bitcast.14, bf16[32,32,256]{2,1,0:T(8,128)(2,1)} %bitcast.9), custom_call_target="tpu_custom_call" | custom-call | bytes 4194304 | tf_op jit(solution)/shard_map/pallas_call | solution.py:678
  2.3 3.0 %collective-permute-start.6 = (bf16[448,256]{1,0:T(8,128)(2,1)S(1)}, bf16[448,256]{1,0:T(8,128)(2,1)S(1)}, u32[]{:S(2)}, u32[]{:S(2)}) collective-permute-start(bf16[448,256]{1,0:T(8,128)(2,1)S(1)} %get-tuple-element.114), channel_id=1, source_target_pairs={{0,4},{4,0},{8,12},{12,8},{16,20},{20,16},{24,28},{28,24},{1,5},{5... | collective-permute-start | bytes 688136 | tf_op jit(solution)/shard_map/ppermute | solution.py:735
  5.4 1.2 %shard_map.87 = bf16[256,128]{1,0:T(8,128)(2,1)S(1)} custom-call(bf16[32,32,256]{2,1,0:T(8,128)(2,1)} %bitcast.10, bf16[32,32,256]{2,1,0:T(8,128)(2,1)S(1)} %bitcast.7), custom_call_target="tpu_custom_call" | custom-call | flops 20000000000 | bytes 4194304 | tf_op jit(solution)/shard_map/pallas_call | solution.py:742
  6.6 1.6 %collective-permute-start.2 = (bf16[256,128]{1,0:T(8,128)(2,1)S(1)}, bf16[256,128]{1,0:T(8,128)(2,1)S(1)}, u32[]{:S(2)}, u32[]{:S(2)}) collective-permute-start(bf16[256,128]{1,0:T(8,128)(2,1)S(1)} %shard_map.87), channel_id=1, source_target_pairs={{0,2},{2,0},{1,3},{3,1},{4,6},{6,4},{5,7},{7,5},{8,10},{10,8},{9,1... | collective-permute-start | bytes 196616 | tf_op jit(solution)/shard_map/ppermute | solution.py:671
  8.2 1.1 %shard_map.88 = bf16[448,256]{1,0:T(8,128)(2,1)S(1)} custom-call(s32[2,32]{1,0:T(2,128)S(1)} %bitcast.15, bf16[32,32,256]{2,1,0:T(8,128)(2,1)S(1)} %bitcast.11), custom_call_target="tpu_custom_call" | custom-call | bytes 4194304 | tf_op jit(solution)/shard_map/pallas_call | solution.py:678
  9.5 1.4 %collective-permute-done.2.rest_0_ = bf16[256,128]{1,0:T(8,128)(2,1)S(1)} collective-permute-done((bf16[256,128]{1,0:T(8,128)(2,1)S(1)}, bf16[256,128]{1,0:T(8,128)(2,1)S(1)}, u32[]{:S(2)}, u32[]{:S(2)}) %collective-permute-start.2) | collective-permute-done | bytes 65568 | tf_op jit(solution)/shard_map/ppermute | solution.py:671
  11.2 0.7 %collective-permute-start.5 = (bf16[288,256]{1,0:T(8,128)(2,1)S(1)}, bf16[288,256]{1,0:T(8,128)(2,1)S(1)}, u32[]{:S(2)}, u32[]{:S(2)}) collective-permute-start(bf16[288,256]{1,0:T(8,128)(2,1)S(1)} %get-tuple-element.113), channel_id=1, source_target_pairs={{4,8},{12,16},{20,24},{8,4},{16,12},{24,20},{5,9},{13,17},{21,25},... | collective-permute-start | bytes 442376 | tf_op jit(solution)/shard_map/ppermute | solution.py:671
  11.8 0.7 %collective-permute-start.7 = (bf16[448,256]{1,0:T(8,128)(2,1)S(1)}, bf16[448,256]{1,0:T(8,128)(2,1)S(1)}, u32[]{:S(2)}, u32[]{:S(2)}) collective-permute-start(bf16[448,256]{1,0:T(8,128)(2,1)S(1)} %shard_map.88), channel_id=1, source_target_pairs={{4,8},{12,16},{20,24},{8,4},{16,12},{24,20},{5,9},{13,17},{21,25},... | collective-permute-start | bytes 688136 | tf_op jit(solution)/shard_map/ppermute | solution.py:749
  12.5 3.7 %collective-permute-done.4.msg_a = bf16[288,256]{1,0:T(8,128)(2,1)S(1)} collective-permute-done((bf16[288,256]{1,0:T(8,128)(2,1)S(1)}, bf16[288,256]{1,0:T(8,128)(2,1)S(1)}, u32[]{:S(2)}, u32[]{:S(2)}) %collective-permute-start.4) | collective-permute-done | bytes 147488 | tf_op jit(solution)/shard_map/ppermute | solution.py:671
  17.4 3.7 %shard_map.90 = (f32[1024,256]{1,0:T(8,128)S(1)}, bf16[1344,384]{1,0:T(8,128)(2,1)S(1)}, bf16[1344,384]{1,0:T(8,128)(2,1)S(1)}, bf16[1344,384]{1,0:T(8,128)(2,1)...) custom-call(bf16[1024,256]{1,0:T(8,128)(2,1)S(1)} %shard_map.86.cot_, ...), custom_call_target="tpu_custom_call" | custom-call | flops 8000000000 | bytes 4194304 | tf_op jit(solution)/shard_map/pallas_call | solution.py:760
  21.2 6.7 %conditional.1 = ((f32[144,128]{1,0:T(8,128)S(1)}, bf16[1088,384]{1,0:T(8,128)(2,1)S(1)})) conditional(s32[]{:T(128)} %bitcast.5, (s32[2,32]{1,0:T(2,128)S(1)}, bf16[32,32,256]{2,1,0:T(8,128)(2,1)S(1)}, bf16[448,256]{1,0:T(8,128)(2,1)S(1)}, bf16[448,256]{1,0:T(8,128)(2,1)S(1)}, bf16[32,96,128]{2,1,0:T(8,128)(2,1)S(1)}, ...), branch_computations={%region_0.0_spmd, %region_1.0_spmd} | conditional | flops 10001703936 | bytes 15859800 | solution.py:783
  21.2 6.4 %branch_1_fun.1 = (f32[144,128]{1,0:T(8,128)S(1)}, bf16[1088,384]{1,0:T(8,128)(2,1)S(1)}) custom-call(s32[2,32]{1,0:T(2,128)S(1)} %get-tuple-element.55.shifts, bf16[32,32,256]{2,1,0:T(8,128)(2,1)S(1)} %get-tuple-element.56.feat, bf16[448,256]{1,0:T(8,128)(2,1)S(1)} %get-tuple-element.57.feat_a, bf16[448,256]{1,0:T(8,128)(2,1)S(1)} %get-tuple-element.58.feat_b, ...), custom_call_target="tpu_custom_call" | custom-call | flops 10000000000 | bytes 4194304 | tf_op jit(solution)/shard_map/cond/branch_1_fun/pallas_call | solution.py:696
  27.9 1.3 %collective-permute-done.8 = f32[144,128]{1,0:T(8,128)S(1)} collective-permute-done((f32[144,128]{1,0:T(8,128)S(1)}, f32[144,128]{1,0:T(8,128)S(1)}, u32[]{:S(2)}, u32[]{:S(2)}) %collective-permute-start.8) | collective-permute-done | bytes 73760 | tf_op jit(solution)/shard_map/ppermute | solution.py:800
  29.2 1.5 %collective-permute-start.9 = (f32[144,128]{1,0:T(8,128)S(1)}, f32[144,128]{1,0:T(8,128)S(1)}, u32[]{:S(2)}, u32[]{:S(2)}) collective-permute-start(f32[144,128]{1,0:T(8,128)S(1)} %add.12), channel_id=1, source_target_pairs={{0,2},{2,0},{1,3},{3,1},{4,6},{6,4},{5,7},{7,5},{8,10},{10,8},{9,1... | collective-permute-start | bytes 221192 | tf_op jit(solution)/shard_map/ppermute | solution.py:800
  30.7 1.7 %shard_map.91.rest_0_ = bf16[32,32,256]{2,1,0:T(8,128)(2,1)} custom-call(bf16[1088,384]{1,0:T(8,128)(2,1)S(1)} %get-tuple-element.133.blended, bf16[384,192]{1,0:T(8,128)(2,1)S(1)} %get-tuple-element.130.bands), custom_call_target="tpu_custom_call" | custom-call | flops 1000000000 | bytes 4194304 | tf_op jit(solution)/shard_map/pallas_call | solution.py:649
  32.4 1.2 %collective-permute-done.9 = f32[144,128]{1,0:T(8,128)S(1)} collective-permute-done((f32[144,128]{1,0:T(8,128)S(1)}, f32[144,128]{1,0:T(8,128)S(1)}, u32[]{:S(2)}, u32[]{:S(2)}) %collective-permute-start.9) | collective-permute-done | bytes 73760 | tf_op jit(solution)/shard_map/ppermute | solution.py:800
  33.6 4.8 %collective-permute-start.10 = (f32[144,128]{1,0:T(8,128)S(1)}, f32[144,128]{1,0:T(8,128)S(1)}, u32[]{:S(2)}, u32[]{:S(2)}) collective-permute-start(f32[144,128]{1,0:T(8,128)S(1)} %add.13), channel_id=1, source_target_pairs={{0,4},{4,0},{8,12},{12,8},{16,20},{20,16},{24,28},{28,24},{1,5},{5... | collective-permute-start | bytes 221192 | tf_op jit(solution)/shard_map/ppermute | solution.py:800
  38.4 1.7 %shard_map.92 = bf16[32,32,256]{2,1,0:T(8,128)(2,1)} custom-call(bf16[1088,384]{1,0:T(8,128)(2,1)S(1)} %get-tuple-element.133.blended, bf16[384,192]{1,0:T(8,128)(2,1)S(1)} %get-tuple-element.130.bands, bf16[32,32,256]{2,1,0:T(8,128)(2,1)} %shard_map.91.rest_0_), custom_call_target="tpu_custom_call", output_to_operand_aliasing={{}: (2, {})} | custom-call | flops 1000000000 | bytes 4194304 | tf_op jit(solution)/shard_map/pallas_call | solution.py:649
  40.1 0.7 %collective-permute-done.10 = f32[144,128]{1,0:T(8,128)S(1)} collective-permute-done((f32[144,128]{1,0:T(8,128)S(1)}, f32[144,128]{1,0:T(8,128)S(1)}, u32[]{:S(2)}, u32[]{:S(2)}) %collective-permute-start.10) | collective-permute-done | bytes 73760 | tf_op jit(solution)/shard_map/ppermute | solution.py:800
  40.7 2.1 %collective-permute-start.11 = (bf16[144,128]{1,0:T(8,128)(2,1)S(1)}, bf16[144,128]{1,0:T(8,128)(2,1)S(1)}, u32[]{:S(2)}, u32[]{:S(2)}) collective-permute-start(bf16[144,128]{1,0:T(8,128)(2,1)S(1)} %add_convert_fusion.1), channel_id=1, source_target_pairs={{0,8},{4,12},{8,0},{12,4},{16,24},{20,28},{24,16},{28,20},{1,9},{5... | collective-permute-start | bytes 110600 | tf_op jit(solution)/shard_map/ppermute | solution.py:800
  42.9 1.9 %collective-permute-done.11 = bf16[144,128]{1,0:T(8,128)(2,1)S(1)} collective-permute-done((bf16[144,128]{1,0:T(8,128)(2,1)S(1)}, bf16[144,128]{1,0:T(8,128)(2,1)S(1)}, u32[]{:S(2)}, u32[]{:S(2)}) %collective-permute-start.11) | collective-permute-done | bytes 36896 | tf_op jit(solution)/shard_map/ppermute | solution.py:800
  44.8 3.2 %collective-permute-start.12 = (bf16[144,128]{1,0:T(8,128)(2,1)S(1)}, bf16[144,128]{1,0:T(8,128)(2,1)S(1)}, u32[]{:S(2)}, u32[]{:S(2)}) collective-permute-start(bf16[144,128]{1,0:T(8,128)(2,1)S(1)} %add_convert_fusion.mine), channel_id=1, source_target_pairs={{0,16},{4,20},{8,24},{12,28},{16,0},{20,4},{24,8},{28,12},{1,17},{... | collective-permute-start | bytes 110600 | tf_op jit(solution)/shard_map/ppermute | solution.py:800
  48.0 1.9 %collective-permute-done.12.other = bf16[144,128]{1,0:T(8,128)(2,1)S(1)} collective-permute-done((bf16[144,128]{1,0:T(8,128)(2,1)S(1)}, bf16[144,128]{1,0:T(8,128)(2,1)S(1)}, u32[]{:S(2)}, u32[]{:S(2)}) %collective-permute-start.12) | collective-permute-done | bytes 36896 | tf_op jit(solution)/shard_map/ppermute | solution.py:800
  49.9 0.9 %shard_map.93 = (f32[9,32,32]{2,1,0:T(8,128)}, f32[9,32,32]{2,1,0:T(8,128)}) custom-call(bf16[144,128]{1,0:T(8,128)(2,1)S(1)} %add_convert_fusion.mine, bf16[144,128]{1,0:T(8,128)(2,1)S(1)} %collective-permute-done.12.other), custom_call_target="tpu_custom_call" | custom-call | bytes 4194304 | tf_op jit(solution)/shard_map/pallas_call | solution.py:812
  (27 shorter events, 1.0 us)
Async XLA Ops:
  0.6 4.7 %copy-start = (bf16[1,32,32,256]{3,2,1,0:T(8,128)(2,1)S(1)}, bf16[1,32,32,256]{3,2,1,0:T(8,128)(2,1)}, u32[]{:S(2)}) copy-start(bf16[1,32,32,256]{3,2,1,0:T(8,128)(2,1)} %param.13) | copy-start | bytes 1572868
  2.3 5.9 %copy-start.4 = (bf16[1,32,32,256]{3,2,1,0:T(8,128)(2,1)S(1)}, bf16[1,32,32,256]{3,2,1,0:T(8,128)(2,1)}, u32[]{:S(2)}) copy-start(bf16[1,32,32,256]{3,2,1,0:T(8,128)(2,1)} %param.8) | copy-start | bytes 1572868
  2.3 5.9 %copy-start.5 = (s32[1,32,2]{1,2,0:T(2,128)S(1)}, s32[1,32,2]{1,2,0:T(2,128)}, u32[]{:S(2)}) copy-start(s32[1,32,2]{1,2,0:T(2,128)} %param.9) | copy-start | bytes 772
  2.3 15.1 %collective-permute-start.6 = (bf16[448,256]{1,0:T(8,128)(2,1)S(1)}, bf16[448,256]{1,0:T(8,128)(2,1)S(1)}, u32[]{:S(2)}, u32[]{:S(2)}) collective-permute-start(bf16[448,256]{1,0:T(8,128)(2,1)S(1)} %get-tuple-element.114), channel_id=1, source_target_pairs={{0,4},{4,0},{8,12},{12,8},{16,20},{20,16},{24,28},{28,24},{1,5},{5... | collective-permute-start | bytes 688136 | tf_op jit(solution)/shard_map/ppermute | solution.py:735
  6.6 4.3 %collective-permute-start.2 = (bf16[256,128]{1,0:T(8,128)(2,1)S(1)}, bf16[256,128]{1,0:T(8,128)(2,1)S(1)}, u32[]{:S(2)}, u32[]{:S(2)}) collective-permute-start(bf16[256,128]{1,0:T(8,128)(2,1)S(1)} %shard_map.87), channel_id=1, source_target_pairs={{0,2},{2,0},{1,3},{3,1},{4,6},{6,4},{5,7},{7,5},{8,10},{10,8},{9,1... | collective-permute-start | bytes 196616 | tf_op jit(solution)/shard_map/ppermute | solution.py:671
  8.2 1.3 %collective-permute-start.3 = (s32[8,128]{1,0:T(8,128)S(1)}, s32[8,128]{1,0:T(8,128)S(1)}, u32[]{:S(2)}, u32[]{:S(2)}) collective-permute-start(s32[8,128]{1,0:T(8,128)S(1)} %get-tuple-element.107), channel_id=1, source_target_pairs={{0,1},{1,0},{2,3},{3,2},{4,5},{5,4},{6,7},{7,6},{8,9},{9,8},{10,11... | collective-permute-start | bytes 12296 | tf_op jit(solution)/shard_map/ppermute | solution.py:738
  9.5 7.9 %copy-start.1 = (bf16[9,32,32]{2,1,0:T(8,128)(2,1)S(1)}, bf16[9,32,32]{2,1,0:T(8,128)(2,1)}, u32[]{:S(2)}) copy-start(bf16[9,32,32]{2,1,0:T(8,128)(2,1)} %rest_1_.1) | copy-start | bytes 55300
  9.5 7.9 %copy-start.2 = (bf16[9,32,32]{2,1,0:T(8,128)(2,1)S(1)}, bf16[9,32,32]{2,1,0:T(8,128)(2,1)}, u32[]{:S(2)}) copy-start(bf16[9,32,32]{2,1,0:T(8,128)(2,1)} %rest_2_.1) | copy-start | bytes 55300
  9.5 7.9 %copy-start.3 = (bf16[9,32,32]{2,1,0:T(8,128)(2,1)S(1)}, bf16[9,32,32]{2,1,0:T(8,128)(2,1)}, u32[]{:S(2)}) copy-start(bf16[9,32,32]{2,1,0:T(8,128)(2,1)} %rest_3_.1) | copy-start | bytes 55300
  11.0 5.2 %collective-permute-start.4 = (bf16[288,256]{1,0:T(8,128)(2,1)S(1)}, bf16[288,256]{1,0:T(8,128)(2,1)S(1)}, u32[]{:S(2)}, u32[]{:S(2)}) collective-permute-start(bf16[288,256]{1,0:T(8,128)(2,1)S(1)} %get-tuple-element.109), channel_id=1, source_target_pairs={{0,4},{4,0},{8,12},{12,8},{16,20},{20,16},{24,28},{28,24},{1,5},{5... | collective-permute-start | bytes 442376 | tf_op jit(solution)/shard_map/ppermute | solution.py:671
  11.2 6.2 %collective-permute-start.5 = (bf16[288,256]{1,0:T(8,128)(2,1)S(1)}, bf16[288,256]{1,0:T(8,128)(2,1)S(1)}, u32[]{:S(2)}, u32[]{:S(2)}) collective-permute-start(bf16[288,256]{1,0:T(8,128)(2,1)S(1)} %get-tuple-element.113), channel_id=1, source_target_pairs={{4,8},{12,16},{20,24},{8,4},{16,12},{24,20},{5,9},{13,17},{21,25},... | collective-permute-start | bytes 442376 | tf_op jit(solution)/shard_map/ppermute | solution.py:671
  11.8 9.4 %collective-permute-start.7 = (bf16[448,256]{1,0:T(8,128)(2,1)S(1)}, bf16[448,256]{1,0:T(8,128)(2,1)S(1)}, u32[]{:S(2)}, u32[]{:S(2)}) collective-permute-start(bf16[448,256]{1,0:T(8,128)(2,1)S(1)} %shard_map.88), channel_id=1, source_target_pairs={{4,8},{12,16},{20,24},{8,4},{16,12},{24,20},{5,9},{13,17},{21,25},... | collective-permute-start | bytes 688136 | tf_op jit(solution)/shard_map/ppermute | solution.py:749
  27.8 1.3 %collective-permute-start.8 = (f32[144,128]{1,0:T(8,128)S(1)}, f32[144,128]{1,0:T(8,128)S(1)}, u32[]{:S(2)}, u32[]{:S(2)}) collective-permute-start(f32[144,128]{1,0:T(8,128)S(1)} %get-tuple-element.126), channel_id=1, source_target_pairs={{0,1},{1,0},{2,3},{3,2},{4,5},{5,4},{6,7},{7,6},{8,9},{9,8},{10,11... | collective-permute-start | bytes 221192 | tf_op jit(solution)/shard_map/ppermute | solution.py:800
  29.2 4.4 %collective-permute-start.9 = (f32[144,128]{1,0:T(8,128)S(1)}, f32[144,128]{1,0:T(8,128)S(1)}, u32[]{:S(2)}, u32[]{:S(2)}) collective-permute-start(f32[144,128]{1,0:T(8,128)S(1)} %add.12), channel_id=1, source_target_pairs={{0,2},{2,0},{1,3},{3,1},{4,6},{6,4},{5,7},{7,5},{8,10},{10,8},{9,1... | collective-permute-start | bytes 221192 | tf_op jit(solution)/shard_map/ppermute | solution.py:800
  33.6 7.1 %collective-permute-start.10 = (f32[144,128]{1,0:T(8,128)S(1)}, f32[144,128]{1,0:T(8,128)S(1)}, u32[]{:S(2)}, u32[]{:S(2)}) collective-permute-start(f32[144,128]{1,0:T(8,128)S(1)} %add.13), channel_id=1, source_target_pairs={{0,4},{4,0},{8,12},{12,8},{16,20},{20,16},{24,28},{28,24},{1,5},{5... | collective-permute-start | bytes 221192 | tf_op jit(solution)/shard_map/ppermute | solution.py:800
  40.7 4.1 %collective-permute-start.11 = (bf16[144,128]{1,0:T(8,128)(2,1)S(1)}, bf16[144,128]{1,0:T(8,128)(2,1)S(1)}, u32[]{:S(2)}, u32[]{:S(2)}) collective-permute-start(bf16[144,128]{1,0:T(8,128)(2,1)S(1)} %add_convert_fusion.1), channel_id=1, source_target_pairs={{0,8},{4,12},{8,0},{12,4},{16,24},{20,28},{24,16},{28,20},{1,9},{5... | collective-permute-start | bytes 110600 | tf_op jit(solution)/shard_map/ppermute | solution.py:800
  44.8 5.1 %collective-permute-start.12 = (bf16[144,128]{1,0:T(8,128)(2,1)S(1)}, bf16[144,128]{1,0:T(8,128)(2,1)S(1)}, u32[]{:S(2)}, u32[]{:S(2)}) collective-permute-start(bf16[144,128]{1,0:T(8,128)(2,1)S(1)} %add_convert_fusion.mine), channel_id=1, source_target_pairs={{0,16},{4,20},{8,24},{12,28},{16,0},{20,4},{24,8},{28,12},{1,17},{... | collective-permute-start | bytes 110600 | tf_op jit(solution)/shard_map/ppermute | solution.py:800

commit v18 on v17

--- a/solution.py
+++ b/solution.py
@@ -236,8 +236,10 @@
 
 def block_sums(high, low):
     matrix = cell_matrix(high.shape[1], False)
-    return jnp.dot(high[...], matrix, preferred_element_type=F32) + jnp.dot(
-        low[...], matrix, preferred_element_type=F32
+    return jnp.dot(
+        jnp.concatenate([high[...], low[...]], axis=1),
+        jnp.concatenate([matrix, matrix], axis=0),
+        preferred_element_type=F32,
     )
 
 
@@ -279,6 +281,17 @@
 
 def stacked(views, at):
     return jnp.concatenate([view[at, :] for view in views], axis=0)
+
+
+def paired(bands, views, g, chans):
+    width = views[0].shape[1]
+    sides = [
+        stacked(views, rows_at((g + i) * POOL, chans, POOL + 2)) for i in (0, 1)
+    ]
+    parts = jnp.dot(
+        bands[...], jnp.concatenate(sides, axis=1), preferred_element_type=F32
+    )
+    return parts[:, 0:width], parts[:, width:]
 
 
 def conv_sum(parts, chans, step):
@@ -360,20 +373,19 @@
         at = rows_at(j, chans)
         cot_m[at] = turn(cot_0[at], 1)
         cot_p[at] = turn(cot_0[at], -1)
-    def group(g, _):
-        at = rows_at(g * POOL, chans, POOL + 2)
-        rows = jnp.dot(
-            bands[...], stacked((cot_m, cot_0, cot_p), at), preferred_element_type=F32
-        ).astype(BF16)
-        back[rows_at(g * POOL, chans, POOL), :] = rows[:, 0:span]
-        rows = rows.astype(F32)
-        total = rows[0:chans]
-        for k in range(1, POOL):
-            total = total + rows[k * chans : (k + 1) * chans]
-        store_split(high, low, rows_at(g, chans), total)
+    def pair(p, _):
+        both = paired(bands, (cot_m, cot_0, cot_p), 2 * p, chans)
+        for g, rows in zip((2 * p, 2 * p + 1), both):
+            rows = rows.astype(BF16)
+            back[rows_at(g * POOL, chans, POOL), :] = rows[:, 0:span]
+            rows = rows.astype(F32)
+            total = rows[0:chans]
+            for k in range(1, POOL):
+                total = total + rows[k * chans : (k + 1) * chans]
+            store_split(high, low, rows_at(g, chans), total)
         return 0
 
-    lax.fori_loop(0, groups + 2, group, 0, unroll=5)
+    lax.fori_loop(0, (groups + 2) // 2, pair, 0, unroll=5)
     sums = block_sums(high, low)
     seen_cells = cells_seen((chans, TILE), span)
     for g in range(groups + 2):
@@ -518,30 +530,23 @@
         warp_m[at] = turn(warp_0[at], 1)
         warp_p[at] = turn(warp_0[at], -1)
 
-    def first_group(g, own):
-        at = rows_at(g * POOL, chans, POOL + 2)
-        pre = jnp.dot(
-            bands[...], stacked((warp_m, warp_0, warp_p), at), preferred_element_type=F32
-        )
-        sigma = 0.5 * jnp.tanh(0.5 * pre) + 0.5
-        rows = (pre * sigma).astype(BF16)
-        act[rows_at(g * POOL, chans, POOL), :] = rows
-        rows = rows.astype(F32)
-        total = rows[0:chans]
-        for k in range(1, POOL):
-            total = total + rows[k * chans : (k + 1) * chans]
-        store_split(high, low, rows_at(g, chans), total)
-        if own:
-            there = rows_at(g * POOL - 2 * POOL, chans, POOL)
-            pre, sigma = pre[:, 0:span], sigma[:, 0:span]
-            pre_grad[there, :] = (
-                act_grad[there, :] * (sigma * (1.0 + pre * (1.0 - sigma)))
-            ).astype(BF16)
-        return 0
-
-    for g in (0, 1, groups + 2, groups + 3):
-        first_group(g, False)
-    lax.fori_loop(2, groups + 2, lambda g, _: first_group(g, True), 0, unroll=8)
+    for g in range(0, groups + 4, 2):
+        both = paired(bands, (warp_m, warp_0, warp_p), g, chans)
+        for g, pre in zip((g, g + 1), both):
+            sigma = 0.5 * jnp.tanh(0.5 * pre) + 0.5
+            rows = (pre * sigma).astype(BF16)
+            act[rows_at(g * POOL, chans, POOL), :] = rows
+            rows = rows.astype(F32)
+            total = rows[0:chans]
+            for k in range(1, POOL):
+                total = total + rows[k * chans : (k + 1) * chans]
+            store_split(high, low, rows_at(g, chans), total)
+            if 2 <= g < groups + 2:
+                there = rows_at(g * POOL - 2 * POOL, chans, POOL)
+                pre, sigma = pre[:, 0:span], sigma[:, 0:span]
+                pre_grad[there, :] = (
+                    act_grad[there, :] * (sigma * (1.0 + pre * (1.0 - sigma)))
+                ).astype(BF16)
     sums = block_sums(high, low)
     seen_cells = cells_seen((chans, TILE), span)
     for g in range(groups + 4):

time: 51.1 us -> 51 us (level)
  Pallas kernels: 18.6 us -> 17.6 us
  starting transfers between devices: 17.8 us -> 18.7 us
    ppermute x5, starting transfers between devices: 11.7 us -> 12.6 us  [shards(): other = lax.ppermute(grads, axis, pairs)]
    pallas_call x1, Pallas kernels: 3.74 us -> 2.85 us  [shards(): call(functools.partial(back_kernel, ncols), (jax.ShapeDtypeStruct((full,...]
  transfers between devices with their start and end apart: 11 -> 11, of which waited for: 7 -> 7; matrix products, arithmetic and copies ran while one was open for 1% -> 1% of each run, Pallas kernels for 19% -> 17%
where the time goes in v18:
time: 51 us; the launch traced here: 50.8 us
  starting transfers between devices  18.7 us (37%)
  Pallas kernels  17.6 us (35%)
  waiting for transfers between devices  12.1 us (24%)
  between operations  1.5 us (3%)
  local copies, waits for them, and re-layouts  0.55 us (1%)
    ppermute x5, starting transfers between devices, shards(): other = lax.ppermute(grads, axis, pairs)  12.6 us
    ppermute x5, waiting for transfers between devices, shards(): other = lax.ppermute(grads, axis, pairs)  6.98 us
    pallas_call x1, Pallas kernels, main_pass(): call(main_kernel, (jax.ShapeDtypeStruct((9 * chans // 2, TILE), F32), bf(...  6.34 us
    ppermute x3, waiting for transfers between devices, swapped(): return [lax.ppermute(m, axis, p) for m, p in zip(messages, pairs)]  5.15 us
    pallas_call x2, Pallas kernels, predict(): call(functools.partial(predict_kernel, part), jax.ShapeDtypeStruct(shape,...  3.34 us
    ppermute x1, starting transfers between devices, shards(): feat_a = lax.ppermute(message, 'rows', row_pairs[0])  3.03 us
    pallas_call x1, Pallas kernels, shards(): call(functools.partial(back_kernel, ncols), (jax.ShapeDtypeStruct((full,...  2.85 us
    pallas_call x2, Pallas kernels, pack_rows(): call(functools.partial(feature_kernel, index, skip), message, [], 2, 16,...  2.75 us
  transfers between devices with their start and end apart: 11, of which 7 were waited for; matrix products, arithmetic and copies ran while one was open for 1% of the time, Pallas kernels for 17%

profile of v18, /device:TPU:0, one launch (start us, length us, event | category | flops | bytes accessed | tf_op | source)
XLA Modules:
  0.0 50.8 jit_solution(2307695620924731486)
XLA Ops:
  0.6 1.7 %shard_map.85 = (bf16[448,256]{1,0:T(8,128)(2,1)S(1)}, s32[8,128]{1,0:T(8,128)S(1)}) custom-call(s32[2,32]{1,0:T(2,128)} %bitcast.14, bf16[32,32,256]{2,1,0:T(8,128)(2,1)} %bitcast.9), custom_call_target="tpu_custom_call" | custom-call | bytes 4194304 | tf_op jit(solution)/shard_map/pallas_call | solution.py:683
  2.3 3.0 %collective-permute-start.6 = (bf16[448,256]{1,0:T(8,128)(2,1)S(1)}, bf16[448,256]{1,0:T(8,128)(2,1)S(1)}, u32[]{:S(2)}, u32[]{:S(2)}) collective-permute-start(bf16[448,256]{1,0:T(8,128)(2,1)S(1)} %get-tuple-element.114), channel_id=1, source_target_pairs={{0,4},{4,0},{8,12},{12,8},{16,20},{20,16},{24,28},{28,24},{1,5},{5... | collective-permute-start | bytes 688136 | tf_op jit(solution)/shard_map/ppermute | solution.py:740
  5.4 1.2 %shard_map.87 = bf16[256,128]{1,0:T(8,128)(2,1)S(1)} custom-call(bf16[32,32,256]{2,1,0:T(8,128)(2,1)} %bitcast.10, bf16[32,32,256]{2,1,0:T(8,128)(2,1)S(1)} %bitcast.7), custom_call_target="tpu_custom_call" | custom-call | flops 20000000000 | bytes 4194304 | tf_op jit(solution)/shard_map/pallas_call | solution.py:747
  6.6 1.6 %collective-permute-start.2 = (bf16[256,128]{1,0:T(8,128)(2,1)S(1)}, bf16[256,128]{1,0:T(8,128)(2,1)S(1)}, u32[]{:S(2)}, u32[]{:S(2)}) collective-permute-start(bf16[256,128]{1,0:T(8,128)(2,1)S(1)} %shard_map.87), channel_id=1, source_target_pairs={{0,2},{2,0},{1,3},{3,1},{4,6},{6,4},{5,7},{7,5},{8,10},{10,8},{9,1... | collective-permute-start | bytes 196616 | tf_op jit(solution)/shard_map/ppermute | solution.py:676
  8.2 1.1 %shard_map.88 = bf16[448,256]{1,0:T(8,128)(2,1)S(1)} custom-call(s32[2,32]{1,0:T(2,128)S(1)} %bitcast.15, bf16[32,32,256]{2,1,0:T(8,128)(2,1)S(1)} %bitcast.11), custom_call_target="tpu_custom_call" | custom-call | bytes 4194304 | tf_op jit(solution)/shard_map/pallas_call | solution.py:683
  9.5 1.4 %collective-permute-done.2.rest_0_ = bf16[256,128]{1,0:T(8,128)(2,1)S(1)} collective-permute-done((bf16[256,128]{1,0:T(8,128)(2,1)S(1)}, bf16[256,128]{1,0:T(8,128)(2,1)S(1)}, u32[]{:S(2)}, u32[]{:S(2)}) %collective-permute-start.2) | collective-permute-done | bytes 65568 | tf_op jit(solution)/shard_map/ppermute | solution.py:676
  11.2 0.7 %collective-permute-start.5 = (bf16[288,256]{1,0:T(8,128)(2,1)S(1)}, bf16[288,256]{1,0:T(8,128)(2,1)S(1)}, u32[]{:S(2)}, u32[]{:S(2)}) collective-permute-start(bf16[288,256]{1,0:T(8,128)(2,1)S(1)} %get-tuple-element.113), channel_id=1, source_target_pairs={{4,8},{12,16},{20,24},{8,4},{16,12},{24,20},{5,9},{13,17},{21,25},... | collective-permute-start | bytes 442376 | tf_op jit(solution)/shard_map/ppermute | solution.py:676
  11.8 0.7 %collective-permute-start.7 = (bf16[448,256]{1,0:T(8,128)(2,1)S(1)}, bf16[448,256]{1,0:T(8,128)(2,1)S(1)}, u32[]{:S(2)}, u32[]{:S(2)}) collective-permute-start(bf16[448,256]{1,0:T(8,128)(2,1)S(1)} %shard_map.88), channel_id=1, source_target_pairs={{4,8},{12,16},{20,24},{8,4},{16,12},{24,20},{5,9},{13,17},{21,25},... | collective-permute-start | bytes 688136 | tf_op jit(solution)/shard_map/ppermute | solution.py:754
  12.5 3.7 %collective-permute-done.4.msg_a = bf16[288,256]{1,0:T(8,128)(2,1)S(1)} collective-permute-done((bf16[288,256]{1,0:T(8,128)(2,1)S(1)}, bf16[288,256]{1,0:T(8,128)(2,1)S(1)}, u32[]{:S(2)}, u32[]{:S(2)}) %collective-permute-start.4) | collective-permute-done | bytes 147488 | tf_op jit(solution)/shard_map/ppermute | solution.py:676
  17.4 2.8 %shard_map.90 = (f32[1024,256]{1,0:T(8,128)S(1)}, bf16[1344,384]{1,0:T(8,128)(2,1)S(1)}, bf16[1344,384]{1,0:T(8,128)(2,1)S(1)}, bf16[1344,384]{1,0:T(8,128)(2,1)...) custom-call(bf16[1024,256]{1,0:T(8,128)(2,1)S(1)} %shard_map.86.cot_, ...), custom_call_target="tpu_custom_call" | custom-call | flops 8000000000 | bytes 4194304 | tf_op jit(solution)/shard_map/pallas_call | solution.py:765
  20.3 6.6 %conditional.1 = ((f32[144,128]{1,0:T(8,128)S(1)}, bf16[1088,384]{1,0:T(8,128)(2,1)S(1)})) conditional(s32[]{:T(128)} %bitcast.5, (s32[2,32]{1,0:T(2,128)S(1)}, bf16[32,32,256]{2,1,0:T(8,128)(2,1)S(1)}, bf16[448,256]{1,0:T(8,128)(2,1)S(1)}, bf16[448,256]{1,0:T(8,128)(2,1)S(1)}, bf16[32,96,128]{2,1,0:T(8,128)(2,1)S(1)}, ...), branch_computations={%region_0.0_spmd, %region_1.0_spmd} | conditional | flops 10001703936 | bytes 15859800 | solution.py:788
  20.3 6.3 %branch_1_fun.1 = (f32[144,128]{1,0:T(8,128)S(1)}, bf16[1088,384]{1,0:T(8,128)(2,1)S(1)}) custom-call(s32[2,32]{1,0:T(2,128)S(1)} %get-tuple-element.55.shifts, bf16[32,32,256]{2,1,0:T(8,128)(2,1)S(1)} %get-tuple-element.56.feat, bf16[448,256]{1,0:T(8,128)(2,1)S(1)} %get-tuple-element.57.feat_a, bf16[448,256]{1,0:T(8,128)(2,1)S(1)} %get-tuple-element.58.feat_b, ...), custom_call_target="tpu_custom_call" | custom-call | flops 10000000000 | bytes 4194304 | tf_op jit(solution)/shard_map/cond/branch_1_fun/pallas_call | solution.py:701
  27.0 1.3 %collective-permute-done.8 = f32[144,128]{1,0:T(8,128)S(1)} collective-permute-done((f32[144,128]{1,0:T(8,128)S(1)}, f32[144,128]{1,0:T(8,128)S(1)}, u32[]{:S(2)}, u32[]{:S(2)}) %collective-permute-start.8) | collective-permute-done | bytes 73760 | tf_op jit(solution)/shard_map/ppermute | solution.py:805
  28.2 1.6 %collective-permute-start.9 = (f32[144,128]{1,0:T(8,128)S(1)}, f32[144,128]{1,0:T(8,128)S(1)}, u32[]{:S(2)}, u32[]{:S(2)}) collective-permute-start(f32[144,128]{1,0:T(8,128)S(1)} %add.12), channel_id=1, source_target_pairs={{0,2},{2,0},{1,3},{3,1},{4,6},{6,4},{5,7},{7,5},{8,10},{10,8},{9,1... | collective-permute-start | bytes 221192 | tf_op jit(solution)/shard_map/ppermute | solution.py:805
  29.8 1.7 %shard_map.91.rest_0_ = bf16[32,32,256]{2,1,0:T(8,128)(2,1)} custom-call(bf16[1088,384]{1,0:T(8,128)(2,1)S(1)} %get-tuple-element.133.blended, bf16[384,192]{1,0:T(8,128)(2,1)S(1)} %get-tuple-element.130.bands), custom_call_target="tpu_custom_call" | custom-call | flops 1000000000 | bytes 4194304 | tf_op jit(solution)/shard_map/pallas_call | solution.py:654
  31.5 1.2 %collective-permute-done.9 = f32[144,128]{1,0:T(8,128)S(1)} collective-permute-done((f32[144,128]{1,0:T(8,128)S(1)}, f32[144,128]{1,0:T(8,128)S(1)}, u32[]{:S(2)}, u32[]{:S(2)}) %collective-permute-start.9) | collective-permute-done | bytes 73760 | tf_op jit(solution)/shard_map/ppermute | solution.py:805
  32.7 5.7 %collective-permute-start.10 = (f32[144,128]{1,0:T(8,128)S(1)}, f32[144,128]{1,0:T(8,128)S(1)}, u32[]{:S(2)}, u32[]{:S(2)}) collective-permute-start(f32[144,128]{1,0:T(8,128)S(1)} %add.13), channel_id=1, source_target_pairs={{0,4},{4,0},{8,12},{12,8},{16,20},{20,16},{24,28},{28,24},{1,5},{5... | collective-permute-start | bytes 221192 | tf_op jit(solution)/shard_map/ppermute | solution.py:805
  38.3 1.7 %shard_map.92 = bf16[32,32,256]{2,1,0:T(8,128)(2,1)} custom-call(bf16[1088,384]{1,0:T(8,128)(2,1)S(1)} %get-tuple-element.133.blended, bf16[384,192]{1,0:T(8,128)(2,1)S(1)} %get-tuple-element.130.bands, bf16[32,32,256]{2,1,0:T(8,128)(2,1)} %shard_map.91.rest_0_), custom_call_target="tpu_custom_call", output_to_operand_aliasing={{}: (2, {})} | custom-call | flops 1000000000 | bytes 4194304 | tf_op jit(solution)/shard_map/pallas_call | solution.py:654
  40.0 0.7 %collective-permute-done.10 = f32[144,128]{1,0:T(8,128)S(1)} collective-permute-done((f32[144,128]{1,0:T(8,128)S(1)}, f32[144,128]{1,0:T(8,128)S(1)}, u32[]{:S(2)}, u32[]{:S(2)}) %collective-permute-start.10) | collective-permute-done | bytes 73760 | tf_op jit(solution)/shard_map/ppermute | solution.py:805
  40.7 2.1 %collective-permute-start.11 = (bf16[144,128]{1,0:T(8,128)(2,1)S(1)}, bf16[144,128]{1,0:T(8,128)(2,1)S(1)}, u32[]{:S(2)}, u32[]{:S(2)}) collective-permute-start(bf16[144,128]{1,0:T(8,128)(2,1)S(1)} %add_convert_fusion.1), channel_id=1, source_target_pairs={{0,8},{4,12},{8,0},{12,4},{16,24},{20,28},{24,16},{28,20},{1,9},{5... | collective-permute-start | bytes 110600 | tf_op jit(solution)/shard_map/ppermute | solution.py:805
  42.8 1.9 %collective-permute-done.11 = bf16[144,128]{1,0:T(8,128)(2,1)S(1)} collective-permute-done((bf16[144,128]{1,0:T(8,128)(2,1)S(1)}, bf16[144,128]{1,0:T(8,128)(2,1)S(1)}, u32[]{:S(2)}, u32[]{:S(2)}) %collective-permute-start.11) | collective-permute-done | bytes 36896 | tf_op jit(solution)/shard_map/ppermute | solution.py:805
  44.8 3.2 %collective-permute-start.12 = (bf16[144,128]{1,0:T(8,128)(2,1)S(1)}, bf16[144,128]{1,0:T(8,128)(2,1)S(1)}, u32[]{:S(2)}, u32[]{:S(2)}) collective-permute-start(bf16[144,128]{1,0:T(8,128)(2,1)S(1)} %add_convert_fusion.mine), channel_id=1, source_target_pairs={{0,16},{4,20},{8,24},{12,28},{16,0},{20,4},{24,8},{28,12},{1,17},{... | collective-permute-start | bytes 110600 | tf_op jit(solution)/shard_map/ppermute | solution.py:805
  47.9 1.9 %collective-permute-done.12.other = bf16[144,128]{1,0:T(8,128)(2,1)S(1)} collective-permute-done((bf16[144,128]{1,0:T(8,128)(2,1)S(1)}, bf16[144,128]{1,0:T(8,128)(2,1)S(1)}, u32[]{:S(2)}, u32[]{:S(2)}) %collective-permute-start.12) | collective-permute-done | bytes 36896 | tf_op jit(solution)/shard_map/ppermute | solution.py:805
  49.9 0.9 %shard_map.93 = (f32[9,32,32]{2,1,0:T(8,128)}, f32[9,32,32]{2,1,0:T(8,128)}) custom-call(bf16[144,128]{1,0:T(8,128)(2,1)S(1)} %add_convert_fusion.mine, bf16[144,128]{1,0:T(8,128)(2,1)S(1)} %collective-permute-done.12.other), custom_call_target="tpu_custom_call" | custom-call | bytes 4194304 | tf_op jit(solution)/shard_map/pallas_call | solution.py:817
  (27 shorter events, 1.0 us)
Async XLA Ops:
  0.6 4.7 %copy-start = (bf16[1,32,32,256]{3,2,1,0:T(8,128)(2,1)S(1)}, bf16[1,32,32,256]{3,2,1,0:T(8,128)(2,1)}, u32[]{:S(2)}) copy-start(bf16[1,32,32,256]{3,2,1,0:T(8,128)(2,1)} %param.13) | copy-start | bytes 1572868
  2.3 5.9 %copy-start.4 = (bf16[1,32,32,256]{3,2,1,0:T(8,128)(2,1)S(1)}, bf16[1,32,32,256]{3,2,1,0:T(8,128)(2,1)}, u32[]{:S(2)}) copy-start(bf16[1,32,32,256]{3,2,1,0:T(8,128)(2,1)} %param.8) | copy-start | bytes 1572868
  2.3 5.9 %copy-start.5 = (s32[1,32,2]{1,2,0:T(2,128)S(1)}, s32[1,32,2]{1,2,0:T(2,128)}, u32[]{:S(2)}) copy-start(s32[1,32,2]{1,2,0:T(2,128)} %param.9) | copy-start | bytes 772
  2.3 15.1 %collective-permute-start.6 = (bf16[448,256]{1,0:T(8,128)(2,1)S(1)}, bf16[448,256]{1,0:T(8,128)(2,1)S(1)}, u32[]{:S(2)}, u32[]{:S(2)}) collective-permute-start(bf16[448,256]{1,0:T(8,128)(2,1)S(1)} %get-tuple-element.114), channel_id=1, source_target_pairs={{0,4},{4,0},{8,12},{12,8},{16,20},{20,16},{24,28},{28,24},{1,5},{5... | collective-permute-start | bytes 688136 | tf_op jit(solution)/shard_map/ppermute | solution.py:740
  6.6 4.3 %collective-permute-start.2 = (bf16[256,128]{1,0:T(8,128)(2,1)S(1)}, bf16[256,128]{1,0:T(8,128)(2,1)S(1)}, u32[]{:S(2)}, u32[]{:S(2)}) collective-permute-start(bf16[256,128]{1,0:T(8,128)(2,1)S(1)} %shard_map.87), channel_id=1, source_target_pairs={{0,2},{2,0},{1,3},{3,1},{4,6},{6,4},{5,7},{7,5},{8,10},{10,8},{9,1... | collective-permute-start | bytes 196616 | tf_op jit(solution)/shard_map/ppermute | solution.py:676
  8.2 1.3 %collective-permute-start.3 = (s32[8,128]{1,0:T(8,128)S(1)}, s32[8,128]{1,0:T(8,128)S(1)}, u32[]{:S(2)}, u32[]{:S(2)}) collective-permute-start(s32[8,128]{1,0:T(8,128)S(1)} %get-tuple-element.107), channel_id=1, source_target_pairs={{0,1},{1,0},{2,3},{3,2},{4,5},{5,4},{6,7},{7,6},{8,9},{9,8},{10,11... | collective-permute-start | bytes 12296 | tf_op jit(solution)/shard_map/ppermute | solution.py:743
  9.5 7.9 %copy-start.1 = (bf16[9,32,32]{2,1,0:T(8,128)(2,1)S(1)}, bf16[9,32,32]{2,1,0:T(8,128)(2,1)}, u32[]{:S(2)}) copy-start(bf16[9,32,32]{2,1,0:T(8,128)(2,1)} %rest_1_.1) | copy-start | bytes 55300
  9.5 7.9 %copy-start.2 = (bf16[9,32,32]{2,1,0:T(8,128)(2,1)S(1)}, bf16[9,32,32]{2,1,0:T(8,128)(2,1)}, u32[]{:S(2)}) copy-start(bf16[9,32,32]{2,1,0:T(8,128)(2,1)} %rest_2_.1) | copy-start | bytes 55300
  9.5 7.9 %copy-start.3 = (bf16[9,32,32]{2,1,0:T(8,128)(2,1)S(1)}, bf16[9,32,32]{2,1,0:T(8,128)(2,1)}, u32[]{:S(2)}) copy-start(bf16[9,32,32]{2,1,0:T(8,128)(2,1)} %rest_3_.1) | copy-start | bytes 55300
  11.0 5.2 %collective-permute-start.4 = (bf16[288,256]{1,0:T(8,128)(2,1)S(1)}, bf16[288,256]{1,0:T(8,128)(2,1)S(1)}, u32[]{:S(2)}, u32[]{:S(2)}) collective-permute-start(bf16[288,256]{1,0:T(8,128)(2,1)S(1)} %get-tuple-element.109), channel_id=1, source_target_pairs={{0,4},{4,0},{8,12},{12,8},{16,20},{20,16},{24,28},{28,24},{1,5},{5... | collective-permute-start | bytes 442376 | tf_op jit(solution)/shard_map/ppermute | solution.py:676
  11.2 6.2 %collective-permute-start.5 = (bf16[288,256]{1,0:T(8,128)(2,1)S(1)}, bf16[288,256]{1,0:T(8,128)(2,1)S(1)}, u32[]{:S(2)}, u32[]{:S(2)}) collective-permute-start(bf16[288,256]{1,0:T(8,128)(2,1)S(1)} %get-tuple-element.113), channel_id=1, source_target_pairs={{4,8},{12,16},{20,24},{8,4},{16,12},{24,20},{5,9},{13,17},{21,25},... | collective-permute-start | bytes 442376 | tf_op jit(solution)/shard_map/ppermute | solution.py:676
  11.8 8.5 %collective-permute-start.7 = (bf16[448,256]{1,0:T(8,128)(2,1)S(1)}, bf16[448,256]{1,0:T(8,128)(2,1)S(1)}, u32[]{:S(2)}, u32[]{:S(2)}) collective-permute-start(bf16[448,256]{1,0:T(8,128)(2,1)S(1)} %shard_map.88), channel_id=1, source_target_pairs={{4,8},{12,16},{20,24},{8,4},{16,12},{24,20},{5,9},{13,17},{21,25},... | collective-permute-start | bytes 688136 | tf_op jit(solution)/shard_map/ppermute | solution.py:754
  26.9 1.3 %collective-permute-start.8 = (f32[144,128]{1,0:T(8,128)S(1)}, f32[144,128]{1,0:T(8,128)S(1)}, u32[]{:S(2)}, u32[]{:S(2)}) collective-permute-start(f32[144,128]{1,0:T(8,128)S(1)} %get-tuple-element.126), channel_id=1, source_target_pairs={{0,1},{1,0},{2,3},{3,2},{4,5},{5,4},{6,7},{7,6},{8,9},{9,8},{10,11... | collective-permute-start | bytes 221192 | tf_op jit(solution)/shard_map/ppermute | solution.py:805
  28.2 4.4 %collective-permute-start.9 = (f32[144,128]{1,0:T(8,128)S(1)}, f32[144,128]{1,0:T(8,128)S(1)}, u32[]{:S(2)}, u32[]{:S(2)}) collective-permute-start(f32[144,128]{1,0:T(8,128)S(1)} %add.12), channel_id=1, source_target_pairs={{0,2},{2,0},{1,3},{3,1},{4,6},{6,4},{5,7},{7,5},{8,10},{10,8},{9,1... | collective-permute-start | bytes 221192 | tf_op jit(solution)/shard_map/ppermute | solution.py:805
  32.7 8.0 %collective-permute-start.10 = (f32[144,128]{1,0:T(8,128)S(1)}, f32[144,128]{1,0:T(8,128)S(1)}, u32[]{:S(2)}, u32[]{:S(2)}) collective-permute-start(f32[144,128]{1,0:T(8,128)S(1)} %add.13), channel_id=1, source_target_pairs={{0,4},{4,0},{8,12},{12,8},{16,20},{20,16},{24,28},{28,24},{1,5},{5... | collective-permute-start | bytes 221192 | tf_op jit(solution)/shard_map/ppermute | solution.py:805
  40.7 4.1 %collective-permute-start.11 = (bf16[144,128]{1,0:T(8,128)(2,1)S(1)}, bf16[144,128]{1,0:T(8,128)(2,1)S(1)}, u32[]{:S(2)}, u32[]{:S(2)}) collective-permute-start(bf16[144,128]{1,0:T(8,128)(2,1)S(1)} %add_convert_fusion.1), channel_id=1, source_target_pairs={{0,8},{4,12},{8,0},{12,4},{16,24},{20,28},{24,16},{28,20},{1,9},{5... | collective-permute-start | bytes 110600 | tf_op jit(solution)/shard_map/ppermute | solution.py:805
  44.8 5.1 %collective-permute-start.12 = (bf16[144,128]{1,0:T(8,128)(2,1)S(1)}, bf16[144,128]{1,0:T(8,128)(2,1)S(1)}, u32[]{:S(2)}, u32[]{:S(2)}) collective-permute-start(bf16[144,128]{1,0:T(8,128)(2,1)S(1)} %add_convert_fusion.mine), channel_id=1, source_target_pairs={{0,16},{4,20},{8,24},{12,28},{16,0},{20,4},{24,8},{28,12},{1,17},{... | collective-permute-start | bytes 110600 | tf_op jit(solution)/shard_map/ppermute | solution.py:805

commit v19 on v18

--- a/solution.py
+++ b/solution.py
@@ -114,8 +114,11 @@
         out[...] = jnp.full(out.shape, jnp.maximum(up, down), jnp.int32)
     place = as_bf(lax.broadcasted_iota(jnp.int32, (chunk, full), 0))
     for p in range(0, size, chunk):
-        pick = one_hot(place == as_bf(target[0:1] - p))
-        msg[p : p + chunk] = jnp.dot(pick, source, preferred_element_type=F32).astype(BF16)
+        late = (p + skip) // FHALO * height // TILE * TILE
+        pick = one_hot(place[:, late:] == as_bf(target[0:1, late:] - p))
+        msg[p : p + chunk] = jnp.dot(
+            pick, source[late:], preferred_element_type=F32
+        ).astype(BF16)
 
 
 def rows_kernel(source, out):
@@ -135,18 +138,27 @@
             yield 2 * h + m, slice(h * half, (h + 1) * half), slice(m * block, (m + 1) * block)
 
 
-def column_kernel(feat, cot, *col_msgs):
+def column_kernel(feat, cot, *rest):
+    col_msgs, (feat_edge, cot_edge, sems) = rest[:-3], rest[-3:]
     chans, height, span = feat.shape
     for index, msg in enumerate(col_msgs):
         right = is_even("cols") if index == 0 else jnp.logical_not(is_even("cols"))
         part = pl.ds(pl.multiple_of(jnp.where(right, span - TILE, 0), TILE), TILE)
+        copies = [
+            pltpu.make_async_copy(ref.at[:, :, part], edge, sems.at[i])
+            for i, (ref, edge) in enumerate(((feat, feat_edge), (cot, cot_edge)))
+        ]
+        for copy in copies:
+            copy.start()
+        for copy in copies:
+            copy.wait()
         shape = (1, height // 2, TILE)
         inner = edge_lanes(shape, right, FHALO)
         outer = edge_lanes(shape, right, SLOT) - inner
         total = None
         for q, channels, rows in slots(chans, height):
-            cots = turn(cot[channels, rows, part], jnp.where(right, TILE - FHALO, FHALO))
-            piece = feat[channels, rows, part] * inner + cots * outer
+            cots = turn(cot_edge[channels, rows, :], jnp.where(right, TILE - FHALO, FHALO))
+            piece = feat_edge[channels, rows, :] * inner + cots * outer
             piece = turn(piece, jnp.where(right, (q + 1) * SLOT % TILE, q * SLOT))
             total = piece if total is None else total + piece
         msg[...] = total.reshape(msg.shape)
@@ -744,8 +756,15 @@
         bit *= 2
 
     packed = chans * (height * SLOT // TILE)
+    anywhere = pl.BlockSpec(memory_space=pl.ANY)
     messages = call(
-        column_kernel, (bf(packed, TILE),) * (1 if cols == 2 else 2), [], 2, 8, flops=2 * 10**10
+        column_kernel,
+        (bf(packed, TILE),) * (1 if cols == 2 else 2),
+        [pltpu.VMEM((chans, height, TILE), BF16)] * 2 + [pltpu.SemaphoreType.DMA((2,))],
+        2,
+        8,
+        flops=2 * 10**10,
+        in_specs=[anywhere, anywhere],
     )(feat, cot)
     col_msgs = swapped(messages, "cols")
     ncols = len(col_msgs)

time: 51 us -> 50.9 us (level)
  no operation moved by 1% of the time
where the time goes in v19:
time: 50.9 us; the launch traced here: 50.7 us
  starting transfers between devices  18.7 us (37%)
  Pallas kernels  17.5 us (34%)
  waiting for transfers between devices  12.2 us (24%)
  between operations  1.5 us (3%)
  local copies, waits for them, and re-layouts  0.55 us (1%)
    ppermute x5, starting transfers between devices, shards(): other = lax.ppermute(grads, axis, pairs)  12.6 us
    ppermute x5, waiting for transfers between devices, shards(): other = lax.ppermute(grads, axis, pairs)  6.98 us
    pallas_call x1, Pallas kernels, main_pass(): call(main_kernel, (jax.ShapeDtypeStruct((9 * chans // 2, TILE), F32), bf(...  6.34 us
    ppermute x3, waiting for transfers between devices, swapped(): return [lax.ppermute(m, axis, p) for m, p in zip(messages, pairs)]  5.2 us
    pallas_call x2, Pallas kernels, predict(): call(functools.partial(predict_kernel, part), jax.ShapeDtypeStruct(shape,...  3.34 us
    ppermute x1, starting transfers between devices, shards(): feat_a = lax.ppermute(message, 'rows', row_pairs[0])  3.03 us
    pallas_call x1, Pallas kernels, shards(): call(functools.partial(back_kernel, ncols), (jax.ShapeDtypeStruct((full,...  2.85 us
    pallas_call x2, Pallas kernels, pack_rows(): call(functools.partial(feature_kernel, index, skip), message, [], 2, 16,...  2.66 us
  transfers between devices with their start and end apart: 11, of which 7 were waited for; matrix products, arithmetic and copies ran while one was open for 1% of the time, Pallas kernels for 17%

profile of v19, /device:TPU:0, one launch (start us, length us, event | category | flops | bytes accessed | tf_op | source)
XLA Modules:
  0.0 50.7 jit_solution(13071315054148425810)
XLA Ops:
  0.6 1.6 %shard_map.85 = (bf16[448,256]{1,0:T(8,128)(2,1)S(1)}, s32[8,128]{1,0:T(8,128)S(1)}) custom-call(s32[2,32]{1,0:T(2,128)} %bitcast.14, bf16[32,32,256]{2,1,0:T(8,128)(2,1)} %bitcast.9), custom_call_target="tpu_custom_call" | custom-call | bytes 4194304 | tf_op jit(solution)/shard_map/pallas_call | solution.py:695
  2.3 3.0 %collective-permute-start.6 = (bf16[448,256]{1,0:T(8,128)(2,1)S(1)}, bf16[448,256]{1,0:T(8,128)(2,1)S(1)}, u32[]{:S(2)}, u32[]{:S(2)}) collective-permute-start(bf16[448,256]{1,0:T(8,128)(2,1)S(1)} %get-tuple-element.114), channel_id=1, source_target_pairs={{0,4},{4,0},{8,12},{12,8},{16,20},{20,16},{24,28},{28,24},{1,5},{5... | collective-permute-start | bytes 688136 | tf_op jit(solution)/shard_map/ppermute | solution.py:752
  5.3 1.2 %shard_map.87 = bf16[256,128]{1,0:T(8,128)(2,1)S(1)} custom-call(bf16[32,32,256]{2,1,0:T(8,128)(2,1)} %bitcast.10, bf16[32,32,256]{2,1,0:T(8,128)(2,1)S(1)} %bitcast.7), custom_call_target="tpu_custom_call" | custom-call | flops 20000000000 | bytes 4194304 | tf_op jit(solution)/shard_map/pallas_call | solution.py:760
  6.6 1.6 %collective-permute-start.2 = (bf16[256,128]{1,0:T(8,128)(2,1)S(1)}, bf16[256,128]{1,0:T(8,128)(2,1)S(1)}, u32[]{:S(2)}, u32[]{:S(2)}) collective-permute-start(bf16[256,128]{1,0:T(8,128)(2,1)S(1)} %shard_map.87), channel_id=1, source_target_pairs={{0,2},{2,0},{1,3},{3,1},{4,6},{6,4},{5,7},{7,5},{8,10},{10,8},{9,1... | collective-permute-start | bytes 196616 | tf_op jit(solution)/shard_map/ppermute | solution.py:688
  8.1 1.0 %shard_map.88 = bf16[448,256]{1,0:T(8,128)(2,1)S(1)} custom-call(s32[2,32]{1,0:T(2,128)S(1)} %bitcast.15, bf16[32,32,256]{2,1,0:T(8,128)(2,1)S(1)} %bitcast.11), custom_call_target="tpu_custom_call" | custom-call | bytes 4194304 | tf_op jit(solution)/shard_map/pallas_call | solution.py:695
  9.4 1.5 %collective-permute-done.2.rest_0_ = bf16[256,128]{1,0:T(8,128)(2,1)S(1)} collective-permute-done((bf16[256,128]{1,0:T(8,128)(2,1)S(1)}, bf16[256,128]{1,0:T(8,128)(2,1)S(1)}, u32[]{:S(2)}, u32[]{:S(2)}) %collective-permute-start.2) | collective-permute-done | bytes 65568 | tf_op jit(solution)/shard_map/ppermute | solution.py:688
  11.1 0.7 %collective-permute-start.5 = (bf16[288,256]{1,0:T(8,128)(2,1)S(1)}, bf16[288,256]{1,0:T(8,128)(2,1)S(1)}, u32[]{:S(2)}, u32[]{:S(2)}) collective-permute-start(bf16[288,256]{1,0:T(8,128)(2,1)S(1)} %get-tuple-element.113), channel_id=1, source_target_pairs={{4,8},{12,16},{20,24},{8,4},{16,12},{24,20},{5,9},{13,17},{21,25},... | collective-permute-start | bytes 442376 | tf_op jit(solution)/shard_map/ppermute | solution.py:688
  11.7 0.7 %collective-permute-start.7 = (bf16[448,256]{1,0:T(8,128)(2,1)S(1)}, bf16[448,256]{1,0:T(8,128)(2,1)S(1)}, u32[]{:S(2)}, u32[]{:S(2)}) collective-permute-start(bf16[448,256]{1,0:T(8,128)(2,1)S(1)} %shard_map.88), channel_id=1, source_target_pairs={{4,8},{12,16},{20,24},{8,4},{16,12},{24,20},{5,9},{13,17},{21,25},... | collective-permute-start | bytes 688136 | tf_op jit(solution)/shard_map/ppermute | solution.py:773
  12.4 3.7 %collective-permute-done.4.msg_a = bf16[288,256]{1,0:T(8,128)(2,1)S(1)} collective-permute-done((bf16[288,256]{1,0:T(8,128)(2,1)S(1)}, bf16[288,256]{1,0:T(8,128)(2,1)S(1)}, u32[]{:S(2)}, u32[]{:S(2)}) %collective-permute-start.4) | collective-permute-done | bytes 147488 | tf_op jit(solution)/shard_map/ppermute | solution.py:688
  17.4 2.8 %shard_map.90 = (f32[1024,256]{1,0:T(8,128)S(1)}, bf16[1344,384]{1,0:T(8,128)(2,1)S(1)}, bf16[1344,384]{1,0:T(8,128)(2,1)S(1)}, bf16[1344,384]{1,0:T(8,128)(2,1)...) custom-call(bf16[1024,256]{1,0:T(8,128)(2,1)S(1)} %shard_map.86.cot_, ...), custom_call_target="tpu_custom_call" | custom-call | flops 8000000000 | bytes 4194304 | tf_op jit(solution)/shard_map/pallas_call | solution.py:784
  20.2 6.6 %conditional.1 = ((f32[144,128]{1,0:T(8,128)S(1)}, bf16[1088,384]{1,0:T(8,128)(2,1)S(1)})) conditional(s32[]{:T(128)} %bitcast.5, (s32[2,32]{1,0:T(2,128)S(1)}, bf16[32,32,256]{2,1,0:T(8,128)(2,1)S(1)}, bf16[448,256]{1,0:T(8,128)(2,1)S(1)}, bf16[448,256]{1,0:T(8,128)(2,1)S(1)}, bf16[32,96,128]{2,1,0:T(8,128)(2,1)S(1)}, ...), branch_computations={%region_0.0_spmd, %region_1.0_spmd} | conditional | flops 10001703936 | bytes 15859800 | solution.py:807
  20.2 6.3 %branch_1_fun.1 = (f32[144,128]{1,0:T(8,128)S(1)}, bf16[1088,384]{1,0:T(8,128)(2,1)S(1)}) custom-call(s32[2,32]{1,0:T(2,128)S(1)} %get-tuple-element.55.shifts, bf16[32,32,256]{2,1,0:T(8,128)(2,1)S(1)} %get-tuple-element.56.feat, bf16[448,256]{1,0:T(8,128)(2,1)S(1)} %get-tuple-element.57.feat_a, bf16[448,256]{1,0:T(8,128)(2,1)S(1)} %get-tuple-element.58.feat_b, ...), custom_call_target="tpu_custom_call" | custom-call | flops 10000000000 | bytes 4194304 | tf_op jit(solution)/shard_map/cond/branch_1_fun/pallas_call | solution.py:713
  26.9 1.3 %collective-permute-done.8 = f32[144,128]{1,0:T(8,128)S(1)} collective-permute-done((f32[144,128]{1,0:T(8,128)S(1)}, f32[144,128]{1,0:T(8,128)S(1)}, u32[]{:S(2)}, u32[]{:S(2)}) %collective-permute-start.8) | collective-permute-done | bytes 73760 | tf_op jit(solution)/shard_map/ppermute | solution.py:824
  28.2 1.6 %collective-permute-start.9 = (f32[144,128]{1,0:T(8,128)S(1)}, f32[144,128]{1,0:T(8,128)S(1)}, u32[]{:S(2)}, u32[]{:S(2)}) collective-permute-start(f32[144,128]{1,0:T(8,128)S(1)} %add.12), channel_id=1, source_target_pairs={{0,2},{2,0},{1,3},{3,1},{4,6},{6,4},{5,7},{7,5},{8,10},{10,8},{9,1... | collective-permute-start | bytes 221192 | tf_op jit(solution)/shard_map/ppermute | solution.py:824
  29.7 1.7 %shard_map.91.rest_0_ = bf16[32,32,256]{2,1,0:T(8,128)(2,1)} custom-call(bf16[1088,384]{1,0:T(8,128)(2,1)S(1)} %get-tuple-element.133.blended, bf16[384,192]{1,0:T(8,128)(2,1)S(1)} %get-tuple-element.130.bands), custom_call_target="tpu_custom_call" | custom-call | flops 1000000000 | bytes 4194304 | tf_op jit(solution)/shard_map/pallas_call | solution.py:666
  31.4 1.2 %collective-permute-done.9 = f32[144,128]{1,0:T(8,128)S(1)} collective-permute-done((f32[144,128]{1,0:T(8,128)S(1)}, f32[144,128]{1,0:T(8,128)S(1)}, u32[]{:S(2)}, u32[]{:S(2)}) %collective-permute-start.9) | collective-permute-done | bytes 73760 | tf_op jit(solution)/shard_map/ppermute | solution.py:824
  32.6 5.7 %collective-permute-start.10 = (f32[144,128]{1,0:T(8,128)S(1)}, f32[144,128]{1,0:T(8,128)S(1)}, u32[]{:S(2)}, u32[]{:S(2)}) collective-permute-start(f32[144,128]{1,0:T(8,128)S(1)} %add.13), channel_id=1, source_target_pairs={{0,4},{4,0},{8,12},{12,8},{16,20},{20,16},{24,28},{28,24},{1,5},{5... | collective-permute-start | bytes 221192 | tf_op jit(solution)/shard_map/ppermute | solution.py:824
  38.3 1.7 %shard_map.92 = bf16[32,32,256]{2,1,0:T(8,128)(2,1)} custom-call(bf16[1088,384]{1,0:T(8,128)(2,1)S(1)} %get-tuple-element.133.blended, bf16[384,192]{1,0:T(8,128)(2,1)S(1)} %get-tuple-element.130.bands, bf16[32,32,256]{2,1,0:T(8,128)(2,1)} %shard_map.91.rest_0_), custom_call_target="tpu_custom_call", output_to_operand_aliasing={{}: (2, {})} | custom-call | flops 1000000000 | bytes 4194304 | tf_op jit(solution)/shard_map/pallas_call | solution.py:666
  39.9 0.7 %collective-permute-done.10 = f32[144,128]{1,0:T(8,128)S(1)} collective-permute-done((f32[144,128]{1,0:T(8,128)S(1)}, f32[144,128]{1,0:T(8,128)S(1)}, u32[]{:S(2)}, u32[]{:S(2)}) %collective-permute-start.10) | collective-permute-done | bytes 73760 | tf_op jit(solution)/shard_map/ppermute | solution.py:824
  40.6 2.1 %collective-permute-start.11 = (bf16[144,128]{1,0:T(8,128)(2,1)S(1)}, bf16[144,128]{1,0:T(8,128)(2,1)S(1)}, u32[]{:S(2)}, u32[]{:S(2)}) collective-permute-start(bf16[144,128]{1,0:T(8,128)(2,1)S(1)} %add_convert_fusion.1), channel_id=1, source_target_pairs={{0,8},{4,12},{8,0},{12,4},{16,24},{20,28},{24,16},{28,20},{1,9},{5... | collective-permute-start | bytes 110600 | tf_op jit(solution)/shard_map/ppermute | solution.py:824
  42.7 1.9 %collective-permute-done.11 = bf16[144,128]{1,0:T(8,128)(2,1)S(1)} collective-permute-done((bf16[144,128]{1,0:T(8,128)(2,1)S(1)}, bf16[144,128]{1,0:T(8,128)(2,1)S(1)}, u32[]{:S(2)}, u32[]{:S(2)}) %collective-permute-start.11) | collective-permute-done | bytes 36896 | tf_op jit(solution)/shard_map/ppermute | solution.py:824
  44.7 3.2 %collective-permute-start.12 = (bf16[144,128]{1,0:T(8,128)(2,1)S(1)}, bf16[144,128]{1,0:T(8,128)(2,1)S(1)}, u32[]{:S(2)}, u32[]{:S(2)}) collective-permute-start(bf16[144,128]{1,0:T(8,128)(2,1)S(1)} %add_convert_fusion.mine), channel_id=1, source_target_pairs={{0,16},{4,20},{8,24},{12,28},{16,0},{20,4},{24,8},{28,12},{1,17},{... | collective-permute-start | bytes 110600 | tf_op jit(solution)/shard_map/ppermute | solution.py:824
  47.9 1.9 %collective-permute-done.12.other = bf16[144,128]{1,0:T(8,128)(2,1)S(1)} collective-permute-done((bf16[144,128]{1,0:T(8,128)(2,1)S(1)}, bf16[144,128]{1,0:T(8,128)(2,1)S(1)}, u32[]{:S(2)}, u32[]{:S(2)}) %collective-permute-start.12) | collective-permute-done | bytes 36896 | tf_op jit(solution)/shard_map/ppermute | solution.py:824
  49.8 0.9 %shard_map.93 = (f32[9,32,32]{2,1,0:T(8,128)}, f32[9,32,32]{2,1,0:T(8,128)}) custom-call(bf16[144,128]{1,0:T(8,128)(2,1)S(1)} %add_convert_fusion.mine, bf16[144,128]{1,0:T(8,128)(2,1)S(1)} %collective-permute-done.12.other), custom_call_target="tpu_custom_call" | custom-call | bytes 4194304 | tf_op jit(solution)/shard_map/pallas_call | solution.py:836
  (27 shorter events, 1.0 us)
Async XLA Ops:
  0.6 4.7 %copy-start = (bf16[1,32,32,256]{3,2,1,0:T(8,128)(2,1)S(1)}, bf16[1,32,32,256]{3,2,1,0:T(8,128)(2,1)}, u32[]{:S(2)}) copy-start(bf16[1,32,32,256]{3,2,1,0:T(8,128)(2,1)} %param.13) | copy-start | bytes 1572868
  2.3 5.8 %copy-start.4 = (bf16[1,32,32,256]{3,2,1,0:T(8,128)(2,1)S(1)}, bf16[1,32,32,256]{3,2,1,0:T(8,128)(2,1)}, u32[]{:S(2)}) copy-start(bf16[1,32,32,256]{3,2,1,0:T(8,128)(2,1)} %param.8) | copy-start | bytes 1572868
  2.3 5.8 %copy-start.5 = (s32[1,32,2]{1,2,0:T(2,128)S(1)}, s32[1,32,2]{1,2,0:T(2,128)}, u32[]{:S(2)}) copy-start(s32[1,32,2]{1,2,0:T(2,128)} %param.9) | copy-start | bytes 772
  2.3 15.0 %collective-permute-start.6 = (bf16[448,256]{1,0:T(8,128)(2,1)S(1)}, bf16[448,256]{1,0:T(8,128)(2,1)S(1)}, u32[]{:S(2)}, u32[]{:S(2)}) collective-permute-start(bf16[448,256]{1,0:T(8,128)(2,1)S(1)} %get-tuple-element.114), channel_id=1, source_target_pairs={{0,4},{4,0},{8,12},{12,8},{16,20},{20,16},{24,28},{28,24},{1,5},{5... | collective-permute-start | bytes 688136 | tf_op jit(solution)/shard_map/ppermute | solution.py:752
  6.6 4.3 %collective-permute-start.2 = (bf16[256,128]{1,0:T(8,128)(2,1)S(1)}, bf16[256,128]{1,0:T(8,128)(2,1)S(1)}, u32[]{:S(2)}, u32[]{:S(2)}) collective-permute-start(bf16[256,128]{1,0:T(8,128)(2,1)S(1)} %shard_map.87), channel_id=1, source_target_pairs={{0,2},{2,0},{1,3},{3,1},{4,6},{6,4},{5,7},{7,5},{8,10},{10,8},{9,1... | collective-permute-start | bytes 196616 | tf_op jit(solution)/shard_map/ppermute | solution.py:688
  8.1 1.2 %collective-permute-start.3 = (s32[8,128]{1,0:T(8,128)S(1)}, s32[8,128]{1,0:T(8,128)S(1)}, u32[]{:S(2)}, u32[]{:S(2)}) collective-permute-start(s32[8,128]{1,0:T(8,128)S(1)} %get-tuple-element.107), channel_id=1, source_target_pairs={{0,1},{1,0},{2,3},{3,2},{4,5},{5,4},{6,7},{7,6},{8,9},{9,8},{10,11... | collective-permute-start | bytes 12296 | tf_op jit(solution)/shard_map/ppermute | solution.py:755
  9.4 8.0 %copy-start.1 = (bf16[9,32,32]{2,1,0:T(8,128)(2,1)S(1)}, bf16[9,32,32]{2,1,0:T(8,128)(2,1)}, u32[]{:S(2)}) copy-start(bf16[9,32,32]{2,1,0:T(8,128)(2,1)} %rest_1_.1) | copy-start | bytes 55300
  9.4 8.0 %copy-start.2 = (bf16[9,32,32]{2,1,0:T(8,128)(2,1)S(1)}, bf16[9,32,32]{2,1,0:T(8,128)(2,1)}, u32[]{:S(2)}) copy-start(bf16[9,32,32]{2,1,0:T(8,128)(2,1)} %rest_2_.1) | copy-start | bytes 55300
  9.4 8.0 %copy-start.3 = (bf16[9,32,32]{2,1,0:T(8,128)(2,1)S(1)}, bf16[9,32,32]{2,1,0:T(8,128)(2,1)}, u32[]{:S(2)}) copy-start(bf16[9,32,32]{2,1,0:T(8,128)(2,1)} %rest_3_.1) | copy-start | bytes 55300
  10.9 5.2 %collective-permute-start.4 = (bf16[288,256]{1,0:T(8,128)(2,1)S(1)}, bf16[288,256]{1,0:T(8,128)(2,1)S(1)}, u32[]{:S(2)}, u32[]{:S(2)}) collective-permute-start(bf16[288,256]{1,0:T(8,128)(2,1)S(1)} %get-tuple-element.109), channel_id=1, source_target_pairs={{0,4},{4,0},{8,12},{12,8},{16,20},{20,16},{24,28},{28,24},{1,5},{5... | collective-permute-start | bytes 442376 | tf_op jit(solution)/shard_map/ppermute | solution.py:688
  11.1 6.2 %collective-permute-start.5 = (bf16[288,256]{1,0:T(8,128)(2,1)S(1)}, bf16[288,256]{1,0:T(8,128)(2,1)S(1)}, u32[]{:S(2)}, u32[]{:S(2)}) collective-permute-start(bf16[288,256]{1,0:T(8,128)(2,1)S(1)} %get-tuple-element.113), channel_id=1, source_target_pairs={{4,8},{12,16},{20,24},{8,4},{16,12},{24,20},{5,9},{13,17},{21,25},... | collective-permute-start | bytes 442376 | tf_op jit(solution)/shard_map/ppermute | solution.py:688
  11.7 8.5 %collective-permute-start.7 = (bf16[448,256]{1,0:T(8,128)(2,1)S(1)}, bf16[448,256]{1,0:T(8,128)(2,1)S(1)}, u32[]{:S(2)}, u32[]{:S(2)}) collective-permute-start(bf16[448,256]{1,0:T(8,128)(2,1)S(1)} %shard_map.88), channel_id=1, source_target_pairs={{4,8},{12,16},{20,24},{8,4},{16,12},{24,20},{5,9},{13,17},{21,25},... | collective-permute-start | bytes 688136 | tf_op jit(solution)/shard_map/ppermute | solution.py:773
  26.8 1.3 %collective-permute-start.8 = (f32[144,128]{1,0:T(8,128)S(1)}, f32[144,128]{1,0:T(8,128)S(1)}, u32[]{:S(2)}, u32[]{:S(2)}) collective-permute-start(f32[144,128]{1,0:T(8,128)S(1)} %get-tuple-element.126), channel_id=1, source_target_pairs={{0,1},{1,0},{2,3},{3,2},{4,5},{5,4},{6,7},{7,6},{8,9},{9,8},{10,11... | collective-permute-start | bytes 221192 | tf_op jit(solution)/shard_map/ppermute | solution.py:824
  28.2 4.4 %collective-permute-start.9 = (f32[144,128]{1,0:T(8,128)S(1)}, f32[144,128]{1,0:T(8,128)S(1)}, u32[]{:S(2)}, u32[]{:S(2)}) collective-permute-start(f32[144,128]{1,0:T(8,128)S(1)} %add.12), channel_id=1, source_target_pairs={{0,2},{2,0},{1,3},{3,1},{4,6},{6,4},{5,7},{7,5},{8,10},{10,8},{9,1... | collective-permute-start | bytes 221192 | tf_op jit(solution)/shard_map/ppermute | solution.py:824
  32.6 8.0 %collective-permute-start.10 = (f32[144,128]{1,0:T(8,128)S(1)}, f32[144,128]{1,0:T(8,128)S(1)}, u32[]{:S(2)}, u32[]{:S(2)}) collective-permute-start(f32[144,128]{1,0:T(8,128)S(1)} %add.13), channel_id=1, source_target_pairs={{0,4},{4,0},{8,12},{12,8},{16,20},{20,16},{24,28},{28,24},{1,5},{5... | collective-permute-start | bytes 221192 | tf_op jit(solution)/shard_map/ppermute | solution.py:824
  40.6 4.1 %collective-permute-start.11 = (bf16[144,128]{1,0:T(8,128)(2,1)S(1)}, bf16[144,128]{1,0:T(8,128)(2,1)S(1)}, u32[]{:S(2)}, u32[]{:S(2)}) collective-permute-start(bf16[144,128]{1,0:T(8,128)(2,1)S(1)} %add_convert_fusion.1), channel_id=1, source_target_pairs={{0,8},{4,12},{8,0},{12,4},{16,24},{20,28},{24,16},{28,20},{1,9},{5... | collective-permute-start | bytes 110600 | tf_op jit(solution)/shard_map/ppermute | solution.py:824
  44.7 5.1 %collective-permute-start.12 = (bf16[144,128]{1,0:T(8,128)(2,1)S(1)}, bf16[144,128]{1,0:T(8,128)(2,1)S(1)}, u32[]{:S(2)}, u32[]{:S(2)}) collective-permute-start(bf16[144,128]{1,0:T(8,128)(2,1)S(1)} %add_convert_fusion.mine), channel_id=1, source_target_pairs={{0,16},{4,20},{8,24},{12,28},{16,0},{20,4},{24,8},{28,12},{1,17},{... | collective-permute-start | bytes 110600 | tf_op jit(solution)/shard_map/ppermute | solution.py:824

commit v20 on v19

--- a/solution.py
+++ b/solution.py
@@ -526,7 +526,7 @@
             moved[c, :, part] = result * seen_halo if t == tiles else result
         return at_up + n_up, at_down + n_down
 
-    lax.fori_loop(0, chans, warp, (jnp.int32(0), jnp.int32(0)), unroll=8)
+    lax.fori_loop(0, chans, warp, (jnp.int32(0), jnp.int32(0)), unroll=16)
     chunk = 16
     for r in range(0, tall, chunk):
         for part in tiles_of(width):
@@ -613,7 +613,7 @@
             rows[rows_at(g * POOL + k, chans), :] = row[:, 0:span].astype(BF16)
         return 0
 
-    lax.fori_loop(0, height // POOL, group, 0, unroll=2)
+    lax.fori_loop(0, height // POOL, group, 0, unroll=4)
     for part in tiles_of(span):
         out[:, :, part] = to_planes(rows[:, part], chans)
 

time: 50.9 us -> 50.5 us (level)
  Pallas kernels: 17.5 us -> 16.6 us
  waiting for transfers between devices: 12.2 us -> 12.8 us
    pallas_call x2, Pallas kernels: 3.34 us -> 2.78 us  [predict(): call(functools.partial(predict_kernel, part), jax.ShapeDtypeStruct(shape,...]
    ppermute x5, waiting for transfers between devices: 6.98 us -> 7.55 us  [shards(): other = lax.ppermute(grads, axis, pairs)]
  transfers between devices with their start and end apart: 11 -> 11, of which waited for: 7 -> 7; matrix products, arithmetic and copies ran while one was open for 1% -> 1% of each run, Pallas kernels for 17% -> 16%
where the time goes in v20:
time: 50.5 us; the launch traced here: 50.3 us
  starting transfers between devices  18.7 us (37%)
  Pallas kernels  16.6 us (33%)
  waiting for transfers between devices  12.8 us (25%)
  between operations  1.5 us (3%)
  local copies, waits for them, and re-layouts  0.55 us (1%)
    ppermute x5, starting transfers between devices, shards(): other = lax.ppermute(grads, axis, pairs)  12.6 us
    ppermute x5, waiting for transfers between devices, shards(): other = lax.ppermute(grads, axis, pairs)  7.55 us
    pallas_call x1, Pallas kernels, main_pass(): call(main_kernel, (jax.ShapeDtypeStruct((9 * chans // 2, TILE), F32), bf(...  5.95 us
    ppermute x3, waiting for transfers between devices, swapped(): return [lax.ppermute(m, axis, p) for m, p in zip(messages, pairs)]  5.2 us
    ppermute x1, starting transfers between devices, shards(): feat_a = lax.ppermute(message, 'rows', row_pairs[0])  3.03 us
    pallas_call x1, Pallas kernels, shards(): call(functools.partial(back_kernel, ncols), (jax.ShapeDtypeStruct((full,...  2.85 us
    pallas_call x2, Pallas kernels, predict(): call(functools.partial(predict_kernel, part), jax.ShapeDtypeStruct(shape,...  2.78 us
    pallas_call x2, Pallas kernels, pack_rows(): call(functools.partial(feature_kernel, index, skip), message, [], 2, 16,...  2.66 us
  transfers between devices with their start and end apart: 11, of which 7 were waited for; matrix products, arithmetic and copies ran while one was open for 1% of the time, Pallas kernels for 16%

profile of v20, /device:TPU:0, one launch (start us, length us, event | category | flops | bytes accessed | tf_op | source)
XLA Modules:
  0.0 50.3 jit_solution(14005892575217345955)
XLA Ops:
  0.6 1.6 %shard_map.85 = (bf16[448,256]{1,0:T(8,128)(2,1)S(1)}, s32[8,128]{1,0:T(8,128)S(1)}) custom-call(s32[2,32]{1,0:T(2,128)} %bitcast.14, bf16[32,32,256]{2,1,0:T(8,128)(2,1)} %bitcast.9), custom_call_target="tpu_custom_call" | custom-call | bytes 4194304 | tf_op jit(solution)/shard_map/pallas_call | solution.py:695
  2.3 3.0 %collective-permute-start.6 = (bf16[448,256]{1,0:T(8,128)(2,1)S(1)}, bf16[448,256]{1,0:T(8,128)(2,1)S(1)}, u32[]{:S(2)}, u32[]{:S(2)}) collective-permute-start(bf16[448,256]{1,0:T(8,128)(2,1)S(1)} %get-tuple-element.114), channel_id=1, source_target_pairs={{0,4},{4,0},{8,12},{12,8},{16,20},{20,16},{24,28},{28,24},{1,5},{5... | collective-permute-start | bytes 688136 | tf_op jit(solution)/shard_map/ppermute | solution.py:752
  5.3 1.2 %shard_map.87 = bf16[256,128]{1,0:T(8,128)(2,1)S(1)} custom-call(bf16[32,32,256]{2,1,0:T(8,128)(2,1)} %bitcast.10, bf16[32,32,256]{2,1,0:T(8,128)(2,1)S(1)} %bitcast.7), custom_call_target="tpu_custom_call" | custom-call | flops 20000000000 | bytes 4194304 | tf_op jit(solution)/shard_map/pallas_call | solution.py:760
  6.6 1.6 %collective-permute-start.2 = (bf16[256,128]{1,0:T(8,128)(2,1)S(1)}, bf16[256,128]{1,0:T(8,128)(2,1)S(1)}, u32[]{:S(2)}, u32[]{:S(2)}) collective-permute-start(bf16[256,128]{1,0:T(8,128)(2,1)S(1)} %shard_map.87), channel_id=1, source_target_pairs={{0,2},{2,0},{1,3},{3,1},{4,6},{6,4},{5,7},{7,5},{8,10},{10,8},{9,1... | collective-permute-start | bytes 196616 | tf_op jit(solution)/shard_map/ppermute | solution.py:688
  8.1 1.0 %shard_map.88 = bf16[448,256]{1,0:T(8,128)(2,1)S(1)} custom-call(s32[2,32]{1,0:T(2,128)S(1)} %bitcast.15, bf16[32,32,256]{2,1,0:T(8,128)(2,1)S(1)} %bitcast.11), custom_call_target="tpu_custom_call" | custom-call | bytes 4194304 | tf_op jit(solution)/shard_map/pallas_call | solution.py:695
  9.4 1.5 %collective-permute-done.2.rest_0_ = bf16[256,128]{1,0:T(8,128)(2,1)S(1)} collective-permute-done((bf16[256,128]{1,0:T(8,128)(2,1)S(1)}, bf16[256,128]{1,0:T(8,128)(2,1)S(1)}, u32[]{:S(2)}, u32[]{:S(2)}) %collective-permute-start.2) | collective-permute-done | bytes 65568 | tf_op jit(solution)/shard_map/ppermute | solution.py:688
  11.1 0.7 %collective-permute-start.5 = (bf16[288,256]{1,0:T(8,128)(2,1)S(1)}, bf16[288,256]{1,0:T(8,128)(2,1)S(1)}, u32[]{:S(2)}, u32[]{:S(2)}) collective-permute-start(bf16[288,256]{1,0:T(8,128)(2,1)S(1)} %get-tuple-element.113), channel_id=1, source_target_pairs={{4,8},{12,16},{20,24},{8,4},{16,12},{24,20},{5,9},{13,17},{21,25},... | collective-permute-start | bytes 442376 | tf_op jit(solution)/shard_map/ppermute | solution.py:688
  11.7 0.7 %collective-permute-start.7 = (bf16[448,256]{1,0:T(8,128)(2,1)S(1)}, bf16[448,256]{1,0:T(8,128)(2,1)S(1)}, u32[]{:S(2)}, u32[]{:S(2)}) collective-permute-start(bf16[448,256]{1,0:T(8,128)(2,1)S(1)} %shard_map.88), channel_id=1, source_target_pairs={{4,8},{12,16},{20,24},{8,4},{16,12},{24,20},{5,9},{13,17},{21,25},... | collective-permute-start | bytes 688136 | tf_op jit(solution)/shard_map/ppermute | solution.py:773
  12.4 3.7 %collective-permute-done.4.msg_a = bf16[288,256]{1,0:T(8,128)(2,1)S(1)} collective-permute-done((bf16[288,256]{1,0:T(8,128)(2,1)S(1)}, bf16[288,256]{1,0:T(8,128)(2,1)S(1)}, u32[]{:S(2)}, u32[]{:S(2)}) %collective-permute-start.4) | collective-permute-done | bytes 147488 | tf_op jit(solution)/shard_map/ppermute | solution.py:688
  17.4 2.8 %shard_map.90 = (f32[1024,256]{1,0:T(8,128)S(1)}, bf16[1344,384]{1,0:T(8,128)(2,1)S(1)}, bf16[1344,384]{1,0:T(8,128)(2,1)S(1)}, bf16[1344,384]{1,0:T(8,128)(2,1)...) custom-call(bf16[1024,256]{1,0:T(8,128)(2,1)S(1)} %shard_map.86.cot_, ...), custom_call_target="tpu_custom_call" | custom-call | flops 8000000000 | bytes 4194304 | tf_op jit(solution)/shard_map/pallas_call | solution.py:784
  20.2 6.2 %conditional.1 = ((f32[144,128]{1,0:T(8,128)S(1)}, bf16[1088,384]{1,0:T(8,128)(2,1)S(1)})) conditional(s32[]{:T(128)} %bitcast.5, (s32[2,32]{1,0:T(2,128)S(1)}, bf16[32,32,256]{2,1,0:T(8,128)(2,1)S(1)}, bf16[448,256]{1,0:T(8,128)(2,1)S(1)}, bf16[448,256]{1,0:T(8,128)(2,1)S(1)}, bf16[32,96,128]{2,1,0:T(8,128)(2,1)S(1)}, ...), branch_computations={%region_0.0_spmd, %region_1.0_spmd} | conditional | flops 10001703936 | bytes 15859800 | solution.py:807
  20.2 6.0 %branch_1_fun.1 = (f32[144,128]{1,0:T(8,128)S(1)}, bf16[1088,384]{1,0:T(8,128)(2,1)S(1)}) custom-call(s32[2,32]{1,0:T(2,128)S(1)} %get-tuple-element.55.shifts, bf16[32,32,256]{2,1,0:T(8,128)(2,1)S(1)} %get-tuple-element.56.feat, bf16[448,256]{1,0:T(8,128)(2,1)S(1)} %get-tuple-element.57.feat_a, bf16[448,256]{1,0:T(8,128)(2,1)S(1)} %get-tuple-element.58.feat_b, ...), custom_call_target="tpu_custom_call" | custom-call | flops 10000000000 | bytes 4194304 | tf_op jit(solution)/shard_map/cond/branch_1_fun/pallas_call | solution.py:713
  26.5 1.3 %collective-permute-done.8 = f32[144,128]{1,0:T(8,128)S(1)} collective-permute-done((f32[144,128]{1,0:T(8,128)S(1)}, f32[144,128]{1,0:T(8,128)S(1)}, u32[]{:S(2)}, u32[]{:S(2)}) %collective-permute-start.8) | collective-permute-done | bytes 73760 | tf_op jit(solution)/shard_map/ppermute | solution.py:824
  27.8 1.6 %collective-permute-start.9 = (f32[144,128]{1,0:T(8,128)S(1)}, f32[144,128]{1,0:T(8,128)S(1)}, u32[]{:S(2)}, u32[]{:S(2)}) collective-permute-start(f32[144,128]{1,0:T(8,128)S(1)} %add.12), channel_id=1, source_target_pairs={{0,2},{2,0},{1,3},{3,1},{4,6},{6,4},{5,7},{7,5},{8,10},{10,8},{9,1... | collective-permute-start | bytes 221192 | tf_op jit(solution)/shard_map/ppermute | solution.py:824
  29.3 1.4 %shard_map.91.rest_0_ = bf16[32,32,256]{2,1,0:T(8,128)(2,1)} custom-call(bf16[1088,384]{1,0:T(8,128)(2,1)S(1)} %get-tuple-element.133.blended, bf16[384,192]{1,0:T(8,128)(2,1)S(1)} %get-tuple-element.130.bands), custom_call_target="tpu_custom_call" | custom-call | flops 1000000000 | bytes 4194304 | tf_op jit(solution)/shard_map/pallas_call | solution.py:666
  30.7 1.5 %collective-permute-done.9 = f32[144,128]{1,0:T(8,128)S(1)} collective-permute-done((f32[144,128]{1,0:T(8,128)S(1)}, f32[144,128]{1,0:T(8,128)S(1)}, u32[]{:S(2)}, u32[]{:S(2)}) %collective-permute-start.9) | collective-permute-done | bytes 73760 | tf_op jit(solution)/shard_map/ppermute | solution.py:824
  32.2 5.7 %collective-permute-start.10 = (f32[144,128]{1,0:T(8,128)S(1)}, f32[144,128]{1,0:T(8,128)S(1)}, u32[]{:S(2)}, u32[]{:S(2)}) collective-permute-start(f32[144,128]{1,0:T(8,128)S(1)} %add.13), channel_id=1, source_target_pairs={{0,4},{4,0},{8,12},{12,8},{16,20},{20,16},{24,28},{28,24},{1,5},{5... | collective-permute-start | bytes 221192 | tf_op jit(solution)/shard_map/ppermute | solution.py:824
  37.9 1.4 %shard_map.92 = bf16[32,32,256]{2,1,0:T(8,128)(2,1)} custom-call(bf16[1088,384]{1,0:T(8,128)(2,1)S(1)} %get-tuple-element.133.blended, bf16[384,192]{1,0:T(8,128)(2,1)S(1)} %get-tuple-element.130.bands, bf16[32,32,256]{2,1,0:T(8,128)(2,1)} %shard_map.91.rest_0_), custom_call_target="tpu_custom_call", output_to_operand_aliasing={{}: (2, {})} | custom-call | flops 1000000000 | bytes 4194304 | tf_op jit(solution)/shard_map/pallas_call | solution.py:666
  39.3 0.9 %collective-permute-done.10 = f32[144,128]{1,0:T(8,128)S(1)} collective-permute-done((f32[144,128]{1,0:T(8,128)S(1)}, f32[144,128]{1,0:T(8,128)S(1)}, u32[]{:S(2)}, u32[]{:S(2)}) %collective-permute-start.10) | collective-permute-done | bytes 73760 | tf_op jit(solution)/shard_map/ppermute | solution.py:824
  40.2 2.1 %collective-permute-start.11 = (bf16[144,128]{1,0:T(8,128)(2,1)S(1)}, bf16[144,128]{1,0:T(8,128)(2,1)S(1)}, u32[]{:S(2)}, u32[]{:S(2)}) collective-permute-start(bf16[144,128]{1,0:T(8,128)(2,1)S(1)} %add_convert_fusion.1), channel_id=1, source_target_pairs={{0,8},{4,12},{8,0},{12,4},{16,24},{20,28},{24,16},{28,20},{1,9},{5... | collective-permute-start | bytes 110600 | tf_op jit(solution)/shard_map/ppermute | solution.py:824
  42.4 1.9 %collective-permute-done.11 = bf16[144,128]{1,0:T(8,128)(2,1)S(1)} collective-permute-done((bf16[144,128]{1,0:T(8,128)(2,1)S(1)}, bf16[144,128]{1,0:T(8,128)(2,1)S(1)}, u32[]{:S(2)}, u32[]{:S(2)}) %collective-permute-start.11) | collective-permute-done | bytes 36896 | tf_op jit(solution)/shard_map/ppermute | solution.py:824
  44.3 3.2 %collective-permute-start.12 = (bf16[144,128]{1,0:T(8,128)(2,1)S(1)}, bf16[144,128]{1,0:T(8,128)(2,1)S(1)}, u32[]{:S(2)}, u32[]{:S(2)}) collective-permute-start(bf16[144,128]{1,0:T(8,128)(2,1)S(1)} %add_convert_fusion.mine), channel_id=1, source_target_pairs={{0,16},{4,20},{8,24},{12,28},{16,0},{20,4},{24,8},{28,12},{1,17},{... | collective-permute-start | bytes 110600 | tf_op jit(solution)/shard_map/ppermute | solution.py:824
  47.5 1.9 %collective-permute-done.12.other = bf16[144,128]{1,0:T(8,128)(2,1)S(1)} collective-permute-done((bf16[144,128]{1,0:T(8,128)(2,1)S(1)}, bf16[144,128]{1,0:T(8,128)(2,1)S(1)}, u32[]{:S(2)}, u32[]{:S(2)}) %collective-permute-start.12) | collective-permute-done | bytes 36896 | tf_op jit(solution)/shard_map/ppermute | solution.py:824
  49.4 0.9 %shard_map.93 = (f32[9,32,32]{2,1,0:T(8,128)}, f32[9,32,32]{2,1,0:T(8,128)}) custom-call(bf16[144,128]{1,0:T(8,128)(2,1)S(1)} %add_convert_fusion.mine, bf16[144,128]{1,0:T(8,128)(2,1)S(1)} %collective-permute-done.12.other), custom_call_target="tpu_custom_call" | custom-call | bytes 4194304 | tf_op jit(solution)/shard_map/pallas_call | solution.py:836
  (27 shorter events, 1.0 us)
Async XLA Ops:
  0.6 4.7 %copy-start = (bf16[1,32,32,256]{3,2,1,0:T(8,128)(2,1)S(1)}, bf16[1,32,32,256]{3,2,1,0:T(8,128)(2,1)}, u32[]{:S(2)}) copy-start(bf16[1,32,32,256]{3,2,1,0:T(8,128)(2,1)} %param.13) | copy-start | bytes 1572868
  2.3 5.8 %copy-start.4 = (bf16[1,32,32,256]{3,2,1,0:T(8,128)(2,1)S(1)}, bf16[1,32,32,256]{3,2,1,0:T(8,128)(2,1)}, u32[]{:S(2)}) copy-start(bf16[1,32,32,256]{3,2,1,0:T(8,128)(2,1)} %param.8) | copy-start | bytes 1572868
  2.3 5.8 %copy-start.5 = (s32[1,32,2]{1,2,0:T(2,128)S(1)}, s32[1,32,2]{1,2,0:T(2,128)}, u32[]{:S(2)}) copy-start(s32[1,32,2]{1,2,0:T(2,128)} %param.9) | copy-start | bytes 772
  2.3 15.0 %collective-permute-start.6 = (bf16[448,256]{1,0:T(8,128)(2,1)S(1)}, bf16[448,256]{1,0:T(8,128)(2,1)S(1)}, u32[]{:S(2)}, u32[]{:S(2)}) collective-permute-start(bf16[448,256]{1,0:T(8,128)(2,1)S(1)} %get-tuple-element.114), channel_id=1, source_target_pairs={{0,4},{4,0},{8,12},{12,8},{16,20},{20,16},{24,28},{28,24},{1,5},{5... | collective-permute-start | bytes 688136 | tf_op jit(solution)/shard_map/ppermute | solution.py:752
  6.6 4.3 %collective-permute-start.2 = (bf16[256,128]{1,0:T(8,128)(2,1)S(1)}, bf16[256,128]{1,0:T(8,128)(2,1)S(1)}, u32[]{:S(2)}, u32[]{:S(2)}) collective-permute-start(bf16[256,128]{1,0:T(8,128)(2,1)S(1)} %shard_map.87), channel_id=1, source_target_pairs={{0,2},{2,0},{1,3},{3,1},{4,6},{6,4},{5,7},{7,5},{8,10},{10,8},{9,1... | collective-permute-start | bytes 196616 | tf_op jit(solution)/shard_map/ppermute | solution.py:688
  8.1 1.2 %collective-permute-start.3 = (s32[8,128]{1,0:T(8,128)S(1)}, s32[8,128]{1,0:T(8,128)S(1)}, u32[]{:S(2)}, u32[]{:S(2)}) collective-permute-start(s32[8,128]{1,0:T(8,128)S(1)} %get-tuple-element.107), channel_id=1, source_target_pairs={{0,1},{1,0},{2,3},{3,2},{4,5},{5,4},{6,7},{7,6},{8,9},{9,8},{10,11... | collective-permute-start | bytes 12296 | tf_op jit(solution)/shard_map/ppermute | solution.py:755
  9.4 8.0 %copy-start.1 = (bf16[9,32,32]{2,1,0:T(8,128)(2,1)S(1)}, bf16[9,32,32]{2,1,0:T(8,128)(2,1)}, u32[]{:S(2)}) copy-start(bf16[9,32,32]{2,1,0:T(8,128)(2,1)} %rest_1_.1) | copy-start | bytes 55300
  9.4 8.0 %copy-start.2 = (bf16[9,32,32]{2,1,0:T(8,128)(2,1)S(1)}, bf16[9,32,32]{2,1,0:T(8,128)(2,1)}, u32[]{:S(2)}) copy-start(bf16[9,32,32]{2,1,0:T(8,128)(2,1)} %rest_2_.1) | copy-start | bytes 55300
  9.4 8.0 %copy-start.3 = (bf16[9,32,32]{2,1,0:T(8,128)(2,1)S(1)}, bf16[9,32,32]{2,1,0:T(8,128)(2,1)}, u32[]{:S(2)}) copy-start(bf16[9,32,32]{2,1,0:T(8,128)(2,1)} %rest_3_.1) | copy-start | bytes 55300
  10.9 5.2 %collective-permute-start.4 = (bf16[288,256]{1,0:T(8,128)(2,1)S(1)}, bf16[288,256]{1,0:T(8,128)(2,1)S(1)}, u32[]{:S(2)}, u32[]{:S(2)}) collective-permute-start(bf16[288,256]{1,0:T(8,128)(2,1)S(1)} %get-tuple-element.109), channel_id=1, source_target_pairs={{0,4},{4,0},{8,12},{12,8},{16,20},{20,16},{24,28},{28,24},{1,5},{5... | collective-permute-start | bytes 442376 | tf_op jit(solution)/shard_map/ppermute | solution.py:688
  11.1 6.2 %collective-permute-start.5 = (bf16[288,256]{1,0:T(8,128)(2,1)S(1)}, bf16[288,256]{1,0:T(8,128)(2,1)S(1)}, u32[]{:S(2)}, u32[]{:S(2)}) collective-permute-start(bf16[288,256]{1,0:T(8,128)(2,1)S(1)} %get-tuple-element.113), channel_id=1, source_target_pairs={{4,8},{12,16},{20,24},{8,4},{16,12},{24,20},{5,9},{13,17},{21,25},... | collective-permute-start | bytes 442376 | tf_op jit(solution)/shard_map/ppermute | solution.py:688
  11.7 8.5 %collective-permute-start.7 = (bf16[448,256]{1,0:T(8,128)(2,1)S(1)}, bf16[448,256]{1,0:T(8,128)(2,1)S(1)}, u32[]{:S(2)}, u32[]{:S(2)}) collective-permute-start(bf16[448,256]{1,0:T(8,128)(2,1)S(1)} %shard_map.88), channel_id=1, source_target_pairs={{4,8},{12,16},{20,24},{8,4},{16,12},{24,20},{5,9},{13,17},{21,25},... | collective-permute-start | bytes 688136 | tf_op jit(solution)/shard_map/ppermute | solution.py:773
  26.4 1.3 %collective-permute-start.8 = (f32[144,128]{1,0:T(8,128)S(1)}, f32[144,128]{1,0:T(8,128)S(1)}, u32[]{:S(2)}, u32[]{:S(2)}) collective-permute-start(f32[144,128]{1,0:T(8,128)S(1)} %get-tuple-element.126), channel_id=1, source_target_pairs={{0,1},{1,0},{2,3},{3,2},{4,5},{5,4},{6,7},{7,6},{8,9},{9,8},{10,11... | collective-permute-start | bytes 221192 | tf_op jit(solution)/shard_map/ppermute | solution.py:824
  27.8 4.4 %collective-permute-start.9 = (f32[144,128]{1,0:T(8,128)S(1)}, f32[144,128]{1,0:T(8,128)S(1)}, u32[]{:S(2)}, u32[]{:S(2)}) collective-permute-start(f32[144,128]{1,0:T(8,128)S(1)} %add.12), channel_id=1, source_target_pairs={{0,2},{2,0},{1,3},{3,1},{4,6},{6,4},{5,7},{7,5},{8,10},{10,8},{9,1... | collective-permute-start | bytes 221192 | tf_op jit(solution)/shard_map/ppermute | solution.py:824
  32.2 8.0 %collective-permute-start.10 = (f32[144,128]{1,0:T(8,128)S(1)}, f32[144,128]{1,0:T(8,128)S(1)}, u32[]{:S(2)}, u32[]{:S(2)}) collective-permute-start(f32[144,128]{1,0:T(8,128)S(1)} %add.13), channel_id=1, source_target_pairs={{0,4},{4,0},{8,12},{12,8},{16,20},{20,16},{24,28},{28,24},{1,5},{5... | collective-permute-start | bytes 221192 | tf_op jit(solution)/shard_map/ppermute | solution.py:824
  40.2 4.1 %collective-permute-start.11 = (bf16[144,128]{1,0:T(8,128)(2,1)S(1)}, bf16[144,128]{1,0:T(8,128)(2,1)S(1)}, u32[]{:S(2)}, u32[]{:S(2)}) collective-permute-start(bf16[144,128]{1,0:T(8,128)(2,1)S(1)} %add_convert_fusion.1), channel_id=1, source_target_pairs={{0,8},{4,12},{8,0},{12,4},{16,24},{20,28},{24,16},{28,20},{1,9},{5... | collective-permute-start | bytes 110600 | tf_op jit(solution)/shard_map/ppermute | solution.py:824
  44.3 5.1 %collective-permute-start.12 = (bf16[144,128]{1,0:T(8,128)(2,1)S(1)}, bf16[144,128]{1,0:T(8,128)(2,1)S(1)}, u32[]{:S(2)}, u32[]{:S(2)}) collective-permute-start(bf16[144,128]{1,0:T(8,128)(2,1)S(1)} %add_convert_fusion.mine), channel_id=1, source_target_pairs={{0,16},{4,20},{8,24},{12,28},{16,0},{20,4},{24,8},{28,12},{1,17},{... | collective-permute-start | bytes 110600 | tf_op jit(solution)/shard_map/ppermute | solution.py:824
